TPU v7x, 32 devices: a whole 2x2x4 slice. The times are simulated.
32 devices in a mesh: seq: 16 (over z, y, x), tp: 2 (over core).
Axes of the slice: x: 2, y: 2, z: 4, core: 2. Of those that a mesh axis runs over, the one named last changes fastest.
Arguments:
- queries: bfloat16 [4096, 1024], P('seq', 'tp'), may hold values from -10 to 10
- key_vectors: bfloat16 [4096, 1024], P('seq', 'tp'), may hold values from -4 to 4
- value_vectors: bfloat16 [4096, 1024], P('seq', 'tp'), may hold values from -10 to 10
- out_grad: bfloat16 [4096, 1024], P('seq', 'tp'), may hold values from -6 to 6
Outputs:
- normed_out: bfloat16 [4096, 1024], P('seq', 'tp')
- query_grad: bfloat16 [4096, 1024], P('seq', 'tp')
- key_grad: bfloat16 [4096, 1024], P('seq', 'tp')
- value_grad: bfloat16 [4096, 1024], P('seq', 'tp')
All inputs are finite; a program needn't handle non-finite values.
Results may differ from a plain program's by a relative error of at most 0.017.
Values may be sent and summed in bfloat16 or wider, within the bound.
No kernel may reach another device: no remote copies, remote signals or barrier semaphores. Data moves between devices by JAX's collectives and lax.ppermute only.
A program may use at most 128 MiB of HBM per device.

v0:
```python
import jax
import jax.numpy as jnp
from jax import lax
from jax.sharding import PartitionSpec as P

DH = 128
HEADS_DEV = 4


EPSILON = 1e-06


def prefix(shard, axis, combine, identity):
    size, index = (lax.axis_size(axis), lax.axis_index(axis))
    everything = lax.all_gather(shard.astype(jnp.bfloat16), axis)
    start = jnp.broadcast_to(jnp.asarray(identity, shard.dtype), shard.shape)

    def step(k, before):
        at = size - 1 - k
        reached = at > index
        new = combine(before, everything[at].astype(shard.dtype))
        return jnp.where(reached, new, before)

    return lax.fori_loop(0, size, step, start)


def add_states(earlier, later):
    return earlier + later


def body(queries, key_vectors, value_vectors, out_grad):
    token_count = queries.shape[0]
    feature_count = queries.shape[1]
    all_features = feature_count * lax.axis_size("tp")
    head_shape = (token_count, HEADS_DEV, DH)
    query_heads = queries.reshape(head_shape)
    key_heads = key_vectors.reshape(head_shape)
    value_heads = value_vectors.reshape(head_shape)
    empty_state = jnp.zeros((HEADS_DEV, DH, DH), jnp.float32)
    causal = jnp.arange(token_count)[:, None] >= jnp.arange(token_count)[None, :]
    own_index = lax.axis_index("seq")
    group_state = jnp.einsum(
        "thd,the->hde", key_heads, value_heads, preferred_element_type=jnp.float32
    ).astype(jnp.bfloat16)
    piece = lax.all_gather(group_state[None], "seq", axis=0, tiled=True)
    group_index = jnp.arange(piece.shape[0], dtype=jnp.int32)
    earlier = (group_index < own_index).astype(jnp.bfloat16)
    prefix_state = jnp.einsum("n,nhde->hde", earlier, piece, preferred_element_type=jnp.float32)
    prefix_low = prefix_state.astype(jnp.bfloat16)
    raw_scores = jnp.einsum(
        "thd,shd->hts", query_heads, key_heads, preferred_element_type=jnp.float32
    )
    scores = jnp.where(causal[None], raw_scores, jnp.zeros_like(raw_scores)).astype(jnp.bfloat16)
    mixed = jnp.einsum("hts,she->the", scores, value_heads, preferred_element_type=jnp.float32)
    mixed = mixed + jnp.einsum(
        "thd,hde->the", query_heads, prefix_low, preferred_element_type=jnp.float32
    )
    mixed = mixed.reshape(token_count, feature_count)
    cotangent = out_grad.astype(jnp.float32)
    square_sum = lax.psum(jnp.sum(mixed * mixed, axis=1), "tp")
    inverse = lax.rsqrt(square_sum / all_features + EPSILON)
    normed = mixed * inverse[:, None]
    cotangent_sum = lax.psum(jnp.sum(cotangent * normed, axis=1), "tp")
    projection = cotangent_sum / all_features
    normed_out = normed.astype(jnp.bfloat16)
    mixed_grad = (inverse[:, None] * (cotangent - normed * projection[:, None])).astype(
        jnp.bfloat16
    )
    mixed_grad = mixed_grad.reshape(head_shape)
    grad_term = jnp.einsum(
        "thd,the->hde", query_heads, mixed_grad, preferred_element_type=jnp.float32
    ).astype(jnp.bfloat16)
    held_grad = lax.optimization_barrier(grad_term).astype(jnp.float32)
    suffix_grad = prefix(held_grad, "seq", add_states, empty_state)
    suffix_low = suffix_grad.astype(jnp.bfloat16)
    raw_coefs = jnp.einsum(
        "the,she->hts", mixed_grad, value_heads, preferred_element_type=jnp.float32
    )
    coefs = jnp.where(causal[None], raw_coefs, jnp.zeros_like(raw_coefs)).astype(jnp.bfloat16)
    query_part = jnp.einsum("hts,shd->thd", coefs, key_heads, preferred_element_type=jnp.float32)
    query_part = query_part + jnp.einsum(
        "the,hde->thd", mixed_grad, prefix_low, preferred_element_type=jnp.float32
    )
    key_part = jnp.einsum("hts,thd->shd", coefs, query_heads, preferred_element_type=jnp.float32)
    key_part = key_part + jnp.einsum(
        "she,hde->shd", value_heads, suffix_low, preferred_element_type=jnp.float32
    )
    value_part = jnp.einsum("hts,the->she", scores, mixed_grad, preferred_element_type=jnp.float32)
    value_part = value_part + jnp.einsum(
        "shd,hde->she", key_heads, suffix_low, preferred_element_type=jnp.float32
    )
    query_grad = query_part.reshape(token_count, feature_count).astype(jnp.bfloat16)
    key_grad = key_part.reshape(token_count, feature_count).astype(jnp.bfloat16)
    value_grad = value_part.reshape(token_count, feature_count).astype(jnp.bfloat16)
    return (normed_out, query_grad, key_grad, value_grad)


def solution(mesh):
    in_specs = (P("seq", "tp"), P("seq", "tp"), P("seq", "tp"), P("seq", "tp"))
    out_specs = (P("seq", "tp"), P("seq", "tp"), P("seq", "tp"), P("seq", "tp"))
    return jax.shard_map(body, mesh=mesh, in_specs=in_specs, out_specs=out_specs, check_vma=False)
```

profile of v0, /device:TPU:0, one launch (start us, length us, event | category | flops | bytes accessed | tf_op | source)
XLA Modules:
  0.0 171.0 jit_solution(1862660001108956131)
XLA Ops:
  7.2 1.1 copy.105
  8.4 1.8 %convolution_convert_fusion.1 = bf16[4,128,128]{2,1,0:T(8,128)(2,1)} fusion(bf16[256,4,128]{0,2,1:T(8,128)(2,1)S(1)} %bitcast.118, bf16[256,512]{1,0:T(8,128)(2,1)} %param.8), kind=kOutput, calls=%fused_computation.21 | convolution fusion | flops 33619968 | bytes 655360 | tf_op jit(solution)/shard_map/thd,the->hde/dot_general | solution.py:42
  10.3 1.2 fusion.2
  11.6 0.3 convolution_bitcast_fusion.5
  11.9 62.9 %all-gather.5.cloned.1.call-done = bf16[64,128,128]{2,1,0:T(8,128)(2,1)} async-done(((bf16[4,128,128]{2,1,0:T(8,128)(2,1)}), bf16[64,128,128]{2,1,0:T(8,128)(2,1)}) %all-gather.5.cloned.1.call-update) | async-done | bytes 2097168 | tf_op jit(solution)/shard_map/all_gather | solution.py:45
  74.8 2.9 %fusion = f32[1,4,128,128]{3,0,2,1:T(1,128)S(1)} fusion(bf16[16,4,128,128]{3,2,1,0:T(8,128)(2,1)} %bitcast.122, s32[]{:T(128)} %axis_index.19), kind=kOutput, calls=%fused_computation.1 | convolution fusion | flops 2097168 | bytes 2359300 | tf_op jit(solution)/shard_map/n,nhde->hde/dot_general | solution.py:48
  78.0 2.5 %psum.14 = f32[256]{0:T(256)S(1)} all-reduce(f32[256]{0:T(256)S(1)} %get-tuple-element.152), channel_id=1, replica_groups=mesh['seq'=16,'tp'=2] {'tp'}, use_global_device_ids=true, to_apply=%region_1.2 | all-reduce | flops 256 | bytes 2048 | tf_op jit(solution)/shard_map/psum | solution.py:60
  80.9 2.5 %psum.15 = f32[256]{0:T(256)S(1)} all-reduce(f32[256]{0:T(256)S(1)} %fusion.11), channel_id=1, replica_groups=mesh['seq'=16,'tp'=2] {'tp'}, use_global_device_ids=true, to_apply=%region_3.4 | all-reduce | flops 256 | bytes 2048 | tf_op jit(solution)/shard_map/psum | solution.py:63
  83.4 0.9 fusion.13
  84.7 0.8 copy.46
  85.5 0.3 fusion.3
  86.3 0.8 copy.51
  87.7 57.3 %all-gather.7.cloned.1.call-done = bf16[64,128,128]{2,1,0:T(8,128)(2,1)} async-done(((bf16[4,128,128]{2,1,0:T(8,128)(2,1)}), bf16[64,128,128]{2,1,0:T(8,128)(2,1)}) %all-gather.7.cloned.1.call-update) | async-done | bytes 2097168 | tf_op jit(solution)/shard_map/all_gather | solution.py:15
  145.0 17.0 %while.16 = (s32[]{:T(128)}, f32[4,128,128]{2,1,0:T(8,128)S(1)}, s32[]{:T(128)}, bf16[16,4,128,128]{3,2,1,0:T(8,128)(2,1)}, s32[]{:T(128)}, /*index=5*/s32[]{:T(128)}, s32[]{:T(128)}, s32[]{:T(128)}) while((s32[]{:T(128)}, f32[4,128,128]{2,1,0:T(8,128)S(1)}, s32[]{:T(128)}, bf16[16,4,128,128]{3,2,1,0:T(8,128)(2,1)}, s32[]{:T(128)}, ...), condition=%wide.region_5.6_spmd.clone, body=%wide.region_4.5_spmd.clone.sunk | while | flops 262152 | bytes 655523 | solution.py:24
  145.0 1.0 add_select_fusion.2
  146.0 1.0 add_select_fusion.2
  147.1 1.0 add_select_fusion.2
  148.2 1.0 add_select_fusion.2
  149.2 1.0 add_select_fusion.2
  150.3 1.0 add_select_fusion.2
  151.4 1.0 add_select_fusion.2
  152.4 1.0 add_select_fusion.2
  153.5 1.0 add_select_fusion.2
  154.6 1.0 add_select_fusion.2
  155.6 1.0 add_select_fusion.2
  156.7 1.0 add_select_fusion.2
  157.7 1.0 add_select_fusion.2
  158.8 1.0 add_select_fusion.2
  159.9 1.0 add_select_fusion.2
  160.9 1.0 add_select_fusion.2
  162.3 0.8 copy.53
  163.3 0.8 copy.52
  (27 shorter events, 2.7 us)
Async XLA Ops:
  7.2 3.1 %copy-start = (bf16[256,512]{1,0:T(8,128)(2,1)S(1)}, bf16[256,512]{1,0:T(8,128)(2,1)}, u32[]{:S(2)}) copy-start(bf16[256,512]{1,0:T(8,128)(2,1)} %param.6) | copy-start | bytes 786436
  7.2 4.4 %copy-start.1 = (bf16[256,512]{1,0:T(8,128)(2,1)S(1)}, bf16[256,512]{1,0:T(8,128)(2,1)}, u32[]{:S(2)}) copy-start(bf16[256,512]{1,0:T(8,128)(2,1)} %param.8) | copy-start | bytes 786436
  7.2 67.6 %all-gather.5.cloned.1.call-start = ((), (), s32[]{:S(2)}) async-start(), calls=%async_computation | async-start | bytes 2228224 | tf_op jit(solution)/shard_map/all_gather | solution.py:45
  10.2 134.7 %all-gather.7.cloned.1.call-start = ((), (), s32[]{:S(2)}) async-start(), calls=%async_computation.1 | async-start | bytes 2228224 | tf_op jit(solution)/shard_map/all_gather | solution.py:15
  74.8 5.9 %copy-start.2 = (bf16[256,512]{1,0:T(8,128)(2,1)S(1)}, bf16[256,512]{1,0:T(8,128)(2,1)}, u32[]{:S(2)}) copy-start(bf16[256,512]{1,0:T(8,128)(2,1)} %param.9) | copy-start | bytes 786436
  87.4 74.6 %copy-start.3 = (bf16[256,512]{1,0:T(8,128)(2,1)S(1)}, bf16[256,512]{1,0:T(8,128)(2,1)}, u32[]{:S(2)}) copy-start(bf16[256,512]{1,0:T(8,128)(2,1)} %param.7) | copy-start | bytes 786436
Sparse Core Ops, SparseCore 0:
  11.4 63.3 all-gather.4
  85.6 59.3 all-gather.6
where the time goes:
time: 172 us; the launch traced here: 171 us
  waiting for transfers between devices  120 us (70%)
  other arithmetic  17.7 us (10%)
  between operations  14.2 us (8%)
  matrix products  8.65 us (5%)
  blocking collectives  4.94 us (3%)
  local copies, waits for them, and re-layouts  4.79 us (3%)
    all_gather x1, waiting for transfers between devices, body(): piece = lax.all_gather(group_state[None], 'seq', axis=0, tiled=True)  62.9 us
    all_gather x1, waiting for transfers between devices, prefix(): everything = lax.all_gather(shard.astype(jnp.bfloat16), axis)  57.3 us
    select_n x16, other arithmetic, step(): return jnp.where(reached, new, before)  16.6 us
  transfers between devices with their start and end apart: 2, of which 2 were waited for; matrix products, arithmetic and copies ran while one was open for 2% of the time, Pallas kernels for 0%

commit v1 on v0

v1 whole, which is shorter than its diff:
```python
import jax
import jax.numpy as jnp
from jax import lax
from jax.sharding import PartitionSpec as P

DH = 128
EPSILON = 1e-06


def exclusive_sum(state, before):
    size = lax.axis_size("seq")
    pieces = state.reshape(size, -1, DH)
    pieces = lax.all_to_all(pieces, "seq", 0, 0, tiled=True)
    index = jnp.arange(size)
    if before:
        mask = index[None, :] < index[:, None]
    else:
        mask = index[None, :] > index[:, None]
    sums = jnp.einsum("cj,jrd->crd", mask.astype(jnp.bfloat16), pieces, preferred_element_type=jnp.float32)
    sums = lax.all_to_all(sums.astype(jnp.bfloat16), "seq", 0, 0, tiled=True)
    return sums.reshape(state.shape)


def body(queries, key_vectors, value_vectors, out_grad):
    token_count, feature_count = queries.shape
    heads = feature_count // DH
    all_features = feature_count * lax.axis_size("tp")
    head_shape = (token_count, heads, DH)
    query_heads = queries.reshape(head_shape)
    key_heads = key_vectors.reshape(head_shape)
    value_heads = value_vectors.reshape(head_shape)
    causal = jnp.arange(token_count)[:, None] >= jnp.arange(token_count)[None, :]
    group_state = jnp.einsum(
        "thd,the->hde", key_heads, value_heads, preferred_element_type=jnp.float32
    ).astype(jnp.bfloat16)
    prefix_low = exclusive_sum(group_state, True)
    raw_scores = jnp.einsum(
        "thd,shd->hts", query_heads, key_heads, preferred_element_type=jnp.float32
    )
    scores = jnp.where(causal[None], raw_scores, jnp.zeros_like(raw_scores)).astype(jnp.bfloat16)
    mixed = jnp.einsum("hts,she->the", scores, value_heads, preferred_element_type=jnp.float32)
    mixed = mixed + jnp.einsum(
        "thd,hde->the", query_heads, prefix_low, preferred_element_type=jnp.float32
    )
    mixed = mixed.reshape(token_count, feature_count)
    cotangent = out_grad.astype(jnp.float32)
    sums = jnp.stack([jnp.sum(mixed * mixed, axis=1), jnp.sum(cotangent * mixed, axis=1)])
    sums = lax.psum(sums, "tp")
    inverse = lax.rsqrt(sums[0] / all_features + EPSILON)
    normed = mixed * inverse[:, None]
    projection = inverse * sums[1] / all_features
    normed_out = normed.astype(jnp.bfloat16)
    mixed_grad = (inverse[:, None] * (cotangent - normed * projection[:, None])).astype(
        jnp.bfloat16
    )
    mixed_grad = mixed_grad.reshape(head_shape)
    grad_term = jnp.einsum(
        "thd,the->hde", query_heads, mixed_grad, preferred_element_type=jnp.float32
    ).astype(jnp.bfloat16)
    suffix_low = exclusive_sum(grad_term, False)
    raw_coefs = jnp.einsum(
        "the,she->hts", mixed_grad, value_heads, preferred_element_type=jnp.float32
    )
    coefs = jnp.where(causal[None], raw_coefs, jnp.zeros_like(raw_coefs)).astype(jnp.bfloat16)
    query_part = jnp.einsum("hts,shd->thd", coefs, key_heads, preferred_element_type=jnp.float32)
    query_part = query_part + jnp.einsum(
        "the,hde->thd", mixed_grad, prefix_low, preferred_element_type=jnp.float32
    )
    key_part = jnp.einsum("hts,thd->shd", coefs, query_heads, preferred_element_type=jnp.float32)
    key_part = key_part + jnp.einsum(
        "she,hde->shd", value_heads, suffix_low, preferred_element_type=jnp.float32
    )
    value_part = jnp.einsum("hts,the->she", scores, mixed_grad, preferred_element_type=jnp.float32)
    value_part = value_part + jnp.einsum(
        "shd,hde->she", key_heads, suffix_low, preferred_element_type=jnp.float32
    )
    query_grad = query_part.reshape(token_count, feature_count).astype(jnp.bfloat16)
    key_grad = key_part.reshape(token_count, feature_count).astype(jnp.bfloat16)
    value_grad = value_part.reshape(token_count, feature_count).astype(jnp.bfloat16)
    return (normed_out, query_grad, key_grad, value_grad)


def solution(mesh):
    spec = P("seq", "tp")
    return jax.shard_map(body, mesh=mesh, in_specs=(spec,) * 4, out_specs=(spec,) * 4, check_vma=False)
```

time: 172 us -> 63.6 us (0.37)
  waiting for transfers between devices: 120 us -> 27.8 us
  starting transfers between devices: 0.08 us -> 19 us
  other arithmetic: 17.7 us -> 1.07 us
  between operations: 14.2 us -> 0.83 us
  matrix products: 8.65 us -> 4.84 us
  blocking collectives: 4.94 us -> 2.47 us
  local copies, waits for them, and re-layouts: 4.79 us -> 7.06 us
    all_gather x2 -> x0, waiting for transfers between devices: 120 us -> none  [the longest x1 62.9 us: body(): piece = lax.all_gather(group_state[None], 'seq', axis=0, tiled=True)]
    all_to_all x0 -> x4, waiting for transfers between devices: none -> 27.8 us  [the longest x2 15 us: exclusive_sum(): sums = lax.all_to_all(sums.astype(jnp.bfloat16), 'seq', 0, 0, tiled=True)]
    all_to_all x0 -> x4, starting transfers between devices: none -> 19 us  [the longest x2 12 us: exclusive_sum(): pieces = lax.all_to_all(pieces, 'seq', 0, 0, tiled=True)]
    select_n x16 -> x0, other arithmetic: 16.6 us -> none  [step(): return jnp.where(reached, new, before)]
    dot_general x1 -> x2, matrix products: 2.91 us -> 0.33 us  [exclusive_sum(): jnp.einsum('cj,jrd->crd', mask.astype(jnp.bfloat16), pieces, preferred_el...]
    psum x2 -> x1, blocking collectives: 4.94 us -> 2.47 us  [body(): sums = lax.psum(sums, 'tp')]
  transfers between devices with their start and end apart: 2 -> 4, of which waited for: 2 -> 4; matrix products, arithmetic and copies ran while one was open for 2% -> 4% of each run, Pallas kernels for 0% -> 0%
where the time goes in v1:
time: 63.6 us; the launch traced here: 63.1 us
  waiting for transfers between devices  27.8 us (44%)
  starting transfers between devices  19 us (30%)
  local copies, waits for them, and re-layouts  7.06 us (11%)
  matrix products  4.84 us (8%)
  blocking collectives  2.47 us (4%)
  other arithmetic  1.07 us (2%)
  between operations  0.83 us (1%)
    all_to_all x2, waiting for transfers between devices, exclusive_sum(): sums = lax.all_to_all(sums.astype(jnp.bfloat16), 'seq', 0, 0, tiled=True)  15 us
    all_to_all x2, waiting for transfers between devices, exclusive_sum(): pieces = lax.all_to_all(pieces, 'seq', 0, 0, tiled=True)  12.9 us
    all_to_all x2, starting transfers between devices, exclusive_sum(): pieces = lax.all_to_all(pieces, 'seq', 0, 0, tiled=True)  12 us
    all_to_all x2, starting transfers between devices, exclusive_sum(): sums = lax.all_to_all(sums.astype(jnp.bfloat16), 'seq', 0, 0, tiled=True)  7.03 us
    unnamed x11, local copies, waits for them, and re-layouts  4.09 us
    psum x1, blocking collectives, body(): sums = lax.psum(sums, 'tp')  2.47 us
    convert_element_type x2, local copies, waits for them, and re-layouts, exclusive_sum(): sums = lax.all_to_all(sums.astype(jnp.bfloat16), 'seq', 0, 0, tiled=True)  1.38 us
  transfers between devices with their start and end apart: 4, of which 4 were waited for; matrix products, arithmetic and copies ran while one was open for 4% of the time, Pallas kernels for 0%

profile of v1, /device:TPU:0, one launch (start us, length us, event | category | flops | bytes accessed | tf_op | source)
XLA Modules:
  0.0 63.1 jit_solution(12261645479709025863)
XLA Ops:
  0.6 1.1 %copy.121 = bf16[256,512]{0,1:T(8,128)(2,1)S(1)} copy(bf16[256,512]{1,0:T(8,128)(2,1)} %param.5) | data formatting | bytes 524288 | tf_op jit(solution)/shard_map/reshape | solution.py:30
  1.8 0.9 %convolution_convert_fusion.1 = bf16[4,128,128]{2,1,0:T(8,128)(2,1)} fusion(bf16[256,4,128]{0,2,1:T(8,128)(2,1)S(1)} %bitcast.107, bf16[256,512]{1,0:T(8,128)(2,1)S(1)} %copy-done), kind=kOutput, calls=%fused_computation.18 | convolution fusion | flops 33619968 | bytes 655360 | tf_op jit(solution)/shard_map/thd,the->hde/dot_general | solution.py:33
  2.7 8.4 %all-to-all-start = ((bf16[16,32,128]{2,1,0:T(8,128)(2,1)}), bf16[16,32,128]{2,1,0:T(8,128)(2,1)S(1)}, u32[]{:S(2)}, u32[]{:S(2)}) async-start(bf16[16,32,128]{2,1,0:T(8,128)(2,1)} %bitcast.2), calls=%async_computation | async-start | bytes 262144 | tf_op jit(solution)/shard_map/all_to_all | solution.py:13
  11.3 0.8 %copy-done.2 = bf16[256,512]{1,0:T(8,128)(2,1)S(1)} copy-done((bf16[256,512]{1,0:T(8,128)(2,1)S(1)}, bf16[256,512]{1,0:T(8,128)(2,1)}, u32[]{:S(2)}) %copy-start.2) | copy-done | bytes 262168
  12.1 0.3 fusion
  12.5 6.5 %all-to-all-done = bf16[16,32,128]{2,1,0:T(8,128)(2,1)S(1)} async-done(((bf16[16,32,128]{2,1,0:T(8,128)(2,1)}), bf16[16,32,128]{2,1,0:T(8,128)(2,1)S(1)}, u32[]{:S(2)}, u32[]{:S(2)}) %all-to-all-start) | async-done | bytes 131104 | tf_op jit(solution)/shard_map/all_to_all | solution.py:13
  19.1 0.7 %copy.66 = bf16[16,32,128]{2,1,0:T(8,128)(2,1)} copy(bf16[16,32,128]{2,0,1:T(8,128)(2,1)S(1)} %convolution_convert_fusion.3) | data formatting | bytes 262144 | tf_op jit(solution)/shard_map/convert_element_type | solution.py:20
  19.8 3.5 %all-to-all-start.1 = ((bf16[16,32,128]{2,1,0:T(8,128)(2,1)}), bf16[16,32,128]{2,1,0:T(8,128)(2,1)S(1)}, u32[]{:S(2)}, u32[]{:S(2)}) async-start(bf16[16,32,128]{2,1,0:T(8,128)(2,1)} %copy.66), calls=%async_computation.1 | async-start | bytes 262144 | tf_op jit(solution)/shard_map/all_to_all | solution.py:20
  23.3 0.3 convolution_bitcast_fusion.5
  23.6 7.4 %all-to-all-done.1 = bf16[16,32,128]{2,1,0:T(8,128)(2,1)S(1)} async-done(((bf16[16,32,128]{2,1,0:T(8,128)(2,1)}), bf16[16,32,128]{2,1,0:T(8,128)(2,1)S(1)}, u32[]{:S(2)}, u32[]{:S(2)}) %all-to-all-start.1) | async-done | bytes 131104 | tf_op jit(solution)/shard_map/all_to_all | solution.py:20
  31.1 0.3 multiply_reduce_fusion
  31.4 0.2 copy.70
  31.6 0.7 %copy-done.1 = bf16[256,512]{1,0:T(8,128)(2,1)S(1)} copy-done((bf16[256,512]{1,0:T(8,128)(2,1)S(1)}, bf16[256,512]{1,0:T(8,128)(2,1)}, u32[]{:S(2)}) %copy-start.1) | copy-done | bytes 262168
  32.5 2.5 %psum.7 = f32[2,256]{1,0:T(2,128)S(1)} all-reduce(f32[2,256]{1,0:T(2,128)S(1)} %pad_maximum_fusion), channel_id=1, replica_groups=mesh['seq'=16,'tp'=2] {'tp'}, use_global_device_ids=true, to_apply=%region_2.3 | all-reduce | flops 512 | bytes 4096 | tf_op jit(solution)/shard_map/psum | solution.py:48
  35.0 0.9 %fusion.10 = (bf16[256,512]{1,0:T(8,128)(2,1)S(1)}, bf16[256,512]{1,0:T(8,128)(2,1)}) fusion(bf16[256,512]{1,0:T(8,128)(2,1)S(1)} %copy-done.1, f32[256,512]{1,0:T(8,128)S(1)} %copy.70, f32[256]{0:T(256)S(1)} %multiply_multiply_fusion, f32[256]{0:T(256)S(1)} %bitcast.118), kind=kLoop, calls=%fused_computation.25 | loop fusion | flops 917504 | bytes 1312768 | tf_op jit(solution)/shard_map/convert_element_type | solution.py:53
  36.0 0.9 %convolution_convert_fusion = bf16[4,128,128]{1,2,0:T(8,128)(2,1)} fusion(bf16[256,4,128]{0,2,1:T(8,128)(2,1)S(1)} %bitcast.101, bf16[256,4,128]{0,2,1:T(8,128)(2,1)S(1)} %bitcast.103), kind=kOutput, calls=%fused_computation.17 | convolution fusion | flops 33619968 | bytes 655360 | tf_op jit(solution)/shard_map/thd,the->hde/dot_general | solution.py:57
  36.9 0.3 fusion.1
  37.2 3.5 %all-to-all-start.2 = ((bf16[16,32,128]{2,1,0:T(8,128)(2,1)}), bf16[16,32,128]{2,1,0:T(8,128)(2,1)S(1)}, u32[]{:S(2)}, u32[]{:S(2)}) async-start(bf16[16,32,128]{2,1,0:T(8,128)(2,1)} %bitcast.16), calls=%async_computation.2 | async-start | bytes 262144 | tf_op jit(solution)/shard_map/all_to_all | solution.py:13
  40.7 0.3 convolution_bitcast_fusion.3
  41.1 0.2 fusion.7
  41.3 0.8 %copy.84 = bf16[256,512]{1,0:T(8,128)(2,1)} copy(bf16[256,512]{0,1:T(8,128)(2,1)S(1)} %bitcast.114) | data formatting | bytes 524288
  42.1 0.2 fusion.32
  42.4 6.4 %all-to-all-done.2 = bf16[16,32,128]{2,1,0:T(8,128)(2,1)S(1)} async-done(((bf16[16,32,128]{2,1,0:T(8,128)(2,1)}), bf16[16,32,128]{2,1,0:T(8,128)(2,1)S(1)}, u32[]{:S(2)}, u32[]{:S(2)}) %all-to-all-start.2) | async-done | bytes 131104 | tf_op jit(solution)/shard_map/all_to_all | solution.py:13
  48.8 0.2 convolution_convert_fusion.2
  48.9 0.7 %copy.79 = bf16[16,32,128]{2,1,0:T(8,128)(2,1)} copy(bf16[16,32,128]{2,0,1:T(8,128)(2,1)S(1)} %convolution_convert_fusion.2) | data formatting | bytes 262144 | tf_op jit(solution)/shard_map/convert_element_type | solution.py:20
  49.6 3.5 %all-to-all-start.3 = ((bf16[16,32,128]{2,1,0:T(8,128)(2,1)}), bf16[16,32,128]{2,1,0:T(8,128)(2,1)S(1)}, u32[]{:S(2)}, u32[]{:S(2)}) async-start(bf16[16,32,128]{2,1,0:T(8,128)(2,1)} %copy.79), calls=%async_computation.3 | async-start | bytes 262144 | tf_op jit(solution)/shard_map/all_to_all | solution.py:20
  53.1 0.2 convolution_bitcast_fusion
  53.4 7.5 %all-to-all-done.3 = bf16[16,32,128]{2,1,0:T(8,128)(2,1)S(1)} async-done(((bf16[16,32,128]{2,1,0:T(8,128)(2,1)}), bf16[16,32,128]{2,1,0:T(8,128)(2,1)S(1)}, u32[]{:S(2)}, u32[]{:S(2)}) %all-to-all-start.3) | async-done | bytes 131104 | tf_op jit(solution)/shard_map/all_to_all | solution.py:20
  60.9 0.3 fusion.5
  61.2 0.8 %copy.86 = bf16[256,512]{1,0:T(8,128)(2,1)} copy(bf16[256,512]{0,1:T(8,128)(2,1)S(1)} %bitcast.116) | data formatting | bytes 524288
  62.0 0.2 fusion.6
  62.3 0.8 %copy.85 = bf16[256,512]{1,0:T(8,128)(2,1)} copy(bf16[256,512]{0,1:T(8,128)(2,1)S(1)} %bitcast.115) | data formatting | bytes 524288
  (14 shorter events, 0.6 us)
Async XLA Ops:
  0.6 1.1 %copy-start = (bf16[256,512]{1,0:T(8,128)(2,1)S(1)}, bf16[256,512]{1,0:T(8,128)(2,1)}, u32[]{:S(2)}) copy-start(bf16[256,512]{1,0:T(8,128)(2,1)} %param.6) | copy-start | bytes 786436
  2.7 8.5 %copy-start.3 = (bf16[256,512]{1,0:T(8,128)(2,1)S(1)}, bf16[256,512]{1,0:T(8,128)(2,1)}, u32[]{:S(2)}) copy-start(bf16[256,512]{1,0:T(8,128)(2,1)} %param.4) | copy-start | bytes 786436
  2.7 16.2 %all-to-all-start = ((bf16[16,32,128]{2,1,0:T(8,128)(2,1)}), bf16[16,32,128]{2,1,0:T(8,128)(2,1)S(1)}, u32[]{:S(2)}, u32[]{:S(2)}) async-start(bf16[16,32,128]{2,1,0:T(8,128)(2,1)} %bitcast.2), calls=%async_computation | async-start | bytes 262144 | tf_op jit(solution)/shard_map/all_to_all | solution.py:13
  11.2 1.0 %copy-start.2 = (bf16[256,512]{1,0:T(8,128)(2,1)S(1)}, bf16[256,512]{1,0:T(8,128)(2,1)}, u32[]{:S(2)}) copy-start(bf16[256,512]{1,0:T(8,128)(2,1)} %param.5) | copy-start | bytes 786436
  19.8 11.3 %all-to-all-start.1 = ((bf16[16,32,128]{2,1,0:T(8,128)(2,1)}), bf16[16,32,128]{2,1,0:T(8,128)(2,1)S(1)}, u32[]{:S(2)}, u32[]{:S(2)}) async-start(bf16[16,32,128]{2,1,0:T(8,128)(2,1)} %copy.66), calls=%async_computation.1 | async-start | bytes 262144 | tf_op jit(solution)/shard_map/all_to_all | solution.py:20
  31.4 1.0 %copy-start.1 = (bf16[256,512]{1,0:T(8,128)(2,1)S(1)}, bf16[256,512]{1,0:T(8,128)(2,1)}, u32[]{:S(2)}) copy-start(bf16[256,512]{1,0:T(8,128)(2,1)} %param.7) | copy-start | bytes 786436
  37.2 11.6 %all-to-all-start.2 = ((bf16[16,32,128]{2,1,0:T(8,128)(2,1)}), bf16[16,32,128]{2,1,0:T(8,128)(2,1)S(1)}, u32[]{:S(2)}, u32[]{:S(2)}) async-start(bf16[16,32,128]{2,1,0:T(8,128)(2,1)} %bitcast.16), calls=%async_computation.2 | async-start | bytes 262144 | tf_op jit(solution)/shard_map/all_to_all | solution.py:13
  49.6 11.3 %all-to-all-start.3 = ((bf16[16,32,128]{2,1,0:T(8,128)(2,1)}), bf16[16,32,128]{2,1,0:T(8,128)(2,1)S(1)}, u32[]{:S(2)}, u32[]{:S(2)}) async-start(bf16[16,32,128]{2,1,0:T(8,128)(2,1)} %copy.79), calls=%async_computation.3 | async-start | bytes 262144 | tf_op jit(solution)/shard_map/all_to_all | solution.py:20

commit v2 on v1

v2 whole, which is shorter than its diff:
```python
import functools

import jax
import jax.numpy as jnp
from jax import lax
from jax.experimental import pallas as pl
from jax.experimental.pallas import tpu as pltpu
from jax.sharding import PartitionSpec as P

DH = 128
EPSILON = 1e-06
QUAD = 4
LOW, WIDE = jnp.bfloat16, jnp.float32


def dot(a, b, contract):
    return lax.dot_general(a, b, ((contract[0], contract[1]), ((), ())), preferred_element_type=WIDE)


def head(ref, h):
    return ref.at[:, pl.ds(pl.multiple_of(h * DH, DH), DH)]


def fixed(ref, h):
    return ref.at[:, h * DH : (h + 1) * DH]


def causal_mask(count):
    row = lax.broadcasted_iota(jnp.int32, (count, count), 0)
    col = lax.broadcasted_iota(jnp.int32, (count, count), 1)
    return row >= col


def member_of_quad():
    return lax.axis_index("seq") % QUAD


def odd_place():
    return lax.axis_index("tp") % 2 == 1


def call(kernel, outs, args, flops, in_specs=None):
    size = sum(x.size * x.dtype.itemsize for x in list(args) + list(outs))
    return pl.pallas_call(
        kernel,
        out_shape=outs,
        in_specs=in_specs or vmem(len(args)),
        out_specs=[pl.BlockSpec(memory_space=pltpu.VMEM)] * len(outs),
        cost_estimate=pl.CostEstimate(flops=flops, bytes_accessed=size, transcendentals=0),
        compiler_params=pltpu.CompilerParams(vmem_limit_bytes=32 * 1024 * 1024),
    )(*args)


def state_kernel(k_ref, v_ref, out_ref):
    for h in range(QUAD):
        out_ref[h] = dot(fixed(k_ref, h)[...], fixed(v_ref, h)[...], ((0,), (0,))).astype(LOW)


def pair_kernel(own_ref, k_ref, v_ref, *outs):
    m = member_of_quad()
    for d in range(QUAD):
        h = m ^ d
        outs[d][0] = own_ref[h]
        outs[d][1] = dot(head(k_ref, h)[...], head(v_ref, h)[...], ((0,), (0,))).astype(LOW)


def local_kernel(q_ref, k_ref, v_ref, scores_ref, mixed_ref):
    mask = causal_mask(q_ref.shape[0])
    for h in range(QUAD):
        raw = dot(fixed(q_ref, h)[...], fixed(k_ref, h)[...], ((1,), (1,)))
        scores = jnp.where(mask, raw, 0.0).astype(LOW)
        scores_ref[h] = scores
        fixed(mixed_ref, h)[...] = dot(scores, fixed(v_ref, h)[...], ((1,), (0,)))


def mixed_kernel(local1, q1, c1, local2, q2, c2, p0, p1, p2, p3, mixed_ref, sums_ref):
    m = member_of_quad()
    count = q1.shape[0]
    square = jnp.zeros((count, DH), WIDE)
    product = jnp.zeros((count, DH), WIDE)
    for core, (local, q_ref, c_ref) in enumerate(((local1, q1, c1), (local2, q2, c2))):
        for e, p_ref in enumerate((p0, p1, p2, p3)):
            h = m ^ e
            mixed = head(local, h)[...] + dot(head(q_ref, h)[...], p_ref[core], ((1,), (0,)))
            mixed_ref[core, e] = mixed
            square = square + mixed * mixed
            product = product + mixed * head(c_ref, h)[...].astype(WIDE)
    sums_ref[0:1, :] = jnp.sum(square.T, axis=0, keepdims=True)
    sums_ref[1:2, :] = jnp.sum(product.T, axis=0, keepdims=True)


def token_scales(sums_ref, features, count):
    inverse = lax.rsqrt(sums_ref[0:1, :] * (1.0 / features) + EPSILON)
    projection = inverse * sums_ref[1:2, :] * (1.0 / features)
    inverse = jnp.broadcast_to(inverse, (DH, count)).T
    projection = jnp.broadcast_to(projection, (DH, count)).T
    return inverse, projection


def term_kernel(features, mixed_ref, q1, c1, q2, c2, sums_ref, *outs):
    m = member_of_quad()
    inverse, projection = token_scales(sums_ref, features, q1.shape[0])
    for core, (q_ref, c_ref) in enumerate(((q1, c1), (q2, c2))):
        for d in range(QUAD):
            h = m ^ d
            normed = mixed_ref[core, d] * inverse
            grad = (inverse * (head(c_ref, h)[...].astype(WIDE) - normed * projection)).astype(LOW)
            outs[d][core] = dot(head(q_ref, h)[...], grad, ((0,), (0,))).astype(LOW)


def query_kernel(features, q_ref, k_ref, v_ref, c_ref, local_ref, own_ref, got_ref, sums_ref,
                 normed_ref, query_ref, g_ref, coefs_ref):
    m = member_of_quad()
    count = q_ref.shape[0]
    mask = causal_mask(count)
    inverse, projection = token_scales(sums_ref, features, count)
    odd = odd_place()
    for e in range(QUAD):
        h = m ^ e
        prefix = jnp.where(odd, own_ref[e], got_ref[e])
        mixed = head(local_ref, h)[...] + dot(head(q_ref, h)[...], prefix, ((1,), (0,)))
        normed = mixed * inverse
        head(normed_ref, h)[...] = normed.astype(LOW)
        grad = (inverse * (head(c_ref, h)[...].astype(WIDE) - normed * projection)).astype(LOW)
        head(g_ref, h)[...] = grad
        raw = dot(grad, head(v_ref, h)[...], ((1,), (1,)))
        coefs = jnp.where(mask, raw, 0.0).astype(LOW)
        coefs_ref[h] = coefs
        query = dot(coefs, head(k_ref, h)[...], ((1,), (0,))) + dot(grad, prefix, ((1,), (1,)))
        head(query_ref, h)[...] = query.astype(LOW)


def inner_kernel(q_ref, g_ref, scores_ref, coefs_ref, key_ref, value_ref):
    for h in range(QUAD):
        fixed(key_ref, h)[...] = dot(coefs_ref[h], fixed(q_ref, h)[...], ((0,), (0,)))
        fixed(value_ref, h)[...] = dot(scores_ref[h], fixed(g_ref, h)[...], ((0,), (0,)))


def last_kernel(k_ref, v_ref, key_local, value_local, own_ref, got_ref, key_ref, value_ref):
    m = member_of_quad()
    odd = odd_place()
    for e in range(QUAD):
        h = m ^ e
        suffix = jnp.where(odd, own_ref[e], got_ref[e])
        key = head(key_local, h)[...] + dot(head(v_ref, h)[...], suffix, ((1,), (1,)))
        head(key_ref, h)[...] = key.astype(LOW)
        value = head(value_local, h)[...] + dot(head(k_ref, h)[...], suffix, ((1,), (0,)))
        head(value_ref, h)[...] = value.astype(LOW)


def exchange(value, bits):
    size = lax.axis_size("tp")
    return lax.ppermute(value, "tp", [(i, i ^ bits) for i in range(size)])


def send(value, bits):
    cores = lax.axis_size("tp")
    idle = QUAD if bits < QUAD else 1
    pairs = [
        (i * cores + t, (i ^ (bits if t % 2 else idle)) * cores + t)
        for i in range(lax.axis_size("seq"))
        for t in range(cores)
    ]
    return lax.ppermute(value, ("seq", "tp"), pairs)


def sums_kernel(before, count, *refs):
    index = lax.axis_index("seq")
    m = index % QUAD
    held, got, outs = refs[:QUAD], refs[QUAD : QUAD + count], refs[-QUAD:]

    def counts(a, b):
        return jnp.where(a < b if before else a > b, 1.0, 0.0).astype(WIDE)

    outer = jnp.zeros(held[0].shape, WIDE)
    for n in range(count):
        outer = outer + got[n][...].astype(WIDE) * counts(index ^ (QUAD * (n + 1)), index)
    pieces = [piece[...].astype(WIDE) for piece in held]
    for e in range(QUAD):
        inner = outer
        for d in range(QUAD):
            if d != e:
                inner = inner + pieces[d] * counts(m ^ d, m ^ e)
        outs[e][...] = inner.astype(LOW)


def stack_kernel(core, p0, p1, p2, p3, *refs):
    for e, p_ref in enumerate((p0, p1, p2, p3)):
        refs[-1][e] = p_ref[core]


def vmem(count):
    return [pl.BlockSpec(memory_space=pltpu.VMEM)] * count


def unused(count):
    return [pl.BlockSpec(memory_space=pl.ANY)] * count


def exclusive_sum(held, before, after=()):
    held = [held[0]] + [send(held[d], d) for d in range(1, QUAD)]
    total = sum(piece.astype(WIDE) for piece in held).astype(LOW)
    got = [send(total, bits) for bits in range(QUAD, lax.axis_size("seq"), QUAD)]
    sums = call(
        functools.partial(sums_kernel, before, len(got)),
        [jax.ShapeDtypeStruct(x.shape, x.dtype) for x in held],
        (*held, *got, *after),
        0,
        in_specs=vmem(QUAD + len(got)) + unused(len(after)),
    )
    return [sums[0]] + [send(sums[e], e) for e in range(1, QUAD)]


def body(q, k, v, c):
    count, width = q.shape
    features = width * lax.axis_size("tp")
    shape = jax.ShapeDtypeStruct
    states = shape((QUAD, DH, DH), LOW)
    pair = shape((2, DH, DH), LOW)
    wide = shape((count, width), WIDE)
    low = shape((count, width), LOW)
    square = shape((QUAD, count, count), LOW)
    unit = 2 * count * DH * DH * QUAD
    odd = odd_place()

    def share(arrays, *after):
        own, other = [
            call(
                functools.partial(stack_kernel, core), [states], (*arrays, *after), 0,
                in_specs=vmem(QUAD) + unused(len(after)),
            )[0]
            for core in range(2)
        ]
        return own, exchange(other, 1)

    k2, v2, q2, c2 = [exchange(x, 1) for x in (k, v, q, c)]
    own = call(state_kernel, [states], (k, v), unit)[0]
    held = call(pair_kernel, [pair] * QUAD, (own, k2, v2), unit)
    scores, local = call(local_kernel, [square, wide], (q, k, v), 4 * unit)
    _, local2 = call(local_kernel, [square, wide], (q2, k2, v2), 4 * unit)
    prefix = exclusive_sum(held, True)
    mixed, sums = call(
        mixed_kernel,
        [shape((2, QUAD, count, DH), WIDE), shape((2, count), WIDE)],
        (local, q, c, local2, q2, c2, *prefix),
        2 * unit,
    )
    bits = 2
    while bits < lax.axis_size("tp"):
        sums = sums + exchange(sums, bits)
        bits *= 2
    terms = call(
        functools.partial(term_kernel, features), [pair] * QUAD, (mixed, q, c, q2, c2, sums), 2 * unit
    )
    own_sums = jnp.where(odd, sums, exchange(sums, 1))
    normed_out, query_grad, g, coefs = call(
        functools.partial(query_kernel, features),
        [low, low, low, square],
        (q, k, v, c, local, *share(prefix), own_sums),
        6 * unit,
    )
    suffix = exclusive_sum(terms, False, (g,))
    key_local, value_local = call(inner_kernel, [wide, wide], (q, g, scores, coefs), 4 * unit)
    key_grad, value_grad = call(
        last_kernel, [low, low], (k, v, key_local, value_local, *share(suffix, key_local)), 2 * unit
    )
    return (normed_out, query_grad, key_grad, value_grad)


def solution(mesh):
    spec = P("seq", "tp")
    return jax.shard_map(body, mesh=mesh, in_specs=(spec,) * 4, out_specs=(spec,) * 4, check_vma=False)
```

time: 63.6 us -> 47.9 us (0.75)
  waiting for transfers between devices: 27.8 us -> 13.4 us
  Pallas kernels: 0 us -> 7.47 us
  local copies, waits for them, and re-layouts: 7.06 us -> 1.92 us
  starting transfers between devices: 19 us -> 24.1 us
  matrix products: 4.84 us -> 0 us
  blocking collectives: 2.47 us -> 0 us
  other arithmetic: 1.07 us -> 0.08 us
    all_to_all x4 -> x0, waiting for transfers between devices: 27.8 us -> none  [the longest x2 15 us: exclusive_sum(): sums = lax.all_to_all(sums.astype(jnp.bfloat16), 'seq', 0, 0, tiled=True)]
    ppermute x0 -> x25, starting transfers between devices: none -> 24.1 us  [the longest x18 22.3 us: send(): return lax.ppermute(value, ('seq', 'tp'), pairs)]
    all_to_all x4 -> x0, starting transfers between devices: 19 us -> none  [the longest x2 12 us: exclusive_sum(): pieces = lax.all_to_all(pieces, 'seq', 0, 0, tiled=True)]
    ppermute x0 -> x25, waiting for transfers between devices: none -> 13.4 us  [the longest x18 12.1 us: send(): return lax.ppermute(value, ('seq', 'tp'), pairs)]
    pallas_call x0 -> x15, Pallas kernels: none -> 7.47 us  [call(): pl.pallas_call(kernel, out_shape=outs, in_specs=in_specs or vmem(len(args...]
    dot_general x14 -> x0, matrix products: 4.84 us -> none  [the longest x1 0.89 us: body(): jnp.einsum('thd,the->hde', query_heads, mixed_grad, preferred_element_typ...]
    psum x1 -> x0, blocking collectives: 2.47 us -> none  [body(): sums = lax.psum(sums, 'tp')]
    unnamed x11 -> x12, local copies, waits for them, and re-layouts: 4.09 us -> 1.92 us
  transfers between devices with their start and end apart: 4 -> 25, of which waited for: 4 -> 16; matrix products, arithmetic and copies ran while one was open for 4% -> 0% of each run, Pallas kernels for 0% -> 10%
where the time goes in v2:
time: 47.9 us; the launch traced here: 47.8 us
  starting transfers between devices  24.1 us (50%)
  waiting for transfers between devices  13.4 us (28%)
  Pallas kernels  7.47 us (16%)
  local copies, waits for them, and re-layouts  1.92 us (4%)
  between operations  0.79 us (2%)
    ppermute x18, starting transfers between devices, send(): return lax.ppermute(value, ('seq', 'tp'), pairs)  22.3 us
    ppermute x18, waiting for transfers between devices, send(): return lax.ppermute(value, ('seq', 'tp'), pairs)  12.1 us
    pallas_call x15, Pallas kernels, call(): pl.pallas_call(kernel, out_shape=outs, in_specs=in_specs or vmem(len(args...  7.47 us
    unnamed x12, local copies, waits for them, and re-layouts  1.92 us
    ppermute x7, starting transfers between devices, exchange(): return lax.ppermute(value, 'tp', [(i, i ^ bits) for i in range(size)])  1.75 us
    ppermute x7, waiting for transfers between devices, exchange(): return lax.ppermute(value, 'tp', [(i, i ^ bits) for i in range(size)])  1.33 us
  transfers between devices with their start and end apart: 25, of which 16 were waited for; matrix products, arithmetic and copies ran while one was open for 0% of the time, Pallas kernels for 10%

profile of v2, /device:TPU:0, one launch (start us, length us, event | category | flops | bytes accessed | tf_op | source)
XLA Modules:
  0.0 47.8 jit_solution(9314841082989860428)
XLA Ops:
  1.2 0.9 %copy-done.1 = bf16[256,512]{1,0:T(8,128)(2,1)S(1)} copy-done((bf16[256,512]{1,0:T(8,128)(2,1)S(1)}, bf16[256,512]{1,0:T(8,128)(2,1)}, u32[]{:S(2)}) %copy-start.1) | copy-done | bytes 262168
  2.2 0.9 %copy-done.3 = bf16[256,512]{1,0:T(8,128)(2,1)S(1)} copy-done((bf16[256,512]{1,0:T(8,128)(2,1)S(1)}, bf16[256,512]{1,0:T(8,128)(2,1)}, u32[]{:S(2)}) %copy-start.3) | copy-done | bytes 262168
  3.7 3.1 %collective-permute-start.2 = (bf16[2,128,128]{2,1,0:T(8,128)(2,1)S(1)}, bf16[2,128,128]{2,1,0:T(8,128)(2,1)S(1)}, u32[]{:S(2)}, u32[]{:S(2)}) collective-permute-start(bf16[2,128,128]{2,1,0:T(8,128)(2,1)S(1)} %get-tuple-element.35), channel_id=1, source_target_pairs={{0,8},{1,3},{2,10},{3,1},{4,12},{5,7},{6,14},{7,5},{8,0},{9,11},{1... | collective-permute-start | bytes 196616 | tf_op jit(solution)/shard_map/ppermute | solution.py:164
  6.9 1.9 %collective-permute-start.4 = (bf16[2,128,128]{2,1,0:T(8,128)(2,1)S(1)}, bf16[2,128,128]{2,1,0:T(8,128)(2,1)S(1)}, u32[]{:S(2)}, u32[]{:S(2)}) collective-permute-start(bf16[2,128,128]{2,1,0:T(8,128)(2,1)S(1)} %get-tuple-element.37), channel_id=1, source_target_pairs={{0,8},{1,7},{2,10},{3,5},{4,12},{5,3},{6,14},{7,1},{8,0},{9,15},{1... | collective-permute-start | bytes 196616 | tf_op jit(solution)/shard_map/ppermute | solution.py:164
  9.4 1.7 %collective-permute-done.3.refs_2_ = bf16[2,128,128]{2,1,0:T(8,128)(2,1)S(1)} collective-permute-done((bf16[2,128,128]{2,1,0:T(8,128)(2,1)S(1)}, bf16[2,128,128]{2,1,0:T(8,128)(2,1)S(1)}, u32[]{:S(2)}, u32[]{:S(2)}) %collective-permute-start.3) | collective-permute-done | bytes 65568 | tf_op jit(solution)/shard_map/ppermute | solution.py:164
  11.1 0.7 %collective-permute-done.4.refs_3_ = bf16[2,128,128]{2,1,0:T(8,128)(2,1)S(1)} collective-permute-done((bf16[2,128,128]{2,1,0:T(8,128)(2,1)S(1)}, bf16[2,128,128]{2,1,0:T(8,128)(2,1)S(1)}, u32[]{:S(2)}, u32[]{:S(2)}) %collective-permute-start.4) | collective-permute-done | bytes 65568 | tf_op jit(solution)/shard_map/ppermute | solution.py:164
  11.8 1.6 %collective-permute-start.5 = (bf16[2,128,128]{2,1,0:T(8,128)(2,1)S(1)}, bf16[2,128,128]{2,1,0:T(8,128)(2,1)S(1)}, u32[]{:S(2)}, u32[]{:S(2)}) collective-permute-start(bf16[2,128,128]{2,1,0:T(8,128)(2,1)S(1)} %add_convert_fusion.1), channel_id=1, source_target_pairs={{0,2},{1,9},{2,0},{3,11},{4,6},{5,13},{6,4},{7,15},{8,10},{9,1},{1... | collective-permute-start | bytes 196616 | tf_op jit(solution)/shard_map/ppermute | solution.py:164
  13.9 1.5 %collective-permute-start.7 = (bf16[2,128,128]{2,1,0:T(8,128)(2,1)S(1)}, bf16[2,128,128]{2,1,0:T(8,128)(2,1)S(1)}, u32[]{:S(2)}, u32[]{:S(2)}) collective-permute-start(bf16[2,128,128]{2,1,0:T(8,128)(2,1)S(1)} %add_convert_fusion.1), channel_id=1, source_target_pairs={{0,2},{1,25},{2,0},{3,27},{4,6},{5,29},{6,4},{7,31},{8,10},{9,17},... | collective-permute-start | bytes 196616 | tf_op jit(solution)/shard_map/ppermute | solution.py:164
  15.4 0.7 %collective-permute-done.5.refs_4_ = bf16[2,128,128]{2,1,0:T(8,128)(2,1)S(1)} collective-permute-done((bf16[2,128,128]{2,1,0:T(8,128)(2,1)S(1)}, bf16[2,128,128]{2,1,0:T(8,128)(2,1)S(1)}, u32[]{:S(2)}, u32[]{:S(2)}) %collective-permute-start.5) | collective-permute-done | bytes 65568 | tf_op jit(solution)/shard_map/ppermute | solution.py:164
  16.2 1.5 %collective-permute-done.6.refs_5_ = bf16[2,128,128]{2,1,0:T(8,128)(2,1)S(1)} collective-permute-done((bf16[2,128,128]{2,1,0:T(8,128)(2,1)S(1)}, bf16[2,128,128]{2,1,0:T(8,128)(2,1)S(1)}, u32[]{:S(2)}, u32[]{:S(2)}) %collective-permute-start.6) | collective-permute-done | bytes 65568 | tf_op jit(solution)/shard_map/ppermute | solution.py:164
  17.7 0.7 %collective-permute-done.7.refs_6_ = bf16[2,128,128]{2,1,0:T(8,128)(2,1)S(1)} collective-permute-done((bf16[2,128,128]{2,1,0:T(8,128)(2,1)S(1)}, bf16[2,128,128]{2,1,0:T(8,128)(2,1)S(1)}, u32[]{:S(2)}, u32[]{:S(2)}) %collective-permute-start.7) | collective-permute-done | bytes 65568 | tf_op jit(solution)/shard_map/ppermute | solution.py:164
  18.5 1.4 %collective-permute-start.10 = (bf16[2,128,128]{2,1,0:T(8,128)(2,1)S(1)}, bf16[2,128,128]{2,1,0:T(8,128)(2,1)S(1)}, u32[]{:S(2)}, u32[]{:S(2)}) collective-permute-start(bf16[2,128,128]{2,1,0:T(8,128)(2,1)S(1)} %get-tuple-element.41), channel_id=1, source_target_pairs={{0,8},{1,7},{2,10},{3,5},{4,12},{5,3},{6,14},{7,1},{8,0},{9,15},{1... | collective-permute-start | bytes 196616 | tf_op jit(solution)/shard_map/ppermute | solution.py:164
  19.9 0.7 %collective-permute-start.8 = (bf16[2,128,128]{2,1,0:T(8,128)(2,1)S(1)}, bf16[2,128,128]{2,1,0:T(8,128)(2,1)S(1)}, u32[]{:S(2)}, u32[]{:S(2)}) collective-permute-start(bf16[2,128,128]{2,1,0:T(8,128)(2,1)S(1)} %get-tuple-element.39), channel_id=1, source_target_pairs={{0,8},{1,3},{2,10},{3,1},{4,12},{5,7},{6,14},{7,5},{8,0},{9,11},{1... | collective-permute-start | bytes 196616 | tf_op jit(solution)/shard_map/ppermute | solution.py:164
  20.6 1.3 %collective-permute-start.9 = (bf16[2,128,128]{2,1,0:T(8,128)(2,1)S(1)}, bf16[2,128,128]{2,1,0:T(8,128)(2,1)S(1)}, u32[]{:S(2)}, u32[]{:S(2)}) collective-permute-start(bf16[2,128,128]{2,1,0:T(8,128)(2,1)S(1)} %get-tuple-element.40), channel_id=1, source_target_pairs={{0,8},{1,5},{2,10},{3,7},{4,12},{5,1},{6,14},{7,3},{8,0},{9,13},{1... | collective-permute-start | bytes 196616 | tf_op jit(solution)/shard_map/ppermute | solution.py:164
  22.6 1.3 %shard_map.81 = (bf16[4,256,256]{2,1,0:T(8,128)(2,1)}, f32[256,512]{1,0:T(8,128)S(1)}) custom-call(bf16[256,512]{1,0:T(8,128)(2,1)S(1)} %collective-permute-done.12.q_ref.q2, bf16[256,512]{1,0:T(8,128)(2,1)S(1)} %collective-permute-done.k_ref, bf16[256,512]{1,0:T(8,128)(2,1)S(1)} %collective-permute-done.1.v_ref), custom_call_target="tpu_custom_call" | custom-call | flops 134217728 | bytes 1835008 | tf_op jit(solution)/shard_map/pallas_call | solution.py:44
  24.2 0.7 %collective-permute-done.9.p2 = bf16[2,128,128]{2,1,0:T(8,128)(2,1)S(1)} collective-permute-done((bf16[2,128,128]{2,1,0:T(8,128)(2,1)S(1)}, bf16[2,128,128]{2,1,0:T(8,128)(2,1)S(1)}, u32[]{:S(2)}, u32[]{:S(2)}) %collective-permute-start.9) | collective-permute-done | bytes 65568 | tf_op jit(solution)/shard_map/ppermute | solution.py:164
  26.0 1.4 %collective-permute-start.15 = (bf16[2,128,128]{2,1,0:T(8,128)(2,1)S(1)}, bf16[2,128,128]{2,1,0:T(8,128)(2,1)S(1)}, u32[]{:S(2)}, u32[]{:S(2)}) collective-permute-start(bf16[2,128,128]{2,1,0:T(8,128)(2,1)S(1)} %get-tuple-element.53), channel_id=1, source_target_pairs={{0,8},{1,3},{2,10},{3,1},{4,12},{5,7},{6,14},{7,5},{8,0},{9,11},{1... | collective-permute-start | bytes 196616 | tf_op jit(solution)/shard_map/ppermute | solution.py:164
  27.4 0.7 %collective-permute-start.16 = (bf16[2,128,128]{2,1,0:T(8,128)(2,1)S(1)}, bf16[2,128,128]{2,1,0:T(8,128)(2,1)S(1)}, u32[]{:S(2)}, u32[]{:S(2)}) collective-permute-start(bf16[2,128,128]{2,1,0:T(8,128)(2,1)S(1)} %get-tuple-element.54), channel_id=1, source_target_pairs={{0,8},{1,5},{2,10},{3,7},{4,12},{5,1},{6,14},{7,3},{8,0},{9,13},{1... | collective-permute-start | bytes 196616 | tf_op jit(solution)/shard_map/ppermute | solution.py:164
  28.1 1.3 %collective-permute-start.17 = (bf16[2,128,128]{2,1,0:T(8,128)(2,1)S(1)}, bf16[2,128,128]{2,1,0:T(8,128)(2,1)S(1)}, u32[]{:S(2)}, u32[]{:S(2)}) collective-permute-start(bf16[2,128,128]{2,1,0:T(8,128)(2,1)S(1)} %get-tuple-element.55), channel_id=1, source_target_pairs={{0,8},{1,7},{2,10},{3,5},{4,12},{5,3},{6,14},{7,1},{8,0},{9,15},{1... | collective-permute-start | bytes 196616 | tf_op jit(solution)/shard_map/ppermute | solution.py:164
  30.3 1.3 %collective-permute-done.16.refs_2_ = bf16[2,128,128]{2,1,0:T(8,128)(2,1)S(1)} collective-permute-done((bf16[2,128,128]{2,1,0:T(8,128)(2,1)S(1)}, bf16[2,128,128]{2,1,0:T(8,128)(2,1)S(1)}, u32[]{:S(2)}, u32[]{:S(2)}) %collective-permute-start.16) | collective-permute-done | bytes 65568 | tf_op jit(solution)/shard_map/ppermute | solution.py:164
  31.6 0.7 %collective-permute-done.17.refs_3_ = bf16[2,128,128]{2,1,0:T(8,128)(2,1)S(1)} collective-permute-done((bf16[2,128,128]{2,1,0:T(8,128)(2,1)S(1)}, bf16[2,128,128]{2,1,0:T(8,128)(2,1)S(1)}, u32[]{:S(2)}, u32[]{:S(2)}) %collective-permute-start.17) | collective-permute-done | bytes 65568 | tf_op jit(solution)/shard_map/ppermute | solution.py:164
  32.4 1.4 %collective-permute-start.18 = (bf16[2,128,128]{2,1,0:T(8,128)(2,1)S(1)}, bf16[2,128,128]{2,1,0:T(8,128)(2,1)S(1)}, u32[]{:S(2)}, u32[]{:S(2)}) collective-permute-start(bf16[2,128,128]{2,1,0:T(8,128)(2,1)S(1)} %add_convert_fusion), channel_id=1, source_target_pairs={{0,2},{1,9},{2,0},{3,11},{4,6},{5,13},{6,4},{7,15},{8,10},{9,1},{1... | collective-permute-start | bytes 196616 | tf_op jit(solution)/shard_map/ppermute | solution.py:164
  33.7 0.7 %collective-permute-start.19 = (bf16[2,128,128]{2,1,0:T(8,128)(2,1)S(1)}, bf16[2,128,128]{2,1,0:T(8,128)(2,1)S(1)}, u32[]{:S(2)}, u32[]{:S(2)}) collective-permute-start(bf16[2,128,128]{2,1,0:T(8,128)(2,1)S(1)} %add_convert_fusion), channel_id=1, source_target_pairs={{0,2},{1,17},{2,0},{3,19},{4,6},{5,21},{6,4},{7,23},{8,10},{9,25},... | collective-permute-start | bytes 196616 | tf_op jit(solution)/shard_map/ppermute | solution.py:164
  34.5 1.3 %collective-permute-start.20 = (bf16[2,128,128]{2,1,0:T(8,128)(2,1)S(1)}, bf16[2,128,128]{2,1,0:T(8,128)(2,1)S(1)}, u32[]{:S(2)}, u32[]{:S(2)}) collective-permute-start(bf16[2,128,128]{2,1,0:T(8,128)(2,1)S(1)} %add_convert_fusion), channel_id=1, source_target_pairs={{0,2},{1,25},{2,0},{3,27},{4,6},{5,29},{6,4},{7,31},{8,10},{9,17},... | collective-permute-start | bytes 196616 | tf_op jit(solution)/shard_map/ppermute | solution.py:164
  35.8 1.9 %shard_map.83 = (bf16[256,512]{1,0:T(8,128)(2,1)}, bf16[256,512]{1,0:T(8,128)(2,1)}, bf16[256,512]{1,0:T(8,128)(2,1)S(1)}, bf16[4,256,256]{2,1,0:T(8,128)(2,1)S(1)}) custom-call(bf16[256,512]{1,0:T(8,128)(2,1)S(1)} %copy-done, bf16[256,512]{1,0:T(8,128)(2,1)S(1)} %copy-done.2, bf16[256,512]{1,0:T(8,128)(2,1)S(1)} %copy-done.4, ...), custom_call_target="tpu_custom_call" | custom-call | flops 201326592 | bytes 3147776 | tf_op jit(solution)/shard_map/pallas_call | solution.py:44
  38.0 0.7 %collective-permute-done.20.refs_6_ = bf16[2,128,128]{2,1,0:T(8,128)(2,1)S(1)} collective-permute-done((bf16[2,128,128]{2,1,0:T(8,128)(2,1)S(1)}, bf16[2,128,128]{2,1,0:T(8,128)(2,1)S(1)}, u32[]{:S(2)}, u32[]{:S(2)}) %collective-permute-start.20) | collective-permute-done | bytes 65568 | tf_op jit(solution)/shard_map/ppermute | solution.py:164
  38.9 1.4 %collective-permute-start.21 = (bf16[2,128,128]{2,1,0:T(8,128)(2,1)S(1)}, bf16[2,128,128]{2,1,0:T(8,128)(2,1)S(1)}, u32[]{:S(2)}, u32[]{:S(2)}) collective-permute-start(bf16[2,128,128]{2,1,0:T(8,128)(2,1)S(1)} %get-tuple-element.57), channel_id=1, source_target_pairs={{0,8},{1,3},{2,10},{3,1},{4,12},{5,7},{6,14},{7,5},{8,0},{9,11},{1... | collective-permute-start | bytes 196616 | tf_op jit(solution)/shard_map/ppermute | solution.py:164
  40.3 0.7 %collective-permute-start.22 = (bf16[2,128,128]{2,1,0:T(8,128)(2,1)S(1)}, bf16[2,128,128]{2,1,0:T(8,128)(2,1)S(1)}, u32[]{:S(2)}, u32[]{:S(2)}) collective-permute-start(bf16[2,128,128]{2,1,0:T(8,128)(2,1)S(1)} %get-tuple-element.58), channel_id=1, source_target_pairs={{0,8},{1,5},{2,10},{3,7},{4,12},{5,1},{6,14},{7,3},{8,0},{9,13},{1... | collective-permute-start | bytes 196616 | tf_op jit(solution)/shard_map/ppermute | solution.py:164
  41.0 1.3 %collective-permute-start.23 = (bf16[2,128,128]{2,1,0:T(8,128)(2,1)S(1)}, bf16[2,128,128]{2,1,0:T(8,128)(2,1)S(1)}, u32[]{:S(2)}, u32[]{:S(2)}) collective-permute-start(bf16[2,128,128]{2,1,0:T(8,128)(2,1)S(1)} %get-tuple-element.59), channel_id=1, source_target_pairs={{0,8},{1,7},{2,10},{3,5},{4,12},{5,3},{6,14},{7,1},{8,0},{9,15},{1... | collective-permute-start | bytes 196616 | tf_op jit(solution)/shard_map/ppermute | solution.py:164
  43.2 1.3 %collective-permute-done.22.p2 = bf16[2,128,128]{2,1,0:T(8,128)(2,1)S(1)} collective-permute-done((bf16[2,128,128]{2,1,0:T(8,128)(2,1)S(1)}, bf16[2,128,128]{2,1,0:T(8,128)(2,1)S(1)}, u32[]{:S(2)}, u32[]{:S(2)}) %collective-permute-start.22) | collective-permute-done | bytes 65568 | tf_op jit(solution)/shard_map/ppermute | solution.py:164
  45.4 1.3 %collective-permute-done.24.got_ref = bf16[4,128,128]{2,1,0:T(8,128)(2,1)S(1)} collective-permute-done((bf16[4,128,128]{2,1,0:T(8,128)(2,1)S(1)}, bf16[4,128,128]{2,1,0:T(8,128)(2,1)S(1)}, u32[]{:S(2)}, u32[]{:S(2)}) %collective-permute-start.24) | collective-permute-done | bytes 131104 | tf_op jit(solution)/shard_map/ppermute | solution.py:153
  46.7 1.1 %shard_map.89 = (bf16[256,512]{1,0:T(8,128)(2,1)}, bf16[256,512]{1,0:T(8,128)(2,1)}) custom-call(bf16[256,512]{1,0:T(8,128)(2,1)S(1)} %copy-done.2, bf16[256,512]{1,0:T(8,128)(2,1)S(1)} %copy-done.4, f32[256,512]{1,0:T(8,128)S(1)} %get-tuple-element.49.refs_0_.key_local, f32[256,512]{1,0:T(8,128)S(1)} %get-tuple-element.50.value_local, ...), custom_call_target="tpu_custom_call" | custom-call | flops 67108864 | bytes 2359296 | tf_op jit(solution)/shard_map/pallas_call | solution.py:44
  (48 shorter events, 7.6 us)
Async XLA Ops:
  0.6 2.8 %collective-permute-start = (bf16[256,512]{1,0:T(8,128)(2,1)}, bf16[256,512]{1,0:T(8,128)(2,1)S(1)}, u32[]{:S(2)}, u32[]{:S(2)}) collective-permute-start(bf16[256,512]{1,0:T(8,128)(2,1)} %k_ref.7), channel_id=1, source_target_pairs={{0,1},{1,0},{2,3},{3,2},{4,5},{5,4},{6,7},{7,6},{8,9},{9,8},{10,11... | collective-permute-start | bytes 786440 | tf_op jit(solution)/shard_map/ppermute | solution.py:153
  1.1 2.3 %collective-permute-start.1 = (bf16[256,512]{1,0:T(8,128)(2,1)}, bf16[256,512]{1,0:T(8,128)(2,1)S(1)}, u32[]{:S(2)}, u32[]{:S(2)}) collective-permute-start(bf16[256,512]{1,0:T(8,128)(2,1)} %v_ref.7), channel_id=1, source_target_pairs={{0,1},{1,0},{2,3},{3,2},{4,5},{5,4},{6,7},{7,6},{8,9},{9,8},{10,11... | collective-permute-start | bytes 786440 | tf_op jit(solution)/shard_map/ppermute | solution.py:153
  1.2 0.9 %copy-start.1 = (bf16[256,512]{1,0:T(8,128)(2,1)S(1)}, bf16[256,512]{1,0:T(8,128)(2,1)}, u32[]{:S(2)}) copy-start(bf16[256,512]{1,0:T(8,128)(2,1)} %k_ref.7) | copy-start | bytes 786436
  2.2 0.9 %copy-start.3 = (bf16[256,512]{1,0:T(8,128)(2,1)S(1)}, bf16[256,512]{1,0:T(8,128)(2,1)}, u32[]{:S(2)}) copy-start(bf16[256,512]{1,0:T(8,128)(2,1)} %v_ref.7) | copy-start | bytes 786436
  3.4 5.4 %copy-start = (bf16[256,512]{1,0:T(8,128)(2,1)S(1)}, bf16[256,512]{1,0:T(8,128)(2,1)}, u32[]{:S(2)}) copy-start(bf16[256,512]{1,0:T(8,128)(2,1)} %q1.3) | copy-start | bytes 786436
  3.4 5.4 %copy-start.5 = (bf16[256,512]{1,0:T(8,128)(2,1)S(1)}, bf16[256,512]{1,0:T(8,128)(2,1)}, u32[]{:S(2)}) copy-start(bf16[256,512]{1,0:T(8,128)(2,1)} %c1.3) | copy-start | bytes 786436
  3.7 5.6 %collective-permute-start.2 = (bf16[2,128,128]{2,1,0:T(8,128)(2,1)S(1)}, bf16[2,128,128]{2,1,0:T(8,128)(2,1)S(1)}, u32[]{:S(2)}, u32[]{:S(2)}) collective-permute-start(bf16[2,128,128]{2,1,0:T(8,128)(2,1)S(1)} %get-tuple-element.35), channel_id=1, source_target_pairs={{0,8},{1,3},{2,10},{3,1},{4,12},{5,7},{6,14},{7,5},{8,0},{9,11},{1... | collective-permute-start | bytes 196616 | tf_op jit(solution)/shard_map/ppermute | solution.py:164
  6.8 4.3 %collective-permute-start.3 = (bf16[2,128,128]{2,1,0:T(8,128)(2,1)S(1)}, bf16[2,128,128]{2,1,0:T(8,128)(2,1)S(1)}, u32[]{:S(2)}, u32[]{:S(2)}) collective-permute-start(bf16[2,128,128]{2,1,0:T(8,128)(2,1)S(1)} %get-tuple-element.36), channel_id=1, source_target_pairs={{0,8},{1,5},{2,10},{3,7},{4,12},{5,1},{6,14},{7,3},{8,0},{9,13},{1... | collective-permute-start | bytes 196616 | tf_op jit(solution)/shard_map/ppermute | solution.py:164
  6.9 4.9 %collective-permute-start.4 = (bf16[2,128,128]{2,1,0:T(8,128)(2,1)S(1)}, bf16[2,128,128]{2,1,0:T(8,128)(2,1)S(1)}, u32[]{:S(2)}, u32[]{:S(2)}) collective-permute-start(bf16[2,128,128]{2,1,0:T(8,128)(2,1)S(1)} %get-tuple-element.37), channel_id=1, source_target_pairs={{0,8},{1,7},{2,10},{3,5},{4,12},{5,3},{6,14},{7,1},{8,0},{9,15},{1... | collective-permute-start | bytes 196616 | tf_op jit(solution)/shard_map/ppermute | solution.py:164
  8.8 13.8 %collective-permute-start.12 = (bf16[256,512]{1,0:T(8,128)(2,1)S(1)}, bf16[256,512]{1,0:T(8,128)(2,1)S(1)}, u32[]{:S(2)}, u32[]{:S(2)}) collective-permute-start(bf16[256,512]{1,0:T(8,128)(2,1)S(1)} %copy-done), channel_id=1, source_target_pairs={{0,1},{1,0},{2,3},{3,2},{4,5},{5,4},{6,7},{7,6},{8,9},{9,8},{10,11... | collective-permute-start | bytes 786440 | tf_op jit(solution)/shard_map/ppermute | solution.py:153
  8.8 15.1 %collective-permute-start.13 = (bf16[256,512]{1,0:T(8,128)(2,1)S(1)}, bf16[256,512]{1,0:T(8,128)(2,1)S(1)}, u32[]{:S(2)}, u32[]{:S(2)}) collective-permute-start(bf16[256,512]{1,0:T(8,128)(2,1)S(1)} %copy-done.5), channel_id=1, source_target_pairs={{0,1},{1,0},{2,3},{3,2},{4,5},{5,4},{6,7},{7,6},{8,9},{9,8},{10,11... | collective-permute-start | bytes 786440 | tf_op jit(solution)/shard_map/ppermute | solution.py:153
  11.8 10.2 %copy-start.4 = (bf16[256,512]{1,0:T(8,128)(2,1)S(1)}, bf16[256,512]{1,0:T(8,128)(2,1)}, u32[]{:S(2)}) copy-start(bf16[256,512]{1,0:T(8,128)(2,1)} %v_ref.7) | copy-start | bytes 786436
  11.8 10.1 %copy-start.2 = (bf16[256,512]{1,0:T(8,128)(2,1)S(1)}, bf16[256,512]{1,0:T(8,128)(2,1)}, u32[]{:S(2)}) copy-start(bf16[256,512]{1,0:T(8,128)(2,1)} %k_ref.7) | copy-start | bytes 786436
  11.8 4.3 %collective-permute-start.5 = (bf16[2,128,128]{2,1,0:T(8,128)(2,1)S(1)}, bf16[2,128,128]{2,1,0:T(8,128)(2,1)S(1)}, u32[]{:S(2)}, u32[]{:S(2)}) collective-permute-start(bf16[2,128,128]{2,1,0:T(8,128)(2,1)S(1)} %add_convert_fusion.1), channel_id=1, source_target_pairs={{0,2},{1,9},{2,0},{3,11},{4,6},{5,13},{6,4},{7,15},{8,10},{9,1},{1... | collective-permute-start | bytes 196616 | tf_op jit(solution)/shard_map/ppermute | solution.py:164
  13.4 4.3 %collective-permute-start.6 = (bf16[2,128,128]{2,1,0:T(8,128)(2,1)S(1)}, bf16[2,128,128]{2,1,0:T(8,128)(2,1)S(1)}, u32[]{:S(2)}, u32[]{:S(2)}) collective-permute-start(bf16[2,128,128]{2,1,0:T(8,128)(2,1)S(1)} %add_convert_fusion.1), channel_id=1, source_target_pairs={{0,2},{1,17},{2,0},{3,19},{4,6},{5,21},{6,4},{7,23},{8,10},{9,25},... | collective-permute-start | bytes 196616 | tf_op jit(solution)/shard_map/ppermute | solution.py:164
  13.9 4.4 %collective-permute-start.7 = (bf16[2,128,128]{2,1,0:T(8,128)(2,1)S(1)}, bf16[2,128,128]{2,1,0:T(8,128)(2,1)S(1)}, u32[]{:S(2)}, u32[]{:S(2)}) collective-permute-start(bf16[2,128,128]{2,1,0:T(8,128)(2,1)S(1)} %add_convert_fusion.1), channel_id=1, source_target_pairs={{0,2},{1,25},{2,0},{3,27},{4,6},{5,29},{6,4},{7,31},{8,10},{9,17},... | collective-permute-start | bytes 196616 | tf_op jit(solution)/shard_map/ppermute | solution.py:164
  18.5 5.4 %collective-permute-start.10 = (bf16[2,128,128]{2,1,0:T(8,128)(2,1)S(1)}, bf16[2,128,128]{2,1,0:T(8,128)(2,1)S(1)}, u32[]{:S(2)}, u32[]{:S(2)}) collective-permute-start(bf16[2,128,128]{2,1,0:T(8,128)(2,1)S(1)} %get-tuple-element.41), channel_id=1, source_target_pairs={{0,8},{1,7},{2,10},{3,5},{4,12},{5,3},{6,14},{7,1},{8,0},{9,15},{1... | collective-permute-start | bytes 196616 | tf_op jit(solution)/shard_map/ppermute | solution.py:164
  19.9 4.3 %collective-permute-start.8 = (bf16[2,128,128]{2,1,0:T(8,128)(2,1)S(1)}, bf16[2,128,128]{2,1,0:T(8,128)(2,1)S(1)}, u32[]{:S(2)}, u32[]{:S(2)}) collective-permute-start(bf16[2,128,128]{2,1,0:T(8,128)(2,1)S(1)} %get-tuple-element.39), channel_id=1, source_target_pairs={{0,8},{1,3},{2,10},{3,1},{4,12},{5,7},{6,14},{7,5},{8,0},{9,11},{1... | collective-permute-start | bytes 196616 | tf_op jit(solution)/shard_map/ppermute | solution.py:164
  20.6 4.3 %collective-permute-start.9 = (bf16[2,128,128]{2,1,0:T(8,128)(2,1)S(1)}, bf16[2,128,128]{2,1,0:T(8,128)(2,1)S(1)}, u32[]{:S(2)}, u32[]{:S(2)}) collective-permute-start(bf16[2,128,128]{2,1,0:T(8,128)(2,1)S(1)} %get-tuple-element.40), channel_id=1, source_target_pairs={{0,8},{1,5},{2,10},{3,7},{4,12},{5,1},{6,14},{7,3},{8,0},{9,13},{1... | collective-permute-start | bytes 196616 | tf_op jit(solution)/shard_map/ppermute | solution.py:164
  26.0 4.3 %collective-permute-start.15 = (bf16[2,128,128]{2,1,0:T(8,128)(2,1)S(1)}, bf16[2,128,128]{2,1,0:T(8,128)(2,1)S(1)}, u32[]{:S(2)}, u32[]{:S(2)}) collective-permute-start(bf16[2,128,128]{2,1,0:T(8,128)(2,1)S(1)} %get-tuple-element.53), channel_id=1, source_target_pairs={{0,8},{1,3},{2,10},{3,1},{4,12},{5,7},{6,14},{7,5},{8,0},{9,11},{1... | collective-permute-start | bytes 196616 | tf_op jit(solution)/shard_map/ppermute | solution.py:164
  27.4 4.3 %collective-permute-start.16 = (bf16[2,128,128]{2,1,0:T(8,128)(2,1)S(1)}, bf16[2,128,128]{2,1,0:T(8,128)(2,1)S(1)}, u32[]{:S(2)}, u32[]{:S(2)}) collective-permute-start(bf16[2,128,128]{2,1,0:T(8,128)(2,1)S(1)} %get-tuple-element.54), channel_id=1, source_target_pairs={{0,8},{1,5},{2,10},{3,7},{4,12},{5,1},{6,14},{7,3},{8,0},{9,13},{1... | collective-permute-start | bytes 196616 | tf_op jit(solution)/shard_map/ppermute | solution.py:164
  28.1 4.3 %collective-permute-start.17 = (bf16[2,128,128]{2,1,0:T(8,128)(2,1)S(1)}, bf16[2,128,128]{2,1,0:T(8,128)(2,1)S(1)}, u32[]{:S(2)}, u32[]{:S(2)}) collective-permute-start(bf16[2,128,128]{2,1,0:T(8,128)(2,1)S(1)} %get-tuple-element.55), channel_id=1, source_target_pairs={{0,8},{1,7},{2,10},{3,5},{4,12},{5,3},{6,14},{7,1},{8,0},{9,15},{1... | collective-permute-start | bytes 196616 | tf_op jit(solution)/shard_map/ppermute | solution.py:164
  29.4 6.4 %collective-permute-start.14 = (f32[2,256]{1,0:T(2,128)S(1)}, f32[2,256]{1,0:T(2,128)S(1)}, u32[]{:S(2)}, u32[]{:S(2)}) collective-permute-start(f32[2,256]{1,0:T(2,128)S(1)} %get-tuple-element.43.sums_ref), channel_id=1, source_target_pairs={{0,1},{1,0},{2,3},{3,2},{4,5},{5,4},{6,7},{7,6},{8,9},{9,8},{10,11... | collective-permute-start | bytes 6152 | tf_op jit(solution)/shard_map/ppermute | solution.py:153
  29.4 6.4 %collective-permute-start.11 = (bf16[4,128,128]{2,1,0:T(8,128)(2,1)S(1)}, bf16[4,128,128]{2,1,0:T(8,128)(2,1)S(1)}, u32[]{:S(2)}, u32[]{:S(2)}) collective-permute-start(bf16[4,128,128]{2,1,0:T(8,128)(2,1)S(1)} %shard_map.80), channel_id=1, source_target_pairs={{0,1},{1,0},{2,3},{3,2},{4,5},{5,4},{6,7},{7,6},{8,9},{9,8},{10,11... | collective-permute-start | bytes 393224 | tf_op jit(solution)/shard_map/ppermute | solution.py:153
  32.4 5.3 %collective-permute-start.18 = (bf16[2,128,128]{2,1,0:T(8,128)(2,1)S(1)}, bf16[2,128,128]{2,1,0:T(8,128)(2,1)S(1)}, u32[]{:S(2)}, u32[]{:S(2)}) collective-permute-start(bf16[2,128,128]{2,1,0:T(8,128)(2,1)S(1)} %add_convert_fusion), channel_id=1, source_target_pairs={{0,2},{1,9},{2,0},{3,11},{4,6},{5,13},{6,4},{7,15},{8,10},{9,1},{1... | collective-permute-start | bytes 196616 | tf_op jit(solution)/shard_map/ppermute | solution.py:164
  33.7 4.3 %collective-permute-start.19 = (bf16[2,128,128]{2,1,0:T(8,128)(2,1)S(1)}, bf16[2,128,128]{2,1,0:T(8,128)(2,1)S(1)}, u32[]{:S(2)}, u32[]{:S(2)}) collective-permute-start(bf16[2,128,128]{2,1,0:T(8,128)(2,1)S(1)} %add_convert_fusion), channel_id=1, source_target_pairs={{0,2},{1,17},{2,0},{3,19},{4,6},{5,21},{6,4},{7,23},{8,10},{9,25},... | collective-permute-start | bytes 196616 | tf_op jit(solution)/shard_map/ppermute | solution.py:164
  34.5 4.3 %collective-permute-start.20 = (bf16[2,128,128]{2,1,0:T(8,128)(2,1)S(1)}, bf16[2,128,128]{2,1,0:T(8,128)(2,1)S(1)}, u32[]{:S(2)}, u32[]{:S(2)}) collective-permute-start(bf16[2,128,128]{2,1,0:T(8,128)(2,1)S(1)} %add_convert_fusion), channel_id=1, source_target_pairs={{0,2},{1,25},{2,0},{3,27},{4,6},{5,29},{6,4},{7,31},{8,10},{9,17},... | collective-permute-start | bytes 196616 | tf_op jit(solution)/shard_map/ppermute | solution.py:164
  38.9 4.3 %collective-permute-start.21 = (bf16[2,128,128]{2,1,0:T(8,128)(2,1)S(1)}, bf16[2,128,128]{2,1,0:T(8,128)(2,1)S(1)}, u32[]{:S(2)}, u32[]{:S(2)}) collective-permute-start(bf16[2,128,128]{2,1,0:T(8,128)(2,1)S(1)} %get-tuple-element.57), channel_id=1, source_target_pairs={{0,8},{1,3},{2,10},{3,1},{4,12},{5,7},{6,14},{7,5},{8,0},{9,11},{1... | collective-permute-start | bytes 196616 | tf_op jit(solution)/shard_map/ppermute | solution.py:164
  40.3 4.3 %collective-permute-start.22 = (bf16[2,128,128]{2,1,0:T(8,128)(2,1)S(1)}, bf16[2,128,128]{2,1,0:T(8,128)(2,1)S(1)}, u32[]{:S(2)}, u32[]{:S(2)}) collective-permute-start(bf16[2,128,128]{2,1,0:T(8,128)(2,1)S(1)} %get-tuple-element.58), channel_id=1, source_target_pairs={{0,8},{1,5},{2,10},{3,7},{4,12},{5,1},{6,14},{7,3},{8,0},{9,13},{1... | collective-permute-start | bytes 196616 | tf_op jit(solution)/shard_map/ppermute | solution.py:164
  41.0 4.3 %collective-permute-start.23 = (bf16[2,128,128]{2,1,0:T(8,128)(2,1)S(1)}, bf16[2,128,128]{2,1,0:T(8,128)(2,1)S(1)}, u32[]{:S(2)}, u32[]{:S(2)}) collective-permute-start(bf16[2,128,128]{2,1,0:T(8,128)(2,1)S(1)} %get-tuple-element.59), channel_id=1, source_target_pairs={{0,8},{1,7},{2,10},{3,5},{4,12},{5,3},{6,14},{7,1},{8,0},{9,15},{1... | collective-permute-start | bytes 196616 | tf_op jit(solution)/shard_map/ppermute | solution.py:164
  45.3 1.4 %collective-permute-start.24 = (bf16[4,128,128]{2,1,0:T(8,128)(2,1)S(1)}, bf16[4,128,128]{2,1,0:T(8,128)(2,1)S(1)}, u32[]{:S(2)}, u32[]{:S(2)}) collective-permute-start(bf16[4,128,128]{2,1,0:T(8,128)(2,1)S(1)} %shard_map.88), channel_id=1, source_target_pairs={{0,1},{1,0},{2,3},{3,2},{4,5},{5,4},{6,7},{7,6},{8,9},{9,8},{10,11... | collective-permute-start | bytes 393224 | tf_op jit(solution)/shard_map/ppermute | solution.py:153

commit v3 on v2

v3 whole, which is shorter than its diff:
```python
import functools

import jax
import jax.numpy as jnp
from jax import lax
from jax.experimental import pallas as pl
from jax.experimental.pallas import tpu as pltpu
from jax.sharding import PartitionSpec as P

DH = 128
EPSILON = 1e-06
QUAD = 4
ORDER = (3, 2, 1, 0)
CHUNKS = 4
LOW, WIDE = jnp.bfloat16, jnp.float32


def dot(a, b, contract):
    return lax.dot_general(a, b, ((contract[0], contract[1]), ((), ())), preferred_element_type=WIDE)


def head(ref, h):
    return ref.at[:, pl.ds(pl.multiple_of(h * DH, DH), DH)]


def fixed(ref, h):
    return ref.at[:, h * DH : (h + 1) * DH]


def causal_mask(count):
    row = lax.broadcasted_iota(jnp.int32, (count, count), 0)
    col = lax.broadcasted_iota(jnp.int32, (count, count), 1)
    return row >= col


def member_of_quad():
    return lax.axis_index("seq") % QUAD


def call(kernel, outs, args, flops, in_specs=None, scratch_shapes=(), room=32):
    size = sum(x.size * x.dtype.itemsize for x in list(args) + list(outs))
    return pl.pallas_call(
        kernel,
        out_shape=outs,
        in_specs=in_specs or [pl.BlockSpec(memory_space=pltpu.VMEM)] * len(args),
        out_specs=[pl.BlockSpec(memory_space=pltpu.VMEM)] * len(outs),
        scratch_shapes=scratch_shapes,
        cost_estimate=pl.CostEstimate(flops=flops, bytes_accessed=size, transcendentals=0),
        compiler_params=pltpu.CompilerParams(vmem_limit_bytes=int(room * 1024 * 1024)),
    )(*args)


def state_kernel(k_ref, v_ref, o0, o1, o2, o3, k_buf, v_buf, sems):
    rows = k_ref.shape[0] // CHUNKS
    copies = []
    for i in range(CHUNKS):
        for n, (ref, buf) in enumerate(((k_ref, k_buf), (v_ref, v_buf))):
            part = pl.ds(i * rows, rows)
            copies.append(pltpu.make_async_copy(ref.at[part], buf.at[part], sems.at[n, i]))
            copies[-1].start()
    for copy in copies:
        copy.wait()
    m = member_of_quad()
    for d, out in enumerate((o0, o1, o2, o3)):
        h = m ^ d
        out[...] = dot(head(k_buf, h)[...], head(v_buf, h)[...], ((0,), (0,))).astype(LOW)


def local_kernel(q_ref, k_ref, v_ref, scores_ref, mixed_ref):
    mask = causal_mask(q_ref.shape[0])
    for h in range(QUAD):
        raw = dot(fixed(q_ref, h)[...], fixed(k_ref, h)[...], ((1,), (1,)))
        scores = jnp.where(mask, raw, 0.0).astype(LOW)
        scores_ref[h] = scores
        fixed(mixed_ref, h)[...] = dot(scores, fixed(v_ref, h)[...], ((1,), (0,)))


def mixed_kernel(local_ref, q_ref, c_ref, p0, p1, p2, p3, mixed_ref, sums_ref):
    m = member_of_quad()
    count = q_ref.shape[0]
    square = jnp.zeros((count, DH), WIDE)
    product = jnp.zeros((count, DH), WIDE)
    for e, p_ref in enumerate((p0, p1, p2, p3)):
        h = m ^ e
        mixed = head(local_ref, h)[...] + dot(head(q_ref, h)[...], p_ref[...], ((1,), (0,)))
        head(mixed_ref, h)[...] = mixed
        square = square + mixed * mixed
        product = product + mixed * head(c_ref, h)[...].astype(WIDE)
    sums_ref[0:1, :] = jnp.sum(square.T, axis=0, keepdims=True)
    sums_ref[1:2, :] = jnp.sum(product.T, axis=0, keepdims=True)


def token_scales(sums_ref, features, count):
    inverse = lax.rsqrt(sums_ref[0:1, :] * (1.0 / features) + EPSILON)
    projection = inverse * sums_ref[1:2, :] * (1.0 / features)
    inverse = jnp.broadcast_to(inverse, (DH, count)).T
    projection = jnp.broadcast_to(projection, (DH, count)).T
    return inverse, projection


def grad_kernel(features, mixed_ref, c_ref, q_ref, sums_ref, g_ref, *outs):
    m = member_of_quad()
    inverse, projection = token_scales(sums_ref, features, q_ref.shape[0])
    for d in range(QUAD):
        h = m ^ d
        normed = head(mixed_ref, h)[...] * inverse
        grad = (inverse * (head(c_ref, h)[...].astype(WIDE) - normed * projection)).astype(LOW)
        head(g_ref, h)[...] = grad
        outs[d][...] = dot(head(q_ref, h)[...], grad, ((0,), (0,))).astype(LOW)


def back_kernel(features, q_ref, k_ref, v_ref, g_ref, scores_ref, mixed_ref, sums_ref, p0, p1, p2, p3,
                normed_ref, query_ref, key_ref, value_ref):
    m = member_of_quad()
    count = q_ref.shape[0]
    mask = causal_mask(count)
    inverse, _ = token_scales(sums_ref, features, count)
    for e, p_ref in enumerate((p0, p1, p2, p3)):
        h = m ^ e
        grad = head(g_ref, h)[...]
        head(normed_ref, h)[...] = (head(mixed_ref, h)[...] * inverse).astype(LOW)
        raw = dot(grad, head(v_ref, h)[...], ((1,), (1,)))
        coefs = jnp.where(mask, raw, 0.0).astype(LOW)
        query = dot(coefs, head(k_ref, h)[...], ((1,), (0,))) + dot(grad, p_ref[...], ((1,), (1,)))
        head(query_ref, h)[...] = query.astype(LOW)
        head(key_ref, h)[...] = dot(coefs, head(q_ref, h)[...], ((0,), (0,)))
        head(value_ref, h)[...] = dot(scores_ref[h], grad, ((0,), (0,)))


def last_kernel(k_ref, v_ref, key_local, value_local, p0, p1, p2, p3, key_ref, value_ref):
    m = member_of_quad()
    for e, p_ref in enumerate((p0, p1, p2, p3)):
        h = m ^ e
        suffix = p_ref[...]
        key = head(key_local, h)[...] + dot(head(v_ref, h)[...], suffix, ((1,), (1,)))
        head(key_ref, h)[...] = key.astype(LOW)
        value = head(value_local, h)[...] + dot(head(k_ref, h)[...], suffix, ((1,), (0,)))
        head(value_ref, h)[...] = value.astype(LOW)


def exchange(value, axis, bits):
    size = lax.axis_size(axis)
    return lax.ppermute(value, axis, [(i, i ^ bits) for i in range(size)])


def cross(value, bits):
    cores = lax.axis_size("tp")
    places = [(i, t) for i in range(lax.axis_size("seq")) for t in range(cores)]
    pairs = [(i * cores + t, (i ^ bits) * cores + (t ^ 1)) for i, t in places]
    return lax.ppermute(value, ("seq", "tp"), pairs)


def exclusive_sum(held, before):
    index = lax.axis_index("seq")
    m = index % QUAD
    held = [cross(held[d], d) for d in ORDER]
    held = [held[ORDER.index(d)].astype(WIDE) for d in range(QUAD)]
    total = (held[0] + held[1] + held[2] + held[3]).astype(LOW)

    def counts(a, b):
        return a < b if before else a > b

    outer = jnp.zeros_like(held[0])
    for bits in range(QUAD, lax.axis_size("seq"), QUAD):
        got = exchange(total, "seq", bits).astype(WIDE)
        outer = outer + jnp.where(counts(index ^ bits, index), got, 0.0)
    sums = []
    for e in range(QUAD):
        inner = outer
        for d in range(QUAD):
            if d != e:
                inner = inner + jnp.where(counts(m ^ d, m ^ e), held[d], 0.0)
        sums.append(inner.astype(LOW))
    sums = [cross(sums[e], e) for e in ORDER]
    return [sums[ORDER.index(e)] for e in range(QUAD)]


def sum_over_heads(value):
    bit = 1
    while bit < lax.axis_size("tp"):
        value = value + exchange(value, "tp", bit)
        bit *= 2
    return value


def body(q, k, v, c):
    count, width = q.shape
    features = width * lax.axis_size("tp")
    shape = jax.ShapeDtypeStruct
    state = shape((DH, DH), LOW)
    wide = shape((count, width), WIDE)
    low = shape((count, width), LOW)
    unit = 2 * count * DH * DH * QUAD
    held = call(
        state_kernel, [state] * QUAD, (k, v), unit, room=53.75,
        in_specs=[pl.BlockSpec(memory_space=pltpu.HBM)] * 2,
        scratch_shapes=[pltpu.VMEM(k.shape, LOW)] * 2 + [pltpu.SemaphoreType.DMA((2, CHUNKS))],
    )
    scores, local = call(
        local_kernel, [shape((QUAD, count, count), LOW), wide], (q, k, v), 4 * unit
    )
    prefix = exclusive_sum(held, True)
    mixed, sums = call(
        mixed_kernel, [wide, shape((2, count), WIDE)], (local, q, c, *prefix), unit
    )
    sums = sum_over_heads(sums)
    g, *terms = call(
        functools.partial(grad_kernel, features), [low] + [state] * QUAD, (mixed, c, q, sums), unit
    )
    normed_out, query_grad, key_local, value_local = call(
        functools.partial(back_kernel, features),
        [low, low, wide, wide],
        (q, k, v, g, scores, mixed, sums, *prefix),
        9 * unit,
    )
    suffix = exclusive_sum(terms, False)
    key_grad, value_grad = call(
        last_kernel, [low, low], (k, v, key_local, value_local, *suffix), 2 * unit
    )
    return (normed_out, query_grad, key_grad, value_grad)


def solution(mesh):
    spec = P("seq", "tp")
    return jax.shard_map(body, mesh=mesh, in_specs=(spec,) * 4, out_specs=(spec,) * 4, check_vma=False)
```

time: 47.9 us -> 46.7 us (0.975)
  waiting for transfers between devices: 13.4 us -> 15.4 us
  local copies, waits for them, and re-layouts: 1.92 us -> 0.02 us
  Pallas kernels: 7.47 us -> 5.99 us
    ppermute x25 -> x23, waiting for transfers between devices: 13.4 us -> 15.4 us  [the longest x16 8.27 us: cross(): return lax.ppermute(value, ('seq', 'tp'), pairs)]
    unnamed x12 -> x8, local copies, waits for them, and re-layouts: 1.92 us -> 0.02 us
    pallas_call x15 -> x6, Pallas kernels: 7.47 us -> 5.99 us  [call(): pl.pallas_call(kernel, out_shape=outs, in_specs=in_specs or [pl.BlockSpec...]
    ppermute x25 -> x23, starting transfers between devices: 24.1 us -> 24.1 us  [the longest x16 14.6 us: cross(): return lax.ppermute(value, ('seq', 'tp'), pairs)]
  transfers between devices with their start and end apart: 25 -> 23, of which waited for: 16 -> 14; matrix products, arithmetic and copies ran while one was open for 0% -> 0% of each run, Pallas kernels for 10% -> 6%
where the time goes in v3:
time: 46.7 us; the launch traced here: 46.5 us
  starting transfers between devices  24.1 us (52%)
  waiting for transfers between devices  15.4 us (33%)
  Pallas kernels  5.99 us (13%)
  between operations  0.72 us (2%)
    ppermute x16, starting transfers between devices, cross(): return lax.ppermute(value, ('seq', 'tp'), pairs)  14.6 us
    ppermute x7, starting transfers between devices, exchange(): return lax.ppermute(value, axis, [(i, i ^ bits) for i in range(size)])  9.48 us
    ppermute x16, waiting for transfers between devices, cross(): return lax.ppermute(value, ('seq', 'tp'), pairs)  8.27 us
    ppermute x7, waiting for transfers between devices, exchange(): return lax.ppermute(value, axis, [(i, i ^ bits) for i in range(size)])  7.13 us
    pallas_call x6, Pallas kernels, call(): pl.pallas_call(kernel, out_shape=outs, in_specs=in_specs or [pl.BlockSpec...  5.99 us
  transfers between devices with their start and end apart: 23, of which 14 were waited for; matrix products, arithmetic and copies ran while one was open for 0% of the time, Pallas kernels for 6%

profile of v3, /device:TPU:0, one launch (start us, length us, event | category | flops | bytes accessed | tf_op | source)
XLA Modules:
  0.0 46.5 jit_solution(16080560538372307405)
XLA Ops:
  0.6 1.4 %shard_map.76 = (bf16[128,128]{1,0:T(8,128)(2,1)S(1)}, bf16[128,128]{1,0:T(8,128)(2,1)S(1)}, bf16[128,128]{1,0:T(8,128)(2,1)S(1)}, bf16[128,128]{1,0:T(8,128)(2,1)S(1)}) custom-call(bf16[256,512]{1,0:T(8,128)(2,1)} %k_ref.7, bf16[256,512]{1,0:T(8,128)(2,1)} %v_ref.7), custom_call_target="tpu_custom_call" | custom-call | flops 33554432 | bytes 655360 | tf_op jit(solution)/shard_map/pallas_call | solution.py:42
  2.0 0.5 %collective-permute-start = (bf16[128,128]{1,0:T(8,128)(2,1)S(1)}, bf16[128,128]{1,0:T(8,128)(2,1)S(1)}, u32[]{:S(2)}, u32[]{:S(2)}) collective-permute-start(bf16[128,128]{1,0:T(8,128)(2,1)S(1)} %get-tuple-element.24), channel_id=1, source_target_pairs={{0,1},{1,0},{2,3},{3,2},{4,5},{5,4},{6,7},{7,6},{8,9},{9,8},{10,11... | collective-permute-start | bytes 98312 | tf_op jit(solution)/shard_map/ppermute | solution.py:150
  2.6 2.6 %collective-permute-start.1 = (bf16[128,128]{1,0:T(8,128)(2,1)S(1)}, bf16[128,128]{1,0:T(8,128)(2,1)S(1)}, u32[]{:S(2)}, u32[]{:S(2)}) collective-permute-start(bf16[128,128]{1,0:T(8,128)(2,1)S(1)} %get-tuple-element.25), channel_id=1, source_target_pairs={{0,3},{1,2},{2,1},{3,0},{4,7},{5,6},{6,5},{7,4},{8,11},{9,10},{10,... | collective-permute-start | bytes 98312 | tf_op jit(solution)/shard_map/ppermute | solution.py:150
  5.2 1.2 %collective-permute-start.2 = (bf16[128,128]{1,0:T(8,128)(2,1)S(1)}, bf16[128,128]{1,0:T(8,128)(2,1)S(1)}, u32[]{:S(2)}, u32[]{:S(2)}) collective-permute-start(bf16[128,128]{1,0:T(8,128)(2,1)S(1)} %get-tuple-element.26), channel_id=1, source_target_pairs={{0,5},{1,4},{2,7},{3,6},{4,1},{5,0},{6,3},{7,2},{8,13},{9,12},{10,... | collective-permute-start | bytes 98312 | tf_op jit(solution)/shard_map/ppermute | solution.py:150
  6.4 0.5 collective-permute-done.1
  6.9 1.8 %collective-permute-done.2 = bf16[128,128]{1,0:T(8,128)(2,1)S(1)} collective-permute-done((bf16[128,128]{1,0:T(8,128)(2,1)S(1)}, bf16[128,128]{1,0:T(8,128)(2,1)S(1)}, u32[]{:S(2)}, u32[]{:S(2)}) %collective-permute-start.2) | collective-permute-done | bytes 32800 | tf_op jit(solution)/shard_map/ppermute | solution.py:150
  8.6 2.0 %collective-permute-done.3 = bf16[128,128]{1,0:T(8,128)(2,1)S(1)} collective-permute-done((bf16[128,128]{1,0:T(8,128)(2,1)S(1)}, bf16[128,128]{1,0:T(8,128)(2,1)S(1)}, u32[]{:S(2)}, u32[]{:S(2)}) %collective-permute-start.3) | collective-permute-done | bytes 32800 | tf_op jit(solution)/shard_map/ppermute | solution.py:150
  10.6 3.7 %collective-permute-start.6 = (bf16[128,128]{1,0:T(8,128)(2,1)S(1)}, bf16[128,128]{1,0:T(8,128)(2,1)S(1)}, u32[]{:S(2)}, u32[]{:S(2)}) collective-permute-start(bf16[128,128]{1,0:T(8,128)(2,1)S(1)} %fusion.16), channel_id=1, source_target_pairs={{0,24},{2,26},{4,28},{6,30},{8,16},{10,18},{12,20},{14,22},{16,8},... | collective-permute-start | bytes 98312 | tf_op jit(solution)/shard_map/ppermute | solution.py:143
  14.3 0.8 %collective-permute-start.4 = (bf16[128,128]{1,0:T(8,128)(2,1)S(1)}, bf16[128,128]{1,0:T(8,128)(2,1)S(1)}, u32[]{:S(2)}, u32[]{:S(2)}) collective-permute-start(bf16[128,128]{1,0:T(8,128)(2,1)S(1)} %fusion.16), channel_id=1, source_target_pairs={{0,8},{2,10},{4,12},{6,14},{8,0},{10,2},{12,4},{14,6},{16,24},{18,... | collective-permute-start | bytes 98312 | tf_op jit(solution)/shard_map/ppermute | solution.py:143
  15.1 1.3 %collective-permute-done.6 = bf16[128,128]{1,0:T(8,128)(2,1)S(1)} collective-permute-done((bf16[128,128]{1,0:T(8,128)(2,1)S(1)}, bf16[128,128]{1,0:T(8,128)(2,1)S(1)}, u32[]{:S(2)}, u32[]{:S(2)}) %collective-permute-start.6) | collective-permute-done | bytes 32800 | tf_op jit(solution)/shard_map/ppermute | solution.py:143
  16.4 2.7 %collective-permute-done.5 = bf16[128,128]{1,0:T(8,128)(2,1)S(1)} collective-permute-done((bf16[128,128]{1,0:T(8,128)(2,1)S(1)}, bf16[128,128]{1,0:T(8,128)(2,1)S(1)}, u32[]{:S(2)}, u32[]{:S(2)}) %collective-permute-start.5) | collective-permute-done | bytes 32800 | tf_op jit(solution)/shard_map/ppermute | solution.py:143
  19.3 0.6 %collective-permute-start.7 = (bf16[128,128]{1,0:T(8,128)(2,1)S(1)}, bf16[128,128]{1,0:T(8,128)(2,1)S(1)}, u32[]{:S(2)}, u32[]{:S(2)}) collective-permute-start(bf16[128,128]{1,0:T(8,128)(2,1)S(1)} %get-tuple-element.46), channel_id=1, source_target_pairs={{0,1},{1,0},{2,3},{3,2},{4,5},{5,4},{6,7},{7,6},{8,9},{9,8},{10,11... | collective-permute-start | bytes 98312 | tf_op jit(solution)/shard_map/ppermute | solution.py:150
  19.9 1.1 %collective-permute-start.8 = (bf16[128,128]{1,0:T(8,128)(2,1)S(1)}, bf16[128,128]{1,0:T(8,128)(2,1)S(1)}, u32[]{:S(2)}, u32[]{:S(2)}) collective-permute-start(bf16[128,128]{1,0:T(8,128)(2,1)S(1)} %get-tuple-element.47), channel_id=1, source_target_pairs={{0,3},{1,2},{2,1},{3,0},{4,7},{5,6},{6,5},{7,4},{8,11},{9,10},{10,... | collective-permute-start | bytes 98312 | tf_op jit(solution)/shard_map/ppermute | solution.py:150
  21.0 1.7 %collective-permute-start.9 = (bf16[128,128]{1,0:T(8,128)(2,1)S(1)}, bf16[128,128]{1,0:T(8,128)(2,1)S(1)}, u32[]{:S(2)}, u32[]{:S(2)}) collective-permute-start(bf16[128,128]{1,0:T(8,128)(2,1)S(1)} %fusion.7), channel_id=1, source_target_pairs={{0,5},{1,4},{2,7},{3,6},{4,1},{5,0},{6,3},{7,2},{8,13},{9,12},{10,... | collective-permute-start | bytes 98312 | tf_op jit(solution)/shard_map/ppermute | solution.py:150
  22.7 0.7 %shard_map.75 = (bf16[4,256,256]{2,1,0:T(8,128)(2,1)S(1)}, f32[256,512]{1,0:T(8,128)S(1)}) custom-call(bf16[256,512]{1,0:T(8,128)(2,1)S(1)} %copy-done.2, bf16[256,512]{1,0:T(8,128)(2,1)S(1)} %copy-done, bf16[256,512]{1,0:T(8,128)(2,1)S(1)} %copy-done.1), custom_call_target="tpu_custom_call" | custom-call | flops 134217728 | bytes 1835008 | tf_op jit(solution)/shard_map/pallas_call | solution.py:42
  23.5 0.9 %collective-permute-done.9.p2 = bf16[128,128]{1,0:T(8,128)(2,1)S(1)} collective-permute-done((bf16[128,128]{1,0:T(8,128)(2,1)S(1)}, bf16[128,128]{1,0:T(8,128)(2,1)S(1)}, u32[]{:S(2)}, u32[]{:S(2)}) %collective-permute-start.9) | collective-permute-done | bytes 32800 | tf_op jit(solution)/shard_map/ppermute | solution.py:150
  24.8 0.6 %collective-permute-start.11 = (f32[2,256]{1,0:T(2,128)S(1)}, f32[2,256]{1,0:T(2,128)S(1)}, u32[]{:S(2)}, u32[]{:S(2)}) collective-permute-start(f32[2,256]{1,0:T(2,128)S(1)} %get-tuple-element.29), channel_id=1, source_target_pairs={{0,1},{1,0},{2,3},{3,2},{4,5},{5,4},{6,7},{7,6},{8,9},{9,8},{10,11... | collective-permute-start | bytes 6152 | tf_op jit(solution)/shard_map/ppermute | solution.py:143
  25.4 0.8 %collective-permute-done.11 = f32[2,256]{1,0:T(2,128)S(1)} collective-permute-done((f32[2,256]{1,0:T(2,128)S(1)}, f32[2,256]{1,0:T(2,128)S(1)}, u32[]{:S(2)}, u32[]{:S(2)}) %collective-permute-start.11) | collective-permute-done | bytes 2080 | tf_op jit(solution)/shard_map/ppermute | solution.py:143
  26.2 0.4 shard_map.78
  27.4 1.4 %collective-permute-start.14 = (bf16[128,128]{1,0:T(8,128)(2,1)S(1)}, bf16[128,128]{1,0:T(8,128)(2,1)S(1)}, u32[]{:S(2)}, u32[]{:S(2)}) collective-permute-start(bf16[128,128]{1,0:T(8,128)(2,1)S(1)} %get-tuple-element.38), channel_id=1, source_target_pairs={{0,5},{1,4},{2,7},{3,6},{4,1},{5,0},{6,3},{7,2},{8,13},{9,12},{10,... | collective-permute-start | bytes 98312 | tf_op jit(solution)/shard_map/ppermute | solution.py:150
  28.8 1.2 %collective-permute-start.15 = (bf16[128,128]{1,0:T(8,128)(2,1)S(1)}, bf16[128,128]{1,0:T(8,128)(2,1)S(1)}, u32[]{:S(2)}, u32[]{:S(2)}) collective-permute-start(bf16[128,128]{1,0:T(8,128)(2,1)S(1)} %get-tuple-element.39), channel_id=1, source_target_pairs={{0,7},{1,6},{2,5},{3,4},{4,3},{5,2},{6,1},{7,0},{8,15},{9,14},{10,... | collective-permute-start | bytes 98312 | tf_op jit(solution)/shard_map/ppermute | solution.py:150
  30.7 2.3 %collective-permute-done.15 = bf16[128,128]{1,0:T(8,128)(2,1)S(1)} collective-permute-done((bf16[128,128]{1,0:T(8,128)(2,1)S(1)}, bf16[128,128]{1,0:T(8,128)(2,1)S(1)}, u32[]{:S(2)}, u32[]{:S(2)}) %collective-permute-start.15) | collective-permute-done | bytes 32800 | tf_op jit(solution)/shard_map/ppermute | solution.py:150
  33.1 1.7 %collective-permute-start.18 = (bf16[128,128]{1,0:T(8,128)(2,1)S(1)}, bf16[128,128]{1,0:T(8,128)(2,1)S(1)}, u32[]{:S(2)}, u32[]{:S(2)}) collective-permute-start(bf16[128,128]{1,0:T(8,128)(2,1)S(1)} %fusion.33), channel_id=1, source_target_pairs={{0,24},{2,26},{4,28},{6,30},{8,16},{10,18},{12,20},{14,22},{16,8},... | collective-permute-start | bytes 98312 | tf_op jit(solution)/shard_map/ppermute | solution.py:143
  34.8 0.5 %collective-permute-start.17 = (bf16[128,128]{1,0:T(8,128)(2,1)S(1)}, bf16[128,128]{1,0:T(8,128)(2,1)S(1)}, u32[]{:S(2)}, u32[]{:S(2)}) collective-permute-start(bf16[128,128]{1,0:T(8,128)(2,1)S(1)} %fusion.33), channel_id=1, source_target_pairs={{0,16},{2,18},{4,20},{6,22},{8,24},{10,26},{12,28},{14,30},{16,0},... | collective-permute-start | bytes 98312 | tf_op jit(solution)/shard_map/ppermute | solution.py:143
  35.3 2.3 %collective-permute-start.16 = (bf16[128,128]{1,0:T(8,128)(2,1)S(1)}, bf16[128,128]{1,0:T(8,128)(2,1)S(1)}, u32[]{:S(2)}, u32[]{:S(2)}) collective-permute-start(bf16[128,128]{1,0:T(8,128)(2,1)S(1)} %fusion.33), channel_id=1, source_target_pairs={{0,8},{2,10},{4,12},{6,14},{8,0},{10,2},{12,4},{14,6},{16,24},{18,... | collective-permute-start | bytes 98312 | tf_op jit(solution)/shard_map/ppermute | solution.py:143
  37.5 1.6 %collective-permute-done.18 = bf16[128,128]{1,0:T(8,128)(2,1)S(1)} collective-permute-done((bf16[128,128]{1,0:T(8,128)(2,1)S(1)}, bf16[128,128]{1,0:T(8,128)(2,1)S(1)}, u32[]{:S(2)}, u32[]{:S(2)}) %collective-permute-start.18) | collective-permute-done | bytes 32800 | tf_op jit(solution)/shard_map/ppermute | solution.py:143
  39.2 0.5 collective-permute-done.17
  39.9 0.5 %collective-permute-start.22 = (bf16[128,128]{1,0:T(8,128)(2,1)S(1)}, bf16[128,128]{1,0:T(8,128)(2,1)S(1)}, u32[]{:S(2)}, u32[]{:S(2)}) collective-permute-start(bf16[128,128]{1,0:T(8,128)(2,1)S(1)} %get-tuple-element.42), channel_id=1, source_target_pairs={{0,7},{1,6},{2,5},{3,4},{4,3},{5,2},{6,1},{7,0},{8,15},{9,14},{10,... | collective-permute-start | bytes 98312 | tf_op jit(solution)/shard_map/ppermute | solution.py:150
  40.4 1.2 %collective-permute-start.19 = (bf16[128,128]{1,0:T(8,128)(2,1)S(1)}, bf16[128,128]{1,0:T(8,128)(2,1)S(1)}, u32[]{:S(2)}, u32[]{:S(2)}) collective-permute-start(bf16[128,128]{1,0:T(8,128)(2,1)S(1)} %get-tuple-element.43), channel_id=1, source_target_pairs={{0,1},{1,0},{2,3},{3,2},{4,5},{5,4},{6,7},{7,6},{8,9},{9,8},{10,11... | collective-permute-start | bytes 98312 | tf_op jit(solution)/shard_map/ppermute | solution.py:150
  41.7 1.7 %collective-permute-start.21 = (bf16[128,128]{1,0:T(8,128)(2,1)S(1)}, bf16[128,128]{1,0:T(8,128)(2,1)S(1)}, u32[]{:S(2)}, u32[]{:S(2)}) collective-permute-start(bf16[128,128]{1,0:T(8,128)(2,1)S(1)} %fusion.24), channel_id=1, source_target_pairs={{0,5},{1,4},{2,7},{3,6},{4,1},{5,0},{6,3},{7,2},{8,13},{9,12},{10,... | collective-permute-start | bytes 98312 | tf_op jit(solution)/shard_map/ppermute | solution.py:150
  43.4 2.0 %shard_map.79 = (bf16[256,512]{1,0:T(8,128)(2,1)}, bf16[256,512]{1,0:T(8,128)(2,1)}, f32[256,512]{1,0:T(8,128)S(1)}, f32[256,512]{1,0:T(8,128)S(1)}) custom-call(bf16[256,512]{1,0:T(8,128)(2,1)S(1)} %copy-done.2, bf16[256,512]{1,0:T(8,128)(2,1)S(1)} %copy-done, bf16[256,512]{1,0:T(8,128)(2,1)S(1)} %copy-done.1, ...), custom_call_target="tpu_custom_call" | custom-call | flops 301989888 | bytes 3803136 | tf_op jit(solution)/shard_map/pallas_call | solution.py:42
  45.5 1.1 %shard_map.80 = (bf16[256,512]{1,0:T(8,128)(2,1)}, bf16[256,512]{1,0:T(8,128)(2,1)}) custom-call(bf16[256,512]{1,0:T(8,128)(2,1)S(1)} %copy-done, bf16[256,512]{1,0:T(8,128)(2,1)S(1)} %copy-done.1, f32[256,512]{1,0:T(8,128)S(1)} %get-tuple-element.34.key_local, f32[256,512]{1,0:T(8,128)S(1)} %get-tuple-element.35.value_local, ...), custom_call_target="tpu_custom_call" | custom-call | flops 67108864 | bytes 2228224 | tf_op jit(solution)/shard_map/pallas_call | solution.py:42
  (35 shorter events, 2.7 us)
Async XLA Ops:
  2.0 4.3 %collective-permute-start = (bf16[128,128]{1,0:T(8,128)(2,1)S(1)}, bf16[128,128]{1,0:T(8,128)(2,1)S(1)}, u32[]{:S(2)}, u32[]{:S(2)}) collective-permute-start(bf16[128,128]{1,0:T(8,128)(2,1)S(1)} %get-tuple-element.24), channel_id=1, source_target_pairs={{0,1},{1,0},{2,3},{3,2},{4,5},{5,4},{6,7},{7,6},{8,9},{9,8},{10,11... | collective-permute-start | bytes 98312 | tf_op jit(solution)/shard_map/ppermute | solution.py:150
  2.6 4.3 %collective-permute-start.1 = (bf16[128,128]{1,0:T(8,128)(2,1)S(1)}, bf16[128,128]{1,0:T(8,128)(2,1)S(1)}, u32[]{:S(2)}, u32[]{:S(2)}) collective-permute-start(bf16[128,128]{1,0:T(8,128)(2,1)S(1)} %get-tuple-element.25), channel_id=1, source_target_pairs={{0,3},{1,2},{2,1},{3,0},{4,7},{5,6},{6,5},{7,4},{8,11},{9,10},{10,... | collective-permute-start | bytes 98312 | tf_op jit(solution)/shard_map/ppermute | solution.py:150
  5.2 3.4 %collective-permute-start.2 = (bf16[128,128]{1,0:T(8,128)(2,1)S(1)}, bf16[128,128]{1,0:T(8,128)(2,1)S(1)}, u32[]{:S(2)}, u32[]{:S(2)}) collective-permute-start(bf16[128,128]{1,0:T(8,128)(2,1)S(1)} %get-tuple-element.26), channel_id=1, source_target_pairs={{0,5},{1,4},{2,7},{3,6},{4,1},{5,0},{6,3},{7,2},{8,13},{9,12},{10,... | collective-permute-start | bytes 98312 | tf_op jit(solution)/shard_map/ppermute | solution.py:150
  6.4 4.2 %collective-permute-start.3 = (bf16[128,128]{1,0:T(8,128)(2,1)S(1)}, bf16[128,128]{1,0:T(8,128)(2,1)S(1)}, u32[]{:S(2)}, u32[]{:S(2)}) collective-permute-start(bf16[128,128]{1,0:T(8,128)(2,1)S(1)} %get-tuple-element.27), channel_id=1, source_target_pairs={{0,7},{1,6},{2,5},{3,4},{4,3},{5,2},{6,1},{7,0},{8,15},{9,14},{10,... | collective-permute-start | bytes 98312 | tf_op jit(solution)/shard_map/ppermute | solution.py:150
  10.6 12.1 %copy-start.2 = (bf16[256,512]{1,0:T(8,128)(2,1)S(1)}, bf16[256,512]{1,0:T(8,128)(2,1)}, u32[]{:S(2)}) copy-start(bf16[256,512]{1,0:T(8,128)(2,1)} %q_ref.7) | copy-start | bytes 786436
  10.6 5.8 %collective-permute-start.6 = (bf16[128,128]{1,0:T(8,128)(2,1)S(1)}, bf16[128,128]{1,0:T(8,128)(2,1)S(1)}, u32[]{:S(2)}, u32[]{:S(2)}) collective-permute-start(bf16[128,128]{1,0:T(8,128)(2,1)S(1)} %fusion.16), channel_id=1, source_target_pairs={{0,24},{2,26},{4,28},{6,30},{8,16},{10,18},{12,20},{14,22},{16,8},... | collective-permute-start | bytes 98312 | tf_op jit(solution)/shard_map/ppermute | solution.py:143
  14.3 4.8 %collective-permute-start.5 = (bf16[128,128]{1,0:T(8,128)(2,1)S(1)}, bf16[128,128]{1,0:T(8,128)(2,1)S(1)}, u32[]{:S(2)}, u32[]{:S(2)}) collective-permute-start(bf16[128,128]{1,0:T(8,128)(2,1)S(1)} %fusion.16), channel_id=1, source_target_pairs={{0,16},{2,18},{4,20},{6,22},{8,24},{10,26},{12,28},{14,30},{16,0},... | collective-permute-start | bytes 98312 | tf_op jit(solution)/shard_map/ppermute | solution.py:143
  14.3 4.8 %collective-permute-start.4 = (bf16[128,128]{1,0:T(8,128)(2,1)S(1)}, bf16[128,128]{1,0:T(8,128)(2,1)S(1)}, u32[]{:S(2)}, u32[]{:S(2)}) collective-permute-start(bf16[128,128]{1,0:T(8,128)(2,1)S(1)} %fusion.16), channel_id=1, source_target_pairs={{0,8},{2,10},{4,12},{6,14},{8,0},{10,2},{12,4},{14,6},{16,24},{18,... | collective-permute-start | bytes 98312 | tf_op jit(solution)/shard_map/ppermute | solution.py:143
  15.1 7.6 %copy-start = (bf16[256,512]{1,0:T(8,128)(2,1)S(1)}, bf16[256,512]{1,0:T(8,128)(2,1)}, u32[]{:S(2)}) copy-start(bf16[256,512]{1,0:T(8,128)(2,1)} %k_ref.7) | copy-start | bytes 786436
  15.1 7.6 %copy-start.1 = (bf16[256,512]{1,0:T(8,128)(2,1)S(1)}, bf16[256,512]{1,0:T(8,128)(2,1)}, u32[]{:S(2)}) copy-start(bf16[256,512]{1,0:T(8,128)(2,1)} %v_ref.7) | copy-start | bytes 786436
  19.2 4.3 %collective-permute-start.10 = (bf16[128,128]{1,0:T(8,128)(2,1)S(1)}, bf16[128,128]{1,0:T(8,128)(2,1)S(1)}, u32[]{:S(2)}, u32[]{:S(2)}) collective-permute-start(bf16[128,128]{1,0:T(8,128)(2,1)S(1)} %get-tuple-element.45), channel_id=1, source_target_pairs={{0,7},{1,6},{2,5},{3,4},{4,3},{5,2},{6,1},{7,0},{8,15},{9,14},{10,... | collective-permute-start | bytes 98312 | tf_op jit(solution)/shard_map/ppermute | solution.py:150
  19.3 4.2 %collective-permute-start.7 = (bf16[128,128]{1,0:T(8,128)(2,1)S(1)}, bf16[128,128]{1,0:T(8,128)(2,1)S(1)}, u32[]{:S(2)}, u32[]{:S(2)}) collective-permute-start(bf16[128,128]{1,0:T(8,128)(2,1)S(1)} %get-tuple-element.46), channel_id=1, source_target_pairs={{0,1},{1,0},{2,3},{3,2},{4,5},{5,4},{6,7},{7,6},{8,9},{9,8},{10,11... | collective-permute-start | bytes 98312 | tf_op jit(solution)/shard_map/ppermute | solution.py:150
  19.9 3.6 %collective-permute-start.8 = (bf16[128,128]{1,0:T(8,128)(2,1)S(1)}, bf16[128,128]{1,0:T(8,128)(2,1)S(1)}, u32[]{:S(2)}, u32[]{:S(2)}) collective-permute-start(bf16[128,128]{1,0:T(8,128)(2,1)S(1)} %get-tuple-element.47), channel_id=1, source_target_pairs={{0,3},{1,2},{2,1},{3,0},{4,7},{5,6},{6,5},{7,4},{8,11},{9,10},{10,... | collective-permute-start | bytes 98312 | tf_op jit(solution)/shard_map/ppermute | solution.py:150
  21.0 3.4 %copy-start.3 = (bf16[256,512]{1,0:T(8,128)(2,1)S(1)}, bf16[256,512]{1,0:T(8,128)(2,1)}, u32[]{:S(2)}) copy-start(bf16[256,512]{1,0:T(8,128)(2,1)} %c_ref.3) | copy-start | bytes 786436
  21.0 3.4 %collective-permute-start.9 = (bf16[128,128]{1,0:T(8,128)(2,1)S(1)}, bf16[128,128]{1,0:T(8,128)(2,1)S(1)}, u32[]{:S(2)}, u32[]{:S(2)}) collective-permute-start(bf16[128,128]{1,0:T(8,128)(2,1)S(1)} %fusion.7), channel_id=1, source_target_pairs={{0,5},{1,4},{2,7},{3,6},{4,1},{5,0},{6,3},{7,2},{8,13},{9,12},{10,... | collective-permute-start | bytes 98312 | tf_op jit(solution)/shard_map/ppermute | solution.py:150
  24.8 1.4 %collective-permute-start.11 = (f32[2,256]{1,0:T(2,128)S(1)}, f32[2,256]{1,0:T(2,128)S(1)}, u32[]{:S(2)}, u32[]{:S(2)}) collective-permute-start(f32[2,256]{1,0:T(2,128)S(1)} %get-tuple-element.29), channel_id=1, source_target_pairs={{0,1},{1,0},{2,3},{3,2},{4,5},{5,4},{6,7},{7,6},{8,9},{9,8},{10,11... | collective-permute-start | bytes 6152 | tf_op jit(solution)/shard_map/ppermute | solution.py:143
  26.7 3.4 %collective-permute-start.12 = (bf16[128,128]{1,0:T(8,128)(2,1)S(1)}, bf16[128,128]{1,0:T(8,128)(2,1)S(1)}, u32[]{:S(2)}, u32[]{:S(2)}) collective-permute-start(bf16[128,128]{1,0:T(8,128)(2,1)S(1)} %get-tuple-element.36), channel_id=1, source_target_pairs={{0,1},{1,0},{2,3},{3,2},{4,5},{5,4},{6,7},{7,6},{8,9},{9,8},{10,11... | collective-permute-start | bytes 98312 | tf_op jit(solution)/shard_map/ppermute | solution.py:150
  27.1 3.3 %collective-permute-start.13 = (bf16[128,128]{1,0:T(8,128)(2,1)S(1)}, bf16[128,128]{1,0:T(8,128)(2,1)S(1)}, u32[]{:S(2)}, u32[]{:S(2)}) collective-permute-start(bf16[128,128]{1,0:T(8,128)(2,1)S(1)} %get-tuple-element.37), channel_id=1, source_target_pairs={{0,3},{1,2},{2,1},{3,0},{4,7},{5,6},{6,5},{7,4},{8,11},{9,10},{10,... | collective-permute-start | bytes 98312 | tf_op jit(solution)/shard_map/ppermute | solution.py:150
  27.4 3.3 %collective-permute-start.14 = (bf16[128,128]{1,0:T(8,128)(2,1)S(1)}, bf16[128,128]{1,0:T(8,128)(2,1)S(1)}, u32[]{:S(2)}, u32[]{:S(2)}) collective-permute-start(bf16[128,128]{1,0:T(8,128)(2,1)S(1)} %get-tuple-element.38), channel_id=1, source_target_pairs={{0,5},{1,4},{2,7},{3,6},{4,1},{5,0},{6,3},{7,2},{8,13},{9,12},{10,... | collective-permute-start | bytes 98312 | tf_op jit(solution)/shard_map/ppermute | solution.py:150
  28.8 4.2 %collective-permute-start.15 = (bf16[128,128]{1,0:T(8,128)(2,1)S(1)}, bf16[128,128]{1,0:T(8,128)(2,1)S(1)}, u32[]{:S(2)}, u32[]{:S(2)}) collective-permute-start(bf16[128,128]{1,0:T(8,128)(2,1)S(1)} %get-tuple-element.39), channel_id=1, source_target_pairs={{0,7},{1,6},{2,5},{3,4},{4,3},{5,2},{6,1},{7,0},{8,15},{9,14},{10,... | collective-permute-start | bytes 98312 | tf_op jit(solution)/shard_map/ppermute | solution.py:150
  33.1 6.1 %collective-permute-start.18 = (bf16[128,128]{1,0:T(8,128)(2,1)S(1)}, bf16[128,128]{1,0:T(8,128)(2,1)S(1)}, u32[]{:S(2)}, u32[]{:S(2)}) collective-permute-start(bf16[128,128]{1,0:T(8,128)(2,1)S(1)} %fusion.33), channel_id=1, source_target_pairs={{0,24},{2,26},{4,28},{6,30},{8,16},{10,18},{12,20},{14,22},{16,8},... | collective-permute-start | bytes 98312 | tf_op jit(solution)/shard_map/ppermute | solution.py:143
  34.8 4.9 %collective-permute-start.17 = (bf16[128,128]{1,0:T(8,128)(2,1)S(1)}, bf16[128,128]{1,0:T(8,128)(2,1)S(1)}, u32[]{:S(2)}, u32[]{:S(2)}) collective-permute-start(bf16[128,128]{1,0:T(8,128)(2,1)S(1)} %fusion.33), channel_id=1, source_target_pairs={{0,16},{2,18},{4,20},{6,22},{8,24},{10,26},{12,28},{14,30},{16,0},... | collective-permute-start | bytes 98312 | tf_op jit(solution)/shard_map/ppermute | solution.py:143
  35.3 4.6 %collective-permute-start.16 = (bf16[128,128]{1,0:T(8,128)(2,1)S(1)}, bf16[128,128]{1,0:T(8,128)(2,1)S(1)}, u32[]{:S(2)}, u32[]{:S(2)}) collective-permute-start(bf16[128,128]{1,0:T(8,128)(2,1)S(1)} %fusion.33), channel_id=1, source_target_pairs={{0,8},{2,10},{4,12},{6,14},{8,0},{10,2},{12,4},{14,6},{16,24},{18,... | collective-permute-start | bytes 98312 | tf_op jit(solution)/shard_map/ppermute | solution.py:143
  39.9 5.5 %collective-permute-start.22 = (bf16[128,128]{1,0:T(8,128)(2,1)S(1)}, bf16[128,128]{1,0:T(8,128)(2,1)S(1)}, u32[]{:S(2)}, u32[]{:S(2)}) collective-permute-start(bf16[128,128]{1,0:T(8,128)(2,1)S(1)} %get-tuple-element.42), channel_id=1, source_target_pairs={{0,7},{1,6},{2,5},{3,4},{4,3},{5,2},{6,1},{7,0},{8,15},{9,14},{10,... | collective-permute-start | bytes 98312 | tf_op jit(solution)/shard_map/ppermute | solution.py:150
  40.4 5.1 %collective-permute-start.19 = (bf16[128,128]{1,0:T(8,128)(2,1)S(1)}, bf16[128,128]{1,0:T(8,128)(2,1)S(1)}, u32[]{:S(2)}, u32[]{:S(2)}) collective-permute-start(bf16[128,128]{1,0:T(8,128)(2,1)S(1)} %get-tuple-element.43), channel_id=1, source_target_pairs={{0,1},{1,0},{2,3},{3,2},{4,5},{5,4},{6,7},{7,6},{8,9},{9,8},{10,11... | collective-permute-start | bytes 98312 | tf_op jit(solution)/shard_map/ppermute | solution.py:150
  41.5 3.9 %collective-permute-start.20 = (bf16[128,128]{1,0:T(8,128)(2,1)S(1)}, bf16[128,128]{1,0:T(8,128)(2,1)S(1)}, u32[]{:S(2)}, u32[]{:S(2)}) collective-permute-start(bf16[128,128]{1,0:T(8,128)(2,1)S(1)} %get-tuple-element.44), channel_id=1, source_target_pairs={{0,3},{1,2},{2,1},{3,0},{4,7},{5,6},{6,5},{7,4},{8,11},{9,10},{10,... | collective-permute-start | bytes 98312 | tf_op jit(solution)/shard_map/ppermute | solution.py:150
  41.7 3.7 %collective-permute-start.21 = (bf16[128,128]{1,0:T(8,128)(2,1)S(1)}, bf16[128,128]{1,0:T(8,128)(2,1)S(1)}, u32[]{:S(2)}, u32[]{:S(2)}) collective-permute-start(bf16[128,128]{1,0:T(8,128)(2,1)S(1)} %fusion.24), channel_id=1, source_target_pairs={{0,5},{1,4},{2,7},{3,6},{4,1},{5,0},{6,3},{7,2},{8,13},{9,12},{10,... | collective-permute-start | bytes 98312 | tf_op jit(solution)/shard_map/ppermute | solution.py:150

commit v4 on v3

v4 whole, which is shorter than its diff:
```python
import functools

import jax
import jax.numpy as jnp
from jax import lax
from jax.experimental import pallas as pl
from jax.experimental.pallas import tpu as pltpu
from jax.sharding import PartitionSpec as P

DH = 128
EPSILON = 1e-06
QUAD = 4
ORDER = (3, 2, 1, 0)
BACK = (2, 1, 0, 3)
CHUNKS = 4
LOW, WIDE = jnp.bfloat16, jnp.float32


def dot(a, b, contract):
    return lax.dot_general(a, b, ((contract[0], contract[1]), ((), ())), preferred_element_type=WIDE)


def head(ref, h):
    return ref.at[:, pl.ds(pl.multiple_of(h * DH, DH), DH)]


def fixed(ref, h):
    return ref.at[:, h * DH : (h + 1) * DH]


def causal_mask(count):
    row = lax.broadcasted_iota(jnp.int32, (count, count), 0)
    col = lax.broadcasted_iota(jnp.int32, (count, count), 1)
    return row >= col


def member_of_quad():
    return lax.axis_index("seq") % QUAD


def call(kernel, outs, args, flops, in_specs=None, out_specs=None, scratch_shapes=(), room=32):
    size = sum(x.size * x.dtype.itemsize for x in list(args) + list(outs))
    return pl.pallas_call(
        kernel,
        out_shape=outs,
        in_specs=in_specs or [pl.BlockSpec(memory_space=pltpu.VMEM)] * len(args),
        out_specs=out_specs or [pl.BlockSpec(memory_space=pltpu.VMEM)] * len(outs),
        scratch_shapes=scratch_shapes,
        cost_estimate=pl.CostEstimate(flops=flops, bytes_accessed=size, transcendentals=0),
        compiler_params=pltpu.CompilerParams(vmem_limit_bytes=int(room * 1024 * 1024)),
    )(*args)


def state_kernel(k_ref, v_ref, o3, o2, o1, o0, k_buf, v_buf, sems):
    rows = k_ref.shape[0] // CHUNKS
    copies = []
    for i in range(CHUNKS):
        for n, (ref, buf) in enumerate(((k_ref, k_buf), (v_ref, v_buf))):
            part = pl.ds(i * rows, rows)
            copies.append(pltpu.make_async_copy(ref.at[part], buf.at[part], sems.at[n, i]))
            copies[-1].start()
    for copy in copies:
        copy.wait()
    m = member_of_quad()
    for d, out in zip(ORDER, (o3, o2, o1, o0)):
        h = m ^ d
        out[...] = dot(head(k_buf, h)[...], head(v_buf, h)[...], ((0,), (0,))).astype(LOW)


def local_kernel(q_ref, k_ref, v_ref, scores_ref, mixed_ref):
    mask = causal_mask(q_ref.shape[0])
    for h in range(QUAD):
        raw = dot(fixed(q_ref, h)[...], fixed(k_ref, h)[...], ((1,), (1,)))
        scores = jnp.where(mask, raw, 0.0).astype(LOW)
        scores_ref[h] = scores
        fixed(mixed_ref, h)[...] = dot(scores, fixed(v_ref, h)[...], ((1,), (0,)))


def pack_kernel(q_ref, k_ref, v_ref, c_ref, *outs):
    m = member_of_quad()
    for d, out in zip(ORDER, outs):
        for n, ref in enumerate((q_ref, k_ref, v_ref, c_ref)):
            out[n] = head(ref, m ^ d)[...]


def owner_local_kernel(*refs):
    mask = causal_mask(refs[0].shape[1])
    for pack, out in zip(refs[:QUAD], refs[QUAD:]):
        raw = dot(pack[0], pack[1], ((1,), (1,)))
        scores = jnp.where(mask, raw, 0.0).astype(LOW)
        out[...] = dot(scores, pack[2], ((1,), (0,)))


def exclusive_sums(before, held, got):
    index = lax.axis_index("seq")
    m = index % QUAD

    def counts(a, b):
        return jnp.where(a < b if before else a > b, 1.0, 0.0).astype(WIDE)

    outer = jnp.zeros((DH, DH), WIDE)
    for n, total in enumerate(got):
        outer = outer + total[...].astype(WIDE) * counts(index ^ (QUAD * (n + 1)), index)
    pieces = [piece[...].astype(WIDE) for piece in held]
    sums = []
    for e in ORDER:
        inner = outer
        for d, piece in zip(ORDER, pieces):
            if d != e:
                inner = inner + piece * counts(m ^ d, m ^ e)
        sums.append(inner.astype(LOW))
    return sums


def mixed_kernel(quads, *refs):
    packs, locals_, held = refs[:QUAD], refs[QUAD : 2 * QUAD], refs[2 * QUAD : 3 * QUAD]
    got = refs[3 * QUAD : 3 * QUAD + quads]
    mixed_ref, *prefixes, sums_ref = refs[3 * QUAD + quads :]
    m = member_of_quad()
    count = packs[0].shape[1]
    lane = lax.broadcasted_iota(jnp.int32, (count, DH), 1)
    columns = jnp.zeros((count, DH), WIDE)
    for n, prefix in enumerate(exclusive_sums(True, held, got)):
        prefixes[n][...] = prefix
        mixed = locals_[n][...] + dot(packs[n][0], prefix, ((1,), (0,)))
        mixed_ref[n] = mixed
        square = jnp.sum(mixed * mixed, axis=1, keepdims=True)
        product = jnp.sum(mixed * packs[n][3].astype(WIDE), axis=1, keepdims=True)
        columns = jnp.where(lane == 2 * n, square, jnp.where(lane == 2 * n + 1, product, columns))
    rows = columns.T
    for n, d in enumerate(ORDER):
        sums_ref[pl.ds(2 * (m ^ d), 1), :] = rows[2 * n : 2 * n + 1, :]
        sums_ref[pl.ds(2 * (m ^ d) + 1, 1), :] = rows[2 * n + 1 : 2 * n + 2, :]


def scales(sums_ref, member, features):
    square = sums_ref[pl.ds(2 * member, 1), :]
    product = sums_ref[pl.ds(2 * member + 1, 1), :]
    inverse = lax.rsqrt(square * (1.0 / features) + EPSILON)
    return inverse, inverse * product * (1.0 / features)


def term_kernel(features, *refs):
    packs, mixed_ref, sums_ref = refs[:QUAD], refs[QUAD], refs[QUAD + 1]
    *terms, total_ref, rows_ref = refs[QUAD + 3 :]
    m = member_of_quad()
    for n, d in enumerate(ORDER):
        inverse, projection = scales(sums_ref, m ^ d, features)
        rows_ref[2 * n : 2 * n + 1, :] = inverse
        rows_ref[2 * n + 1 : 2 * n + 2, :] = projection
    columns = rows_ref[...].T
    total = jnp.zeros((DH, DH), WIDE)
    for n in range(QUAD):
        inverse = columns[:, 2 * n : 2 * n + 1]
        projection = columns[:, 2 * n + 1 : 2 * n + 2]
        normed = mixed_ref[n] * inverse
        grad = (inverse * (packs[n][3].astype(WIDE) - normed * projection)).astype(LOW)
        term = dot(packs[n][0], grad, ((0,), (0,))).astype(LOW)
        terms[n][...] = term
        total = total + term.astype(WIDE)
    total_ref[...] = total.astype(LOW)


def suffix_kernel(quads, *refs):
    outs = refs[QUAD + quads :]
    for out, suffix in zip(outs, exclusive_sums(False, refs[:QUAD], refs[QUAD : QUAD + quads])):
        out[...] = suffix


def back_kernel(features, q_ref, k_ref, v_ref, c_ref, scores_ref, local_ref, sums_ref, p2, p1, p0, p3,
                normed_ref, query_ref, key_ref, value_ref):
    m = member_of_quad()
    count = q_ref.shape[0]
    mask = causal_mask(count)
    inverse, projection = scales(sums_ref, m, features)
    inverse = jnp.broadcast_to(inverse, (DH, count)).T
    projection = jnp.broadcast_to(projection, (DH, count)).T
    for e, p_ref in zip(BACK, (p2, p1, p0, p3)):
        h = m ^ e
        prefix = p_ref[...]
        normed = (head(local_ref, h)[...] + dot(head(q_ref, h)[...], prefix, ((1,), (0,)))) * inverse
        head(normed_ref, h)[...] = normed.astype(LOW)
        grad = (inverse * (head(c_ref, h)[...].astype(WIDE) - normed * projection)).astype(LOW)
        raw = dot(grad, head(v_ref, h)[...], ((1,), (1,)))
        coefs = jnp.where(mask, raw, 0.0).astype(LOW)
        query = dot(coefs, head(k_ref, h)[...], ((1,), (0,))) + dot(grad, prefix, ((1,), (1,)))
        head(query_ref, h)[...] = query.astype(LOW)
        head(key_ref, h)[...] = dot(coefs, head(q_ref, h)[...], ((0,), (0,)))
        head(value_ref, h)[...] = dot(scores_ref[h], grad, ((0,), (0,)))


def last_kernel(k_ref, v_ref, key_local, value_local, p2, p1, p0, p3, key_ref, value_ref):
    m = member_of_quad()
    for e, p_ref in zip(BACK, (p2, p1, p0, p3)):
        h = m ^ e
        suffix = p_ref[...]
        key = head(key_local, h)[...] + dot(head(v_ref, h)[...], suffix, ((1,), (1,)))
        head(key_ref, h)[...] = key.astype(LOW)
        value = head(value_local, h)[...] + dot(head(k_ref, h)[...], suffix, ((1,), (0,)))
        head(value_ref, h)[...] = value.astype(LOW)


def exchange(value, axis, bits):
    size = lax.axis_size(axis)
    return lax.ppermute(value, axis, [(i, i ^ bits) for i in range(size)])


def cross(value, bits):
    cores = lax.axis_size("tp")
    places = [(i, t) for i in range(lax.axis_size("seq")) for t in range(cores)]
    pairs = [(i * cores + t, (i ^ bits) * cores + (t ^ 1)) for i, t in places]
    return lax.ppermute(value, ("seq", "tp"), pairs)


def to_owners(pieces):
    return [cross(piece, d) for piece, d in zip(pieces, ORDER)]


def from_owners(pieces):
    pieces = dict(zip(ORDER, pieces))
    return [cross(pieces[d], d) for d in BACK]


def other_quads(total):
    return [exchange(total, "seq", bits) for bits in range(QUAD, lax.axis_size("seq"), QUAD)]


def add_over_heads(sums):
    bit = 1
    while bit < lax.axis_size("tp"):
        sums = sums + exchange(sums, "tp", bit)
        bit *= 2
    got = [exchange(sums, "seq", d) for d in ORDER[:-1]]
    return got[0] + got[1] + got[2] + sums


def body(q, k, v, c):
    count, width = q.shape
    features = width * lax.axis_size("tp")
    quads = lax.axis_size("seq") // QUAD - 1
    shape = jax.ShapeDtypeStruct
    state = shape((DH, DH), LOW)
    wide = shape((count, width), WIDE)
    low = shape((count, width), LOW)
    unit = 2 * count * DH * DH * QUAD
    held = call(
        state_kernel, [state] * QUAD, (k, v), unit, room=53.75,
        in_specs=[pl.BlockSpec(memory_space=pltpu.HBM)] * 2,
        scratch_shapes=[pltpu.VMEM(k.shape, LOW)] * 2 + [pltpu.SemaphoreType.DMA((2, CHUNKS))],
    )
    held = to_owners(held)
    packs = to_owners(call(pack_kernel, [shape((4, count, DH), LOW)] * QUAD, (q, k, v, c), 0))
    total = sum(piece.astype(WIDE) for piece in held).astype(LOW)
    got = other_quads(total)
    owner_local = call(owner_local_kernel, [shape((count, DH), WIDE)] * QUAD, packs, 4 * unit)
    mixed, *prefixes, sums = call(
        functools.partial(mixed_kernel, quads),
        [shape((QUAD, count, DH), WIDE)] + [state] * QUAD + [shape((2 * QUAD, count), WIDE)],
        (*packs, *owner_local, *held, *got),
        unit,
    )
    sums = add_over_heads(sums)
    scores, local = call(local_kernel, [shape((QUAD, count, count), LOW), wide], (q, k, v), 4 * unit)
    *terms, total = call(
        functools.partial(term_kernel, features),
        [state] * (QUAD + 1),
        (*packs, mixed, sums, local),
        unit,
        in_specs=[pl.BlockSpec(memory_space=pltpu.VMEM)] * (QUAD + 2) + [pl.BlockSpec(memory_space=pl.ANY)],
        scratch_shapes=[pltpu.VMEM((DH, count), WIDE)],
    )
    got = other_quads(total)
    prefixes = from_owners(prefixes)
    suffixes = call(functools.partial(suffix_kernel, quads), [state] * QUAD, (*terms, *got), 0)
    suffixes = from_owners(suffixes)
    normed_out, query_grad, key_local, value_local = call(
        functools.partial(back_kernel, features),
        [low, low, wide, wide],
        (q, k, v, c, scores, local, sums, *prefixes),
        10 * unit,
    )
    key_grad, value_grad = call(
        last_kernel, [low, low], (k, v, key_local, value_local, *suffixes), 2 * unit
    )
    return (normed_out, query_grad, key_grad, value_grad)


def solution(mesh):
    spec = P("seq", "tp")
    return jax.shard_map(body, mesh=mesh, in_specs=(spec,) * 4, out_specs=(spec,) * 4, check_vma=False)
```

time: 46.7 us -> 54.8 us (1.17)
  starting transfers between devices: 24.1 us -> 29 us
  local copies, waits for them, and re-layouts: 0.02 us -> 1.92 us
  Pallas kernels: 5.99 us -> 7.83 us
    ppermute x7 -> x10, starting transfers between devices: 9.48 us -> 15.8 us  [exchange(): return lax.ppermute(value, axis, [(i, i ^ bits) for i in range(size)])]
    unnamed x8 -> x12, local copies, waits for them, and re-layouts: 0.02 us -> 1.92 us
    pallas_call x6 -> x9, Pallas kernels: 5.99 us -> 7.83 us  [call(): pl.pallas_call(kernel, out_shape=outs, in_specs=in_specs or [pl.BlockSpec...]
    ppermute x16, starting transfers between devices: 14.6 us -> 13.2 us  [cross(): return lax.ppermute(value, ('seq', 'tp'), pairs)]
    ppermute x16, waiting for transfers between devices: 8.27 us -> 7.03 us  [cross(): return lax.ppermute(value, ('seq', 'tp'), pairs)]
    ppermute x7 -> x10, waiting for transfers between devices: 7.13 us -> 8.09 us  [exchange(): return lax.ppermute(value, axis, [(i, i ^ bits) for i in range(size)])]
  transfers between devices with their start and end apart: 23 -> 26, of which waited for: 14 -> 10; matrix products, arithmetic and copies ran while one was open for 0% -> 0% of each run, Pallas kernels for 6% -> 7%
where the time goes in v4:
time: 54.8 us; the launch traced here: 54.6 us
  starting transfers between devices  29 us (53%)
  waiting for transfers between devices  15.1 us (28%)
  Pallas kernels  7.83 us (14%)
  local copies, waits for them, and re-layouts  1.92 us (4%)
  between operations  0.75 us (1%)
    ppermute x10, starting transfers between devices, exchange(): return lax.ppermute(value, axis, [(i, i ^ bits) for i in range(size)])  15.8 us
    ppermute x16, starting transfers between devices, cross(): return lax.ppermute(value, ('seq', 'tp'), pairs)  13.2 us
    ppermute x10, waiting for transfers between devices, exchange(): return lax.ppermute(value, axis, [(i, i ^ bits) for i in range(size)])  8.09 us
    pallas_call x9, Pallas kernels, call(): pl.pallas_call(kernel, out_shape=outs, in_specs=in_specs or [pl.BlockSpec...  7.83 us
    ppermute x16, waiting for transfers between devices, cross(): return lax.ppermute(value, ('seq', 'tp'), pairs)  7.03 us
    unnamed x12, local copies, waits for them, and re-layouts  1.92 us
  transfers between devices with their start and end apart: 26, of which 10 were waited for; matrix products, arithmetic and copies ran while one was open for 0% of the time, Pallas kernels for 7%

profile of v4, /device:TPU:0, one launch (start us, length us, event | category | flops | bytes accessed | tf_op | source)
XLA Modules:
  0.0 54.6 jit_solution(8097655264284740284)
XLA Ops:
  0.7 1.5 %shard_map.78 = (bf16[128,128]{1,0:T(8,128)(2,1)S(1)}, bf16[128,128]{1,0:T(8,128)(2,1)S(1)}, bf16[128,128]{1,0:T(8,128)(2,1)S(1)}, bf16[128,128]{1,0:T(8,128)(2,1)S(1)}) custom-call(bf16[256,512]{1,0:T(8,128)(2,1)} %k_ref.9, bf16[256,512]{1,0:T(8,128)(2,1)} %v_ref.9), custom_call_target="tpu_custom_call" | custom-call | flops 33554432 | bytes 655360 | tf_op jit(solution)/shard_map/pallas_call | solution.py:43
  2.1 3.4 %collective-permute-start.4 = (bf16[128,128]{1,0:T(8,128)(2,1)S(1)}, bf16[128,128]{1,0:T(8,128)(2,1)S(1)}, u32[]{:S(2)}, u32[]{:S(2)}) collective-permute-start(bf16[128,128]{1,0:T(8,128)(2,1)S(1)} %get-tuple-element.49), channel_id=1, source_target_pairs={{0,7},{1,6},{2,5},{3,4},{4,3},{5,2},{6,1},{7,0},{8,15},{9,14},{10,... | collective-permute-start | bytes 98312 | tf_op jit(solution)/shard_map/ppermute | solution.py:212
  5.5 0.8 %collective-permute-start.5 = (bf16[128,128]{1,0:T(8,128)(2,1)S(1)}, bf16[128,128]{1,0:T(8,128)(2,1)S(1)}, u32[]{:S(2)}, u32[]{:S(2)}) collective-permute-start(bf16[128,128]{1,0:T(8,128)(2,1)S(1)} %get-tuple-element.50), channel_id=1, source_target_pairs={{0,5},{1,4},{2,7},{3,6},{4,1},{5,0},{6,3},{7,2},{8,13},{9,12},{10,... | collective-permute-start | bytes 98312 | tf_op jit(solution)/shard_map/ppermute | solution.py:212
  6.4 0.9 %copy-done.2 = bf16[256,512]{1,0:T(8,128)(2,1)S(1)} copy-done((bf16[256,512]{1,0:T(8,128)(2,1)S(1)}, bf16[256,512]{1,0:T(8,128)(2,1)}, u32[]{:S(2)}) %copy-start.2) | copy-done | bytes 262168
  7.4 0.9 %copy-done.4 = bf16[256,512]{1,0:T(8,128)(2,1)S(1)} copy-done((bf16[256,512]{1,0:T(8,128)(2,1)S(1)}, bf16[256,512]{1,0:T(8,128)(2,1)}, u32[]{:S(2)}) %copy-start.4) | copy-done | bytes 262168
  8.5 2.6 %collective-permute-start = (bf16[4,256,128]{2,1,0:T(8,128)(2,1)S(1)}, bf16[4,256,128]{2,1,0:T(8,128)(2,1)S(1)}, u32[]{:S(2)}, u32[]{:S(2)}) collective-permute-start(bf16[4,256,128]{2,1,0:T(8,128)(2,1)S(1)} %get-tuple-element.41), channel_id=1, source_target_pairs={{0,7},{1,6},{2,5},{3,4},{4,3},{5,2},{6,1},{7,0},{8,15},{9,14},{10,... | collective-permute-start | bytes 786440 | tf_op jit(solution)/shard_map/ppermute | solution.py:212
  11.2 0.6 %collective-permute-start.7 = (bf16[128,128]{1,0:T(8,128)(2,1)S(1)}, bf16[128,128]{1,0:T(8,128)(2,1)S(1)}, u32[]{:S(2)}, u32[]{:S(2)}) collective-permute-start(bf16[128,128]{1,0:T(8,128)(2,1)S(1)} %get-tuple-element.52), channel_id=1, source_target_pairs={{0,1},{1,0},{2,3},{3,2},{4,5},{5,4},{6,7},{7,6},{8,9},{9,8},{10,11... | collective-permute-start | bytes 98312 | tf_op jit(solution)/shard_map/ppermute | solution.py:212
  12.0 0.6 %collective-permute-done.7.refs_11_ = bf16[128,128]{1,0:T(8,128)(2,1)S(1)} collective-permute-done((bf16[128,128]{1,0:T(8,128)(2,1)S(1)}, bf16[128,128]{1,0:T(8,128)(2,1)S(1)}, u32[]{:S(2)}, u32[]{:S(2)}) %collective-permute-start.7) | collective-permute-done | bytes 32800 | tf_op jit(solution)/shard_map/ppermute | solution.py:212
  12.7 3.7 %collective-permute-start.10 = (bf16[128,128]{1,0:T(8,128)(2,1)S(1)}, bf16[128,128]{1,0:T(8,128)(2,1)S(1)}, u32[]{:S(2)}, u32[]{:S(2)}) collective-permute-start(bf16[128,128]{1,0:T(8,128)(2,1)S(1)} %add_convert_fusion), channel_id=1, source_target_pairs={{0,24},{2,26},{4,28},{6,30},{8,16},{10,18},{12,20},{14,22},{16,8},... | collective-permute-start | bytes 98312 | tf_op jit(solution)/shard_map/ppermute | solution.py:205
  16.3 1.8 %collective-permute-done.refs_0_ = bf16[4,256,128]{2,1,0:T(8,128)(2,1)S(1)} collective-permute-done((bf16[4,256,128]{2,1,0:T(8,128)(2,1)S(1)}, bf16[4,256,128]{2,1,0:T(8,128)(2,1)S(1)}, u32[]{:S(2)}, u32[]{:S(2)}) %collective-permute-start) | collective-permute-done | bytes 262176 | tf_op jit(solution)/shard_map/ppermute | solution.py:212
  18.2 2.3 %collective-permute-start.9 = (bf16[128,128]{1,0:T(8,128)(2,1)S(1)}, bf16[128,128]{1,0:T(8,128)(2,1)S(1)}, u32[]{:S(2)}, u32[]{:S(2)}) collective-permute-start(bf16[128,128]{1,0:T(8,128)(2,1)S(1)} %add_convert_fusion), channel_id=1, source_target_pairs={{0,16},{2,18},{4,20},{6,22},{8,24},{10,26},{12,28},{14,30},{16,0},... | collective-permute-start | bytes 98312 | tf_op jit(solution)/shard_map/ppermute | solution.py:205
  20.5 3.2 %collective-permute-done.1.refs_1_ = bf16[4,256,128]{2,1,0:T(8,128)(2,1)S(1)} collective-permute-done((bf16[4,256,128]{2,1,0:T(8,128)(2,1)S(1)}, bf16[4,256,128]{2,1,0:T(8,128)(2,1)S(1)}, u32[]{:S(2)}, u32[]{:S(2)}) %collective-permute-start.1) | collective-permute-done | bytes 262176 | tf_op jit(solution)/shard_map/ppermute | solution.py:212
  23.7 1.6 %collective-permute-start.8 = (bf16[128,128]{1,0:T(8,128)(2,1)S(1)}, bf16[128,128]{1,0:T(8,128)(2,1)S(1)}, u32[]{:S(2)}, u32[]{:S(2)}) collective-permute-start(bf16[128,128]{1,0:T(8,128)(2,1)S(1)} %add_convert_fusion), channel_id=1, source_target_pairs={{0,8},{2,10},{4,12},{6,14},{8,0},{10,2},{12,4},{14,6},{16,24},{18,... | collective-permute-start | bytes 98312 | tf_op jit(solution)/shard_map/ppermute | solution.py:205
  25.3 0.7 %shard_map.77 = (f32[256,128]{1,0:T(8,128)S(1)}, f32[256,128]{1,0:T(8,128)S(1)}, f32[256,128]{1,0:T(8,128)S(1)}, f32[256,128]{1,0:T(8,128)S(1)}) custom-call(bf16[4,256,128]{2,1,0:T(8,128)(2,1)S(1)} %collective-permute-done.refs_0_, bf16[4,256,128]{2,1,0:T(8,128)(2,1)S(1)} %collective-permute-done.1.refs_1_, ...), custom_call_target="tpu_custom_call" | custom-call | flops 134217728 | bytes 1572864 | tf_op jit(solution)/shard_map/pallas_call | solution.py:43
  26.0 1.6 %collective-permute-done.8.refs_12_ = bf16[128,128]{1,0:T(8,128)(2,1)S(1)} collective-permute-done((bf16[128,128]{1,0:T(8,128)(2,1)S(1)}, bf16[128,128]{1,0:T(8,128)(2,1)S(1)}, u32[]{:S(2)}, u32[]{:S(2)}) %collective-permute-start.8) | collective-permute-done | bytes 32800 | tf_op jit(solution)/shard_map/ppermute | solution.py:205
  28.3 1.2 %collective-permute-done.11 = f32[8,256]{1,0:T(8,128)S(1)} collective-permute-done((f32[8,256]{1,0:T(8,128)S(1)}, f32[8,256]{1,0:T(8,128)S(1)}, u32[]{:S(2)}, u32[]{:S(2)}) %collective-permute-start.11) | collective-permute-done | bytes 8224 | tf_op jit(solution)/shard_map/ppermute | solution.py:205
  29.4 1.4 %collective-permute-start.14 = (f32[8,256]{1,0:T(8,128)S(1)}, f32[8,256]{1,0:T(8,128)S(1)}, u32[]{:S(2)}, u32[]{:S(2)}) collective-permute-start(f32[8,256]{1,0:T(8,128)S(1)} %add.24), channel_id=1, source_target_pairs={{0,2},{2,0},{4,6},{6,4},{8,10},{10,8},{12,14},{14,12},{16,18},{18,... | collective-permute-start | bytes 24584 | tf_op jit(solution)/shard_map/ppermute | solution.py:205
  30.8 0.7 %collective-permute-start.13 = (f32[8,256]{1,0:T(8,128)S(1)}, f32[8,256]{1,0:T(8,128)S(1)}, u32[]{:S(2)}, u32[]{:S(2)}) collective-permute-start(f32[8,256]{1,0:T(8,128)S(1)} %add.24), channel_id=1, source_target_pairs={{0,4},{2,6},{4,0},{6,2},{8,12},{10,14},{12,8},{14,10},{16,20},{18,... | collective-permute-start | bytes 24584 | tf_op jit(solution)/shard_map/ppermute | solution.py:205
  31.5 1.4 %collective-permute-start.12 = (f32[8,256]{1,0:T(8,128)S(1)}, f32[8,256]{1,0:T(8,128)S(1)}, u32[]{:S(2)}, u32[]{:S(2)}) collective-permute-start(f32[8,256]{1,0:T(8,128)S(1)} %add.24), channel_id=1, source_target_pairs={{0,6},{2,4},{4,2},{6,0},{8,14},{10,12},{12,10},{14,8},{16,22},{18,... | collective-permute-start | bytes 24584 | tf_op jit(solution)/shard_map/ppermute | solution.py:205
  32.9 0.7 %shard_map.75 = (bf16[4,256,256]{2,1,0:T(8,128)(2,1)S(1)}, f32[256,512]{1,0:T(8,128)S(1)}) custom-call(bf16[256,512]{1,0:T(8,128)(2,1)S(1)} %copy-done.3, bf16[256,512]{1,0:T(8,128)(2,1)S(1)} %copy-done, bf16[256,512]{1,0:T(8,128)(2,1)S(1)} %copy-done.1), custom_call_target="tpu_custom_call" | custom-call | flops 134217728 | bytes 1835008 | tf_op jit(solution)/shard_map/pallas_call | solution.py:43
  33.6 0.9 %collective-permute-done.13 = f32[8,256]{1,0:T(8,128)S(1)} collective-permute-done((f32[8,256]{1,0:T(8,128)S(1)}, f32[8,256]{1,0:T(8,128)S(1)}, u32[]{:S(2)}, u32[]{:S(2)}) %collective-permute-start.13) | collective-permute-done | bytes 8224 | tf_op jit(solution)/shard_map/ppermute | solution.py:205
  34.5 1.6 %collective-permute-done.12 = f32[8,256]{1,0:T(8,128)S(1)} collective-permute-done((f32[8,256]{1,0:T(8,128)S(1)}, f32[8,256]{1,0:T(8,128)S(1)}, u32[]{:S(2)}, u32[]{:S(2)}) %collective-permute-start.12) | collective-permute-done | bytes 8224 | tf_op jit(solution)/shard_map/ppermute | solution.py:205
  36.1 0.7 %shard_map.81 = (bf16[128,128]{1,0:T(8,128)(2,1)S(1)}, bf16[128,128]{1,0:T(8,128)(2,1)S(1)}, bf16[128,128]{1,0:T(8,128)(2,1)S(1)}, bf16[128,128]{1,0:T(8,128)(2,1)S(1)}, bf16[128,128]{1,0:T(8,128)(2,1)S(1)}) custom-call(bf16[4,256,128]{2,1,0:T(8,128)(2,1)S(1)} %collective-permute-done.refs_0_, bf16[4,256,128]{2,1,0:T(8,128)(2,1)S(1)} %collective-permute-done.1.refs_1_, ...), custom_call_target="tpu_custom_call" | custom-call | flops 33554432 | bytes 2269184 | tf_op jit(solution)/shard_map/pallas_call | solution.py:43
  36.8 4.1 %collective-permute-start.21 = (bf16[128,128]{1,0:T(8,128)(2,1)S(1)}, bf16[128,128]{1,0:T(8,128)(2,1)S(1)}, u32[]{:S(2)}, u32[]{:S(2)}) collective-permute-start(bf16[128,128]{1,0:T(8,128)(2,1)S(1)} %get-tuple-element.67), channel_id=1, source_target_pairs={{0,24},{2,26},{4,28},{6,30},{8,16},{10,18},{12,20},{14,22},{16,8},... | collective-permute-start | bytes 98312 | tf_op jit(solution)/shard_map/ppermute | solution.py:205
  40.9 0.6 %collective-permute-start.19 = (bf16[128,128]{1,0:T(8,128)(2,1)S(1)}, bf16[128,128]{1,0:T(8,128)(2,1)S(1)}, u32[]{:S(2)}, u32[]{:S(2)}) collective-permute-start(bf16[128,128]{1,0:T(8,128)(2,1)S(1)} %get-tuple-element.67), channel_id=1, source_target_pairs={{0,8},{2,10},{4,12},{6,14},{8,0},{10,2},{12,4},{14,6},{16,24},{18,... | collective-permute-start | bytes 98312 | tf_op jit(solution)/shard_map/ppermute | solution.py:205
  41.5 1.4 %collective-permute-start.16 = (bf16[128,128]{1,0:T(8,128)(2,1)S(1)}, bf16[128,128]{1,0:T(8,128)(2,1)S(1)}, u32[]{:S(2)}, u32[]{:S(2)}) collective-permute-start(bf16[128,128]{1,0:T(8,128)(2,1)S(1)} %get-tuple-element.55), channel_id=1, source_target_pairs={{0,3},{1,2},{2,1},{3,0},{4,7},{5,6},{6,5},{7,4},{8,11},{9,10},{10,... | collective-permute-start | bytes 98312 | tf_op jit(solution)/shard_map/ppermute | solution.py:212
  42.9 2.8 %collective-permute-done.20.refs_5_ = bf16[128,128]{1,0:T(8,128)(2,1)S(1)} collective-permute-done((bf16[128,128]{1,0:T(8,128)(2,1)S(1)}, bf16[128,128]{1,0:T(8,128)(2,1)S(1)}, u32[]{:S(2)}, u32[]{:S(2)}) %collective-permute-start.20) | collective-permute-done | bytes 32800 | tf_op jit(solution)/shard_map/ppermute | solution.py:205
  45.8 2.1 %collective-permute-start.22 = (bf16[128,128]{1,0:T(8,128)(2,1)S(1)}, bf16[128,128]{1,0:T(8,128)(2,1)S(1)}, u32[]{:S(2)}, u32[]{:S(2)}) collective-permute-start(bf16[128,128]{1,0:T(8,128)(2,1)S(1)} %get-tuple-element.68), channel_id=1, source_target_pairs={{0,5},{1,4},{2,7},{3,6},{4,1},{5,0},{6,3},{7,2},{8,13},{9,12},{10,... | collective-permute-start | bytes 98312 | tf_op jit(solution)/shard_map/ppermute | solution.py:212
  48.0 1.2 %collective-permute-start.24 = (bf16[128,128]{1,0:T(8,128)(2,1)S(1)}, bf16[128,128]{1,0:T(8,128)(2,1)S(1)}, u32[]{:S(2)}, u32[]{:S(2)}) collective-permute-start(bf16[128,128]{1,0:T(8,128)(2,1)S(1)} %get-tuple-element.70), channel_id=1, source_target_pairs={{0,1},{1,0},{2,3},{3,2},{4,5},{5,4},{6,7},{7,6},{8,9},{9,8},{10,11... | collective-permute-start | bytes 98312 | tf_op jit(solution)/shard_map/ppermute | solution.py:212
  50.0 2.4 %shard_map.80 = (bf16[256,512]{1,0:T(8,128)(2,1)}, bf16[256,512]{1,0:T(8,128)(2,1)}, f32[256,512]{1,0:T(8,128)S(1)}, f32[256,512]{1,0:T(8,128)S(1)}) custom-call(bf16[256,512]{1,0:T(8,128)(2,1)S(1)} %copy-done.3, bf16[256,512]{1,0:T(8,128)(2,1)S(1)} %copy-done, bf16[256,512]{1,0:T(8,128)(2,1)S(1)} %copy-done.1, bf16[256,512]{1,0:T(8,128)(2,1)S(1)} %copy-done.5, ...), custom_call_target="tpu_custom_call" | custom-call | flops 335544320 | bytes 3809280 | tf_op jit(solution)/shard_map/pallas_call | solution.py:43
  52.4 1.1 %collective-permute-done.25.p3 = bf16[128,128]{1,0:T(8,128)(2,1)S(1)} collective-permute-done((bf16[128,128]{1,0:T(8,128)(2,1)S(1)}, bf16[128,128]{1,0:T(8,128)(2,1)S(1)}, u32[]{:S(2)}, u32[]{:S(2)}) %collective-permute-start.25) | collective-permute-done | bytes 32800 | tf_op jit(solution)/shard_map/ppermute | solution.py:212
  53.6 1.1 %shard_map.83 = (bf16[256,512]{1,0:T(8,128)(2,1)}, bf16[256,512]{1,0:T(8,128)(2,1)}) custom-call(bf16[256,512]{1,0:T(8,128)(2,1)S(1)} %copy-done, bf16[256,512]{1,0:T(8,128)(2,1)S(1)} %copy-done.1, f32[256,512]{1,0:T(8,128)S(1)} %get-tuple-element.60.key_local, f32[256,512]{1,0:T(8,128)S(1)} %get-tuple-element.61.value_local, ...), custom_call_target="tpu_custom_call" | custom-call | flops 67108864 | bytes 2228224 | tf_op jit(solution)/shard_map/pallas_call | solution.py:43
  (44 shorter events, 2.2 us)
Async XLA Ops:
  0.6 5.8 %copy-start.1 = (bf16[256,512]{1,0:T(8,128)(2,1)S(1)}, bf16[256,512]{1,0:T(8,128)(2,1)}, u32[]{:S(2)}) copy-start(bf16[256,512]{1,0:T(8,128)(2,1)} %v_ref.9) | copy-start | bytes 786436
  0.6 5.8 %copy-start = (bf16[256,512]{1,0:T(8,128)(2,1)S(1)}, bf16[256,512]{1,0:T(8,128)(2,1)}, u32[]{:S(2)}) copy-start(bf16[256,512]{1,0:T(8,128)(2,1)} %k_ref.9) | copy-start | bytes 786436
  2.1 9.1 %collective-permute-start.4 = (bf16[128,128]{1,0:T(8,128)(2,1)S(1)}, bf16[128,128]{1,0:T(8,128)(2,1)S(1)}, u32[]{:S(2)}, u32[]{:S(2)}) collective-permute-start(bf16[128,128]{1,0:T(8,128)(2,1)S(1)} %get-tuple-element.49), channel_id=1, source_target_pairs={{0,7},{1,6},{2,5},{3,4},{4,3},{5,2},{6,1},{7,0},{8,15},{9,14},{10,... | collective-permute-start | bytes 98312 | tf_op jit(solution)/shard_map/ppermute | solution.py:212
  5.5 6.3 %collective-permute-start.5 = (bf16[128,128]{1,0:T(8,128)(2,1)S(1)}, bf16[128,128]{1,0:T(8,128)(2,1)S(1)}, u32[]{:S(2)}, u32[]{:S(2)}) collective-permute-start(bf16[128,128]{1,0:T(8,128)(2,1)S(1)} %get-tuple-element.50), channel_id=1, source_target_pairs={{0,5},{1,4},{2,7},{3,6},{4,1},{5,0},{6,3},{7,2},{8,13},{9,12},{10,... | collective-permute-start | bytes 98312 | tf_op jit(solution)/shard_map/ppermute | solution.py:212
  6.3 5.6 %collective-permute-start.6 = (bf16[128,128]{1,0:T(8,128)(2,1)S(1)}, bf16[128,128]{1,0:T(8,128)(2,1)S(1)}, u32[]{:S(2)}, u32[]{:S(2)}) collective-permute-start(bf16[128,128]{1,0:T(8,128)(2,1)S(1)} %get-tuple-element.51), channel_id=1, source_target_pairs={{0,3},{1,2},{2,1},{3,0},{4,7},{5,6},{6,5},{7,4},{8,11},{9,10},{10,... | collective-permute-start | bytes 98312 | tf_op jit(solution)/shard_map/ppermute | solution.py:212
  6.4 1.0 %copy-start.2 = (bf16[256,512]{1,0:T(8,128)(2,1)S(1)}, bf16[256,512]{1,0:T(8,128)(2,1)}, u32[]{:S(2)}) copy-start(bf16[256,512]{1,0:T(8,128)(2,1)} %q_ref.5) | copy-start | bytes 786436
  7.4 0.9 %copy-start.4 = (bf16[256,512]{1,0:T(8,128)(2,1)S(1)}, bf16[256,512]{1,0:T(8,128)(2,1)}, u32[]{:S(2)}) copy-start(bf16[256,512]{1,0:T(8,128)(2,1)} %c_ref.3) | copy-start | bytes 786436
  8.5 9.7 %collective-permute-start = (bf16[4,256,128]{2,1,0:T(8,128)(2,1)S(1)}, bf16[4,256,128]{2,1,0:T(8,128)(2,1)S(1)}, u32[]{:S(2)}, u32[]{:S(2)}) collective-permute-start(bf16[4,256,128]{2,1,0:T(8,128)(2,1)S(1)} %get-tuple-element.41), channel_id=1, source_target_pairs={{0,7},{1,6},{2,5},{3,4},{4,3},{5,2},{6,1},{7,0},{8,15},{9,14},{10,... | collective-permute-start | bytes 786440 | tf_op jit(solution)/shard_map/ppermute | solution.py:212
  11.2 12.6 %collective-permute-start.1 = (bf16[4,256,128]{2,1,0:T(8,128)(2,1)S(1)}, bf16[4,256,128]{2,1,0:T(8,128)(2,1)S(1)}, u32[]{:S(2)}, u32[]{:S(2)}) collective-permute-start(bf16[4,256,128]{2,1,0:T(8,128)(2,1)S(1)} %get-tuple-element.42), channel_id=1, source_target_pairs={{0,5},{1,4},{2,7},{3,6},{4,1},{5,0},{6,3},{7,2},{8,13},{9,12},{10,... | collective-permute-start | bytes 786440 | tf_op jit(solution)/shard_map/ppermute | solution.py:212
  11.2 1.5 %collective-permute-start.7 = (bf16[128,128]{1,0:T(8,128)(2,1)S(1)}, bf16[128,128]{1,0:T(8,128)(2,1)S(1)}, u32[]{:S(2)}, u32[]{:S(2)}) collective-permute-start(bf16[128,128]{1,0:T(8,128)(2,1)S(1)} %get-tuple-element.52), channel_id=1, source_target_pairs={{0,1},{1,0},{2,3},{3,2},{4,5},{5,4},{6,7},{7,6},{8,9},{9,8},{10,11... | collective-permute-start | bytes 98312 | tf_op jit(solution)/shard_map/ppermute | solution.py:212
  11.8 13.5 %collective-permute-start.2 = (bf16[4,256,128]{2,1,0:T(8,128)(2,1)S(1)}, bf16[4,256,128]{2,1,0:T(8,128)(2,1)S(1)}, u32[]{:S(2)}, u32[]{:S(2)}) collective-permute-start(bf16[4,256,128]{2,1,0:T(8,128)(2,1)S(1)} %get-tuple-element.43), channel_id=1, source_target_pairs={{0,3},{1,2},{2,1},{3,0},{4,7},{5,6},{6,5},{7,4},{8,11},{9,10},{10,... | collective-permute-start | bytes 786440 | tf_op jit(solution)/shard_map/ppermute | solution.py:212
  11.9 13.4 %collective-permute-start.3 = (bf16[4,256,128]{2,1,0:T(8,128)(2,1)S(1)}, bf16[4,256,128]{2,1,0:T(8,128)(2,1)S(1)}, u32[]{:S(2)}, u32[]{:S(2)}) collective-permute-start(bf16[4,256,128]{2,1,0:T(8,128)(2,1)S(1)} %get-tuple-element.44), channel_id=1, source_target_pairs={{0,1},{1,0},{2,3},{3,2},{4,5},{5,4},{6,7},{7,6},{8,9},{9,8},{10,11... | collective-permute-start | bytes 786440 | tf_op jit(solution)/shard_map/ppermute | solution.py:212
  12.7 13.3 %collective-permute-start.10 = (bf16[128,128]{1,0:T(8,128)(2,1)S(1)}, bf16[128,128]{1,0:T(8,128)(2,1)S(1)}, u32[]{:S(2)}, u32[]{:S(2)}) collective-permute-start(bf16[128,128]{1,0:T(8,128)(2,1)S(1)} %add_convert_fusion), channel_id=1, source_target_pairs={{0,24},{2,26},{4,28},{6,30},{8,16},{10,18},{12,20},{14,22},{16,8},... | collective-permute-start | bytes 98312 | tf_op jit(solution)/shard_map/ppermute | solution.py:205
  18.2 7.8 %collective-permute-start.9 = (bf16[128,128]{1,0:T(8,128)(2,1)S(1)}, bf16[128,128]{1,0:T(8,128)(2,1)S(1)}, u32[]{:S(2)}, u32[]{:S(2)}) collective-permute-start(bf16[128,128]{1,0:T(8,128)(2,1)S(1)} %add_convert_fusion), channel_id=1, source_target_pairs={{0,16},{2,18},{4,20},{6,22},{8,24},{10,26},{12,28},{14,30},{16,0},... | collective-permute-start | bytes 98312 | tf_op jit(solution)/shard_map/ppermute | solution.py:205
  23.7 3.9 %collective-permute-start.8 = (bf16[128,128]{1,0:T(8,128)(2,1)S(1)}, bf16[128,128]{1,0:T(8,128)(2,1)S(1)}, u32[]{:S(2)}, u32[]{:S(2)}) collective-permute-start(bf16[128,128]{1,0:T(8,128)(2,1)S(1)} %add_convert_fusion), channel_id=1, source_target_pairs={{0,8},{2,10},{4,12},{6,14},{8,0},{10,2},{12,4},{14,6},{16,24},{18,... | collective-permute-start | bytes 98312 | tf_op jit(solution)/shard_map/ppermute | solution.py:205
  27.6 5.3 %copy-start.3 = (bf16[256,512]{1,0:T(8,128)(2,1)S(1)}, bf16[256,512]{1,0:T(8,128)(2,1)}, u32[]{:S(2)}) copy-start(bf16[256,512]{1,0:T(8,128)(2,1)} %q_ref.5) | copy-start | bytes 786436
  28.2 1.2 %collective-permute-start.11 = (f32[8,256]{1,0:T(8,128)S(1)}, f32[8,256]{1,0:T(8,128)S(1)}, u32[]{:S(2)}, u32[]{:S(2)}) collective-permute-start(f32[8,256]{1,0:T(8,128)S(1)} %get-tuple-element.53), channel_id=1, source_target_pairs={{0,1},{1,0},{2,3},{3,2},{4,5},{5,4},{6,7},{7,6},{8,9},{9,8},{10,11... | collective-permute-start | bytes 24584 | tf_op jit(solution)/shard_map/ppermute | solution.py:205
  29.4 4.2 %collective-permute-start.14 = (f32[8,256]{1,0:T(8,128)S(1)}, f32[8,256]{1,0:T(8,128)S(1)}, u32[]{:S(2)}, u32[]{:S(2)}) collective-permute-start(f32[8,256]{1,0:T(8,128)S(1)} %add.24), channel_id=1, source_target_pairs={{0,2},{2,0},{4,6},{6,4},{8,10},{10,8},{12,14},{14,12},{16,18},{18,... | collective-permute-start | bytes 24584 | tf_op jit(solution)/shard_map/ppermute | solution.py:205
  30.8 3.7 %collective-permute-start.13 = (f32[8,256]{1,0:T(8,128)S(1)}, f32[8,256]{1,0:T(8,128)S(1)}, u32[]{:S(2)}, u32[]{:S(2)}) collective-permute-start(f32[8,256]{1,0:T(8,128)S(1)} %add.24), channel_id=1, source_target_pairs={{0,4},{2,6},{4,0},{6,2},{8,12},{10,14},{12,8},{14,10},{16,20},{18,... | collective-permute-start | bytes 24584 | tf_op jit(solution)/shard_map/ppermute | solution.py:205
  31.5 4.5 %collective-permute-start.12 = (f32[8,256]{1,0:T(8,128)S(1)}, f32[8,256]{1,0:T(8,128)S(1)}, u32[]{:S(2)}, u32[]{:S(2)}) collective-permute-start(f32[8,256]{1,0:T(8,128)S(1)} %add.24), channel_id=1, source_target_pairs={{0,6},{2,4},{4,2},{6,0},{8,14},{10,12},{12,10},{14,8},{16,22},{18,... | collective-permute-start | bytes 24584 | tf_op jit(solution)/shard_map/ppermute | solution.py:205
  36.1 13.9 %copy-start.5 = (bf16[256,512]{1,0:T(8,128)(2,1)S(1)}, bf16[256,512]{1,0:T(8,128)(2,1)}, u32[]{:S(2)}) copy-start(bf16[256,512]{1,0:T(8,128)(2,1)} %c_ref.3) | copy-start | bytes 786436
  36.8 6.1 %collective-permute-start.21 = (bf16[128,128]{1,0:T(8,128)(2,1)S(1)}, bf16[128,128]{1,0:T(8,128)(2,1)S(1)}, u32[]{:S(2)}, u32[]{:S(2)}) collective-permute-start(bf16[128,128]{1,0:T(8,128)(2,1)S(1)} %get-tuple-element.67), channel_id=1, source_target_pairs={{0,24},{2,26},{4,28},{6,30},{8,16},{10,18},{12,20},{14,22},{16,8},... | collective-permute-start | bytes 98312 | tf_op jit(solution)/shard_map/ppermute | solution.py:205
  40.9 4.8 %collective-permute-start.20 = (bf16[128,128]{1,0:T(8,128)(2,1)S(1)}, bf16[128,128]{1,0:T(8,128)(2,1)S(1)}, u32[]{:S(2)}, u32[]{:S(2)}) collective-permute-start(bf16[128,128]{1,0:T(8,128)(2,1)S(1)} %get-tuple-element.67), channel_id=1, source_target_pairs={{0,16},{2,18},{4,20},{6,22},{8,24},{10,26},{12,28},{14,30},{16,0},... | collective-permute-start | bytes 98312 | tf_op jit(solution)/shard_map/ppermute | solution.py:205
  40.9 4.8 %collective-permute-start.19 = (bf16[128,128]{1,0:T(8,128)(2,1)S(1)}, bf16[128,128]{1,0:T(8,128)(2,1)S(1)}, u32[]{:S(2)}, u32[]{:S(2)}) collective-permute-start(bf16[128,128]{1,0:T(8,128)(2,1)S(1)} %get-tuple-element.67), channel_id=1, source_target_pairs={{0,8},{2,10},{4,12},{6,14},{8,0},{10,2},{12,4},{14,6},{16,24},{18,... | collective-permute-start | bytes 98312 | tf_op jit(solution)/shard_map/ppermute | solution.py:205
  41.5 6.4 %collective-permute-start.15 = (bf16[128,128]{1,0:T(8,128)(2,1)S(1)}, bf16[128,128]{1,0:T(8,128)(2,1)S(1)}, u32[]{:S(2)}, u32[]{:S(2)}) collective-permute-start(bf16[128,128]{1,0:T(8,128)(2,1)S(1)} %get-tuple-element.54), channel_id=1, source_target_pairs={{0,5},{1,4},{2,7},{3,6},{4,1},{5,0},{6,3},{7,2},{8,13},{9,12},{10,... | collective-permute-start | bytes 98312 | tf_op jit(solution)/shard_map/ppermute | solution.py:212
  41.5 6.5 %collective-permute-start.16 = (bf16[128,128]{1,0:T(8,128)(2,1)S(1)}, bf16[128,128]{1,0:T(8,128)(2,1)S(1)}, u32[]{:S(2)}, u32[]{:S(2)}) collective-permute-start(bf16[128,128]{1,0:T(8,128)(2,1)S(1)} %get-tuple-element.55), channel_id=1, source_target_pairs={{0,3},{1,2},{2,1},{3,0},{4,7},{5,6},{6,5},{7,4},{8,11},{9,10},{10,... | collective-permute-start | bytes 98312 | tf_op jit(solution)/shard_map/ppermute | solution.py:212
  42.9 6.3 %collective-permute-start.17 = (bf16[128,128]{1,0:T(8,128)(2,1)S(1)}, bf16[128,128]{1,0:T(8,128)(2,1)S(1)}, u32[]{:S(2)}, u32[]{:S(2)}) collective-permute-start(bf16[128,128]{1,0:T(8,128)(2,1)S(1)} %get-tuple-element.56), channel_id=1, source_target_pairs={{0,1},{1,0},{2,3},{3,2},{4,5},{5,4},{6,7},{7,6},{8,9},{9,8},{10,11... | collective-permute-start | bytes 98312 | tf_op jit(solution)/shard_map/ppermute | solution.py:212
  45.7 4.2 %collective-permute-start.18 = (bf16[128,128]{1,0:T(8,128)(2,1)S(1)}, bf16[128,128]{1,0:T(8,128)(2,1)S(1)}, u32[]{:S(2)}, u32[]{:S(2)}) collective-permute-start(bf16[128,128]{1,0:T(8,128)(2,1)S(1)} %get-tuple-element.57), channel_id=1, source_target_pairs={{0,7},{1,6},{2,5},{3,4},{4,3},{5,2},{6,1},{7,0},{8,15},{9,14},{10,... | collective-permute-start | bytes 98312 | tf_op jit(solution)/shard_map/ppermute | solution.py:212
  45.8 6.6 %collective-permute-start.22 = (bf16[128,128]{1,0:T(8,128)(2,1)S(1)}, bf16[128,128]{1,0:T(8,128)(2,1)S(1)}, u32[]{:S(2)}, u32[]{:S(2)}) collective-permute-start(bf16[128,128]{1,0:T(8,128)(2,1)S(1)} %get-tuple-element.68), channel_id=1, source_target_pairs={{0,5},{1,4},{2,7},{3,6},{4,1},{5,0},{6,3},{7,2},{8,13},{9,12},{10,... | collective-permute-start | bytes 98312 | tf_op jit(solution)/shard_map/ppermute | solution.py:212
  47.9 4.5 %collective-permute-start.23 = (bf16[128,128]{1,0:T(8,128)(2,1)S(1)}, bf16[128,128]{1,0:T(8,128)(2,1)S(1)}, u32[]{:S(2)}, u32[]{:S(2)}) collective-permute-start(bf16[128,128]{1,0:T(8,128)(2,1)S(1)} %get-tuple-element.69), channel_id=1, source_target_pairs={{0,3},{1,2},{2,1},{3,0},{4,7},{5,6},{6,5},{7,4},{8,11},{9,10},{10,... | collective-permute-start | bytes 98312 | tf_op jit(solution)/shard_map/ppermute | solution.py:212
  48.0 4.4 %collective-permute-start.24 = (bf16[128,128]{1,0:T(8,128)(2,1)S(1)}, bf16[128,128]{1,0:T(8,128)(2,1)S(1)}, u32[]{:S(2)}, u32[]{:S(2)}) collective-permute-start(bf16[128,128]{1,0:T(8,128)(2,1)S(1)} %get-tuple-element.70), channel_id=1, source_target_pairs={{0,1},{1,0},{2,3},{3,2},{4,5},{5,4},{6,7},{7,6},{8,9},{9,8},{10,11... | collective-permute-start | bytes 98312 | tf_op jit(solution)/shard_map/ppermute | solution.py:212
  49.2 4.3 %collective-permute-start.25 = (bf16[128,128]{1,0:T(8,128)(2,1)S(1)}, bf16[128,128]{1,0:T(8,128)(2,1)S(1)}, u32[]{:S(2)}, u32[]{:S(2)}) collective-permute-start(bf16[128,128]{1,0:T(8,128)(2,1)S(1)} %get-tuple-element.71), channel_id=1, source_target_pairs={{0,7},{1,6},{2,5},{3,4},{4,3},{5,2},{6,1},{7,0},{8,15},{9,14},{10,... | collective-permute-start | bytes 98312 | tf_op jit(solution)/shard_map/ppermute | solution.py:212

commit v5 on v3

--- a/solution.py
+++ b/solution.py
@@ -10,7 +10,7 @@
 DH = 128
 EPSILON = 1e-06
 QUAD = 4
-ORDER = (3, 2, 1, 0)
+OPS = (0, 1, 2, 3)
 CHUNKS = 4
 LOW, WIDE = jnp.bfloat16, jnp.float32
 
@@ -37,13 +37,23 @@
     return lax.axis_index("seq") % QUAD
 
 
-def call(kernel, outs, args, flops, in_specs=None, scratch_shapes=(), room=32):
+def sent(op):
+    odd = lax.axis_index("tp") % 2
+    return (3, 2 - odd, 1 + odd, 0)[op]
+
+
+def came(op):
+    odd = lax.axis_index("tp") % 2
+    return (3, 1 + odd, 2 - odd, 0)[op]
+
+
+def call(kernel, outs, args, flops, in_specs=None, out_specs=None, scratch_shapes=(), room=32):
     size = sum(x.size * x.dtype.itemsize for x in list(args) + list(outs))
     return pl.pallas_call(
         kernel,
         out_shape=outs,
         in_specs=in_specs or [pl.BlockSpec(memory_space=pltpu.VMEM)] * len(args),
-        out_specs=[pl.BlockSpec(memory_space=pltpu.VMEM)] * len(outs),
+        out_specs=out_specs or [pl.BlockSpec(memory_space=pltpu.VMEM)] * len(outs),
         scratch_shapes=scratch_shapes,
         cost_estimate=pl.CostEstimate(flops=flops, bytes_accessed=size, transcendentals=0),
         compiler_params=pltpu.CompilerParams(vmem_limit_bytes=int(room * 1024 * 1024)),
@@ -61,8 +71,8 @@
     for copy in copies:
         copy.wait()
     m = member_of_quad()
-    for d, out in enumerate((o0, o1, o2, o3)):
-        h = m ^ d
+    for op, out in enumerate((o0, o1, o2, o3)):
+        h = m ^ sent(op)
         out[...] = dot(head(k_buf, h)[...], head(v_buf, h)[...], ((0,), (0,))).astype(LOW)
 
 
@@ -80,8 +90,8 @@
     count = q_ref.shape[0]
     square = jnp.zeros((count, DH), WIDE)
     product = jnp.zeros((count, DH), WIDE)
-    for e, p_ref in enumerate((p0, p1, p2, p3)):
-        h = m ^ e
+    for op, p_ref in enumerate((p0, p1, p2, p3)):
+        h = m ^ came(op)
         mixed = head(local_ref, h)[...] + dot(head(q_ref, h)[...], p_ref[...], ((1,), (0,)))
         head(mixed_ref, h)[...] = mixed
         square = square + mixed * mixed
@@ -98,15 +108,15 @@
     return inverse, projection
 
 
-def grad_kernel(features, mixed_ref, c_ref, q_ref, sums_ref, g_ref, *outs):
+def grad_kernel(features, mixed_ref, c_ref, q_ref, sums_ref, o0, o1, o2, o3, g_ref):
     m = member_of_quad()
     inverse, projection = token_scales(sums_ref, features, q_ref.shape[0])
-    for d in range(QUAD):
-        h = m ^ d
+    for op, out in enumerate((o0, o1, o2, o3)):
+        h = m ^ sent(op)
         normed = head(mixed_ref, h)[...] * inverse
         grad = (inverse * (head(c_ref, h)[...].astype(WIDE) - normed * projection)).astype(LOW)
         head(g_ref, h)[...] = grad
-        outs[d][...] = dot(head(q_ref, h)[...], grad, ((0,), (0,))).astype(LOW)
+        out[...] = dot(head(q_ref, h)[...], grad, ((0,), (0,))).astype(LOW)
 
 
 def back_kernel(features, q_ref, k_ref, v_ref, g_ref, scores_ref, mixed_ref, sums_ref, p0, p1, p2, p3,
@@ -115,8 +125,8 @@
     count = q_ref.shape[0]
     mask = causal_mask(count)
     inverse, _ = token_scales(sums_ref, features, count)
-    for e, p_ref in enumerate((p0, p1, p2, p3)):
-        h = m ^ e
+    for op, p_ref in enumerate((p0, p1, p2, p3)):
+        h = m ^ came(op)
         grad = head(g_ref, h)[...]
         head(normed_ref, h)[...] = (head(mixed_ref, h)[...] * inverse).astype(LOW)
         raw = dot(grad, head(v_ref, h)[...], ((1,), (1,)))
@@ -129,8 +139,8 @@
 
 def last_kernel(k_ref, v_ref, key_local, value_local, p0, p1, p2, p3, key_ref, value_ref):
     m = member_of_quad()
-    for e, p_ref in enumerate((p0, p1, p2, p3)):
-        h = m ^ e
+    for op, p_ref in enumerate((p0, p1, p2, p3)):
+        h = m ^ came(op)
         suffix = p_ref[...]
         key = head(key_local, h)[...] + dot(head(v_ref, h)[...], suffix, ((1,), (1,)))
         head(key_ref, h)[...] = key.astype(LOW)
@@ -138,41 +148,52 @@
         head(value_ref, h)[...] = value.astype(LOW)
 
 
+def sums_kernel(before, far, *refs):
+    index = lax.axis_index("seq")
+    m = index % QUAD
+    held, got, outs = refs[:QUAD], refs[QUAD : QUAD + len(far)], refs[-QUAD:]
+
+    def counts(a, b):
+        return jnp.where(a < b if before else a > b, 1.0, 0.0).astype(WIDE)
+
+    outer = jnp.zeros((DH, DH), WIDE)
+    for bits, total in zip(far, got):
+        outer = outer + total[...].astype(WIDE) * counts(index ^ bits, index)
+    pieces = [piece[...].astype(WIDE) for piece in held]
+    for to in OPS:
+        inner = outer
+        for op in OPS:
+            inner = inner + pieces[op] * counts(m ^ came(op), m ^ sent(to))
+        outs[to][...] = inner.astype(LOW)
+
+
 def exchange(value, axis, bits):
     size = lax.axis_size(axis)
     return lax.ppermute(value, axis, [(i, i ^ bits) for i in range(size)])
 
 
-def cross(value, bits):
+def cross(value, op):
     cores = lax.axis_size("tp")
     places = [(i, t) for i in range(lax.axis_size("seq")) for t in range(cores)]
-    pairs = [(i * cores + t, (i ^ bits) * cores + (t ^ 1)) for i, t in places]
+    bits = (3, 2, 1, 0), (3, 1, 2, 0)
+    pairs = [(i * cores + t, (i ^ bits[t % 2][op]) * cores + (t ^ 1)) for i, t in places]
     return lax.ppermute(value, ("seq", "tp"), pairs)
 
 
-def exclusive_sum(held, before):
-    index = lax.axis_index("seq")
-    m = index % QUAD
-    held = [cross(held[d], d) for d in ORDER]
-    held = [held[ORDER.index(d)].astype(WIDE) for d in range(QUAD)]
-    total = (held[0] + held[1] + held[2] + held[3]).astype(LOW)
-
-    def counts(a, b):
-        return a < b if before else a > b
-
-    outer = jnp.zeros_like(held[0])
-    for bits in range(QUAD, lax.axis_size("seq"), QUAD):
-        got = exchange(total, "seq", bits).astype(WIDE)
-        outer = outer + jnp.where(counts(index ^ bits, index), got, 0.0)
-    sums = []
-    for e in range(QUAD):
-        inner = outer
-        for d in range(QUAD):
-            if d != e:
-                inner = inner + jnp.where(counts(m ^ d, m ^ e), held[d], 0.0)
-        sums.append(inner.astype(LOW))
-    sums = [cross(sums[e], e) for e in ORDER]
-    return [sums[ORDER.index(e)] for e in range(QUAD)]
+def exclusive_sum(held, before, *after):
+    held = [cross(held[op], op) for op in OPS]
+    total = sum(piece.astype(WIDE) for piece in held).astype(LOW)
+    far = range(lax.axis_size("seq") - QUAD, 0, -QUAD)
+    got = [exchange(total, "seq", bits) for bits in far]
+    vmem = [pl.BlockSpec(memory_space=pltpu.VMEM)] * (QUAD + len(got))
+    sums = call(
+        functools.partial(sums_kernel, before, far),
+        [jax.ShapeDtypeStruct(x.shape, x.dtype) for x in held],
+        (*held, *got, *after),
+        0,
+        in_specs=vmem + [pl.BlockSpec(memory_space=pl.ANY)] * len(after),
+    )
+    return [cross(sums[op], op) for op in OPS]
 
 
 def sum_over_heads(value):
@@ -191,10 +212,11 @@
     wide = shape((count, width), WIDE)
     low = shape((count, width), LOW)
     unit = 2 * count * DH * DH * QUAD
+    buffers = [pltpu.VMEM(k.shape, LOW)] * 2 + [pltpu.SemaphoreType.DMA((2, CHUNKS))]
     held = call(
         state_kernel, [state] * QUAD, (k, v), unit, room=53.75,
         in_specs=[pl.BlockSpec(memory_space=pltpu.HBM)] * 2,
-        scratch_shapes=[pltpu.VMEM(k.shape, LOW)] * 2 + [pltpu.SemaphoreType.DMA((2, CHUNKS))],
+        scratch_shapes=buffers,
     )
     scores, local = call(
         local_kernel, [shape((QUAD, count, count), LOW), wide], (q, k, v), 4 * unit
@@ -204,8 +226,8 @@
         mixed_kernel, [wide, shape((2, count), WIDE)], (local, q, c, *prefix), unit
     )
     sums = sum_over_heads(sums)
-    g, *terms = call(
-        functools.partial(grad_kernel, features), [low] + [state] * QUAD, (mixed, c, q, sums), unit
+    *terms, g = call(
+        functools.partial(grad_kernel, features), [state] * QUAD + [low], (mixed, c, q, sums), unit
     )
     normed_out, query_grad, key_local, value_local = call(
         functools.partial(back_kernel, features),
@@ -213,7 +235,7 @@
         (q, k, v, g, scores, mixed, sums, *prefix),
         9 * unit,
     )
-    suffix = exclusive_sum(terms, False)
+    suffix = exclusive_sum(terms, False, key_local)
     key_grad, value_grad = call(
         last_kernel, [low, low], (k, v, key_local, value_local, *suffix), 2 * unit
     )

time: 46.7 us -> 45.8 us (0.981)
  waiting for transfers between devices: 15.4 us -> 13.3 us
  starting transfers between devices: 24.1 us -> 25.3 us
    ppermute x7, waiting for transfers between devices: 7.13 us -> 5.46 us  [exchange(): return lax.ppermute(value, axis, [(i, i ^ bits) for i in range(size)])]
    ppermute x16, starting transfers between devices: 14.6 us -> 16.3 us  [cross(): return lax.ppermute(value, ('seq', 'tp'), pairs)]
    ppermute x7, starting transfers between devices: 9.48 us -> 8.99 us  [exchange(): return lax.ppermute(value, axis, [(i, i ^ bits) for i in range(size)])]
    pallas_call x6 -> x8, Pallas kernels: 5.99 us -> 6.25 us  [call(): pl.pallas_call(kernel, out_shape=outs, in_specs=in_specs or [pl.BlockSpec...]
where the time goes in v5:
time: 45.8 us; the launch traced here: 45.6 us
  starting transfers between devices  25.3 us (55%)
  waiting for transfers between devices  13.3 us (29%)
  Pallas kernels  6.25 us (14%)
  between operations  0.73 us (2%)
    ppermute x16, starting transfers between devices, cross(): return lax.ppermute(value, ('seq', 'tp'), pairs)  16.3 us
    ppermute x7, starting transfers between devices, exchange(): return lax.ppermute(value, axis, [(i, i ^ bits) for i in range(size)])  8.99 us
    ppermute x16, waiting for transfers between devices, cross(): return lax.ppermute(value, ('seq', 'tp'), pairs)  7.88 us
    pallas_call x8, Pallas kernels, call(): pl.pallas_call(kernel, out_shape=outs, in_specs=in_specs or [pl.BlockSpec...  6.25 us
    ppermute x7, waiting for transfers between devices, exchange(): return lax.ppermute(value, axis, [(i, i ^ bits) for i in range(size)])  5.46 us
  transfers between devices with their start and end apart: 23, of which 14 were waited for; matrix products, arithmetic and copies ran while one was open for 0% of the time, Pallas kernels for 6%

profile of v5, /device:TPU:0, one launch (start us, length us, event | category | flops | bytes accessed | tf_op | source)
XLA Modules:
  0.0 45.6 jit_solution(13867876278379080196)
XLA Ops:
  0.7 1.5 %shard_map.76 = (bf16[128,128]{1,0:T(8,128)(2,1)S(1)}, bf16[128,128]{1,0:T(8,128)(2,1)S(1)}, bf16[128,128]{1,0:T(8,128)(2,1)S(1)}, bf16[128,128]{1,0:T(8,128)(2,1)S(1)}) custom-call(bf16[256,512]{1,0:T(8,128)(2,1)} %k_ref.7, bf16[256,512]{1,0:T(8,128)(2,1)} %v_ref.7), custom_call_target="tpu_custom_call" | custom-call | flops 33554432 | bytes 655360 | tf_op jit(solution)/shard_map/pallas_call | solution.py:52
  2.1 3.4 %collective-permute-start = (bf16[128,128]{1,0:T(8,128)(2,1)S(1)}, bf16[128,128]{1,0:T(8,128)(2,1)S(1)}, u32[]{:S(2)}, u32[]{:S(2)}) collective-permute-start(bf16[128,128]{1,0:T(8,128)(2,1)S(1)} %get-tuple-element.32), channel_id=1, source_target_pairs={{0,7},{1,6},{2,5},{3,4},{4,3},{5,2},{6,1},{7,0},{8,15},{9,14},{10,... | collective-permute-start | bytes 98312 | tf_op jit(solution)/shard_map/ppermute | solution.py:180
  5.5 0.8 %collective-permute-start.1 = (bf16[128,128]{1,0:T(8,128)(2,1)S(1)}, bf16[128,128]{1,0:T(8,128)(2,1)S(1)}, u32[]{:S(2)}, u32[]{:S(2)}) collective-permute-start(bf16[128,128]{1,0:T(8,128)(2,1)S(1)} %get-tuple-element.33), channel_id=1, source_target_pairs={{0,5},{1,2},{2,7},{3,0},{4,1},{5,6},{6,3},{7,4},{8,13},{9,10},{10,... | collective-permute-start | bytes 98312 | tf_op jit(solution)/shard_map/ppermute | solution.py:180
  6.3 1.0 %collective-permute-start.2 = (bf16[128,128]{1,0:T(8,128)(2,1)S(1)}, bf16[128,128]{1,0:T(8,128)(2,1)S(1)}, u32[]{:S(2)}, u32[]{:S(2)}) collective-permute-start(bf16[128,128]{1,0:T(8,128)(2,1)S(1)} %get-tuple-element.34), channel_id=1, source_target_pairs={{0,3},{1,4},{2,1},{3,6},{4,7},{5,0},{6,5},{7,2},{8,11},{9,12},{10,... | collective-permute-start | bytes 98312 | tf_op jit(solution)/shard_map/ppermute | solution.py:180
  7.3 0.7 %collective-permute-start.3 = (bf16[128,128]{1,0:T(8,128)(2,1)S(1)}, bf16[128,128]{1,0:T(8,128)(2,1)S(1)}, u32[]{:S(2)}, u32[]{:S(2)}) collective-permute-start(bf16[128,128]{1,0:T(8,128)(2,1)S(1)} %get-tuple-element.35), channel_id=1, source_target_pairs={{0,1},{1,0},{2,3},{3,2},{4,5},{5,4},{6,7},{7,6},{8,9},{9,8},{10,11... | collective-permute-start | bytes 98312 | tf_op jit(solution)/shard_map/ppermute | solution.py:180
  8.0 0.9 %collective-permute-done.1.refs_1_ = bf16[128,128]{1,0:T(8,128)(2,1)S(1)} collective-permute-done((bf16[128,128]{1,0:T(8,128)(2,1)S(1)}, bf16[128,128]{1,0:T(8,128)(2,1)S(1)}, u32[]{:S(2)}, u32[]{:S(2)}) %collective-permute-start.1) | collective-permute-done | bytes 32800 | tf_op jit(solution)/shard_map/ppermute | solution.py:180
  8.9 1.1 %collective-permute-done.2.refs_2_ = bf16[128,128]{1,0:T(8,128)(2,1)S(1)} collective-permute-done((bf16[128,128]{1,0:T(8,128)(2,1)S(1)}, bf16[128,128]{1,0:T(8,128)(2,1)S(1)}, u32[]{:S(2)}, u32[]{:S(2)}) %collective-permute-start.2) | collective-permute-done | bytes 32800 | tf_op jit(solution)/shard_map/ppermute | solution.py:180
  10.0 3.7 %collective-permute-start.4 = (bf16[128,128]{1,0:T(8,128)(2,1)S(1)}, bf16[128,128]{1,0:T(8,128)(2,1)S(1)}, u32[]{:S(2)}, u32[]{:S(2)}) collective-permute-start(bf16[128,128]{1,0:T(8,128)(2,1)S(1)} %add_convert_fusion.1), channel_id=1, source_target_pairs={{0,24},{2,26},{4,28},{6,30},{8,16},{10,18},{12,20},{14,22},{16,8},... | collective-permute-start | bytes 98312 | tf_op jit(solution)/shard_map/ppermute | solution.py:172
  13.6 0.8 %collective-permute-start.6 = (bf16[128,128]{1,0:T(8,128)(2,1)S(1)}, bf16[128,128]{1,0:T(8,128)(2,1)S(1)}, u32[]{:S(2)}, u32[]{:S(2)}) collective-permute-start(bf16[128,128]{1,0:T(8,128)(2,1)S(1)} %add_convert_fusion.1), channel_id=1, source_target_pairs={{0,8},{2,10},{4,12},{6,14},{8,0},{10,2},{12,4},{14,6},{16,24},{18,... | collective-permute-start | bytes 98312 | tf_op jit(solution)/shard_map/ppermute | solution.py:172
  14.4 1.3 %collective-permute-done.4.refs_4_ = bf16[128,128]{1,0:T(8,128)(2,1)S(1)} collective-permute-done((bf16[128,128]{1,0:T(8,128)(2,1)S(1)}, bf16[128,128]{1,0:T(8,128)(2,1)S(1)}, u32[]{:S(2)}, u32[]{:S(2)}) %collective-permute-start.4) | collective-permute-done | bytes 32800 | tf_op jit(solution)/shard_map/ppermute | solution.py:172
  15.7 2.7 %collective-permute-done.5.refs_5_ = bf16[128,128]{1,0:T(8,128)(2,1)S(1)} collective-permute-done((bf16[128,128]{1,0:T(8,128)(2,1)S(1)}, bf16[128,128]{1,0:T(8,128)(2,1)S(1)}, u32[]{:S(2)}, u32[]{:S(2)}) %collective-permute-start.5) | collective-permute-done | bytes 32800 | tf_op jit(solution)/shard_map/ppermute | solution.py:172
  18.6 1.7 %collective-permute-start.8 = (bf16[128,128]{1,0:T(8,128)(2,1)S(1)}, bf16[128,128]{1,0:T(8,128)(2,1)S(1)}, u32[]{:S(2)}, u32[]{:S(2)}) collective-permute-start(bf16[128,128]{1,0:T(8,128)(2,1)S(1)} %get-tuple-element.37), channel_id=1, source_target_pairs={{0,5},{1,2},{2,7},{3,0},{4,1},{5,6},{6,3},{7,4},{8,13},{9,10},{10,... | collective-permute-start | bytes 98312 | tf_op jit(solution)/shard_map/ppermute | solution.py:180
  20.3 0.7 %collective-permute-start.9 = (bf16[128,128]{1,0:T(8,128)(2,1)S(1)}, bf16[128,128]{1,0:T(8,128)(2,1)S(1)}, u32[]{:S(2)}, u32[]{:S(2)}) collective-permute-start(bf16[128,128]{1,0:T(8,128)(2,1)S(1)} %get-tuple-element.38), channel_id=1, source_target_pairs={{0,3},{1,4},{2,1},{3,6},{4,7},{5,0},{6,5},{7,2},{8,11},{9,12},{10,... | collective-permute-start | bytes 98312 | tf_op jit(solution)/shard_map/ppermute | solution.py:180
  21.1 0.8 %collective-permute-start.10 = (bf16[128,128]{1,0:T(8,128)(2,1)S(1)}, bf16[128,128]{1,0:T(8,128)(2,1)S(1)}, u32[]{:S(2)}, u32[]{:S(2)}) collective-permute-start(bf16[128,128]{1,0:T(8,128)(2,1)S(1)} %get-tuple-element.39), channel_id=1, source_target_pairs={{0,1},{1,0},{2,3},{3,2},{4,5},{5,4},{6,7},{7,6},{8,9},{9,8},{10,11... | collective-permute-start | bytes 98312 | tf_op jit(solution)/shard_map/ppermute | solution.py:180
  21.8 0.7 %shard_map.75 = (bf16[4,256,256]{2,1,0:T(8,128)(2,1)S(1)}, f32[256,512]{1,0:T(8,128)S(1)}) custom-call(bf16[256,512]{1,0:T(8,128)(2,1)S(1)} %copy-done.2, bf16[256,512]{1,0:T(8,128)(2,1)S(1)} %copy-done, bf16[256,512]{1,0:T(8,128)(2,1)S(1)} %copy-done.1), custom_call_target="tpu_custom_call" | custom-call | flops 134217728 | bytes 1835008 | tf_op jit(solution)/shard_map/pallas_call | solution.py:52
  23.0 0.9 %collective-permute-done.9.p2 = bf16[128,128]{1,0:T(8,128)(2,1)S(1)} collective-permute-done((bf16[128,128]{1,0:T(8,128)(2,1)S(1)}, bf16[128,128]{1,0:T(8,128)(2,1)S(1)}, u32[]{:S(2)}, u32[]{:S(2)}) %collective-permute-start.9) | collective-permute-done | bytes 32800 | tf_op jit(solution)/shard_map/ppermute | solution.py:180
  24.4 1.1 %collective-permute-done.11 = f32[2,256]{1,0:T(2,128)S(1)} collective-permute-done((f32[2,256]{1,0:T(2,128)S(1)}, f32[2,256]{1,0:T(2,128)S(1)}, u32[]{:S(2)}, u32[]{:S(2)}) %collective-permute-start.11) | collective-permute-done | bytes 2080 | tf_op jit(solution)/shard_map/ppermute | solution.py:172
  26.0 1.8 %collective-permute-start.12 = (bf16[128,128]{1,0:T(8,128)(2,1)S(1)}, bf16[128,128]{1,0:T(8,128)(2,1)S(1)}, u32[]{:S(2)}, u32[]{:S(2)}) collective-permute-start(bf16[128,128]{1,0:T(8,128)(2,1)S(1)} %get-tuple-element.48), channel_id=1, source_target_pairs={{0,7},{1,6},{2,5},{3,4},{4,3},{5,2},{6,1},{7,0},{8,15},{9,14},{10,... | collective-permute-start | bytes 98312 | tf_op jit(solution)/shard_map/ppermute | solution.py:180
  27.8 0.9 %collective-permute-start.13 = (bf16[128,128]{1,0:T(8,128)(2,1)S(1)}, bf16[128,128]{1,0:T(8,128)(2,1)S(1)}, u32[]{:S(2)}, u32[]{:S(2)}) collective-permute-start(bf16[128,128]{1,0:T(8,128)(2,1)S(1)} %get-tuple-element.49), channel_id=1, source_target_pairs={{0,5},{1,2},{2,7},{3,0},{4,1},{5,6},{6,3},{7,4},{8,13},{9,10},{10,... | collective-permute-start | bytes 98312 | tf_op jit(solution)/shard_map/ppermute | solution.py:180
  28.6 0.9 %collective-permute-start.14 = (bf16[128,128]{1,0:T(8,128)(2,1)S(1)}, bf16[128,128]{1,0:T(8,128)(2,1)S(1)}, u32[]{:S(2)}, u32[]{:S(2)}) collective-permute-start(bf16[128,128]{1,0:T(8,128)(2,1)S(1)} %get-tuple-element.50), channel_id=1, source_target_pairs={{0,3},{1,4},{2,1},{3,6},{4,7},{5,0},{6,5},{7,2},{8,11},{9,12},{10,... | collective-permute-start | bytes 98312 | tf_op jit(solution)/shard_map/ppermute | solution.py:180
  30.3 0.8 %collective-permute-done.13.refs_1_ = bf16[128,128]{1,0:T(8,128)(2,1)S(1)} collective-permute-done((bf16[128,128]{1,0:T(8,128)(2,1)S(1)}, bf16[128,128]{1,0:T(8,128)(2,1)S(1)}, u32[]{:S(2)}, u32[]{:S(2)}) %collective-permute-start.13) | collective-permute-done | bytes 32800 | tf_op jit(solution)/shard_map/ppermute | solution.py:180
  31.1 0.9 %collective-permute-done.14.refs_2_ = bf16[128,128]{1,0:T(8,128)(2,1)S(1)} collective-permute-done((bf16[128,128]{1,0:T(8,128)(2,1)S(1)}, bf16[128,128]{1,0:T(8,128)(2,1)S(1)}, u32[]{:S(2)}, u32[]{:S(2)}) %collective-permute-start.14) | collective-permute-done | bytes 32800 | tf_op jit(solution)/shard_map/ppermute | solution.py:180
  32.0 1.5 %collective-permute-start.16 = (bf16[128,128]{1,0:T(8,128)(2,1)S(1)}, bf16[128,128]{1,0:T(8,128)(2,1)S(1)}, u32[]{:S(2)}, u32[]{:S(2)}) collective-permute-start(bf16[128,128]{1,0:T(8,128)(2,1)S(1)} %add_convert_fusion), channel_id=1, source_target_pairs={{0,24},{2,26},{4,28},{6,30},{8,16},{10,18},{12,20},{14,22},{16,8},... | collective-permute-start | bytes 98312 | tf_op jit(solution)/shard_map/ppermute | solution.py:172
  33.5 0.6 %collective-permute-start.17 = (bf16[128,128]{1,0:T(8,128)(2,1)S(1)}, bf16[128,128]{1,0:T(8,128)(2,1)S(1)}, u32[]{:S(2)}, u32[]{:S(2)}) collective-permute-start(bf16[128,128]{1,0:T(8,128)(2,1)S(1)} %add_convert_fusion), channel_id=1, source_target_pairs={{0,16},{2,18},{4,20},{6,22},{8,24},{10,26},{12,28},{14,30},{16,0},... | collective-permute-start | bytes 98312 | tf_op jit(solution)/shard_map/ppermute | solution.py:172
  34.2 2.3 %collective-permute-start.18 = (bf16[128,128]{1,0:T(8,128)(2,1)S(1)}, bf16[128,128]{1,0:T(8,128)(2,1)S(1)}, u32[]{:S(2)}, u32[]{:S(2)}) collective-permute-start(bf16[128,128]{1,0:T(8,128)(2,1)S(1)} %add_convert_fusion), channel_id=1, source_target_pairs={{0,8},{2,10},{4,12},{6,14},{8,0},{10,2},{12,4},{14,6},{16,24},{18,... | collective-permute-start | bytes 98312 | tf_op jit(solution)/shard_map/ppermute | solution.py:172
  36.4 2.0 %shard_map.80 = (bf16[256,512]{1,0:T(8,128)(2,1)}, bf16[256,512]{1,0:T(8,128)(2,1)}, f32[256,512]{1,0:T(8,128)S(1)}, f32[256,512]{1,0:T(8,128)S(1)}) custom-call(bf16[256,512]{1,0:T(8,128)(2,1)S(1)} %copy-done.2, bf16[256,512]{1,0:T(8,128)(2,1)S(1)} %copy-done, bf16[256,512]{1,0:T(8,128)(2,1)S(1)} %copy-done.1, ...), custom_call_target="tpu_custom_call" | custom-call | flops 301989888 | bytes 3803136 | tf_op jit(solution)/shard_map/pallas_call | solution.py:52
  38.9 1.0 %collective-permute-start.19 = (bf16[128,128]{1,0:T(8,128)(2,1)S(1)}, bf16[128,128]{1,0:T(8,128)(2,1)S(1)}, u32[]{:S(2)}, u32[]{:S(2)}) collective-permute-start(bf16[128,128]{1,0:T(8,128)(2,1)S(1)} %get-tuple-element.52), channel_id=1, source_target_pairs={{0,7},{1,6},{2,5},{3,4},{4,3},{5,2},{6,1},{7,0},{8,15},{9,14},{10,... | collective-permute-start | bytes 98312 | tf_op jit(solution)/shard_map/ppermute | solution.py:180
  39.9 1.3 %collective-permute-start.20 = (bf16[128,128]{1,0:T(8,128)(2,1)S(1)}, bf16[128,128]{1,0:T(8,128)(2,1)S(1)}, u32[]{:S(2)}, u32[]{:S(2)}) collective-permute-start(bf16[128,128]{1,0:T(8,128)(2,1)S(1)} %get-tuple-element.53), channel_id=1, source_target_pairs={{0,5},{1,2},{2,7},{3,0},{4,1},{5,6},{6,3},{7,4},{8,13},{9,10},{10,... | collective-permute-start | bytes 98312 | tf_op jit(solution)/shard_map/ppermute | solution.py:180
  41.6 0.6 %collective-permute-start.22 = (bf16[128,128]{1,0:T(8,128)(2,1)S(1)}, bf16[128,128]{1,0:T(8,128)(2,1)S(1)}, u32[]{:S(2)}, u32[]{:S(2)}) collective-permute-start(bf16[128,128]{1,0:T(8,128)(2,1)S(1)} %get-tuple-element.55), channel_id=1, source_target_pairs={{0,1},{1,0},{2,3},{3,2},{4,5},{5,4},{6,7},{7,6},{8,9},{9,8},{10,11... | collective-permute-start | bytes 98312 | tf_op jit(solution)/shard_map/ppermute | solution.py:180
  42.2 0.9 %collective-permute-done.19.p0 = bf16[128,128]{1,0:T(8,128)(2,1)S(1)} collective-permute-done((bf16[128,128]{1,0:T(8,128)(2,1)S(1)}, bf16[128,128]{1,0:T(8,128)(2,1)S(1)}, u32[]{:S(2)}, u32[]{:S(2)}) %collective-permute-start.19) | collective-permute-done | bytes 32800 | tf_op jit(solution)/shard_map/ppermute | solution.py:180
  43.2 1.3 %collective-permute-done.21.p2 = bf16[128,128]{1,0:T(8,128)(2,1)S(1)} collective-permute-done((bf16[128,128]{1,0:T(8,128)(2,1)S(1)}, bf16[128,128]{1,0:T(8,128)(2,1)S(1)}, u32[]{:S(2)}, u32[]{:S(2)}) %collective-permute-start.21) | collective-permute-done | bytes 32800 | tf_op jit(solution)/shard_map/ppermute | solution.py:180
  44.6 1.1 %shard_map.82 = (bf16[256,512]{1,0:T(8,128)(2,1)}, bf16[256,512]{1,0:T(8,128)(2,1)}) custom-call(bf16[256,512]{1,0:T(8,128)(2,1)S(1)} %copy-done, bf16[256,512]{1,0:T(8,128)(2,1)S(1)} %copy-done.1, f32[256,512]{1,0:T(8,128)S(1)} %get-tuple-element.46.refs_7_.key_local, f32[256,512]{1,0:T(8,128)S(1)} %get-tuple-element.47.value_local, ...), custom_call_target="tpu_custom_call" | custom-call | flops 67108864 | bytes 2228224 | tf_op jit(solution)/shard_map/pallas_call | solution.py:52
  (33 shorter events, 3.3 us)
Async XLA Ops:
  0.6 21.2 %copy-start.1 = (bf16[256,512]{1,0:T(8,128)(2,1)S(1)}, bf16[256,512]{1,0:T(8,128)(2,1)}, u32[]{:S(2)}) copy-start(bf16[256,512]{1,0:T(8,128)(2,1)} %v_ref.7) | copy-start | bytes 786436
  0.6 21.2 %copy-start.2 = (bf16[256,512]{1,0:T(8,128)(2,1)S(1)}, bf16[256,512]{1,0:T(8,128)(2,1)}, u32[]{:S(2)}) copy-start(bf16[256,512]{1,0:T(8,128)(2,1)} %q_ref.7) | copy-start | bytes 786436
  2.1 19.7 %copy-start = (bf16[256,512]{1,0:T(8,128)(2,1)S(1)}, bf16[256,512]{1,0:T(8,128)(2,1)}, u32[]{:S(2)}) copy-start(bf16[256,512]{1,0:T(8,128)(2,1)} %k_ref.7) | copy-start | bytes 786436
  2.1 5.8 %collective-permute-start = (bf16[128,128]{1,0:T(8,128)(2,1)S(1)}, bf16[128,128]{1,0:T(8,128)(2,1)S(1)}, u32[]{:S(2)}, u32[]{:S(2)}) collective-permute-start(bf16[128,128]{1,0:T(8,128)(2,1)S(1)} %get-tuple-element.32), channel_id=1, source_target_pairs={{0,7},{1,6},{2,5},{3,4},{4,3},{5,2},{6,1},{7,0},{8,15},{9,14},{10,... | collective-permute-start | bytes 98312 | tf_op jit(solution)/shard_map/ppermute | solution.py:180
  5.5 3.3 %collective-permute-start.1 = (bf16[128,128]{1,0:T(8,128)(2,1)S(1)}, bf16[128,128]{1,0:T(8,128)(2,1)S(1)}, u32[]{:S(2)}, u32[]{:S(2)}) collective-permute-start(bf16[128,128]{1,0:T(8,128)(2,1)S(1)} %get-tuple-element.33), channel_id=1, source_target_pairs={{0,5},{1,2},{2,7},{3,0},{4,1},{5,6},{6,3},{7,4},{8,13},{9,10},{10,... | collective-permute-start | bytes 98312 | tf_op jit(solution)/shard_map/ppermute | solution.py:180
  6.3 3.6 %collective-permute-start.2 = (bf16[128,128]{1,0:T(8,128)(2,1)S(1)}, bf16[128,128]{1,0:T(8,128)(2,1)S(1)}, u32[]{:S(2)}, u32[]{:S(2)}) collective-permute-start(bf16[128,128]{1,0:T(8,128)(2,1)S(1)} %get-tuple-element.34), channel_id=1, source_target_pairs={{0,3},{1,4},{2,1},{3,6},{4,7},{5,0},{6,5},{7,2},{8,11},{9,12},{10,... | collective-permute-start | bytes 98312 | tf_op jit(solution)/shard_map/ppermute | solution.py:180
  7.3 2.7 %collective-permute-start.3 = (bf16[128,128]{1,0:T(8,128)(2,1)S(1)}, bf16[128,128]{1,0:T(8,128)(2,1)S(1)}, u32[]{:S(2)}, u32[]{:S(2)}) collective-permute-start(bf16[128,128]{1,0:T(8,128)(2,1)S(1)} %get-tuple-element.35), channel_id=1, source_target_pairs={{0,1},{1,0},{2,3},{3,2},{4,5},{5,4},{6,7},{7,6},{8,9},{9,8},{10,11... | collective-permute-start | bytes 98312 | tf_op jit(solution)/shard_map/ppermute | solution.py:180
  10.0 5.8 %collective-permute-start.4 = (bf16[128,128]{1,0:T(8,128)(2,1)S(1)}, bf16[128,128]{1,0:T(8,128)(2,1)S(1)}, u32[]{:S(2)}, u32[]{:S(2)}) collective-permute-start(bf16[128,128]{1,0:T(8,128)(2,1)S(1)} %add_convert_fusion.1), channel_id=1, source_target_pairs={{0,24},{2,26},{4,28},{6,30},{8,16},{10,18},{12,20},{14,22},{16,8},... | collective-permute-start | bytes 98312 | tf_op jit(solution)/shard_map/ppermute | solution.py:172
  13.6 4.8 %collective-permute-start.5 = (bf16[128,128]{1,0:T(8,128)(2,1)S(1)}, bf16[128,128]{1,0:T(8,128)(2,1)S(1)}, u32[]{:S(2)}, u32[]{:S(2)}) collective-permute-start(bf16[128,128]{1,0:T(8,128)(2,1)S(1)} %add_convert_fusion.1), channel_id=1, source_target_pairs={{0,16},{2,18},{4,20},{6,22},{8,24},{10,26},{12,28},{14,30},{16,0},... | collective-permute-start | bytes 98312 | tf_op jit(solution)/shard_map/ppermute | solution.py:172
  13.6 4.8 %collective-permute-start.6 = (bf16[128,128]{1,0:T(8,128)(2,1)S(1)}, bf16[128,128]{1,0:T(8,128)(2,1)S(1)}, u32[]{:S(2)}, u32[]{:S(2)}) collective-permute-start(bf16[128,128]{1,0:T(8,128)(2,1)S(1)} %add_convert_fusion.1), channel_id=1, source_target_pairs={{0,8},{2,10},{4,12},{6,14},{8,0},{10,2},{12,4},{14,6},{16,24},{18,... | collective-permute-start | bytes 98312 | tf_op jit(solution)/shard_map/ppermute | solution.py:172
  18.6 4.3 %collective-permute-start.7 = (bf16[128,128]{1,0:T(8,128)(2,1)S(1)}, bf16[128,128]{1,0:T(8,128)(2,1)S(1)}, u32[]{:S(2)}, u32[]{:S(2)}) collective-permute-start(bf16[128,128]{1,0:T(8,128)(2,1)S(1)} %get-tuple-element.36), channel_id=1, source_target_pairs={{0,7},{1,6},{2,5},{3,4},{4,3},{5,2},{6,1},{7,0},{8,15},{9,14},{10,... | collective-permute-start | bytes 98312 | tf_op jit(solution)/shard_map/ppermute | solution.py:180
  18.6 4.4 %collective-permute-start.8 = (bf16[128,128]{1,0:T(8,128)(2,1)S(1)}, bf16[128,128]{1,0:T(8,128)(2,1)S(1)}, u32[]{:S(2)}, u32[]{:S(2)}) collective-permute-start(bf16[128,128]{1,0:T(8,128)(2,1)S(1)} %get-tuple-element.37), channel_id=1, source_target_pairs={{0,5},{1,2},{2,7},{3,0},{4,1},{5,6},{6,3},{7,4},{8,13},{9,10},{10,... | collective-permute-start | bytes 98312 | tf_op jit(solution)/shard_map/ppermute | solution.py:180
  20.3 3.6 %collective-permute-start.9 = (bf16[128,128]{1,0:T(8,128)(2,1)S(1)}, bf16[128,128]{1,0:T(8,128)(2,1)S(1)}, u32[]{:S(2)}, u32[]{:S(2)}) collective-permute-start(bf16[128,128]{1,0:T(8,128)(2,1)S(1)} %get-tuple-element.38), channel_id=1, source_target_pairs={{0,3},{1,4},{2,1},{3,6},{4,7},{5,0},{6,5},{7,2},{8,11},{9,12},{10,... | collective-permute-start | bytes 98312 | tf_op jit(solution)/shard_map/ppermute | solution.py:180
  21.1 2.9 %copy-start.3 = (bf16[256,512]{1,0:T(8,128)(2,1)S(1)}, bf16[256,512]{1,0:T(8,128)(2,1)}, u32[]{:S(2)}) copy-start(bf16[256,512]{1,0:T(8,128)(2,1)} %c_ref.3) | copy-start | bytes 786436
  21.1 2.9 %collective-permute-start.10 = (bf16[128,128]{1,0:T(8,128)(2,1)S(1)}, bf16[128,128]{1,0:T(8,128)(2,1)S(1)}, u32[]{:S(2)}, u32[]{:S(2)}) collective-permute-start(bf16[128,128]{1,0:T(8,128)(2,1)S(1)} %get-tuple-element.39), channel_id=1, source_target_pairs={{0,1},{1,0},{2,3},{3,2},{4,5},{5,4},{6,7},{7,6},{8,9},{9,8},{10,11... | collective-permute-start | bytes 98312 | tf_op jit(solution)/shard_map/ppermute | solution.py:180
  24.3 1.2 %collective-permute-start.11 = (f32[2,256]{1,0:T(2,128)S(1)}, f32[2,256]{1,0:T(2,128)S(1)}, u32[]{:S(2)}, u32[]{:S(2)}) collective-permute-start(f32[2,256]{1,0:T(2,128)S(1)} %get-tuple-element.41), channel_id=1, source_target_pairs={{0,1},{1,0},{2,3},{3,2},{4,5},{5,4},{6,7},{7,6},{8,9},{9,8},{10,11... | collective-permute-start | bytes 6152 | tf_op jit(solution)/shard_map/ppermute | solution.py:172
  26.0 4.3 %collective-permute-start.12 = (bf16[128,128]{1,0:T(8,128)(2,1)S(1)}, bf16[128,128]{1,0:T(8,128)(2,1)S(1)}, u32[]{:S(2)}, u32[]{:S(2)}) collective-permute-start(bf16[128,128]{1,0:T(8,128)(2,1)S(1)} %get-tuple-element.48), channel_id=1, source_target_pairs={{0,7},{1,6},{2,5},{3,4},{4,3},{5,2},{6,1},{7,0},{8,15},{9,14},{10,... | collective-permute-start | bytes 98312 | tf_op jit(solution)/shard_map/ppermute | solution.py:180
  27.8 3.3 %collective-permute-start.13 = (bf16[128,128]{1,0:T(8,128)(2,1)S(1)}, bf16[128,128]{1,0:T(8,128)(2,1)S(1)}, u32[]{:S(2)}, u32[]{:S(2)}) collective-permute-start(bf16[128,128]{1,0:T(8,128)(2,1)S(1)} %get-tuple-element.49), channel_id=1, source_target_pairs={{0,5},{1,2},{2,7},{3,0},{4,1},{5,6},{6,3},{7,4},{8,13},{9,10},{10,... | collective-permute-start | bytes 98312 | tf_op jit(solution)/shard_map/ppermute | solution.py:180
  28.6 3.3 %collective-permute-start.14 = (bf16[128,128]{1,0:T(8,128)(2,1)S(1)}, bf16[128,128]{1,0:T(8,128)(2,1)S(1)}, u32[]{:S(2)}, u32[]{:S(2)}) collective-permute-start(bf16[128,128]{1,0:T(8,128)(2,1)S(1)} %get-tuple-element.50), channel_id=1, source_target_pairs={{0,3},{1,4},{2,1},{3,6},{4,7},{5,0},{6,5},{7,2},{8,11},{9,12},{10,... | collective-permute-start | bytes 98312 | tf_op jit(solution)/shard_map/ppermute | solution.py:180
  29.5 2.5 %collective-permute-start.15 = (bf16[128,128]{1,0:T(8,128)(2,1)S(1)}, bf16[128,128]{1,0:T(8,128)(2,1)S(1)}, u32[]{:S(2)}, u32[]{:S(2)}) collective-permute-start(bf16[128,128]{1,0:T(8,128)(2,1)S(1)} %get-tuple-element.51), channel_id=1, source_target_pairs={{0,1},{1,0},{2,3},{3,2},{4,5},{5,4},{6,7},{7,6},{8,9},{9,8},{10,11... | collective-permute-start | bytes 98312 | tf_op jit(solution)/shard_map/ppermute | solution.py:180
  32.0 6.5 %collective-permute-start.16 = (bf16[128,128]{1,0:T(8,128)(2,1)S(1)}, bf16[128,128]{1,0:T(8,128)(2,1)S(1)}, u32[]{:S(2)}, u32[]{:S(2)}) collective-permute-start(bf16[128,128]{1,0:T(8,128)(2,1)S(1)} %add_convert_fusion), channel_id=1, source_target_pairs={{0,24},{2,26},{4,28},{6,30},{8,16},{10,18},{12,20},{14,22},{16,8},... | collective-permute-start | bytes 98312 | tf_op jit(solution)/shard_map/ppermute | solution.py:172
  33.5 5.0 %collective-permute-start.17 = (bf16[128,128]{1,0:T(8,128)(2,1)S(1)}, bf16[128,128]{1,0:T(8,128)(2,1)S(1)}, u32[]{:S(2)}, u32[]{:S(2)}) collective-permute-start(bf16[128,128]{1,0:T(8,128)(2,1)S(1)} %add_convert_fusion), channel_id=1, source_target_pairs={{0,16},{2,18},{4,20},{6,22},{8,24},{10,26},{12,28},{14,30},{16,0},... | collective-permute-start | bytes 98312 | tf_op jit(solution)/shard_map/ppermute | solution.py:172
  34.2 4.6 %collective-permute-start.18 = (bf16[128,128]{1,0:T(8,128)(2,1)S(1)}, bf16[128,128]{1,0:T(8,128)(2,1)S(1)}, u32[]{:S(2)}, u32[]{:S(2)}) collective-permute-start(bf16[128,128]{1,0:T(8,128)(2,1)S(1)} %add_convert_fusion), channel_id=1, source_target_pairs={{0,8},{2,10},{4,12},{6,14},{8,0},{10,2},{12,4},{14,6},{16,24},{18,... | collective-permute-start | bytes 98312 | tf_op jit(solution)/shard_map/ppermute | solution.py:172
  38.9 4.3 %collective-permute-start.19 = (bf16[128,128]{1,0:T(8,128)(2,1)S(1)}, bf16[128,128]{1,0:T(8,128)(2,1)S(1)}, u32[]{:S(2)}, u32[]{:S(2)}) collective-permute-start(bf16[128,128]{1,0:T(8,128)(2,1)S(1)} %get-tuple-element.52), channel_id=1, source_target_pairs={{0,7},{1,6},{2,5},{3,4},{4,3},{5,2},{6,1},{7,0},{8,15},{9,14},{10,... | collective-permute-start | bytes 98312 | tf_op jit(solution)/shard_map/ppermute | solution.py:180
  39.9 3.3 %collective-permute-start.20 = (bf16[128,128]{1,0:T(8,128)(2,1)S(1)}, bf16[128,128]{1,0:T(8,128)(2,1)S(1)}, u32[]{:S(2)}, u32[]{:S(2)}) collective-permute-start(bf16[128,128]{1,0:T(8,128)(2,1)S(1)} %get-tuple-element.53), channel_id=1, source_target_pairs={{0,5},{1,2},{2,7},{3,0},{4,1},{5,6},{6,3},{7,4},{8,13},{9,10},{10,... | collective-permute-start | bytes 98312 | tf_op jit(solution)/shard_map/ppermute | solution.py:180
  41.2 3.3 %collective-permute-start.21 = (bf16[128,128]{1,0:T(8,128)(2,1)S(1)}, bf16[128,128]{1,0:T(8,128)(2,1)S(1)}, u32[]{:S(2)}, u32[]{:S(2)}) collective-permute-start(bf16[128,128]{1,0:T(8,128)(2,1)S(1)} %get-tuple-element.54), channel_id=1, source_target_pairs={{0,3},{1,4},{2,1},{3,6},{4,7},{5,0},{6,5},{7,2},{8,11},{9,12},{10,... | collective-permute-start | bytes 98312 | tf_op jit(solution)/shard_map/ppermute | solution.py:180
  41.6 2.9 %collective-permute-start.22 = (bf16[128,128]{1,0:T(8,128)(2,1)S(1)}, bf16[128,128]{1,0:T(8,128)(2,1)S(1)}, u32[]{:S(2)}, u32[]{:S(2)}) collective-permute-start(bf16[128,128]{1,0:T(8,128)(2,1)S(1)} %get-tuple-element.55), channel_id=1, source_target_pairs={{0,1},{1,0},{2,3},{3,2},{4,5},{5,4},{6,7},{7,6},{8,9},{9,8},{10,11... | collective-permute-start | bytes 98312 | tf_op jit(solution)/shard_map/ppermute | solution.py:180

commit v6 on v5

--- a/solution.py
+++ b/solution.py
@@ -68,12 +68,18 @@
             part = pl.ds(i * rows, rows)
             copies.append(pltpu.make_async_copy(ref.at[part], buf.at[part], sems.at[n, i]))
             copies[-1].start()
-    for copy in copies:
-        copy.wait()
-    m = member_of_quad()
+    m = member_of_quad()
+    states = [0.0] * QUAD
+    half = rows * CHUNKS // 2
+    for part in range(2):
+        for copy in copies[part * CHUNKS : (part + 1) * CHUNKS]:
+            copy.wait()
+        tokens = pl.ds(part * half, half)
+        for op in OPS:
+            cols = pl.ds(pl.multiple_of((m ^ sent(op)) * DH, DH), DH)
+            states[op] = states[op] + dot(k_buf[tokens, cols], v_buf[tokens, cols], ((0,), (0,)))
     for op, out in enumerate((o0, o1, o2, o3)):
-        h = m ^ sent(op)
-        out[...] = dot(head(k_buf, h)[...], head(v_buf, h)[...], ((0,), (0,))).astype(LOW)
+        out[...] = states[op].astype(LOW)
 
 
 def local_kernel(q_ref, k_ref, v_ref, scores_ref, mixed_ref):
@@ -148,17 +154,24 @@
         head(value_ref, h)[...] = value.astype(LOW)
 
 
-def sums_kernel(before, far, *refs):
+def quad_targets(quads, step, before):
+    targets = [z ^ step for z in range(quads)]
+    if quads == 4 and step == 3:
+        targets = [3, 2, 0, 1] if before else [2, 3, 1, 0]
+    return targets
+
+
+def sums_kernel(before, quads, *refs):
     index = lax.axis_index("seq")
-    m = index % QUAD
-    held, got, outs = refs[:QUAD], refs[QUAD : QUAD + len(far)], refs[-QUAD:]
+    m, quad = index % QUAD, index // QUAD
+    held, got, outs = refs[:QUAD], refs[QUAD : QUAD + quads - 1], refs[-QUAD:]
 
     def counts(a, b):
         return jnp.where(a < b if before else a > b, 1.0, 0.0).astype(WIDE)
 
     outer = jnp.zeros((DH, DH), WIDE)
-    for bits, total in zip(far, got):
-        outer = outer + total[...].astype(WIDE) * counts(index ^ bits, index)
+    for step, total in zip(range(quads - 1, 0, -1), got):
+        outer = outer + total[...].astype(WIDE) * counts(quad ^ step, quad)
     pieces = [piece[...].astype(WIDE) for piece in held]
     for to in OPS:
         inner = outer
@@ -183,11 +196,15 @@
 def exclusive_sum(held, before, *after):
     held = [cross(held[op], op) for op in OPS]
     total = sum(piece.astype(WIDE) for piece in held).astype(LOW)
-    far = range(lax.axis_size("seq") - QUAD, 0, -QUAD)
-    got = [exchange(total, "seq", bits) for bits in far]
+    quads = lax.axis_size("seq") // QUAD
+    got = []
+    for step in range(quads - 1, 0, -1):
+        targets = quad_targets(quads, step, before)
+        pairs = [(z * QUAD + i, targets[z] * QUAD + i) for z in range(quads) for i in range(QUAD)]
+        got.append(lax.ppermute(total, "seq", pairs))
     vmem = [pl.BlockSpec(memory_space=pltpu.VMEM)] * (QUAD + len(got))
     sums = call(
-        functools.partial(sums_kernel, before, far),
+        functools.partial(sums_kernel, before, quads),
         [jax.ShapeDtypeStruct(x.shape, x.dtype) for x in held],
         (*held, *got, *after),
         0,

time: 45.8 us -> 45.8 us (level)
    ppermute x0 -> x6, starting transfers between devices: none -> 8.99 us  [exclusive_sum(): got.append(lax.ppermute(total, 'seq', pairs))]
    ppermute x7 -> x1, starting transfers between devices: 8.99 us -> 0.08 us  [exchange(): return lax.ppermute(value, axis, [(i, i ^ bits) for i in range(size)])]
    ppermute x0 -> x6, waiting for transfers between devices: none -> 4.35 us  [exclusive_sum(): got.append(lax.ppermute(total, 'seq', pairs))]
    ppermute x7 -> x1, waiting for transfers between devices: 5.46 us -> 1.14 us  [exchange(): return lax.ppermute(value, axis, [(i, i ^ bits) for i in range(size)])]
where the time goes in v6:
time: 45.8 us; the launch traced here: 45.6 us
  starting transfers between devices  25.2 us (55%)
  waiting for transfers between devices  13.4 us (29%)
  Pallas kernels  6.25 us (14%)
  between operations  0.73 us (2%)
    ppermute x16, starting transfers between devices, cross(): return lax.ppermute(value, ('seq', 'tp'), pairs)  16.1 us
    ppermute x6, starting transfers between devices, exclusive_sum(): got.append(lax.ppermute(total, 'seq', pairs))  8.99 us
    ppermute x16, waiting for transfers between devices, cross(): return lax.ppermute(value, ('seq', 'tp'), pairs)  7.88 us
    pallas_call x8, Pallas kernels, call(): pl.pallas_call(kernel, out_shape=outs, in_specs=in_specs or [pl.BlockSpec...  6.25 us
    ppermute x6, waiting for transfers between devices, exclusive_sum(): got.append(lax.ppermute(total, 'seq', pairs))  4.35 us
    ppermute x1, waiting for transfers between devices, exchange(): return lax.ppermute(value, axis, [(i, i ^ bits) for i in range(size)])  1.14 us
  transfers between devices with their start and end apart: 23, of which 14 were waited for; matrix products, arithmetic and copies ran while one was open for 0% of the time, Pallas kernels for 6%

profile of v6, /device:TPU:0, one launch (start us, length us, event | category | flops | bytes accessed | tf_op | source)
XLA Modules:
  0.0 45.6 jit_solution(775125559238268256)
XLA Ops:
  0.7 1.4 %shard_map.76 = (bf16[128,128]{1,0:T(8,128)(2,1)S(1)}, bf16[128,128]{1,0:T(8,128)(2,1)S(1)}, bf16[128,128]{1,0:T(8,128)(2,1)S(1)}, bf16[128,128]{1,0:T(8,128)(2,1)S(1)}) custom-call(bf16[256,512]{1,0:T(8,128)(2,1)} %k_ref.7, bf16[256,512]{1,0:T(8,128)(2,1)} %v_ref.7), custom_call_target="tpu_custom_call" | custom-call | flops 33554432 | bytes 655360 | tf_op jit(solution)/shard_map/pallas_call | solution.py:52
  2.1 3.4 %collective-permute-start = (bf16[128,128]{1,0:T(8,128)(2,1)S(1)}, bf16[128,128]{1,0:T(8,128)(2,1)S(1)}, u32[]{:S(2)}, u32[]{:S(2)}) collective-permute-start(bf16[128,128]{1,0:T(8,128)(2,1)S(1)} %get-tuple-element.32), channel_id=1, source_target_pairs={{0,7},{1,6},{2,5},{3,4},{4,3},{5,2},{6,1},{7,0},{8,15},{9,14},{10,... | collective-permute-start | bytes 98312 | tf_op jit(solution)/shard_map/ppermute | solution.py:193
  5.5 0.8 %collective-permute-start.1 = (bf16[128,128]{1,0:T(8,128)(2,1)S(1)}, bf16[128,128]{1,0:T(8,128)(2,1)S(1)}, u32[]{:S(2)}, u32[]{:S(2)}) collective-permute-start(bf16[128,128]{1,0:T(8,128)(2,1)S(1)} %get-tuple-element.33), channel_id=1, source_target_pairs={{0,5},{1,2},{2,7},{3,0},{4,1},{5,6},{6,3},{7,4},{8,13},{9,10},{10,... | collective-permute-start | bytes 98312 | tf_op jit(solution)/shard_map/ppermute | solution.py:193
  6.3 1.0 %collective-permute-start.2 = (bf16[128,128]{1,0:T(8,128)(2,1)S(1)}, bf16[128,128]{1,0:T(8,128)(2,1)S(1)}, u32[]{:S(2)}, u32[]{:S(2)}) collective-permute-start(bf16[128,128]{1,0:T(8,128)(2,1)S(1)} %get-tuple-element.34), channel_id=1, source_target_pairs={{0,3},{1,4},{2,1},{3,6},{4,7},{5,0},{6,5},{7,2},{8,11},{9,12},{10,... | collective-permute-start | bytes 98312 | tf_op jit(solution)/shard_map/ppermute | solution.py:193
  7.3 0.7 %collective-permute-start.3 = (bf16[128,128]{1,0:T(8,128)(2,1)S(1)}, bf16[128,128]{1,0:T(8,128)(2,1)S(1)}, u32[]{:S(2)}, u32[]{:S(2)}) collective-permute-start(bf16[128,128]{1,0:T(8,128)(2,1)S(1)} %get-tuple-element.35), channel_id=1, source_target_pairs={{0,1},{1,0},{2,3},{3,2},{4,5},{5,4},{6,7},{7,6},{8,9},{9,8},{10,11... | collective-permute-start | bytes 98312 | tf_op jit(solution)/shard_map/ppermute | solution.py:193
  7.9 0.9 %collective-permute-done.1.refs_1_ = bf16[128,128]{1,0:T(8,128)(2,1)S(1)} collective-permute-done((bf16[128,128]{1,0:T(8,128)(2,1)S(1)}, bf16[128,128]{1,0:T(8,128)(2,1)S(1)}, u32[]{:S(2)}, u32[]{:S(2)}) %collective-permute-start.1) | collective-permute-done | bytes 32800 | tf_op jit(solution)/shard_map/ppermute | solution.py:193
  8.9 1.1 %collective-permute-done.2.refs_2_ = bf16[128,128]{1,0:T(8,128)(2,1)S(1)} collective-permute-done((bf16[128,128]{1,0:T(8,128)(2,1)S(1)}, bf16[128,128]{1,0:T(8,128)(2,1)S(1)}, u32[]{:S(2)}, u32[]{:S(2)}) %collective-permute-start.2) | collective-permute-done | bytes 32800 | tf_op jit(solution)/shard_map/ppermute | solution.py:193
  10.0 3.7 %collective-permute-start.4 = (bf16[128,128]{1,0:T(8,128)(2,1)S(1)}, bf16[128,128]{1,0:T(8,128)(2,1)S(1)}, u32[]{:S(2)}, u32[]{:S(2)}) collective-permute-start(bf16[128,128]{1,0:T(8,128)(2,1)S(1)} %add_convert_fusion.1), channel_id=1, source_target_pairs={{0,24},{2,26},{4,28},{6,30},{8,16},{10,18},{12,20},{14,22},{16,0},... | collective-permute-start | bytes 98312 | tf_op jit(solution)/shard_map/ppermute | solution.py:204
  13.6 0.9 %collective-permute-start.6 = (bf16[128,128]{1,0:T(8,128)(2,1)S(1)}, bf16[128,128]{1,0:T(8,128)(2,1)S(1)}, u32[]{:S(2)}, u32[]{:S(2)}) collective-permute-start(bf16[128,128]{1,0:T(8,128)(2,1)S(1)} %add_convert_fusion.1), channel_id=1, source_target_pairs={{0,8},{2,10},{4,12},{6,14},{8,0},{10,2},{12,4},{14,6},{16,24},{18,... | collective-permute-start | bytes 98312 | tf_op jit(solution)/shard_map/ppermute | solution.py:204
  14.5 0.7 %collective-permute-done.4.refs_4_ = bf16[128,128]{1,0:T(8,128)(2,1)S(1)} collective-permute-done((bf16[128,128]{1,0:T(8,128)(2,1)S(1)}, bf16[128,128]{1,0:T(8,128)(2,1)S(1)}, u32[]{:S(2)}, u32[]{:S(2)}) %collective-permute-start.4) | collective-permute-done | bytes 32800 | tf_op jit(solution)/shard_map/ppermute | solution.py:204
  15.2 3.2 %collective-permute-done.5.refs_5_ = bf16[128,128]{1,0:T(8,128)(2,1)S(1)} collective-permute-done((bf16[128,128]{1,0:T(8,128)(2,1)S(1)}, bf16[128,128]{1,0:T(8,128)(2,1)S(1)}, u32[]{:S(2)}, u32[]{:S(2)}) %collective-permute-start.5) | collective-permute-done | bytes 32800 | tf_op jit(solution)/shard_map/ppermute | solution.py:204
  18.6 1.7 %collective-permute-start.8 = (bf16[128,128]{1,0:T(8,128)(2,1)S(1)}, bf16[128,128]{1,0:T(8,128)(2,1)S(1)}, u32[]{:S(2)}, u32[]{:S(2)}) collective-permute-start(bf16[128,128]{1,0:T(8,128)(2,1)S(1)} %get-tuple-element.37), channel_id=1, source_target_pairs={{0,5},{1,2},{2,7},{3,0},{4,1},{5,6},{6,3},{7,4},{8,13},{9,10},{10,... | collective-permute-start | bytes 98312 | tf_op jit(solution)/shard_map/ppermute | solution.py:193
  20.3 0.7 %collective-permute-start.9 = (bf16[128,128]{1,0:T(8,128)(2,1)S(1)}, bf16[128,128]{1,0:T(8,128)(2,1)S(1)}, u32[]{:S(2)}, u32[]{:S(2)}) collective-permute-start(bf16[128,128]{1,0:T(8,128)(2,1)S(1)} %get-tuple-element.38), channel_id=1, source_target_pairs={{0,3},{1,4},{2,1},{3,6},{4,7},{5,0},{6,5},{7,2},{8,11},{9,12},{10,... | collective-permute-start | bytes 98312 | tf_op jit(solution)/shard_map/ppermute | solution.py:193
  21.0 0.8 %collective-permute-start.10 = (bf16[128,128]{1,0:T(8,128)(2,1)S(1)}, bf16[128,128]{1,0:T(8,128)(2,1)S(1)}, u32[]{:S(2)}, u32[]{:S(2)}) collective-permute-start(bf16[128,128]{1,0:T(8,128)(2,1)S(1)} %get-tuple-element.39), channel_id=1, source_target_pairs={{0,1},{1,0},{2,3},{3,2},{4,5},{5,4},{6,7},{7,6},{8,9},{9,8},{10,11... | collective-permute-start | bytes 98312 | tf_op jit(solution)/shard_map/ppermute | solution.py:193
  21.8 0.7 %shard_map.75 = (bf16[4,256,256]{2,1,0:T(8,128)(2,1)S(1)}, f32[256,512]{1,0:T(8,128)S(1)}) custom-call(bf16[256,512]{1,0:T(8,128)(2,1)S(1)} %copy-done.2, bf16[256,512]{1,0:T(8,128)(2,1)S(1)} %copy-done, bf16[256,512]{1,0:T(8,128)(2,1)S(1)} %copy-done.1), custom_call_target="tpu_custom_call" | custom-call | flops 134217728 | bytes 1835008 | tf_op jit(solution)/shard_map/pallas_call | solution.py:52
  23.0 0.9 %collective-permute-done.9.p2 = bf16[128,128]{1,0:T(8,128)(2,1)S(1)} collective-permute-done((bf16[128,128]{1,0:T(8,128)(2,1)S(1)}, bf16[128,128]{1,0:T(8,128)(2,1)S(1)}, u32[]{:S(2)}, u32[]{:S(2)}) %collective-permute-start.9) | collective-permute-done | bytes 32800 | tf_op jit(solution)/shard_map/ppermute | solution.py:193
  24.4 1.1 %collective-permute-done.11 = f32[2,256]{1,0:T(2,128)S(1)} collective-permute-done((f32[2,256]{1,0:T(2,128)S(1)}, f32[2,256]{1,0:T(2,128)S(1)}, u32[]{:S(2)}, u32[]{:S(2)}) %collective-permute-start.11) | collective-permute-done | bytes 2080 | tf_op jit(solution)/shard_map/ppermute | solution.py:185
  26.0 1.8 %collective-permute-start.12 = (bf16[128,128]{1,0:T(8,128)(2,1)S(1)}, bf16[128,128]{1,0:T(8,128)(2,1)S(1)}, u32[]{:S(2)}, u32[]{:S(2)}) collective-permute-start(bf16[128,128]{1,0:T(8,128)(2,1)S(1)} %get-tuple-element.48), channel_id=1, source_target_pairs={{0,7},{1,6},{2,5},{3,4},{4,3},{5,2},{6,1},{7,0},{8,15},{9,14},{10,... | collective-permute-start | bytes 98312 | tf_op jit(solution)/shard_map/ppermute | solution.py:193
  27.7 0.9 %collective-permute-start.13 = (bf16[128,128]{1,0:T(8,128)(2,1)S(1)}, bf16[128,128]{1,0:T(8,128)(2,1)S(1)}, u32[]{:S(2)}, u32[]{:S(2)}) collective-permute-start(bf16[128,128]{1,0:T(8,128)(2,1)S(1)} %get-tuple-element.49), channel_id=1, source_target_pairs={{0,5},{1,2},{2,7},{3,0},{4,1},{5,6},{6,3},{7,4},{8,13},{9,10},{10,... | collective-permute-start | bytes 98312 | tf_op jit(solution)/shard_map/ppermute | solution.py:193
  28.6 0.9 %collective-permute-start.14 = (bf16[128,128]{1,0:T(8,128)(2,1)S(1)}, bf16[128,128]{1,0:T(8,128)(2,1)S(1)}, u32[]{:S(2)}, u32[]{:S(2)}) collective-permute-start(bf16[128,128]{1,0:T(8,128)(2,1)S(1)} %get-tuple-element.50), channel_id=1, source_target_pairs={{0,3},{1,4},{2,1},{3,6},{4,7},{5,0},{6,5},{7,2},{8,11},{9,12},{10,... | collective-permute-start | bytes 98312 | tf_op jit(solution)/shard_map/ppermute | solution.py:193
  29.8 0.5 collective-permute-done.12.refs_0_
  30.3 0.8 %collective-permute-done.13.refs_1_ = bf16[128,128]{1,0:T(8,128)(2,1)S(1)} collective-permute-done((bf16[128,128]{1,0:T(8,128)(2,1)S(1)}, bf16[128,128]{1,0:T(8,128)(2,1)S(1)}, u32[]{:S(2)}, u32[]{:S(2)}) %collective-permute-start.13) | collective-permute-done | bytes 32800 | tf_op jit(solution)/shard_map/ppermute | solution.py:193
  31.1 0.9 %collective-permute-done.14.refs_2_ = bf16[128,128]{1,0:T(8,128)(2,1)S(1)} collective-permute-done((bf16[128,128]{1,0:T(8,128)(2,1)S(1)}, bf16[128,128]{1,0:T(8,128)(2,1)S(1)}, u32[]{:S(2)}, u32[]{:S(2)}) %collective-permute-start.14) | collective-permute-done | bytes 32800 | tf_op jit(solution)/shard_map/ppermute | solution.py:193
  32.0 2.1 %collective-permute-start.16 = (bf16[128,128]{1,0:T(8,128)(2,1)S(1)}, bf16[128,128]{1,0:T(8,128)(2,1)S(1)}, u32[]{:S(2)}, u32[]{:S(2)}) collective-permute-start(bf16[128,128]{1,0:T(8,128)(2,1)S(1)} %add_convert_fusion), channel_id=1, source_target_pairs={{0,16},{2,18},{4,20},{6,22},{8,24},{10,26},{12,28},{14,30},{16,8},... | collective-permute-start | bytes 98312 | tf_op jit(solution)/shard_map/ppermute | solution.py:204
  34.1 2.3 %collective-permute-start.18 = (bf16[128,128]{1,0:T(8,128)(2,1)S(1)}, bf16[128,128]{1,0:T(8,128)(2,1)S(1)}, u32[]{:S(2)}, u32[]{:S(2)}) collective-permute-start(bf16[128,128]{1,0:T(8,128)(2,1)S(1)} %add_convert_fusion), channel_id=1, source_target_pairs={{0,8},{2,10},{4,12},{6,14},{8,0},{10,2},{12,4},{14,6},{16,24},{18,... | collective-permute-start | bytes 98312 | tf_op jit(solution)/shard_map/ppermute | solution.py:204
  36.4 2.0 %shard_map.80 = (bf16[256,512]{1,0:T(8,128)(2,1)}, bf16[256,512]{1,0:T(8,128)(2,1)}, f32[256,512]{1,0:T(8,128)S(1)}, f32[256,512]{1,0:T(8,128)S(1)}) custom-call(bf16[256,512]{1,0:T(8,128)(2,1)S(1)} %copy-done.2, bf16[256,512]{1,0:T(8,128)(2,1)S(1)} %copy-done, bf16[256,512]{1,0:T(8,128)(2,1)S(1)} %copy-done.1, ...), custom_call_target="tpu_custom_call" | custom-call | flops 301989888 | bytes 3803136 | tf_op jit(solution)/shard_map/pallas_call | solution.py:52
  39.0 0.4 collective-permute-start.19
  39.4 1.8 %collective-permute-start.20 = (bf16[128,128]{1,0:T(8,128)(2,1)S(1)}, bf16[128,128]{1,0:T(8,128)(2,1)S(1)}, u32[]{:S(2)}, u32[]{:S(2)}) collective-permute-start(bf16[128,128]{1,0:T(8,128)(2,1)S(1)} %get-tuple-element.53), channel_id=1, source_target_pairs={{0,5},{1,2},{2,7},{3,0},{4,1},{5,6},{6,3},{7,4},{8,13},{9,10},{10,... | collective-permute-start | bytes 98312 | tf_op jit(solution)/shard_map/ppermute | solution.py:193
  41.3 0.9 %collective-permute-start.22 = (bf16[128,128]{1,0:T(8,128)(2,1)S(1)}, bf16[128,128]{1,0:T(8,128)(2,1)S(1)}, u32[]{:S(2)}, u32[]{:S(2)}) collective-permute-start(bf16[128,128]{1,0:T(8,128)(2,1)S(1)} %get-tuple-element.55), channel_id=1, source_target_pairs={{0,1},{1,0},{2,3},{3,2},{4,5},{5,4},{6,7},{7,6},{8,9},{9,8},{10,11... | collective-permute-start | bytes 98312 | tf_op jit(solution)/shard_map/ppermute | solution.py:193
  42.2 1.1 %collective-permute-done.19.p0 = bf16[128,128]{1,0:T(8,128)(2,1)S(1)} collective-permute-done((bf16[128,128]{1,0:T(8,128)(2,1)S(1)}, bf16[128,128]{1,0:T(8,128)(2,1)S(1)}, u32[]{:S(2)}, u32[]{:S(2)}) %collective-permute-start.19) | collective-permute-done | bytes 32800 | tf_op jit(solution)/shard_map/ppermute | solution.py:193
  43.3 1.2 %collective-permute-done.21.p2 = bf16[128,128]{1,0:T(8,128)(2,1)S(1)} collective-permute-done((bf16[128,128]{1,0:T(8,128)(2,1)S(1)}, bf16[128,128]{1,0:T(8,128)(2,1)S(1)}, u32[]{:S(2)}, u32[]{:S(2)}) %collective-permute-start.21) | collective-permute-done | bytes 32800 | tf_op jit(solution)/shard_map/ppermute | solution.py:193
  44.5 1.1 %shard_map.82 = (bf16[256,512]{1,0:T(8,128)(2,1)}, bf16[256,512]{1,0:T(8,128)(2,1)}) custom-call(bf16[256,512]{1,0:T(8,128)(2,1)S(1)} %copy-done, bf16[256,512]{1,0:T(8,128)(2,1)S(1)} %copy-done.1, f32[256,512]{1,0:T(8,128)S(1)} %get-tuple-element.46.refs_7_.key_local, f32[256,512]{1,0:T(8,128)S(1)} %get-tuple-element.47.value_local, ...), custom_call_target="tpu_custom_call" | custom-call | flops 67108864 | bytes 2228224 | tf_op jit(solution)/shard_map/pallas_call | solution.py:52
  (33 shorter events, 2.8 us)
Async XLA Ops:
  0.6 21.2 %copy-start.1 = (bf16[256,512]{1,0:T(8,128)(2,1)S(1)}, bf16[256,512]{1,0:T(8,128)(2,1)}, u32[]{:S(2)}) copy-start(bf16[256,512]{1,0:T(8,128)(2,1)} %v_ref.7) | copy-start | bytes 786436
  0.6 21.2 %copy-start.2 = (bf16[256,512]{1,0:T(8,128)(2,1)S(1)}, bf16[256,512]{1,0:T(8,128)(2,1)}, u32[]{:S(2)}) copy-start(bf16[256,512]{1,0:T(8,128)(2,1)} %q_ref.7) | copy-start | bytes 786436
  2.1 19.7 %copy-start = (bf16[256,512]{1,0:T(8,128)(2,1)S(1)}, bf16[256,512]{1,0:T(8,128)(2,1)}, u32[]{:S(2)}) copy-start(bf16[256,512]{1,0:T(8,128)(2,1)} %k_ref.7) | copy-start | bytes 786436
  2.1 5.8 %collective-permute-start = (bf16[128,128]{1,0:T(8,128)(2,1)S(1)}, bf16[128,128]{1,0:T(8,128)(2,1)S(1)}, u32[]{:S(2)}, u32[]{:S(2)}) collective-permute-start(bf16[128,128]{1,0:T(8,128)(2,1)S(1)} %get-tuple-element.32), channel_id=1, source_target_pairs={{0,7},{1,6},{2,5},{3,4},{4,3},{5,2},{6,1},{7,0},{8,15},{9,14},{10,... | collective-permute-start | bytes 98312 | tf_op jit(solution)/shard_map/ppermute | solution.py:193
  5.5 3.3 %collective-permute-start.1 = (bf16[128,128]{1,0:T(8,128)(2,1)S(1)}, bf16[128,128]{1,0:T(8,128)(2,1)S(1)}, u32[]{:S(2)}, u32[]{:S(2)}) collective-permute-start(bf16[128,128]{1,0:T(8,128)(2,1)S(1)} %get-tuple-element.33), channel_id=1, source_target_pairs={{0,5},{1,2},{2,7},{3,0},{4,1},{5,6},{6,3},{7,4},{8,13},{9,10},{10,... | collective-permute-start | bytes 98312 | tf_op jit(solution)/shard_map/ppermute | solution.py:193
  6.3 3.6 %collective-permute-start.2 = (bf16[128,128]{1,0:T(8,128)(2,1)S(1)}, bf16[128,128]{1,0:T(8,128)(2,1)S(1)}, u32[]{:S(2)}, u32[]{:S(2)}) collective-permute-start(bf16[128,128]{1,0:T(8,128)(2,1)S(1)} %get-tuple-element.34), channel_id=1, source_target_pairs={{0,3},{1,4},{2,1},{3,6},{4,7},{5,0},{6,5},{7,2},{8,11},{9,12},{10,... | collective-permute-start | bytes 98312 | tf_op jit(solution)/shard_map/ppermute | solution.py:193
  7.3 2.7 %collective-permute-start.3 = (bf16[128,128]{1,0:T(8,128)(2,1)S(1)}, bf16[128,128]{1,0:T(8,128)(2,1)S(1)}, u32[]{:S(2)}, u32[]{:S(2)}) collective-permute-start(bf16[128,128]{1,0:T(8,128)(2,1)S(1)} %get-tuple-element.35), channel_id=1, source_target_pairs={{0,1},{1,0},{2,3},{3,2},{4,5},{5,4},{6,7},{7,6},{8,9},{9,8},{10,11... | collective-permute-start | bytes 98312 | tf_op jit(solution)/shard_map/ppermute | solution.py:193
  10.0 5.3 %collective-permute-start.4 = (bf16[128,128]{1,0:T(8,128)(2,1)S(1)}, bf16[128,128]{1,0:T(8,128)(2,1)S(1)}, u32[]{:S(2)}, u32[]{:S(2)}) collective-permute-start(bf16[128,128]{1,0:T(8,128)(2,1)S(1)} %add_convert_fusion.1), channel_id=1, source_target_pairs={{0,24},{2,26},{4,28},{6,30},{8,16},{10,18},{12,20},{14,22},{16,0},... | collective-permute-start | bytes 98312 | tf_op jit(solution)/shard_map/ppermute | solution.py:204
  13.6 4.8 %collective-permute-start.5 = (bf16[128,128]{1,0:T(8,128)(2,1)S(1)}, bf16[128,128]{1,0:T(8,128)(2,1)S(1)}, u32[]{:S(2)}, u32[]{:S(2)}) collective-permute-start(bf16[128,128]{1,0:T(8,128)(2,1)S(1)} %add_convert_fusion.1), channel_id=1, source_target_pairs={{0,16},{2,18},{4,20},{6,22},{8,24},{10,26},{12,28},{14,30},{16,0},... | collective-permute-start | bytes 98312 | tf_op jit(solution)/shard_map/ppermute | solution.py:204
  13.6 4.8 %collective-permute-start.6 = (bf16[128,128]{1,0:T(8,128)(2,1)S(1)}, bf16[128,128]{1,0:T(8,128)(2,1)S(1)}, u32[]{:S(2)}, u32[]{:S(2)}) collective-permute-start(bf16[128,128]{1,0:T(8,128)(2,1)S(1)} %add_convert_fusion.1), channel_id=1, source_target_pairs={{0,8},{2,10},{4,12},{6,14},{8,0},{10,2},{12,4},{14,6},{16,24},{18,... | collective-permute-start | bytes 98312 | tf_op jit(solution)/shard_map/ppermute | solution.py:204
  18.5 4.3 %collective-permute-start.7 = (bf16[128,128]{1,0:T(8,128)(2,1)S(1)}, bf16[128,128]{1,0:T(8,128)(2,1)S(1)}, u32[]{:S(2)}, u32[]{:S(2)}) collective-permute-start(bf16[128,128]{1,0:T(8,128)(2,1)S(1)} %get-tuple-element.36), channel_id=1, source_target_pairs={{0,7},{1,6},{2,5},{3,4},{4,3},{5,2},{6,1},{7,0},{8,15},{9,14},{10,... | collective-permute-start | bytes 98312 | tf_op jit(solution)/shard_map/ppermute | solution.py:193
  18.6 4.4 %collective-permute-start.8 = (bf16[128,128]{1,0:T(8,128)(2,1)S(1)}, bf16[128,128]{1,0:T(8,128)(2,1)S(1)}, u32[]{:S(2)}, u32[]{:S(2)}) collective-permute-start(bf16[128,128]{1,0:T(8,128)(2,1)S(1)} %get-tuple-element.37), channel_id=1, source_target_pairs={{0,5},{1,2},{2,7},{3,0},{4,1},{5,6},{6,3},{7,4},{8,13},{9,10},{10,... | collective-permute-start | bytes 98312 | tf_op jit(solution)/shard_map/ppermute | solution.py:193
  20.3 3.6 %collective-permute-start.9 = (bf16[128,128]{1,0:T(8,128)(2,1)S(1)}, bf16[128,128]{1,0:T(8,128)(2,1)S(1)}, u32[]{:S(2)}, u32[]{:S(2)}) collective-permute-start(bf16[128,128]{1,0:T(8,128)(2,1)S(1)} %get-tuple-element.38), channel_id=1, source_target_pairs={{0,3},{1,4},{2,1},{3,6},{4,7},{5,0},{6,5},{7,2},{8,11},{9,12},{10,... | collective-permute-start | bytes 98312 | tf_op jit(solution)/shard_map/ppermute | solution.py:193
  21.0 2.9 %copy-start.3 = (bf16[256,512]{1,0:T(8,128)(2,1)S(1)}, bf16[256,512]{1,0:T(8,128)(2,1)}, u32[]{:S(2)}) copy-start(bf16[256,512]{1,0:T(8,128)(2,1)} %c_ref.3) | copy-start | bytes 786436
  21.0 2.9 %collective-permute-start.10 = (bf16[128,128]{1,0:T(8,128)(2,1)S(1)}, bf16[128,128]{1,0:T(8,128)(2,1)S(1)}, u32[]{:S(2)}, u32[]{:S(2)}) collective-permute-start(bf16[128,128]{1,0:T(8,128)(2,1)S(1)} %get-tuple-element.39), channel_id=1, source_target_pairs={{0,1},{1,0},{2,3},{3,2},{4,5},{5,4},{6,7},{7,6},{8,9},{9,8},{10,11... | collective-permute-start | bytes 98312 | tf_op jit(solution)/shard_map/ppermute | solution.py:193
  24.3 1.2 %collective-permute-start.11 = (f32[2,256]{1,0:T(2,128)S(1)}, f32[2,256]{1,0:T(2,128)S(1)}, u32[]{:S(2)}, u32[]{:S(2)}) collective-permute-start(f32[2,256]{1,0:T(2,128)S(1)} %get-tuple-element.41), channel_id=1, source_target_pairs={{0,1},{1,0},{2,3},{3,2},{4,5},{5,4},{6,7},{7,6},{8,9},{9,8},{10,11... | collective-permute-start | bytes 6152 | tf_op jit(solution)/shard_map/ppermute | solution.py:185
  26.0 4.3 %collective-permute-start.12 = (bf16[128,128]{1,0:T(8,128)(2,1)S(1)}, bf16[128,128]{1,0:T(8,128)(2,1)S(1)}, u32[]{:S(2)}, u32[]{:S(2)}) collective-permute-start(bf16[128,128]{1,0:T(8,128)(2,1)S(1)} %get-tuple-element.48), channel_id=1, source_target_pairs={{0,7},{1,6},{2,5},{3,4},{4,3},{5,2},{6,1},{7,0},{8,15},{9,14},{10,... | collective-permute-start | bytes 98312 | tf_op jit(solution)/shard_map/ppermute | solution.py:193
  27.7 3.3 %collective-permute-start.13 = (bf16[128,128]{1,0:T(8,128)(2,1)S(1)}, bf16[128,128]{1,0:T(8,128)(2,1)S(1)}, u32[]{:S(2)}, u32[]{:S(2)}) collective-permute-start(bf16[128,128]{1,0:T(8,128)(2,1)S(1)} %get-tuple-element.49), channel_id=1, source_target_pairs={{0,5},{1,2},{2,7},{3,0},{4,1},{5,6},{6,3},{7,4},{8,13},{9,10},{10,... | collective-permute-start | bytes 98312 | tf_op jit(solution)/shard_map/ppermute | solution.py:193
  28.6 3.3 %collective-permute-start.14 = (bf16[128,128]{1,0:T(8,128)(2,1)S(1)}, bf16[128,128]{1,0:T(8,128)(2,1)S(1)}, u32[]{:S(2)}, u32[]{:S(2)}) collective-permute-start(bf16[128,128]{1,0:T(8,128)(2,1)S(1)} %get-tuple-element.50), channel_id=1, source_target_pairs={{0,3},{1,4},{2,1},{3,6},{4,7},{5,0},{6,5},{7,2},{8,11},{9,12},{10,... | collective-permute-start | bytes 98312 | tf_op jit(solution)/shard_map/ppermute | solution.py:193
  29.5 2.5 %collective-permute-start.15 = (bf16[128,128]{1,0:T(8,128)(2,1)S(1)}, bf16[128,128]{1,0:T(8,128)(2,1)S(1)}, u32[]{:S(2)}, u32[]{:S(2)}) collective-permute-start(bf16[128,128]{1,0:T(8,128)(2,1)S(1)} %get-tuple-element.51), channel_id=1, source_target_pairs={{0,1},{1,0},{2,3},{3,2},{4,5},{5,4},{6,7},{7,6},{8,9},{9,8},{10,11... | collective-permute-start | bytes 98312 | tf_op jit(solution)/shard_map/ppermute | solution.py:193
  32.0 6.5 %collective-permute-start.16 = (bf16[128,128]{1,0:T(8,128)(2,1)S(1)}, bf16[128,128]{1,0:T(8,128)(2,1)S(1)}, u32[]{:S(2)}, u32[]{:S(2)}) collective-permute-start(bf16[128,128]{1,0:T(8,128)(2,1)S(1)} %add_convert_fusion), channel_id=1, source_target_pairs={{0,16},{2,18},{4,20},{6,22},{8,24},{10,26},{12,28},{14,30},{16,8},... | collective-permute-start | bytes 98312 | tf_op jit(solution)/shard_map/ppermute | solution.py:204
  34.1 4.8 %collective-permute-start.17 = (bf16[128,128]{1,0:T(8,128)(2,1)S(1)}, bf16[128,128]{1,0:T(8,128)(2,1)S(1)}, u32[]{:S(2)}, u32[]{:S(2)}) collective-permute-start(bf16[128,128]{1,0:T(8,128)(2,1)S(1)} %add_convert_fusion), channel_id=1, source_target_pairs={{0,16},{2,18},{4,20},{6,22},{8,24},{10,26},{12,28},{14,30},{16,0},... | collective-permute-start | bytes 98312 | tf_op jit(solution)/shard_map/ppermute | solution.py:204
  34.1 4.7 %collective-permute-start.18 = (bf16[128,128]{1,0:T(8,128)(2,1)S(1)}, bf16[128,128]{1,0:T(8,128)(2,1)S(1)}, u32[]{:S(2)}, u32[]{:S(2)}) collective-permute-start(bf16[128,128]{1,0:T(8,128)(2,1)S(1)} %add_convert_fusion), channel_id=1, source_target_pairs={{0,8},{2,10},{4,12},{6,14},{8,0},{10,2},{12,4},{14,6},{16,24},{18,... | collective-permute-start | bytes 98312 | tf_op jit(solution)/shard_map/ppermute | solution.py:204
  39.0 4.3 %collective-permute-start.19 = (bf16[128,128]{1,0:T(8,128)(2,1)S(1)}, bf16[128,128]{1,0:T(8,128)(2,1)S(1)}, u32[]{:S(2)}, u32[]{:S(2)}) collective-permute-start(bf16[128,128]{1,0:T(8,128)(2,1)S(1)} %get-tuple-element.52), channel_id=1, source_target_pairs={{0,7},{1,6},{2,5},{3,4},{4,3},{5,2},{6,1},{7,0},{8,15},{9,14},{10,... | collective-permute-start | bytes 98312 | tf_op jit(solution)/shard_map/ppermute | solution.py:193
  39.4 3.9 %collective-permute-start.20 = (bf16[128,128]{1,0:T(8,128)(2,1)S(1)}, bf16[128,128]{1,0:T(8,128)(2,1)S(1)}, u32[]{:S(2)}, u32[]{:S(2)}) collective-permute-start(bf16[128,128]{1,0:T(8,128)(2,1)S(1)} %get-tuple-element.53), channel_id=1, source_target_pairs={{0,5},{1,2},{2,7},{3,0},{4,1},{5,6},{6,3},{7,4},{8,13},{9,10},{10,... | collective-permute-start | bytes 98312 | tf_op jit(solution)/shard_map/ppermute | solution.py:193
  41.2 3.3 %collective-permute-start.21 = (bf16[128,128]{1,0:T(8,128)(2,1)S(1)}, bf16[128,128]{1,0:T(8,128)(2,1)S(1)}, u32[]{:S(2)}, u32[]{:S(2)}) collective-permute-start(bf16[128,128]{1,0:T(8,128)(2,1)S(1)} %get-tuple-element.54), channel_id=1, source_target_pairs={{0,3},{1,4},{2,1},{3,6},{4,7},{5,0},{6,5},{7,2},{8,11},{9,12},{10,... | collective-permute-start | bytes 98312 | tf_op jit(solution)/shard_map/ppermute | solution.py:193
  41.3 3.2 %collective-permute-start.22 = (bf16[128,128]{1,0:T(8,128)(2,1)S(1)}, bf16[128,128]{1,0:T(8,128)(2,1)S(1)}, u32[]{:S(2)}, u32[]{:S(2)}) collective-permute-start(bf16[128,128]{1,0:T(8,128)(2,1)S(1)} %get-tuple-element.55), channel_id=1, source_target_pairs={{0,1},{1,0},{2,3},{3,2},{4,5},{5,4},{6,7},{7,6},{8,9},{9,8},{10,11... | collective-permute-start | bytes 98312 | tf_op jit(solution)/shard_map/ppermute | solution.py:193

commit v7 on v6

--- a/solution.py
+++ b/solution.py
@@ -11,6 +11,7 @@
 EPSILON = 1e-06
 QUAD = 4
 OPS = (0, 1, 2, 3)
+BACK = (3, 2, 1, 0)
 CHUNKS = 4
 LOW, WIDE = jnp.bfloat16, jnp.float32
 
@@ -40,11 +41,6 @@
 def sent(op):
     odd = lax.axis_index("tp") % 2
     return (3, 2 - odd, 1 + odd, 0)[op]
-
-
-def came(op):
-    odd = lax.axis_index("tp") % 2
-    return (3, 1 + odd, 2 - odd, 0)[op]
 
 
 def call(kernel, outs, args, flops, in_specs=None, out_specs=None, scratch_shapes=(), room=32):
@@ -91,13 +87,13 @@
         fixed(mixed_ref, h)[...] = dot(scores, fixed(v_ref, h)[...], ((1,), (0,)))
 
 
-def mixed_kernel(local_ref, q_ref, c_ref, p0, p1, p2, p3, mixed_ref, sums_ref):
+def mixed_kernel(local_ref, q_ref, c_ref, p3, p2, p1, p0, mixed_ref, sums_ref):
     m = member_of_quad()
     count = q_ref.shape[0]
     square = jnp.zeros((count, DH), WIDE)
     product = jnp.zeros((count, DH), WIDE)
-    for op, p_ref in enumerate((p0, p1, p2, p3)):
-        h = m ^ came(op)
+    for d, p_ref in zip(BACK, (p3, p2, p1, p0)):
+        h = m ^ d
         mixed = head(local_ref, h)[...] + dot(head(q_ref, h)[...], p_ref[...], ((1,), (0,)))
         head(mixed_ref, h)[...] = mixed
         square = square + mixed * mixed
@@ -125,14 +121,14 @@
         out[...] = dot(head(q_ref, h)[...], grad, ((0,), (0,))).astype(LOW)
 
 
-def back_kernel(features, q_ref, k_ref, v_ref, g_ref, scores_ref, mixed_ref, sums_ref, p0, p1, p2, p3,
+def back_kernel(features, q_ref, k_ref, v_ref, g_ref, scores_ref, mixed_ref, sums_ref, p3, p2, p1, p0,
                 normed_ref, query_ref, key_ref, value_ref):
     m = member_of_quad()
     count = q_ref.shape[0]
     mask = causal_mask(count)
     inverse, _ = token_scales(sums_ref, features, count)
-    for op, p_ref in enumerate((p0, p1, p2, p3)):
-        h = m ^ came(op)
+    for d, p_ref in zip(BACK, (p3, p2, p1, p0)):
+        h = m ^ d
         grad = head(g_ref, h)[...]
         head(normed_ref, h)[...] = (head(mixed_ref, h)[...] * inverse).astype(LOW)
         raw = dot(grad, head(v_ref, h)[...], ((1,), (1,)))
@@ -143,10 +139,10 @@
         head(value_ref, h)[...] = dot(scores_ref[h], grad, ((0,), (0,)))
 
 
-def last_kernel(k_ref, v_ref, key_local, value_local, p0, p1, p2, p3, key_ref, value_ref):
-    m = member_of_quad()
-    for op, p_ref in enumerate((p0, p1, p2, p3)):
-        h = m ^ came(op)
+def last_kernel(k_ref, v_ref, key_local, value_local, p3, p2, p1, p0, key_ref, value_ref):
+    m = member_of_quad()
+    for d, p_ref in zip(BACK, (p3, p2, p1, p0)):
+        h = m ^ d
         suffix = p_ref[...]
         key = head(key_local, h)[...] + dot(head(v_ref, h)[...], suffix, ((1,), (1,)))
         head(key_ref, h)[...] = key.astype(LOW)
@@ -164,7 +160,7 @@
 def sums_kernel(before, quads, *refs):
     index = lax.axis_index("seq")
     m, quad = index % QUAD, index // QUAD
-    held, got, outs = refs[:QUAD], refs[QUAD : QUAD + quads - 1], refs[-QUAD:]
+    got, held, outs = refs[: quads - 1], refs[quads - 1], refs[-QUAD:]
 
     def counts(a, b):
         return jnp.where(a < b if before else a > b, 1.0, 0.0).astype(WIDE)
@@ -172,12 +168,21 @@
     outer = jnp.zeros((DH, DH), WIDE)
     for step, total in zip(range(quads - 1, 0, -1), got):
         outer = outer + total[...].astype(WIDE) * counts(quad ^ step, quad)
-    pieces = [piece[...].astype(WIDE) for piece in held]
-    for to in OPS:
+    pieces = [held[op].astype(WIDE) for op in OPS]
+    for out, to in zip(outs, BACK):
         inner = outer
         for op in OPS:
-            inner = inner + pieces[op] * counts(m ^ came(op), m ^ sent(to))
-        outs[to][...] = inner.astype(LOW)
+            inner = inner + pieces[op] * counts(m ^ sent(op), m ^ to)
+        out[...] = inner.astype(LOW)
+
+
+def total_kernel(*refs):
+    total_ref, stack_ref = refs[QUAD:]
+    total = jnp.zeros((DH, DH), WIDE)
+    for n, ref in enumerate(refs[:QUAD]):
+        stack_ref[n] = ref[...]
+        total = total + ref[...].astype(WIDE)
+    total_ref[...] = total.astype(LOW)
 
 
 def exchange(value, axis, bits):
@@ -195,22 +200,24 @@
 
 def exclusive_sum(held, before, *after):
     held = [cross(held[op], op) for op in OPS]
-    total = sum(piece.astype(WIDE) for piece in held).astype(LOW)
-    quads = lax.axis_size("seq") // QUAD
+    state = jax.ShapeDtypeStruct((DH, DH), LOW)
+    total, held = call(total_kernel, [state, jax.ShapeDtypeStruct((QUAD, DH, DH), LOW)], held, 0)
+    quads, cores = lax.axis_size("seq") // QUAD, lax.axis_size("tp")
     got = []
     for step in range(quads - 1, 0, -1):
         targets = quad_targets(quads, step, before)
-        pairs = [(z * QUAD + i, targets[z] * QUAD + i) for z in range(quads) for i in range(QUAD)]
-        got.append(lax.ppermute(total, "seq", pairs))
-    vmem = [pl.BlockSpec(memory_space=pltpu.VMEM)] * (QUAD + len(got))
+        places = [(z, i, t) for z in range(quads) for i in range(QUAD) for t in range(cores)]
+        pairs = [((z * QUAD + i) * cores + t, (targets[z] * QUAD + i) * cores + (t ^ 1)) for z, i, t in places]
+        got.append(lax.ppermute(total, ("seq", "tp"), pairs))
+    held = exchange(held, "tp", 1)
     sums = call(
         functools.partial(sums_kernel, before, quads),
-        [jax.ShapeDtypeStruct(x.shape, x.dtype) for x in held],
-        (*held, *got, *after),
+        [state] * QUAD,
+        (*got, held, *after),
         0,
-        in_specs=vmem + [pl.BlockSpec(memory_space=pl.ANY)] * len(after),
-    )
-    return [cross(sums[op], op) for op in OPS]
+        in_specs=[pl.BlockSpec(memory_space=pltpu.VMEM)] * quads + [pl.BlockSpec(memory_space=pl.ANY)] * len(after),
+    )
+    return [exchange(x, "seq", d) for x, d in zip(sums, BACK) if d] + [sums[-1]]
 
 
 def sum_over_heads(value):

time: 45.8 us -> 47.5 us (1.037)
  waiting for transfers between devices: 13.4 us -> 14.6 us
  starting transfers between devices: 25.2 us -> 25.7 us
    ppermute x1 -> x9, starting transfers between devices: 0.08 us -> 7.54 us  [exchange(): return lax.ppermute(value, axis, [(i, i ^ bits) for i in range(size)])]
    ppermute x16 -> x8, starting transfers between devices: 16.1 us -> 9.84 us  [cross(): return lax.ppermute(value, ('seq', 'tp'), pairs)]
    ppermute x1 -> x9, waiting for transfers between devices: 1.14 us -> 5.94 us  [exchange(): return lax.ppermute(value, axis, [(i, i ^ bits) for i in range(size)])]
    ppermute x16 -> x8, waiting for transfers between devices: 7.88 us -> 4.11 us  [cross(): return lax.ppermute(value, ('seq', 'tp'), pairs)]
    ppermute x6, starting transfers between devices: 8.99 us -> 8.32 us  [exclusive_sum(): got.append(lax.ppermute(total, ('seq', 'tp'), pairs))]
    pallas_call x8 -> x10, Pallas kernels: 6.25 us -> 6.29 us  [call(): pl.pallas_call(kernel, out_shape=outs, in_specs=in_specs or [pl.BlockSpec...]
  transfers between devices with their start and end apart: 23 -> 23, of which waited for: 14 -> 15; matrix products, arithmetic and copies ran while one was open for 0% -> 0% of each run, Pallas kernels for 6% -> 6%
where the time goes in v7:
time: 47.5 us; the launch traced here: 47.3 us
  starting transfers between devices  25.7 us (54%)
  waiting for transfers between devices  14.6 us (31%)
  Pallas kernels  6.29 us (13%)
  between operations  0.73 us (2%)
    ppermute x8, starting transfers between devices, cross(): return lax.ppermute(value, ('seq', 'tp'), pairs)  9.84 us
    ppermute x6, starting transfers between devices, exclusive_sum(): got.append(lax.ppermute(total, ('seq', 'tp'), pairs))  8.32 us
    ppermute x9, starting transfers between devices, exchange(): return lax.ppermute(value, axis, [(i, i ^ bits) for i in range(size)])  7.54 us
    pallas_call x10, Pallas kernels, call(): pl.pallas_call(kernel, out_shape=outs, in_specs=in_specs or [pl.BlockSpec...  6.29 us
    ppermute x9, waiting for transfers between devices, exchange(): return lax.ppermute(value, axis, [(i, i ^ bits) for i in range(size)])  5.94 us
    ppermute x6, waiting for transfers between devices, exclusive_sum(): got.append(lax.ppermute(total, ('seq', 'tp'), pairs))  4.54 us
    ppermute x8, waiting for transfers between devices, cross(): return lax.ppermute(value, ('seq', 'tp'), pairs)  4.11 us
  transfers between devices with their start and end apart: 23, of which 15 were waited for; matrix products, arithmetic and copies ran while one was open for 0% of the time, Pallas kernels for 6%

profile of v7, /device:TPU:0, one launch (start us, length us, event | category | flops | bytes accessed | tf_op | source)
XLA Modules:
  0.0 47.3 jit_solution(16002439873457994328)
XLA Ops:
  0.7 1.4 %shard_map.76 = (bf16[128,128]{1,0:T(8,128)(2,1)S(1)}, bf16[128,128]{1,0:T(8,128)(2,1)S(1)}, bf16[128,128]{1,0:T(8,128)(2,1)S(1)}, bf16[128,128]{1,0:T(8,128)(2,1)S(1)}) custom-call(bf16[256,512]{1,0:T(8,128)(2,1)} %k_ref.7, bf16[256,512]{1,0:T(8,128)(2,1)} %v_ref.7), custom_call_target="tpu_custom_call" | custom-call | flops 33554432 | bytes 655360 | tf_op jit(solution)/shard_map/pallas_call | solution.py:48
  2.1 3.4 %collective-permute-start = (bf16[128,128]{1,0:T(8,128)(2,1)S(1)}, bf16[128,128]{1,0:T(8,128)(2,1)S(1)}, u32[]{:S(2)}, u32[]{:S(2)}) collective-permute-start(bf16[128,128]{1,0:T(8,128)(2,1)S(1)} %get-tuple-element.36), channel_id=1, source_target_pairs={{0,7},{1,6},{2,5},{3,4},{4,3},{5,2},{6,1},{7,0},{8,15},{9,14},{10,... | collective-permute-start | bytes 98312 | tf_op jit(solution)/shard_map/ppermute | solution.py:198
  5.5 0.8 %collective-permute-start.1 = (bf16[128,128]{1,0:T(8,128)(2,1)S(1)}, bf16[128,128]{1,0:T(8,128)(2,1)S(1)}, u32[]{:S(2)}, u32[]{:S(2)}) collective-permute-start(bf16[128,128]{1,0:T(8,128)(2,1)S(1)} %get-tuple-element.37), channel_id=1, source_target_pairs={{0,5},{1,2},{2,7},{3,0},{4,1},{5,6},{6,3},{7,4},{8,13},{9,10},{10,... | collective-permute-start | bytes 98312 | tf_op jit(solution)/shard_map/ppermute | solution.py:198
  6.3 1.0 %collective-permute-start.2 = (bf16[128,128]{1,0:T(8,128)(2,1)S(1)}, bf16[128,128]{1,0:T(8,128)(2,1)S(1)}, u32[]{:S(2)}, u32[]{:S(2)}) collective-permute-start(bf16[128,128]{1,0:T(8,128)(2,1)S(1)} %get-tuple-element.38), channel_id=1, source_target_pairs={{0,3},{1,4},{2,1},{3,6},{4,7},{5,0},{6,5},{7,2},{8,11},{9,12},{10,... | collective-permute-start | bytes 98312 | tf_op jit(solution)/shard_map/ppermute | solution.py:198
  7.3 0.7 %collective-permute-start.3 = (bf16[128,128]{1,0:T(8,128)(2,1)S(1)}, bf16[128,128]{1,0:T(8,128)(2,1)S(1)}, u32[]{:S(2)}, u32[]{:S(2)}) collective-permute-start(bf16[128,128]{1,0:T(8,128)(2,1)S(1)} %get-tuple-element.39), channel_id=1, source_target_pairs={{0,1},{1,0},{2,3},{3,2},{4,5},{5,4},{6,7},{7,6},{8,9},{9,8},{10,11... | collective-permute-start | bytes 98312 | tf_op jit(solution)/shard_map/ppermute | solution.py:198
  7.9 0.9 %collective-permute-done.1.refs_1_ = bf16[128,128]{1,0:T(8,128)(2,1)S(1)} collective-permute-done((bf16[128,128]{1,0:T(8,128)(2,1)S(1)}, bf16[128,128]{1,0:T(8,128)(2,1)S(1)}, u32[]{:S(2)}, u32[]{:S(2)}) %collective-permute-start.1) | collective-permute-done | bytes 32800 | tf_op jit(solution)/shard_map/ppermute | solution.py:198
  8.9 1.1 %collective-permute-done.2.refs_2_ = bf16[128,128]{1,0:T(8,128)(2,1)S(1)} collective-permute-done((bf16[128,128]{1,0:T(8,128)(2,1)S(1)}, bf16[128,128]{1,0:T(8,128)(2,1)S(1)}, u32[]{:S(2)}, u32[]{:S(2)}) %collective-permute-start.2) | collective-permute-done | bytes 32800 | tf_op jit(solution)/shard_map/ppermute | solution.py:198
  10.1 3.6 %collective-permute-start.4 = (bf16[128,128]{1,0:T(8,128)(2,1)S(1)}, bf16[128,128]{1,0:T(8,128)(2,1)S(1)}, u32[]{:S(2)}, u32[]{:S(2)}) collective-permute-start(bf16[128,128]{1,0:T(8,128)(2,1)S(1)} %get-tuple-element.40), channel_id=1, source_target_pairs={{0,25},{1,24},{2,27},{3,26},{4,29},{5,28},{6,31},{7,30},{8,17},{9,... | collective-permute-start | bytes 98312 | tf_op jit(solution)/shard_map/ppermute | solution.py:211
  14.4 1.1 %collective-permute-done.4.refs_0_ = bf16[128,128]{1,0:T(8,128)(2,1)S(1)} collective-permute-done((bf16[128,128]{1,0:T(8,128)(2,1)S(1)}, bf16[128,128]{1,0:T(8,128)(2,1)S(1)}, u32[]{:S(2)}, u32[]{:S(2)}) %collective-permute-start.4) | collective-permute-done | bytes 32800 | tf_op jit(solution)/shard_map/ppermute | solution.py:211
  15.5 2.5 %collective-permute-done.5.refs_1_ = bf16[128,128]{1,0:T(8,128)(2,1)S(1)} collective-permute-done((bf16[128,128]{1,0:T(8,128)(2,1)S(1)}, bf16[128,128]{1,0:T(8,128)(2,1)S(1)}, u32[]{:S(2)}, u32[]{:S(2)}) %collective-permute-start.5) | collective-permute-done | bytes 32800 | tf_op jit(solution)/shard_map/ppermute | solution.py:211
  18.1 1.5 %collective-permute-start.8 = (bf16[128,128]{1,0:T(8,128)(2,1)S(1)}, bf16[128,128]{1,0:T(8,128)(2,1)S(1)}, u32[]{:S(2)}, u32[]{:S(2)}) collective-permute-start(bf16[128,128]{1,0:T(8,128)(2,1)S(1)} %get-tuple-element.42), channel_id=1, source_target_pairs={{0,6},{2,4},{4,2},{6,0},{8,14},{10,12},{12,10},{14,8},{16,22},{18,... | collective-permute-start | bytes 98312 | tf_op jit(solution)/shard_map/ppermute | solution.py:190
  19.6 0.8 %collective-permute-start.9 = (bf16[128,128]{1,0:T(8,128)(2,1)S(1)}, bf16[128,128]{1,0:T(8,128)(2,1)S(1)}, u32[]{:S(2)}, u32[]{:S(2)}) collective-permute-start(bf16[128,128]{1,0:T(8,128)(2,1)S(1)} %get-tuple-element.43), channel_id=1, source_target_pairs={{0,4},{2,6},{4,0},{6,2},{8,12},{10,14},{12,8},{14,10},{16,20},{18,... | collective-permute-start | bytes 98312 | tf_op jit(solution)/shard_map/ppermute | solution.py:190
  20.4 1.3 %collective-permute-start.10 = (bf16[128,128]{1,0:T(8,128)(2,1)S(1)}, bf16[128,128]{1,0:T(8,128)(2,1)S(1)}, u32[]{:S(2)}, u32[]{:S(2)}) collective-permute-start(bf16[128,128]{1,0:T(8,128)(2,1)S(1)} %get-tuple-element.44), channel_id=1, source_target_pairs={{0,2},{2,0},{4,6},{6,4},{8,10},{10,8},{12,14},{14,12},{16,18},{18,... | collective-permute-start | bytes 98312 | tf_op jit(solution)/shard_map/ppermute | solution.py:190
  21.7 0.7 %shard_map.75 = (bf16[4,256,256]{2,1,0:T(8,128)(2,1)S(1)}, f32[256,512]{1,0:T(8,128)S(1)}) custom-call(bf16[256,512]{1,0:T(8,128)(2,1)S(1)} %copy-done.2, bf16[256,512]{1,0:T(8,128)(2,1)S(1)} %copy-done, bf16[256,512]{1,0:T(8,128)(2,1)S(1)} %copy-done.1), custom_call_target="tpu_custom_call" | custom-call | flops 134217728 | bytes 1835008 | tf_op jit(solution)/shard_map/pallas_call | solution.py:48
  22.4 0.7 %collective-permute-done.8.p3 = bf16[128,128]{1,0:T(8,128)(2,1)S(1)} collective-permute-done((bf16[128,128]{1,0:T(8,128)(2,1)S(1)}, bf16[128,128]{1,0:T(8,128)(2,1)S(1)}, u32[]{:S(2)}, u32[]{:S(2)}) %collective-permute-start.8) | collective-permute-done | bytes 32800 | tf_op jit(solution)/shard_map/ppermute | solution.py:190
  23.5 0.8 %collective-permute-done.10.p1 = bf16[128,128]{1,0:T(8,128)(2,1)S(1)} collective-permute-done((bf16[128,128]{1,0:T(8,128)(2,1)S(1)}, bf16[128,128]{1,0:T(8,128)(2,1)S(1)}, u32[]{:S(2)}, u32[]{:S(2)}) %collective-permute-start.10) | collective-permute-done | bytes 32800 | tf_op jit(solution)/shard_map/ppermute | solution.py:190
  24.7 1.1 %collective-permute-done.11 = f32[2,256]{1,0:T(2,128)S(1)} collective-permute-done((f32[2,256]{1,0:T(2,128)S(1)}, f32[2,256]{1,0:T(2,128)S(1)}, u32[]{:S(2)}, u32[]{:S(2)}) %collective-permute-start.11) | collective-permute-done | bytes 2080 | tf_op jit(solution)/shard_map/ppermute | solution.py:190
  26.3 1.9 %collective-permute-start.12 = (bf16[128,128]{1,0:T(8,128)(2,1)S(1)}, bf16[128,128]{1,0:T(8,128)(2,1)S(1)}, u32[]{:S(2)}, u32[]{:S(2)}) collective-permute-start(bf16[128,128]{1,0:T(8,128)(2,1)S(1)} %get-tuple-element.54), channel_id=1, source_target_pairs={{0,7},{1,6},{2,5},{3,4},{4,3},{5,2},{6,1},{7,0},{8,15},{9,14},{10,... | collective-permute-start | bytes 98312 | tf_op jit(solution)/shard_map/ppermute | solution.py:198
  28.3 0.6 %collective-permute-start.13 = (bf16[128,128]{1,0:T(8,128)(2,1)S(1)}, bf16[128,128]{1,0:T(8,128)(2,1)S(1)}, u32[]{:S(2)}, u32[]{:S(2)}) collective-permute-start(bf16[128,128]{1,0:T(8,128)(2,1)S(1)} %get-tuple-element.55), channel_id=1, source_target_pairs={{0,5},{1,2},{2,7},{3,0},{4,1},{5,6},{6,3},{7,4},{8,13},{9,10},{10,... | collective-permute-start | bytes 98312 | tf_op jit(solution)/shard_map/ppermute | solution.py:198
  28.9 1.1 %collective-permute-start.14 = (bf16[128,128]{1,0:T(8,128)(2,1)S(1)}, bf16[128,128]{1,0:T(8,128)(2,1)S(1)}, u32[]{:S(2)}, u32[]{:S(2)}) collective-permute-start(bf16[128,128]{1,0:T(8,128)(2,1)S(1)} %get-tuple-element.56), channel_id=1, source_target_pairs={{0,3},{1,4},{2,1},{3,6},{4,7},{5,0},{6,5},{7,2},{8,11},{9,12},{10,... | collective-permute-start | bytes 98312 | tf_op jit(solution)/shard_map/ppermute | solution.py:198
  30.6 1.0 %collective-permute-done.13.refs_1_ = bf16[128,128]{1,0:T(8,128)(2,1)S(1)} collective-permute-done((bf16[128,128]{1,0:T(8,128)(2,1)S(1)}, bf16[128,128]{1,0:T(8,128)(2,1)S(1)}, u32[]{:S(2)}, u32[]{:S(2)}) %collective-permute-start.13) | collective-permute-done | bytes 32800 | tf_op jit(solution)/shard_map/ppermute | solution.py:198
  31.6 0.9 %collective-permute-done.14.refs_2_ = bf16[128,128]{1,0:T(8,128)(2,1)S(1)} collective-permute-done((bf16[128,128]{1,0:T(8,128)(2,1)S(1)}, bf16[128,128]{1,0:T(8,128)(2,1)S(1)}, u32[]{:S(2)}, u32[]{:S(2)}) %collective-permute-start.14) | collective-permute-done | bytes 32800 | tf_op jit(solution)/shard_map/ppermute | solution.py:198
  32.7 1.6 %collective-permute-start.16 = (bf16[128,128]{1,0:T(8,128)(2,1)S(1)}, bf16[128,128]{1,0:T(8,128)(2,1)S(1)}, u32[]{:S(2)}, u32[]{:S(2)}) collective-permute-start(bf16[128,128]{1,0:T(8,128)(2,1)S(1)} %get-tuple-element.58), channel_id=1, source_target_pairs={{0,17},{1,16},{2,19},{3,18},{4,21},{5,20},{6,23},{7,22},{8,25},{9,... | collective-permute-start | bytes 98312 | tf_op jit(solution)/shard_map/ppermute | solution.py:211
  34.3 2.5 %collective-permute-start.18 = (bf16[128,128]{1,0:T(8,128)(2,1)S(1)}, bf16[128,128]{1,0:T(8,128)(2,1)S(1)}, u32[]{:S(2)}, u32[]{:S(2)}) collective-permute-start(bf16[128,128]{1,0:T(8,128)(2,1)S(1)} %get-tuple-element.58), channel_id=1, source_target_pairs={{0,9},{1,8},{2,11},{3,10},{4,13},{5,12},{6,15},{7,14},{8,1},{9,0},... | collective-permute-start | bytes 98312 | tf_op jit(solution)/shard_map/ppermute | solution.py:211
  36.8 2.0 %shard_map.81 = (bf16[256,512]{1,0:T(8,128)(2,1)}, bf16[256,512]{1,0:T(8,128)(2,1)}, f32[256,512]{1,0:T(8,128)S(1)}, f32[256,512]{1,0:T(8,128)S(1)}) custom-call(bf16[256,512]{1,0:T(8,128)(2,1)S(1)} %copy-done.2, bf16[256,512]{1,0:T(8,128)(2,1)S(1)} %copy-done, bf16[256,512]{1,0:T(8,128)(2,1)S(1)} %copy-done.1, ...), custom_call_target="tpu_custom_call" | custom-call | flops 301989888 | bytes 3803136 | tf_op jit(solution)/shard_map/pallas_call | solution.py:48
  38.8 0.9 %collective-permute-done.17.refs_1_ = bf16[128,128]{1,0:T(8,128)(2,1)S(1)} collective-permute-done((bf16[128,128]{1,0:T(8,128)(2,1)S(1)}, bf16[128,128]{1,0:T(8,128)(2,1)S(1)}, u32[]{:S(2)}, u32[]{:S(2)}) %collective-permute-start.17) | collective-permute-done | bytes 32800 | tf_op jit(solution)/shard_map/ppermute | solution.py:211
  39.8 1.3 %collective-permute-start.20 = (bf16[128,128]{1,0:T(8,128)(2,1)S(1)}, bf16[128,128]{1,0:T(8,128)(2,1)S(1)}, u32[]{:S(2)}, u32[]{:S(2)}) collective-permute-start(bf16[128,128]{1,0:T(8,128)(2,1)S(1)} %get-tuple-element.60), channel_id=1, source_target_pairs={{0,6},{2,4},{4,2},{6,0},{8,14},{10,12},{12,10},{14,8},{16,22},{18,... | collective-permute-start | bytes 98312 | tf_op jit(solution)/shard_map/ppermute | solution.py:190
  41.2 1.2 %collective-permute-start.21 = (bf16[128,128]{1,0:T(8,128)(2,1)S(1)}, bf16[128,128]{1,0:T(8,128)(2,1)S(1)}, u32[]{:S(2)}, u32[]{:S(2)}) collective-permute-start(bf16[128,128]{1,0:T(8,128)(2,1)S(1)} %get-tuple-element.61), channel_id=1, source_target_pairs={{0,4},{2,6},{4,0},{6,2},{8,12},{10,14},{12,8},{14,10},{16,20},{18,... | collective-permute-start | bytes 98312 | tf_op jit(solution)/shard_map/ppermute | solution.py:190
  42.3 1.0 %collective-permute-start.22 = (bf16[128,128]{1,0:T(8,128)(2,1)S(1)}, bf16[128,128]{1,0:T(8,128)(2,1)S(1)}, u32[]{:S(2)}, u32[]{:S(2)}) collective-permute-start(bf16[128,128]{1,0:T(8,128)(2,1)S(1)} %get-tuple-element.62), channel_id=1, source_target_pairs={{0,2},{2,0},{4,6},{6,4},{8,10},{10,8},{12,14},{14,12},{16,18},{18,... | collective-permute-start | bytes 98312 | tf_op jit(solution)/shard_map/ppermute | solution.py:190
  43.4 1.3 %collective-permute-done.20.p3 = bf16[128,128]{1,0:T(8,128)(2,1)S(1)} collective-permute-done((bf16[128,128]{1,0:T(8,128)(2,1)S(1)}, bf16[128,128]{1,0:T(8,128)(2,1)S(1)}, u32[]{:S(2)}, u32[]{:S(2)}) %collective-permute-start.20) | collective-permute-done | bytes 32800 | tf_op jit(solution)/shard_map/ppermute | solution.py:190
  45.1 1.2 %collective-permute-done.22.p1 = bf16[128,128]{1,0:T(8,128)(2,1)S(1)} collective-permute-done((bf16[128,128]{1,0:T(8,128)(2,1)S(1)}, bf16[128,128]{1,0:T(8,128)(2,1)S(1)}, u32[]{:S(2)}, u32[]{:S(2)}) %collective-permute-start.22) | collective-permute-done | bytes 32800 | tf_op jit(solution)/shard_map/ppermute | solution.py:190
  46.3 1.1 %shard_map.84 = (bf16[256,512]{1,0:T(8,128)(2,1)}, bf16[256,512]{1,0:T(8,128)(2,1)}) custom-call(bf16[256,512]{1,0:T(8,128)(2,1)S(1)} %copy-done, bf16[256,512]{1,0:T(8,128)(2,1)S(1)} %copy-done.1, f32[256,512]{1,0:T(8,128)S(1)} %get-tuple-element.52.refs_4_.key_local, f32[256,512]{1,0:T(8,128)S(1)} %get-tuple-element.53.value_local, ...), custom_call_target="tpu_custom_call" | custom-call | flops 67108864 | bytes 2228224 | tf_op jit(solution)/shard_map/pallas_call | solution.py:48
  (33 shorter events, 3.7 us)
Async XLA Ops:
  0.6 21.1 %copy-start.1 = (bf16[256,512]{1,0:T(8,128)(2,1)S(1)}, bf16[256,512]{1,0:T(8,128)(2,1)}, u32[]{:S(2)}) copy-start(bf16[256,512]{1,0:T(8,128)(2,1)} %v_ref.7) | copy-start | bytes 786436
  0.6 21.1 %copy-start.2 = (bf16[256,512]{1,0:T(8,128)(2,1)S(1)}, bf16[256,512]{1,0:T(8,128)(2,1)}, u32[]{:S(2)}) copy-start(bf16[256,512]{1,0:T(8,128)(2,1)} %q_ref.7) | copy-start | bytes 786436
  2.1 19.6 %copy-start = (bf16[256,512]{1,0:T(8,128)(2,1)S(1)}, bf16[256,512]{1,0:T(8,128)(2,1)}, u32[]{:S(2)}) copy-start(bf16[256,512]{1,0:T(8,128)(2,1)} %k_ref.7) | copy-start | bytes 786436
  2.1 5.8 %collective-permute-start = (bf16[128,128]{1,0:T(8,128)(2,1)S(1)}, bf16[128,128]{1,0:T(8,128)(2,1)S(1)}, u32[]{:S(2)}, u32[]{:S(2)}) collective-permute-start(bf16[128,128]{1,0:T(8,128)(2,1)S(1)} %get-tuple-element.36), channel_id=1, source_target_pairs={{0,7},{1,6},{2,5},{3,4},{4,3},{5,2},{6,1},{7,0},{8,15},{9,14},{10,... | collective-permute-start | bytes 98312 | tf_op jit(solution)/shard_map/ppermute | solution.py:198
  5.5 3.3 %collective-permute-start.1 = (bf16[128,128]{1,0:T(8,128)(2,1)S(1)}, bf16[128,128]{1,0:T(8,128)(2,1)S(1)}, u32[]{:S(2)}, u32[]{:S(2)}) collective-permute-start(bf16[128,128]{1,0:T(8,128)(2,1)S(1)} %get-tuple-element.37), channel_id=1, source_target_pairs={{0,5},{1,2},{2,7},{3,0},{4,1},{5,6},{6,3},{7,4},{8,13},{9,10},{10,... | collective-permute-start | bytes 98312 | tf_op jit(solution)/shard_map/ppermute | solution.py:198
  6.3 3.6 %collective-permute-start.2 = (bf16[128,128]{1,0:T(8,128)(2,1)S(1)}, bf16[128,128]{1,0:T(8,128)(2,1)S(1)}, u32[]{:S(2)}, u32[]{:S(2)}) collective-permute-start(bf16[128,128]{1,0:T(8,128)(2,1)S(1)} %get-tuple-element.38), channel_id=1, source_target_pairs={{0,3},{1,4},{2,1},{3,6},{4,7},{5,0},{6,5},{7,2},{8,11},{9,12},{10,... | collective-permute-start | bytes 98312 | tf_op jit(solution)/shard_map/ppermute | solution.py:198
  7.3 2.7 %collective-permute-start.3 = (bf16[128,128]{1,0:T(8,128)(2,1)S(1)}, bf16[128,128]{1,0:T(8,128)(2,1)S(1)}, u32[]{:S(2)}, u32[]{:S(2)}) collective-permute-start(bf16[128,128]{1,0:T(8,128)(2,1)S(1)} %get-tuple-element.39), channel_id=1, source_target_pairs={{0,1},{1,0},{2,3},{3,2},{4,5},{5,4},{6,7},{7,6},{8,9},{9,8},{10,11... | collective-permute-start | bytes 98312 | tf_op jit(solution)/shard_map/ppermute | solution.py:198
  10.0 8.0 %collective-permute-start.7 = (bf16[4,128,128]{2,1,0:T(8,128)(2,1)S(1)}, bf16[4,128,128]{2,1,0:T(8,128)(2,1)S(1)}, u32[]{:S(2)}, u32[]{:S(2)}) collective-permute-start(bf16[4,128,128]{2,1,0:T(8,128)(2,1)S(1)} %get-tuple-element.41), channel_id=1, source_target_pairs={{0,1},{1,0},{2,3},{3,2},{4,5},{5,4},{6,7},{7,6},{8,9},{9,8},{10,11... | collective-permute-start | bytes 393224 | tf_op jit(solution)/shard_map/ppermute | solution.py:190
  10.1 5.3 %collective-permute-start.4 = (bf16[128,128]{1,0:T(8,128)(2,1)S(1)}, bf16[128,128]{1,0:T(8,128)(2,1)S(1)}, u32[]{:S(2)}, u32[]{:S(2)}) collective-permute-start(bf16[128,128]{1,0:T(8,128)(2,1)S(1)} %get-tuple-element.40), channel_id=1, source_target_pairs={{0,25},{1,24},{2,27},{3,26},{4,29},{5,28},{6,31},{7,30},{8,17},{9,... | collective-permute-start | bytes 98312 | tf_op jit(solution)/shard_map/ppermute | solution.py:211
  13.7 4.3 %collective-permute-start.5 = (bf16[128,128]{1,0:T(8,128)(2,1)S(1)}, bf16[128,128]{1,0:T(8,128)(2,1)S(1)}, u32[]{:S(2)}, u32[]{:S(2)}) collective-permute-start(bf16[128,128]{1,0:T(8,128)(2,1)S(1)} %get-tuple-element.40), channel_id=1, source_target_pairs={{0,17},{1,16},{2,19},{3,18},{4,21},{5,20},{6,23},{7,22},{8,25},{9,... | collective-permute-start | bytes 98312 | tf_op jit(solution)/shard_map/ppermute | solution.py:211
  13.7 4.3 %collective-permute-start.6 = (bf16[128,128]{1,0:T(8,128)(2,1)S(1)}, bf16[128,128]{1,0:T(8,128)(2,1)S(1)}, u32[]{:S(2)}, u32[]{:S(2)}) collective-permute-start(bf16[128,128]{1,0:T(8,128)(2,1)S(1)} %get-tuple-element.40), channel_id=1, source_target_pairs={{0,9},{1,8},{2,11},{3,10},{4,13},{5,12},{6,15},{7,14},{8,1},{9,0},... | collective-permute-start | bytes 98312 | tf_op jit(solution)/shard_map/ppermute | solution.py:211
  18.1 4.9 %collective-permute-start.8 = (bf16[128,128]{1,0:T(8,128)(2,1)S(1)}, bf16[128,128]{1,0:T(8,128)(2,1)S(1)}, u32[]{:S(2)}, u32[]{:S(2)}) collective-permute-start(bf16[128,128]{1,0:T(8,128)(2,1)S(1)} %get-tuple-element.42), channel_id=1, source_target_pairs={{0,6},{2,4},{4,2},{6,0},{8,14},{10,12},{12,10},{14,8},{16,22},{18,... | collective-permute-start | bytes 98312 | tf_op jit(solution)/shard_map/ppermute | solution.py:190
  19.6 3.9 %collective-permute-start.9 = (bf16[128,128]{1,0:T(8,128)(2,1)S(1)}, bf16[128,128]{1,0:T(8,128)(2,1)S(1)}, u32[]{:S(2)}, u32[]{:S(2)}) collective-permute-start(bf16[128,128]{1,0:T(8,128)(2,1)S(1)} %get-tuple-element.43), channel_id=1, source_target_pairs={{0,4},{2,6},{4,0},{6,2},{8,12},{10,14},{12,8},{14,10},{16,20},{18,... | collective-permute-start | bytes 98312 | tf_op jit(solution)/shard_map/ppermute | solution.py:190
  20.4 3.9 %copy-start.3 = (bf16[256,512]{1,0:T(8,128)(2,1)S(1)}, bf16[256,512]{1,0:T(8,128)(2,1)}, u32[]{:S(2)}) copy-start(bf16[256,512]{1,0:T(8,128)(2,1)} %c_ref.3) | copy-start | bytes 786436
  20.4 3.9 %collective-permute-start.10 = (bf16[128,128]{1,0:T(8,128)(2,1)S(1)}, bf16[128,128]{1,0:T(8,128)(2,1)S(1)}, u32[]{:S(2)}, u32[]{:S(2)}) collective-permute-start(bf16[128,128]{1,0:T(8,128)(2,1)S(1)} %get-tuple-element.44), channel_id=1, source_target_pairs={{0,2},{2,0},{4,6},{6,4},{8,10},{10,8},{12,14},{14,12},{16,18},{18,... | collective-permute-start | bytes 98312 | tf_op jit(solution)/shard_map/ppermute | solution.py:190
  24.7 1.2 %collective-permute-start.11 = (f32[2,256]{1,0:T(2,128)S(1)}, f32[2,256]{1,0:T(2,128)S(1)}, u32[]{:S(2)}, u32[]{:S(2)}) collective-permute-start(f32[2,256]{1,0:T(2,128)S(1)} %get-tuple-element.47), channel_id=1, source_target_pairs={{0,1},{1,0},{2,3},{3,2},{4,5},{5,4},{6,7},{7,6},{8,9},{9,8},{10,11... | collective-permute-start | bytes 6152 | tf_op jit(solution)/shard_map/ppermute | solution.py:190
  26.3 4.3 %collective-permute-start.12 = (bf16[128,128]{1,0:T(8,128)(2,1)S(1)}, bf16[128,128]{1,0:T(8,128)(2,1)S(1)}, u32[]{:S(2)}, u32[]{:S(2)}) collective-permute-start(bf16[128,128]{1,0:T(8,128)(2,1)S(1)} %get-tuple-element.54), channel_id=1, source_target_pairs={{0,7},{1,6},{2,5},{3,4},{4,3},{5,2},{6,1},{7,0},{8,15},{9,14},{10,... | collective-permute-start | bytes 98312 | tf_op jit(solution)/shard_map/ppermute | solution.py:198
  28.3 3.3 %collective-permute-start.13 = (bf16[128,128]{1,0:T(8,128)(2,1)S(1)}, bf16[128,128]{1,0:T(8,128)(2,1)S(1)}, u32[]{:S(2)}, u32[]{:S(2)}) collective-permute-start(bf16[128,128]{1,0:T(8,128)(2,1)S(1)} %get-tuple-element.55), channel_id=1, source_target_pairs={{0,5},{1,2},{2,7},{3,0},{4,1},{5,6},{6,3},{7,4},{8,13},{9,10},{10,... | collective-permute-start | bytes 98312 | tf_op jit(solution)/shard_map/ppermute | solution.py:198
  28.9 3.6 %collective-permute-start.14 = (bf16[128,128]{1,0:T(8,128)(2,1)S(1)}, bf16[128,128]{1,0:T(8,128)(2,1)S(1)}, u32[]{:S(2)}, u32[]{:S(2)}) collective-permute-start(bf16[128,128]{1,0:T(8,128)(2,1)S(1)} %get-tuple-element.56), channel_id=1, source_target_pairs={{0,3},{1,4},{2,1},{3,6},{4,7},{5,0},{6,5},{7,2},{8,11},{9,12},{10,... | collective-permute-start | bytes 98312 | tf_op jit(solution)/shard_map/ppermute | solution.py:198
  30.0 2.5 %collective-permute-start.15 = (bf16[128,128]{1,0:T(8,128)(2,1)S(1)}, bf16[128,128]{1,0:T(8,128)(2,1)S(1)}, u32[]{:S(2)}, u32[]{:S(2)}) collective-permute-start(bf16[128,128]{1,0:T(8,128)(2,1)S(1)} %get-tuple-element.57), channel_id=1, source_target_pairs={{0,1},{1,0},{2,3},{3,2},{4,5},{5,4},{6,7},{7,6},{8,9},{9,8},{10,11... | collective-permute-start | bytes 98312 | tf_op jit(solution)/shard_map/ppermute | solution.py:198
  32.5 7.2 %collective-permute-start.19 = (bf16[4,128,128]{2,1,0:T(8,128)(2,1)S(1)}, bf16[4,128,128]{2,1,0:T(8,128)(2,1)S(1)}, u32[]{:S(2)}, u32[]{:S(2)}) collective-permute-start(bf16[4,128,128]{2,1,0:T(8,128)(2,1)S(1)} %get-tuple-element.59), channel_id=1, source_target_pairs={{0,1},{1,0},{2,3},{3,2},{4,5},{5,4},{6,7},{7,6},{8,9},{9,8},{10,11... | collective-permute-start | bytes 393224 | tf_op jit(solution)/shard_map/ppermute | solution.py:190
  32.7 6.1 %collective-permute-start.16 = (bf16[128,128]{1,0:T(8,128)(2,1)S(1)}, bf16[128,128]{1,0:T(8,128)(2,1)S(1)}, u32[]{:S(2)}, u32[]{:S(2)}) collective-permute-start(bf16[128,128]{1,0:T(8,128)(2,1)S(1)} %get-tuple-element.58), channel_id=1, source_target_pairs={{0,17},{1,16},{2,19},{3,18},{4,21},{5,20},{6,23},{7,22},{8,25},{9,... | collective-permute-start | bytes 98312 | tf_op jit(solution)/shard_map/ppermute | solution.py:211
  34.3 5.4 %collective-permute-start.17 = (bf16[128,128]{1,0:T(8,128)(2,1)S(1)}, bf16[128,128]{1,0:T(8,128)(2,1)S(1)}, u32[]{:S(2)}, u32[]{:S(2)}) collective-permute-start(bf16[128,128]{1,0:T(8,128)(2,1)S(1)} %get-tuple-element.58), channel_id=1, source_target_pairs={{0,17},{1,16},{2,19},{3,18},{4,21},{5,20},{6,23},{7,22},{8,25},{9,... | collective-permute-start | bytes 98312 | tf_op jit(solution)/shard_map/ppermute | solution.py:211
  34.3 5.4 %collective-permute-start.18 = (bf16[128,128]{1,0:T(8,128)(2,1)S(1)}, bf16[128,128]{1,0:T(8,128)(2,1)S(1)}, u32[]{:S(2)}, u32[]{:S(2)}) collective-permute-start(bf16[128,128]{1,0:T(8,128)(2,1)S(1)} %get-tuple-element.58), channel_id=1, source_target_pairs={{0,9},{1,8},{2,11},{3,10},{4,13},{5,12},{6,15},{7,14},{8,1},{9,0},... | collective-permute-start | bytes 98312 | tf_op jit(solution)/shard_map/ppermute | solution.py:211
  39.8 4.9 %collective-permute-start.20 = (bf16[128,128]{1,0:T(8,128)(2,1)S(1)}, bf16[128,128]{1,0:T(8,128)(2,1)S(1)}, u32[]{:S(2)}, u32[]{:S(2)}) collective-permute-start(bf16[128,128]{1,0:T(8,128)(2,1)S(1)} %get-tuple-element.60), channel_id=1, source_target_pairs={{0,6},{2,4},{4,2},{6,0},{8,14},{10,12},{12,10},{14,8},{16,22},{18,... | collective-permute-start | bytes 98312 | tf_op jit(solution)/shard_map/ppermute | solution.py:190
  41.2 3.9 %collective-permute-start.21 = (bf16[128,128]{1,0:T(8,128)(2,1)S(1)}, bf16[128,128]{1,0:T(8,128)(2,1)S(1)}, u32[]{:S(2)}, u32[]{:S(2)}) collective-permute-start(bf16[128,128]{1,0:T(8,128)(2,1)S(1)} %get-tuple-element.61), channel_id=1, source_target_pairs={{0,4},{2,6},{4,0},{6,2},{8,12},{10,14},{12,8},{14,10},{16,20},{18,... | collective-permute-start | bytes 98312 | tf_op jit(solution)/shard_map/ppermute | solution.py:190
  42.3 3.9 %collective-permute-start.22 = (bf16[128,128]{1,0:T(8,128)(2,1)S(1)}, bf16[128,128]{1,0:T(8,128)(2,1)S(1)}, u32[]{:S(2)}, u32[]{:S(2)}) collective-permute-start(bf16[128,128]{1,0:T(8,128)(2,1)S(1)} %get-tuple-element.62), channel_id=1, source_target_pairs={{0,2},{2,0},{4,6},{6,4},{8,10},{10,8},{12,14},{14,12},{16,18},{18,... | collective-permute-start | bytes 98312 | tf_op jit(solution)/shard_map/ppermute | solution.py:190

commit v8 on v6

--- a/solution.py
+++ b/solution.py
@@ -143,15 +143,26 @@
         head(value_ref, h)[...] = dot(scores_ref[h], grad, ((0,), (0,)))
 
 
-def last_kernel(k_ref, v_ref, key_local, value_local, p0, p1, p2, p3, key_ref, value_ref):
-    m = member_of_quad()
-    for op, p_ref in enumerate((p0, p1, p2, p3)):
-        h = m ^ came(op)
-        suffix = p_ref[...]
-        key = head(key_local, h)[...] + dot(head(v_ref, h)[...], suffix, ((1,), (1,)))
-        head(key_ref, h)[...] = key.astype(LOW)
-        value = head(value_local, h)[...] + dot(head(k_ref, h)[...], suffix, ((1,), (0,)))
-        head(value_ref, h)[...] = value.astype(LOW)
+def last_kernel(k_ref, v_ref, key_local, value_local, p0, p1, p2, p3, key_ref, value_ref, key_buf, value_buf, sems):
+    m = member_of_quad()
+    rows = k_ref.shape[0] // CHUNKS
+    copies = []
+    parts = (key_local, v_ref, 1, key_buf, key_ref), (value_local, k_ref, 0, value_buf, value_ref)
+    for n, (local, other, side, buf, out) in enumerate(parts):
+        for op, p_ref in enumerate((p0, p1, p2, p3)):
+            h = m ^ came(op)
+            total = head(local, h)[...] + dot(head(other, h)[...], p_ref[...], ((1,), (side,)))
+            head(buf, h)[...] = total.astype(LOW)
+        for i in range(CHUNKS):
+            part = pl.ds(i * rows, rows)
+            copies.append(pltpu.make_async_copy(buf.at[part], out.at[part], sems.at[n, i]))
+            copies[-1].start()
+    for copy in copies:
+        copy.wait()
+
+
+def quad_steps(quads, before):
+    return (2, 3, 1) if quads == 4 and before else range(quads - 1, 0, -1)
 
 
 def quad_targets(quads, step, before):
@@ -170,7 +181,7 @@
         return jnp.where(a < b if before else a > b, 1.0, 0.0).astype(WIDE)
 
     outer = jnp.zeros((DH, DH), WIDE)
-    for step, total in zip(range(quads - 1, 0, -1), got):
+    for step, total in zip(quad_steps(quads, before), got):
         outer = outer + total[...].astype(WIDE) * counts(quad ^ step, quad)
     pieces = [piece[...].astype(WIDE) for piece in held]
     for to in OPS:
@@ -198,7 +209,7 @@
     total = sum(piece.astype(WIDE) for piece in held).astype(LOW)
     quads = lax.axis_size("seq") // QUAD
     got = []
-    for step in range(quads - 1, 0, -1):
+    for step in quad_steps(quads, before):
         targets = quad_targets(quads, step, before)
         pairs = [(z * QUAD + i, targets[z] * QUAD + i) for z in range(quads) for i in range(QUAD)]
         got.append(lax.ppermute(total, "seq", pairs))
@@ -254,7 +265,9 @@
     )
     suffix = exclusive_sum(terms, False, key_local)
     key_grad, value_grad = call(
-        last_kernel, [low, low], (k, v, key_local, value_local, *suffix), 2 * unit
+        last_kernel, [low, low], (k, v, key_local, value_local, *suffix), 2 * unit,
+        out_specs=[pl.BlockSpec(memory_space=pltpu.HBM)] * 2,
+        scratch_shapes=buffers,
     )
     return (normed_out, query_grad, key_grad, value_grad)
 

time: 45.8 us -> 45.2 us (0.987)
  transfers between devices with their start and end apart: 23 -> 23, of which waited for: 14 -> 15; matrix products, arithmetic and copies ran while one was open for 0% -> 0% of each run, Pallas kernels for 6% -> 6%
where the time goes in v8:
time: 45.2 us; the launch traced here: 45.1 us
  starting transfers between devices  24.8 us (55%)
  waiting for transfers between devices  13.2 us (29%)
  Pallas kernels  6.26 us (14%)
  between operations  0.72 us (2%)
    ppermute x16, starting transfers between devices, cross(): return lax.ppermute(value, ('seq', 'tp'), pairs)  16 us
    ppermute x6, starting transfers between devices, exclusive_sum(): got.append(lax.ppermute(total, 'seq', pairs))  8.67 us
    ppermute x16, waiting for transfers between devices, cross(): return lax.ppermute(value, ('seq', 'tp'), pairs)  7.87 us
    pallas_call x8, Pallas kernels, call(): pl.pallas_call(kernel, out_shape=outs, in_specs=in_specs or [pl.BlockSpec...  6.26 us
    ppermute x6, waiting for transfers between devices, exclusive_sum(): got.append(lax.ppermute(total, 'seq', pairs))  4.26 us
    ppermute x1, waiting for transfers between devices, exchange(): return lax.ppermute(value, axis, [(i, i ^ bits) for i in range(size)])  1.07 us
  transfers between devices with their start and end apart: 23, of which 15 were waited for; matrix products, arithmetic and copies ran while one was open for 0% of the time, Pallas kernels for 6%

profile of v8, /device:TPU:0, one launch (start us, length us, event | category | flops | bytes accessed | tf_op | source)
XLA Modules:
  0.0 45.1 jit_solution(4680170571418902172)
XLA Ops:
  0.7 1.4 %shard_map.76 = (bf16[128,128]{1,0:T(8,128)(2,1)S(1)}, bf16[128,128]{1,0:T(8,128)(2,1)S(1)}, bf16[128,128]{1,0:T(8,128)(2,1)S(1)}, bf16[128,128]{1,0:T(8,128)(2,1)S(1)}) custom-call(bf16[256,512]{1,0:T(8,128)(2,1)} %k_ref.7, bf16[256,512]{1,0:T(8,128)(2,1)} %v_ref.7), custom_call_target="tpu_custom_call" | custom-call | flops 33554432 | bytes 655360 | tf_op jit(solution)/shard_map/pallas_call | solution.py:52
  2.1 3.4 %collective-permute-start = (bf16[128,128]{1,0:T(8,128)(2,1)S(1)}, bf16[128,128]{1,0:T(8,128)(2,1)S(1)}, u32[]{:S(2)}, u32[]{:S(2)}) collective-permute-start(bf16[128,128]{1,0:T(8,128)(2,1)S(1)} %get-tuple-element.32), channel_id=1, source_target_pairs={{0,7},{1,6},{2,5},{3,4},{4,3},{5,2},{6,1},{7,0},{8,15},{9,14},{10,... | collective-permute-start | bytes 98312 | tf_op jit(solution)/shard_map/ppermute | solution.py:204
  5.5 0.8 %collective-permute-start.1 = (bf16[128,128]{1,0:T(8,128)(2,1)S(1)}, bf16[128,128]{1,0:T(8,128)(2,1)S(1)}, u32[]{:S(2)}, u32[]{:S(2)}) collective-permute-start(bf16[128,128]{1,0:T(8,128)(2,1)S(1)} %get-tuple-element.33), channel_id=1, source_target_pairs={{0,5},{1,2},{2,7},{3,0},{4,1},{5,6},{6,3},{7,4},{8,13},{9,10},{10,... | collective-permute-start | bytes 98312 | tf_op jit(solution)/shard_map/ppermute | solution.py:204
  6.3 1.0 %collective-permute-start.2 = (bf16[128,128]{1,0:T(8,128)(2,1)S(1)}, bf16[128,128]{1,0:T(8,128)(2,1)S(1)}, u32[]{:S(2)}, u32[]{:S(2)}) collective-permute-start(bf16[128,128]{1,0:T(8,128)(2,1)S(1)} %get-tuple-element.34), channel_id=1, source_target_pairs={{0,3},{1,4},{2,1},{3,6},{4,7},{5,0},{6,5},{7,2},{8,11},{9,12},{10,... | collective-permute-start | bytes 98312 | tf_op jit(solution)/shard_map/ppermute | solution.py:204
  7.3 0.7 %collective-permute-start.3 = (bf16[128,128]{1,0:T(8,128)(2,1)S(1)}, bf16[128,128]{1,0:T(8,128)(2,1)S(1)}, u32[]{:S(2)}, u32[]{:S(2)}) collective-permute-start(bf16[128,128]{1,0:T(8,128)(2,1)S(1)} %get-tuple-element.35), channel_id=1, source_target_pairs={{0,1},{1,0},{2,3},{3,2},{4,5},{5,4},{6,7},{7,6},{8,9},{9,8},{10,11... | collective-permute-start | bytes 98312 | tf_op jit(solution)/shard_map/ppermute | solution.py:204
  7.9 0.9 %collective-permute-done.1.refs_1_ = bf16[128,128]{1,0:T(8,128)(2,1)S(1)} collective-permute-done((bf16[128,128]{1,0:T(8,128)(2,1)S(1)}, bf16[128,128]{1,0:T(8,128)(2,1)S(1)}, u32[]{:S(2)}, u32[]{:S(2)}) %collective-permute-start.1) | collective-permute-done | bytes 32800 | tf_op jit(solution)/shard_map/ppermute | solution.py:204
  8.9 1.1 %collective-permute-done.2.refs_2_ = bf16[128,128]{1,0:T(8,128)(2,1)S(1)} collective-permute-done((bf16[128,128]{1,0:T(8,128)(2,1)S(1)}, bf16[128,128]{1,0:T(8,128)(2,1)S(1)}, u32[]{:S(2)}, u32[]{:S(2)}) %collective-permute-start.2) | collective-permute-done | bytes 32800 | tf_op jit(solution)/shard_map/ppermute | solution.py:204
  10.0 2.7 %collective-permute-start.4 = (bf16[128,128]{1,0:T(8,128)(2,1)S(1)}, bf16[128,128]{1,0:T(8,128)(2,1)S(1)}, u32[]{:S(2)}, u32[]{:S(2)}) collective-permute-start(bf16[128,128]{1,0:T(8,128)(2,1)S(1)} %add_convert_fusion.1), channel_id=1, source_target_pairs={{0,16},{2,18},{4,20},{6,22},{8,24},{10,26},{12,28},{14,30},{16,0},... | collective-permute-start | bytes 98312 | tf_op jit(solution)/shard_map/ppermute | solution.py:215
  12.6 1.3 %collective-permute-start.5 = (bf16[128,128]{1,0:T(8,128)(2,1)S(1)}, bf16[128,128]{1,0:T(8,128)(2,1)S(1)}, u32[]{:S(2)}, u32[]{:S(2)}) collective-permute-start(bf16[128,128]{1,0:T(8,128)(2,1)S(1)} %add_convert_fusion.1), channel_id=1, source_target_pairs={{0,24},{2,26},{4,28},{6,30},{8,16},{10,18},{12,20},{14,22},{16,0},... | collective-permute-start | bytes 98312 | tf_op jit(solution)/shard_map/ppermute | solution.py:215
  14.2 1.0 %collective-permute-done.4.refs_4_ = bf16[128,128]{1,0:T(8,128)(2,1)S(1)} collective-permute-done((bf16[128,128]{1,0:T(8,128)(2,1)S(1)}, bf16[128,128]{1,0:T(8,128)(2,1)S(1)}, u32[]{:S(2)}, u32[]{:S(2)}) %collective-permute-start.4) | collective-permute-done | bytes 32800 | tf_op jit(solution)/shard_map/ppermute | solution.py:215
  15.2 2.5 %collective-permute-done.5.refs_5_ = bf16[128,128]{1,0:T(8,128)(2,1)S(1)} collective-permute-done((bf16[128,128]{1,0:T(8,128)(2,1)S(1)}, bf16[128,128]{1,0:T(8,128)(2,1)S(1)}, u32[]{:S(2)}, u32[]{:S(2)}) %collective-permute-start.5) | collective-permute-done | bytes 32800 | tf_op jit(solution)/shard_map/ppermute | solution.py:215
  18.2 1.6 %collective-permute-start.8 = (bf16[128,128]{1,0:T(8,128)(2,1)S(1)}, bf16[128,128]{1,0:T(8,128)(2,1)S(1)}, u32[]{:S(2)}, u32[]{:S(2)}) collective-permute-start(bf16[128,128]{1,0:T(8,128)(2,1)S(1)} %get-tuple-element.37), channel_id=1, source_target_pairs={{0,5},{1,2},{2,7},{3,0},{4,1},{5,6},{6,3},{7,4},{8,13},{9,10},{10,... | collective-permute-start | bytes 98312 | tf_op jit(solution)/shard_map/ppermute | solution.py:204
  19.8 0.7 %collective-permute-start.9 = (bf16[128,128]{1,0:T(8,128)(2,1)S(1)}, bf16[128,128]{1,0:T(8,128)(2,1)S(1)}, u32[]{:S(2)}, u32[]{:S(2)}) collective-permute-start(bf16[128,128]{1,0:T(8,128)(2,1)S(1)} %get-tuple-element.38), channel_id=1, source_target_pairs={{0,3},{1,4},{2,1},{3,6},{4,7},{5,0},{6,5},{7,2},{8,11},{9,12},{10,... | collective-permute-start | bytes 98312 | tf_op jit(solution)/shard_map/ppermute | solution.py:204
  20.5 0.8 %collective-permute-start.10 = (bf16[128,128]{1,0:T(8,128)(2,1)S(1)}, bf16[128,128]{1,0:T(8,128)(2,1)S(1)}, u32[]{:S(2)}, u32[]{:S(2)}) collective-permute-start(bf16[128,128]{1,0:T(8,128)(2,1)S(1)} %get-tuple-element.39), channel_id=1, source_target_pairs={{0,1},{1,0},{2,3},{3,2},{4,5},{5,4},{6,7},{7,6},{8,9},{9,8},{10,11... | collective-permute-start | bytes 98312 | tf_op jit(solution)/shard_map/ppermute | solution.py:204
  21.3 0.7 %shard_map.75 = (bf16[4,256,256]{2,1,0:T(8,128)(2,1)S(1)}, f32[256,512]{1,0:T(8,128)S(1)}) custom-call(bf16[256,512]{1,0:T(8,128)(2,1)S(1)} %copy-done.2, bf16[256,512]{1,0:T(8,128)(2,1)S(1)} %copy-done, bf16[256,512]{1,0:T(8,128)(2,1)S(1)} %copy-done.1), custom_call_target="tpu_custom_call" | custom-call | flops 134217728 | bytes 1835008 | tf_op jit(solution)/shard_map/pallas_call | solution.py:52
  22.4 1.0 %collective-permute-done.9.p2 = bf16[128,128]{1,0:T(8,128)(2,1)S(1)} collective-permute-done((bf16[128,128]{1,0:T(8,128)(2,1)S(1)}, bf16[128,128]{1,0:T(8,128)(2,1)S(1)}, u32[]{:S(2)}, u32[]{:S(2)}) %collective-permute-start.9) | collective-permute-done | bytes 32800 | tf_op jit(solution)/shard_map/ppermute | solution.py:204
  24.0 1.1 %collective-permute-done.11 = f32[2,256]{1,0:T(2,128)S(1)} collective-permute-done((f32[2,256]{1,0:T(2,128)S(1)}, f32[2,256]{1,0:T(2,128)S(1)}, u32[]{:S(2)}, u32[]{:S(2)}) %collective-permute-start.11) | collective-permute-done | bytes 2080 | tf_op jit(solution)/shard_map/ppermute | solution.py:196
  25.5 1.7 %collective-permute-start.12 = (bf16[128,128]{1,0:T(8,128)(2,1)S(1)}, bf16[128,128]{1,0:T(8,128)(2,1)S(1)}, u32[]{:S(2)}, u32[]{:S(2)}) collective-permute-start(bf16[128,128]{1,0:T(8,128)(2,1)S(1)} %get-tuple-element.48), channel_id=1, source_target_pairs={{0,7},{1,6},{2,5},{3,4},{4,3},{5,2},{6,1},{7,0},{8,15},{9,14},{10,... | collective-permute-start | bytes 98312 | tf_op jit(solution)/shard_map/ppermute | solution.py:204
  27.2 0.9 %collective-permute-start.13 = (bf16[128,128]{1,0:T(8,128)(2,1)S(1)}, bf16[128,128]{1,0:T(8,128)(2,1)S(1)}, u32[]{:S(2)}, u32[]{:S(2)}) collective-permute-start(bf16[128,128]{1,0:T(8,128)(2,1)S(1)} %get-tuple-element.49), channel_id=1, source_target_pairs={{0,5},{1,2},{2,7},{3,0},{4,1},{5,6},{6,3},{7,4},{8,13},{9,10},{10,... | collective-permute-start | bytes 98312 | tf_op jit(solution)/shard_map/ppermute | solution.py:204
  28.1 0.9 %collective-permute-start.14 = (bf16[128,128]{1,0:T(8,128)(2,1)S(1)}, bf16[128,128]{1,0:T(8,128)(2,1)S(1)}, u32[]{:S(2)}, u32[]{:S(2)}) collective-permute-start(bf16[128,128]{1,0:T(8,128)(2,1)S(1)} %get-tuple-element.50), channel_id=1, source_target_pairs={{0,3},{1,4},{2,1},{3,6},{4,7},{5,0},{6,5},{7,2},{8,11},{9,12},{10,... | collective-permute-start | bytes 98312 | tf_op jit(solution)/shard_map/ppermute | solution.py:204
  29.3 0.5 %collective-permute-done.12.refs_0_ = bf16[128,128]{1,0:T(8,128)(2,1)S(1)} collective-permute-done((bf16[128,128]{1,0:T(8,128)(2,1)S(1)}, bf16[128,128]{1,0:T(8,128)(2,1)S(1)}, u32[]{:S(2)}, u32[]{:S(2)}) %collective-permute-start.12) | collective-permute-done | bytes 32800 | tf_op jit(solution)/shard_map/ppermute | solution.py:204
  29.8 0.7 %collective-permute-done.13.refs_1_ = bf16[128,128]{1,0:T(8,128)(2,1)S(1)} collective-permute-done((bf16[128,128]{1,0:T(8,128)(2,1)S(1)}, bf16[128,128]{1,0:T(8,128)(2,1)S(1)}, u32[]{:S(2)}, u32[]{:S(2)}) %collective-permute-start.13) | collective-permute-done | bytes 32800 | tf_op jit(solution)/shard_map/ppermute | solution.py:204
  30.5 0.9 %collective-permute-done.14.refs_2_ = bf16[128,128]{1,0:T(8,128)(2,1)S(1)} collective-permute-done((bf16[128,128]{1,0:T(8,128)(2,1)S(1)}, bf16[128,128]{1,0:T(8,128)(2,1)S(1)}, u32[]{:S(2)}, u32[]{:S(2)}) %collective-permute-start.14) | collective-permute-done | bytes 32800 | tf_op jit(solution)/shard_map/ppermute | solution.py:204
  31.4 1.6 %collective-permute-start.16 = (bf16[128,128]{1,0:T(8,128)(2,1)S(1)}, bf16[128,128]{1,0:T(8,128)(2,1)S(1)}, u32[]{:S(2)}, u32[]{:S(2)}) collective-permute-start(bf16[128,128]{1,0:T(8,128)(2,1)S(1)} %add_convert_fusion), channel_id=1, source_target_pairs={{0,16},{2,18},{4,20},{6,22},{8,24},{10,26},{12,28},{14,30},{16,8},... | collective-permute-start | bytes 98312 | tf_op jit(solution)/shard_map/ppermute | solution.py:215
  33.1 1.0 %collective-permute-start.17 = (bf16[128,128]{1,0:T(8,128)(2,1)S(1)}, bf16[128,128]{1,0:T(8,128)(2,1)S(1)}, u32[]{:S(2)}, u32[]{:S(2)}) collective-permute-start(bf16[128,128]{1,0:T(8,128)(2,1)S(1)} %add_convert_fusion), channel_id=1, source_target_pairs={{0,16},{2,18},{4,20},{6,22},{8,24},{10,26},{12,28},{14,30},{16,0},... | collective-permute-start | bytes 98312 | tf_op jit(solution)/shard_map/ppermute | solution.py:215
  34.1 1.8 %collective-permute-start.18 = (bf16[128,128]{1,0:T(8,128)(2,1)S(1)}, bf16[128,128]{1,0:T(8,128)(2,1)S(1)}, u32[]{:S(2)}, u32[]{:S(2)}) collective-permute-start(bf16[128,128]{1,0:T(8,128)(2,1)S(1)} %add_convert_fusion), channel_id=1, source_target_pairs={{0,8},{2,10},{4,12},{6,14},{8,0},{10,2},{12,4},{14,6},{16,24},{18,... | collective-permute-start | bytes 98312 | tf_op jit(solution)/shard_map/ppermute | solution.py:215
  35.9 2.0 %shard_map.80 = (bf16[256,512]{1,0:T(8,128)(2,1)}, bf16[256,512]{1,0:T(8,128)(2,1)}, f32[256,512]{1,0:T(8,128)S(1)}, f32[256,512]{1,0:T(8,128)S(1)}) custom-call(bf16[256,512]{1,0:T(8,128)(2,1)S(1)} %copy-done.2, bf16[256,512]{1,0:T(8,128)(2,1)S(1)} %copy-done, bf16[256,512]{1,0:T(8,128)(2,1)S(1)} %copy-done.1, ...), custom_call_target="tpu_custom_call" | custom-call | flops 301989888 | bytes 3803136 | tf_op jit(solution)/shard_map/pallas_call | solution.py:52
  39.0 1.7 %collective-permute-start.20 = (bf16[128,128]{1,0:T(8,128)(2,1)S(1)}, bf16[128,128]{1,0:T(8,128)(2,1)S(1)}, u32[]{:S(2)}, u32[]{:S(2)}) collective-permute-start(bf16[128,128]{1,0:T(8,128)(2,1)S(1)} %get-tuple-element.53), channel_id=1, source_target_pairs={{0,5},{1,2},{2,7},{3,0},{4,1},{5,6},{6,3},{7,4},{8,13},{9,10},{10,... | collective-permute-start | bytes 98312 | tf_op jit(solution)/shard_map/ppermute | solution.py:204
  40.8 0.9 %collective-permute-start.22 = (bf16[128,128]{1,0:T(8,128)(2,1)S(1)}, bf16[128,128]{1,0:T(8,128)(2,1)S(1)}, u32[]{:S(2)}, u32[]{:S(2)}) collective-permute-start(bf16[128,128]{1,0:T(8,128)(2,1)S(1)} %get-tuple-element.55), channel_id=1, source_target_pairs={{0,1},{1,0},{2,3},{3,2},{4,5},{5,4},{6,7},{7,6},{8,9},{9,8},{10,11... | collective-permute-start | bytes 98312 | tf_op jit(solution)/shard_map/ppermute | solution.py:204
  41.7 1.1 %collective-permute-done.19.p0 = bf16[128,128]{1,0:T(8,128)(2,1)S(1)} collective-permute-done((bf16[128,128]{1,0:T(8,128)(2,1)S(1)}, bf16[128,128]{1,0:T(8,128)(2,1)S(1)}, u32[]{:S(2)}, u32[]{:S(2)}) %collective-permute-start.19) | collective-permute-done | bytes 32800 | tf_op jit(solution)/shard_map/ppermute | solution.py:204
  42.8 1.2 %collective-permute-done.21.p2 = bf16[128,128]{1,0:T(8,128)(2,1)S(1)} collective-permute-done((bf16[128,128]{1,0:T(8,128)(2,1)S(1)}, bf16[128,128]{1,0:T(8,128)(2,1)S(1)}, u32[]{:S(2)}, u32[]{:S(2)}) %collective-permute-start.21) | collective-permute-done | bytes 32800 | tf_op jit(solution)/shard_map/ppermute | solution.py:204
  44.0 1.1 %shard_map.82 = (bf16[256,512]{1,0:T(8,128)(2,1)}, bf16[256,512]{1,0:T(8,128)(2,1)}) custom-call(bf16[256,512]{1,0:T(8,128)(2,1)S(1)} %copy-done, bf16[256,512]{1,0:T(8,128)(2,1)S(1)} %copy-done.1, f32[256,512]{1,0:T(8,128)S(1)} %get-tuple-element.46.refs_7_.key_local, f32[256,512]{1,0:T(8,128)S(1)} %get-tuple-element.47.value_local, ...), custom_call_target="tpu_custom_call" | custom-call | flops 67108864 | bytes 2228224 | tf_op jit(solution)/shard_map/pallas_call | solution.py:52
  (33 shorter events, 3.8 us)
Async XLA Ops:
  0.6 20.7 %copy-start.1 = (bf16[256,512]{1,0:T(8,128)(2,1)S(1)}, bf16[256,512]{1,0:T(8,128)(2,1)}, u32[]{:S(2)}) copy-start(bf16[256,512]{1,0:T(8,128)(2,1)} %v_ref.7) | copy-start | bytes 786436
  0.6 20.7 %copy-start.2 = (bf16[256,512]{1,0:T(8,128)(2,1)S(1)}, bf16[256,512]{1,0:T(8,128)(2,1)}, u32[]{:S(2)}) copy-start(bf16[256,512]{1,0:T(8,128)(2,1)} %q_ref.7) | copy-start | bytes 786436
  2.1 19.2 %copy-start = (bf16[256,512]{1,0:T(8,128)(2,1)S(1)}, bf16[256,512]{1,0:T(8,128)(2,1)}, u32[]{:S(2)}) copy-start(bf16[256,512]{1,0:T(8,128)(2,1)} %k_ref.7) | copy-start | bytes 786436
  2.1 5.8 %collective-permute-start = (bf16[128,128]{1,0:T(8,128)(2,1)S(1)}, bf16[128,128]{1,0:T(8,128)(2,1)S(1)}, u32[]{:S(2)}, u32[]{:S(2)}) collective-permute-start(bf16[128,128]{1,0:T(8,128)(2,1)S(1)} %get-tuple-element.32), channel_id=1, source_target_pairs={{0,7},{1,6},{2,5},{3,4},{4,3},{5,2},{6,1},{7,0},{8,15},{9,14},{10,... | collective-permute-start | bytes 98312 | tf_op jit(solution)/shard_map/ppermute | solution.py:204
  5.5 3.3 %collective-permute-start.1 = (bf16[128,128]{1,0:T(8,128)(2,1)S(1)}, bf16[128,128]{1,0:T(8,128)(2,1)S(1)}, u32[]{:S(2)}, u32[]{:S(2)}) collective-permute-start(bf16[128,128]{1,0:T(8,128)(2,1)S(1)} %get-tuple-element.33), channel_id=1, source_target_pairs={{0,5},{1,2},{2,7},{3,0},{4,1},{5,6},{6,3},{7,4},{8,13},{9,10},{10,... | collective-permute-start | bytes 98312 | tf_op jit(solution)/shard_map/ppermute | solution.py:204
  6.3 3.6 %collective-permute-start.2 = (bf16[128,128]{1,0:T(8,128)(2,1)S(1)}, bf16[128,128]{1,0:T(8,128)(2,1)S(1)}, u32[]{:S(2)}, u32[]{:S(2)}) collective-permute-start(bf16[128,128]{1,0:T(8,128)(2,1)S(1)} %get-tuple-element.34), channel_id=1, source_target_pairs={{0,3},{1,4},{2,1},{3,6},{4,7},{5,0},{6,5},{7,2},{8,11},{9,12},{10,... | collective-permute-start | bytes 98312 | tf_op jit(solution)/shard_map/ppermute | solution.py:204
  7.3 2.7 %collective-permute-start.3 = (bf16[128,128]{1,0:T(8,128)(2,1)S(1)}, bf16[128,128]{1,0:T(8,128)(2,1)S(1)}, u32[]{:S(2)}, u32[]{:S(2)}) collective-permute-start(bf16[128,128]{1,0:T(8,128)(2,1)S(1)} %get-tuple-element.35), channel_id=1, source_target_pairs={{0,1},{1,0},{2,3},{3,2},{4,5},{5,4},{6,7},{7,6},{8,9},{9,8},{10,11... | collective-permute-start | bytes 98312 | tf_op jit(solution)/shard_map/ppermute | solution.py:204
  10.0 5.2 %collective-permute-start.4 = (bf16[128,128]{1,0:T(8,128)(2,1)S(1)}, bf16[128,128]{1,0:T(8,128)(2,1)S(1)}, u32[]{:S(2)}, u32[]{:S(2)}) collective-permute-start(bf16[128,128]{1,0:T(8,128)(2,1)S(1)} %add_convert_fusion.1), channel_id=1, source_target_pairs={{0,16},{2,18},{4,20},{6,22},{8,24},{10,26},{12,28},{14,30},{16,0},... | collective-permute-start | bytes 98312 | tf_op jit(solution)/shard_map/ppermute | solution.py:215
  12.6 5.1 %collective-permute-start.5 = (bf16[128,128]{1,0:T(8,128)(2,1)S(1)}, bf16[128,128]{1,0:T(8,128)(2,1)S(1)}, u32[]{:S(2)}, u32[]{:S(2)}) collective-permute-start(bf16[128,128]{1,0:T(8,128)(2,1)S(1)} %add_convert_fusion.1), channel_id=1, source_target_pairs={{0,24},{2,26},{4,28},{6,30},{8,16},{10,18},{12,20},{14,22},{16,0},... | collective-permute-start | bytes 98312 | tf_op jit(solution)/shard_map/ppermute | solution.py:215
  14.0 4.0 %collective-permute-start.6 = (bf16[128,128]{1,0:T(8,128)(2,1)S(1)}, bf16[128,128]{1,0:T(8,128)(2,1)S(1)}, u32[]{:S(2)}, u32[]{:S(2)}) collective-permute-start(bf16[128,128]{1,0:T(8,128)(2,1)S(1)} %add_convert_fusion.1), channel_id=1, source_target_pairs={{0,8},{2,10},{4,12},{6,14},{8,0},{10,2},{12,4},{14,6},{16,24},{18,... | collective-permute-start | bytes 98312 | tf_op jit(solution)/shard_map/ppermute | solution.py:215
  18.1 4.3 %collective-permute-start.7 = (bf16[128,128]{1,0:T(8,128)(2,1)S(1)}, bf16[128,128]{1,0:T(8,128)(2,1)S(1)}, u32[]{:S(2)}, u32[]{:S(2)}) collective-permute-start(bf16[128,128]{1,0:T(8,128)(2,1)S(1)} %get-tuple-element.36), channel_id=1, source_target_pairs={{0,7},{1,6},{2,5},{3,4},{4,3},{5,2},{6,1},{7,0},{8,15},{9,14},{10,... | collective-permute-start | bytes 98312 | tf_op jit(solution)/shard_map/ppermute | solution.py:204
  18.2 4.2 %collective-permute-start.8 = (bf16[128,128]{1,0:T(8,128)(2,1)S(1)}, bf16[128,128]{1,0:T(8,128)(2,1)S(1)}, u32[]{:S(2)}, u32[]{:S(2)}) collective-permute-start(bf16[128,128]{1,0:T(8,128)(2,1)S(1)} %get-tuple-element.37), channel_id=1, source_target_pairs={{0,5},{1,2},{2,7},{3,0},{4,1},{5,6},{6,3},{7,4},{8,13},{9,10},{10,... | collective-permute-start | bytes 98312 | tf_op jit(solution)/shard_map/ppermute | solution.py:204
  19.8 3.7 %collective-permute-start.9 = (bf16[128,128]{1,0:T(8,128)(2,1)S(1)}, bf16[128,128]{1,0:T(8,128)(2,1)S(1)}, u32[]{:S(2)}, u32[]{:S(2)}) collective-permute-start(bf16[128,128]{1,0:T(8,128)(2,1)S(1)} %get-tuple-element.38), channel_id=1, source_target_pairs={{0,3},{1,4},{2,1},{3,6},{4,7},{5,0},{6,5},{7,2},{8,11},{9,12},{10,... | collective-permute-start | bytes 98312 | tf_op jit(solution)/shard_map/ppermute | solution.py:204
  20.5 3.0 %copy-start.3 = (bf16[256,512]{1,0:T(8,128)(2,1)S(1)}, bf16[256,512]{1,0:T(8,128)(2,1)}, u32[]{:S(2)}) copy-start(bf16[256,512]{1,0:T(8,128)(2,1)} %c_ref.3) | copy-start | bytes 786436
  20.5 2.9 %collective-permute-start.10 = (bf16[128,128]{1,0:T(8,128)(2,1)S(1)}, bf16[128,128]{1,0:T(8,128)(2,1)S(1)}, u32[]{:S(2)}, u32[]{:S(2)}) collective-permute-start(bf16[128,128]{1,0:T(8,128)(2,1)S(1)} %get-tuple-element.39), channel_id=1, source_target_pairs={{0,1},{1,0},{2,3},{3,2},{4,5},{5,4},{6,7},{7,6},{8,9},{9,8},{10,11... | collective-permute-start | bytes 98312 | tf_op jit(solution)/shard_map/ppermute | solution.py:204
  23.8 1.2 %collective-permute-start.11 = (f32[2,256]{1,0:T(2,128)S(1)}, f32[2,256]{1,0:T(2,128)S(1)}, u32[]{:S(2)}, u32[]{:S(2)}) collective-permute-start(f32[2,256]{1,0:T(2,128)S(1)} %get-tuple-element.41), channel_id=1, source_target_pairs={{0,1},{1,0},{2,3},{3,2},{4,5},{5,4},{6,7},{7,6},{8,9},{9,8},{10,11... | collective-permute-start | bytes 6152 | tf_op jit(solution)/shard_map/ppermute | solution.py:196
  25.5 4.3 %collective-permute-start.12 = (bf16[128,128]{1,0:T(8,128)(2,1)S(1)}, bf16[128,128]{1,0:T(8,128)(2,1)S(1)}, u32[]{:S(2)}, u32[]{:S(2)}) collective-permute-start(bf16[128,128]{1,0:T(8,128)(2,1)S(1)} %get-tuple-element.48), channel_id=1, source_target_pairs={{0,7},{1,6},{2,5},{3,4},{4,3},{5,2},{6,1},{7,0},{8,15},{9,14},{10,... | collective-permute-start | bytes 98312 | tf_op jit(solution)/shard_map/ppermute | solution.py:204
  27.2 3.3 %collective-permute-start.13 = (bf16[128,128]{1,0:T(8,128)(2,1)S(1)}, bf16[128,128]{1,0:T(8,128)(2,1)S(1)}, u32[]{:S(2)}, u32[]{:S(2)}) collective-permute-start(bf16[128,128]{1,0:T(8,128)(2,1)S(1)} %get-tuple-element.49), channel_id=1, source_target_pairs={{0,5},{1,2},{2,7},{3,0},{4,1},{5,6},{6,3},{7,4},{8,13},{9,10},{10,... | collective-permute-start | bytes 98312 | tf_op jit(solution)/shard_map/ppermute | solution.py:204
  28.1 3.3 %collective-permute-start.14 = (bf16[128,128]{1,0:T(8,128)(2,1)S(1)}, bf16[128,128]{1,0:T(8,128)(2,1)S(1)}, u32[]{:S(2)}, u32[]{:S(2)}) collective-permute-start(bf16[128,128]{1,0:T(8,128)(2,1)S(1)} %get-tuple-element.50), channel_id=1, source_target_pairs={{0,3},{1,4},{2,1},{3,6},{4,7},{5,0},{6,5},{7,2},{8,11},{9,12},{10,... | collective-permute-start | bytes 98312 | tf_op jit(solution)/shard_map/ppermute | solution.py:204
  28.9 2.5 %collective-permute-start.15 = (bf16[128,128]{1,0:T(8,128)(2,1)S(1)}, bf16[128,128]{1,0:T(8,128)(2,1)S(1)}, u32[]{:S(2)}, u32[]{:S(2)}) collective-permute-start(bf16[128,128]{1,0:T(8,128)(2,1)S(1)} %get-tuple-element.51), channel_id=1, source_target_pairs={{0,1},{1,0},{2,3},{3,2},{4,5},{5,4},{6,7},{7,6},{8,9},{9,8},{10,11... | collective-permute-start | bytes 98312 | tf_op jit(solution)/shard_map/ppermute | solution.py:204
  31.4 6.5 %collective-permute-start.16 = (bf16[128,128]{1,0:T(8,128)(2,1)S(1)}, bf16[128,128]{1,0:T(8,128)(2,1)S(1)}, u32[]{:S(2)}, u32[]{:S(2)}) collective-permute-start(bf16[128,128]{1,0:T(8,128)(2,1)S(1)} %add_convert_fusion), channel_id=1, source_target_pairs={{0,16},{2,18},{4,20},{6,22},{8,24},{10,26},{12,28},{14,30},{16,8},... | collective-permute-start | bytes 98312 | tf_op jit(solution)/shard_map/ppermute | solution.py:215
  33.1 5.1 %collective-permute-start.17 = (bf16[128,128]{1,0:T(8,128)(2,1)S(1)}, bf16[128,128]{1,0:T(8,128)(2,1)S(1)}, u32[]{:S(2)}, u32[]{:S(2)}) collective-permute-start(bf16[128,128]{1,0:T(8,128)(2,1)S(1)} %add_convert_fusion), channel_id=1, source_target_pairs={{0,16},{2,18},{4,20},{6,22},{8,24},{10,26},{12,28},{14,30},{16,0},... | collective-permute-start | bytes 98312 | tf_op jit(solution)/shard_map/ppermute | solution.py:215
  34.1 4.3 %collective-permute-start.18 = (bf16[128,128]{1,0:T(8,128)(2,1)S(1)}, bf16[128,128]{1,0:T(8,128)(2,1)S(1)}, u32[]{:S(2)}, u32[]{:S(2)}) collective-permute-start(bf16[128,128]{1,0:T(8,128)(2,1)S(1)} %add_convert_fusion), channel_id=1, source_target_pairs={{0,8},{2,10},{4,12},{6,14},{8,0},{10,2},{12,4},{14,6},{16,24},{18,... | collective-permute-start | bytes 98312 | tf_op jit(solution)/shard_map/ppermute | solution.py:215
  38.4 4.3 %collective-permute-start.19 = (bf16[128,128]{1,0:T(8,128)(2,1)S(1)}, bf16[128,128]{1,0:T(8,128)(2,1)S(1)}, u32[]{:S(2)}, u32[]{:S(2)}) collective-permute-start(bf16[128,128]{1,0:T(8,128)(2,1)S(1)} %get-tuple-element.52), channel_id=1, source_target_pairs={{0,7},{1,6},{2,5},{3,4},{4,3},{5,2},{6,1},{7,0},{8,15},{9,14},{10,... | collective-permute-start | bytes 98312 | tf_op jit(solution)/shard_map/ppermute | solution.py:204
  39.0 3.8 %collective-permute-start.20 = (bf16[128,128]{1,0:T(8,128)(2,1)S(1)}, bf16[128,128]{1,0:T(8,128)(2,1)S(1)}, u32[]{:S(2)}, u32[]{:S(2)}) collective-permute-start(bf16[128,128]{1,0:T(8,128)(2,1)S(1)} %get-tuple-element.53), channel_id=1, source_target_pairs={{0,5},{1,2},{2,7},{3,0},{4,1},{5,6},{6,3},{7,4},{8,13},{9,10},{10,... | collective-permute-start | bytes 98312 | tf_op jit(solution)/shard_map/ppermute | solution.py:204
  40.6 3.3 %collective-permute-start.21 = (bf16[128,128]{1,0:T(8,128)(2,1)S(1)}, bf16[128,128]{1,0:T(8,128)(2,1)S(1)}, u32[]{:S(2)}, u32[]{:S(2)}) collective-permute-start(bf16[128,128]{1,0:T(8,128)(2,1)S(1)} %get-tuple-element.54), channel_id=1, source_target_pairs={{0,3},{1,4},{2,1},{3,6},{4,7},{5,0},{6,5},{7,2},{8,11},{9,12},{10,... | collective-permute-start | bytes 98312 | tf_op jit(solution)/shard_map/ppermute | solution.py:204
  40.8 3.2 %collective-permute-start.22 = (bf16[128,128]{1,0:T(8,128)(2,1)S(1)}, bf16[128,128]{1,0:T(8,128)(2,1)S(1)}, u32[]{:S(2)}, u32[]{:S(2)}) collective-permute-start(bf16[128,128]{1,0:T(8,128)(2,1)S(1)} %get-tuple-element.55), channel_id=1, source_target_pairs={{0,1},{1,0},{2,3},{3,2},{4,5},{5,4},{6,7},{7,6},{8,9},{9,8},{10,11... | collective-permute-start | bytes 98312 | tf_op jit(solution)/shard_map/ppermute | solution.py:204

commit v9 on v6

--- a/solution.py
+++ b/solution.py
@@ -37,14 +37,32 @@
     return lax.axis_index("seq") % QUAD
 
 
-def sent(op):
-    odd = lax.axis_index("tp") % 2
-    return (3, 2 - odd, 1 + odd, 0)[op]
-
-
-def came(op):
-    odd = lax.axis_index("tp") % 2
-    return (3, 1 + odd, 2 - odd, 0)[op]
+FIRST = (((3, 2, 1, 0), (1, 3, 0, 2), (2, 0, 3, 1)), ((2, 3, 1, 0), (3, 2, 0, 1), (1, 0, 3, 2)))
+BACK = (((3, 2, 1, 0), (2, 3, 0, 1), (1, 0, 3, 2)), ((3, 2, 0, 1), (2, 3, 1, 0), (1, 0, 3, 2)))
+FIRST_GRAD = (((3, 2, 1, 0), (2, 3, 0, 1), (1, 0, 3, 2)), ((3, 2, 1, 0), (1, 0, 3, 2), (2, 3, 0, 1)))
+BACK_GRAD = (((3, 2, 1, 0), (2, 3, 0, 1), (1, 0, 3, 2)), ((2, 3, 0, 1), (1, 2, 3, 0), (3, 0, 1, 2)))
+SAME = (0, 1, 2, 3)
+
+
+def targets(wave, odd, op):
+    return SAME if op == 3 else wave[odd][op]
+
+
+def look_up(table):
+    packed = 0
+    for odd in range(2):
+        for member in range(QUAD):
+            packed |= table[odd][member] << 2 * (QUAD * odd + member)
+    place = QUAD * (lax.axis_index("tp") % 2) + member_of_quad()
+    return (packed >> (2 * place)) & 3
+
+
+def sent(wave, op):
+    return look_up([targets(wave, odd, op) for odd in range(2)])
+
+
+def came(wave, op):
+    return look_up([[targets(wave, 1 - odd, op).index(m) for m in SAME] for odd in range(2)])
 
 
 def call(kernel, outs, args, flops, in_specs=None, out_specs=None, scratch_shapes=(), room=32):
@@ -68,7 +86,6 @@
             part = pl.ds(i * rows, rows)
             copies.append(pltpu.make_async_copy(ref.at[part], buf.at[part], sems.at[n, i]))
             copies[-1].start()
-    m = member_of_quad()
     states = [0.0] * QUAD
     half = rows * CHUNKS // 2
     for part in range(2):
@@ -76,7 +93,7 @@
             copy.wait()
         tokens = pl.ds(part * half, half)
         for op in OPS:
-            cols = pl.ds(pl.multiple_of((m ^ sent(op)) * DH, DH), DH)
+            cols = pl.ds(pl.multiple_of(sent(FIRST, op) * DH, DH), DH)
             states[op] = states[op] + dot(k_buf[tokens, cols], v_buf[tokens, cols], ((0,), (0,)))
     for op, out in enumerate((o0, o1, o2, o3)):
         out[...] = states[op].astype(LOW)
@@ -92,12 +109,11 @@
 
 
 def mixed_kernel(local_ref, q_ref, c_ref, p0, p1, p2, p3, mixed_ref, sums_ref):
-    m = member_of_quad()
     count = q_ref.shape[0]
     square = jnp.zeros((count, DH), WIDE)
     product = jnp.zeros((count, DH), WIDE)
     for op, p_ref in enumerate((p0, p1, p2, p3)):
-        h = m ^ came(op)
+        h = came(BACK, op)
         mixed = head(local_ref, h)[...] + dot(head(q_ref, h)[...], p_ref[...], ((1,), (0,)))
         head(mixed_ref, h)[...] = mixed
         square = square + mixed * mixed
@@ -115,10 +131,9 @@
 
 
 def grad_kernel(features, mixed_ref, c_ref, q_ref, sums_ref, o0, o1, o2, o3, g_ref):
-    m = member_of_quad()
     inverse, projection = token_scales(sums_ref, features, q_ref.shape[0])
     for op, out in enumerate((o0, o1, o2, o3)):
-        h = m ^ sent(op)
+        h = sent(FIRST_GRAD, op)
         normed = head(mixed_ref, h)[...] * inverse
         grad = (inverse * (head(c_ref, h)[...].astype(WIDE) - normed * projection)).astype(LOW)
         head(g_ref, h)[...] = grad
@@ -127,12 +142,11 @@
 
 def back_kernel(features, q_ref, k_ref, v_ref, g_ref, scores_ref, mixed_ref, sums_ref, p0, p1, p2, p3,
                 normed_ref, query_ref, key_ref, value_ref):
-    m = member_of_quad()
     count = q_ref.shape[0]
     mask = causal_mask(count)
     inverse, _ = token_scales(sums_ref, features, count)
     for op, p_ref in enumerate((p0, p1, p2, p3)):
-        h = m ^ came(op)
+        h = came(BACK, op)
         grad = head(g_ref, h)[...]
         head(normed_ref, h)[...] = (head(mixed_ref, h)[...] * inverse).astype(LOW)
         raw = dot(grad, head(v_ref, h)[...], ((1,), (1,)))
@@ -144,9 +158,8 @@
 
 
 def last_kernel(k_ref, v_ref, key_local, value_local, p0, p1, p2, p3, key_ref, value_ref):
-    m = member_of_quad()
     for op, p_ref in enumerate((p0, p1, p2, p3)):
-        h = m ^ came(op)
+        h = came(BACK_GRAD, op)
         suffix = p_ref[...]
         key = head(key_local, h)[...] + dot(head(v_ref, h)[...], suffix, ((1,), (1,)))
         head(key_ref, h)[...] = key.astype(LOW)
@@ -154,6 +167,10 @@
         head(value_ref, h)[...] = value.astype(LOW)
 
 
+def quad_steps(quads, before):
+    return (2, 3, 1) if quads == 4 and before else range(quads - 1, 0, -1)
+
+
 def quad_targets(quads, step, before):
     targets = [z ^ step for z in range(quads)]
     if quads == 4 and step == 3:
@@ -163,20 +180,21 @@
 
 def sums_kernel(before, quads, *refs):
     index = lax.axis_index("seq")
-    m, quad = index % QUAD, index // QUAD
+    quad = index // QUAD
+    first, back = (FIRST, BACK) if before else (FIRST_GRAD, BACK_GRAD)
     held, got, outs = refs[:QUAD], refs[QUAD : QUAD + quads - 1], refs[-QUAD:]
 
     def counts(a, b):
         return jnp.where(a < b if before else a > b, 1.0, 0.0).astype(WIDE)
 
     outer = jnp.zeros((DH, DH), WIDE)
-    for step, total in zip(range(quads - 1, 0, -1), got):
+    for step, total in zip(quad_steps(quads, before), got):
         outer = outer + total[...].astype(WIDE) * counts(quad ^ step, quad)
     pieces = [piece[...].astype(WIDE) for piece in held]
     for to in OPS:
         inner = outer
         for op in OPS:
-            inner = inner + pieces[op] * counts(m ^ came(op), m ^ sent(to))
+            inner = inner + pieces[op] * counts(came(first, op), sent(back, to))
         outs[to][...] = inner.astype(LOW)
 
 
@@ -185,20 +203,23 @@
     return lax.ppermute(value, axis, [(i, i ^ bits) for i in range(size)])
 
 
-def cross(value, op):
+def cross(value, wave, op):
     cores = lax.axis_size("tp")
-    places = [(i, t) for i in range(lax.axis_size("seq")) for t in range(cores)]
-    bits = (3, 2, 1, 0), (3, 1, 2, 0)
-    pairs = [(i * cores + t, (i ^ bits[t % 2][op]) * cores + (t ^ 1)) for i, t in places]
+    pairs = []
+    for i in range(lax.axis_size("seq")):
+        for t in range(cores):
+            member = targets(wave, t % 2, op)[i % QUAD]
+            pairs.append((i * cores + t, (i - i % QUAD + member) * cores + (t ^ 1)))
     return lax.ppermute(value, ("seq", "tp"), pairs)
 
 
 def exclusive_sum(held, before, *after):
-    held = [cross(held[op], op) for op in OPS]
+    first, back = (FIRST, BACK) if before else (FIRST_GRAD, BACK_GRAD)
+    held = [cross(held[op], first, op) for op in OPS]
     total = sum(piece.astype(WIDE) for piece in held).astype(LOW)
     quads = lax.axis_size("seq") // QUAD
     got = []
-    for step in range(quads - 1, 0, -1):
+    for step in quad_steps(quads, before):
         targets = quad_targets(quads, step, before)
         pairs = [(z * QUAD + i, targets[z] * QUAD + i) for z in range(quads) for i in range(QUAD)]
         got.append(lax.ppermute(total, "seq", pairs))
@@ -210,7 +231,7 @@
         0,
         in_specs=vmem + [pl.BlockSpec(memory_space=pl.ANY)] * len(after),
     )
-    return [cross(sums[op], op) for op in OPS]
+    return [cross(sums[op], back, op) for op in OPS]
 
 
 def sum_over_heads(value):

time: 45.8 us -> 44.6 us (0.974)
  starting transfers between devices: 25.2 us -> 22.9 us
  waiting for transfers between devices: 13.4 us -> 14.6 us
    ppermute x16, starting transfers between devices: 16.1 us -> 14 us  [cross(): return lax.ppermute(value, ('seq', 'tp'), pairs)]
    ppermute x16, waiting for transfers between devices: 7.88 us -> 8.96 us  [cross(): return lax.ppermute(value, ('seq', 'tp'), pairs)]
  transfers between devices with their start and end apart: 23 -> 23, of which waited for: 14 -> 16; matrix products, arithmetic and copies ran while one was open for 0% -> 0% of each run, Pallas kernels for 6% -> 6%
where the time goes in v9:
time: 44.6 us; the launch traced here: 44.5 us
  starting transfers between devices  22.9 us (51%)
  waiting for transfers between devices  14.6 us (33%)
  Pallas kernels  6.24 us (14%)
  between operations  0.73 us (2%)
    ppermute x16, starting transfers between devices, cross(): return lax.ppermute(value, ('seq', 'tp'), pairs)  14 us
    ppermute x16, waiting for transfers between devices, cross(): return lax.ppermute(value, ('seq', 'tp'), pairs)  8.96 us
    ppermute x6, starting transfers between devices, exclusive_sum(): got.append(lax.ppermute(total, 'seq', pairs))  8.67 us
    pallas_call x8, Pallas kernels, call(): pl.pallas_call(kernel, out_shape=outs, in_specs=in_specs or [pl.BlockSpec...  6.24 us
    ppermute x6, waiting for transfers between devices, exclusive_sum(): got.append(lax.ppermute(total, 'seq', pairs))  4.54 us
    ppermute x1, waiting for transfers between devices, exchange(): return lax.ppermute(value, axis, [(i, i ^ bits) for i in range(size)])  1.06 us
  transfers between devices with their start and end apart: 23, of which 16 were waited for; matrix products, arithmetic and copies ran while one was open for 0% of the time, Pallas kernels for 6%

profile of v9, /device:TPU:0, one launch (start us, length us, event | category | flops | bytes accessed | tf_op | source)
XLA Modules:
  0.0 44.5 jit_solution(17847050420550875712)
XLA Ops:
  0.7 1.4 %shard_map.76 = (bf16[128,128]{1,0:T(8,128)(2,1)S(1)}, bf16[128,128]{1,0:T(8,128)(2,1)S(1)}, bf16[128,128]{1,0:T(8,128)(2,1)S(1)}, bf16[128,128]{1,0:T(8,128)(2,1)S(1)}) custom-call(bf16[256,512]{1,0:T(8,128)(2,1)} %k_ref.7, bf16[256,512]{1,0:T(8,128)(2,1)} %v_ref.7), custom_call_target="tpu_custom_call" | custom-call | flops 33554432 | bytes 655360 | tf_op jit(solution)/shard_map/pallas_call | solution.py:70
  2.1 3.4 %collective-permute-start = (bf16[128,128]{1,0:T(8,128)(2,1)S(1)}, bf16[128,128]{1,0:T(8,128)(2,1)S(1)}, u32[]{:S(2)}, u32[]{:S(2)}) collective-permute-start(bf16[128,128]{1,0:T(8,128)(2,1)S(1)} %get-tuple-element.32), channel_id=1, source_target_pairs={{0,7},{1,4},{2,5},{3,6},{4,3},{5,2},{6,1},{7,0},{8,15},{9,12},{10,... | collective-permute-start | bytes 98312 | tf_op jit(solution)/shard_map/ppermute | solution.py:213
  5.5 0.8 %collective-permute-start.1 = (bf16[128,128]{1,0:T(8,128)(2,1)S(1)}, bf16[128,128]{1,0:T(8,128)(2,1)S(1)}, u32[]{:S(2)}, u32[]{:S(2)}) collective-permute-start(bf16[128,128]{1,0:T(8,128)(2,1)S(1)} %get-tuple-element.33), channel_id=1, source_target_pairs={{0,3},{1,6},{2,7},{3,4},{4,1},{5,0},{6,5},{7,2},{8,11},{9,14},{10,... | collective-permute-start | bytes 98312 | tf_op jit(solution)/shard_map/ppermute | solution.py:213
  6.4 0.9 %collective-permute-start.2 = (bf16[128,128]{1,0:T(8,128)(2,1)S(1)}, bf16[128,128]{1,0:T(8,128)(2,1)S(1)}, u32[]{:S(2)}, u32[]{:S(2)}) collective-permute-start(bf16[128,128]{1,0:T(8,128)(2,1)S(1)} %get-tuple-element.34), channel_id=1, source_target_pairs={{0,5},{1,2},{2,1},{3,0},{4,7},{5,6},{6,3},{7,4},{8,13},{9,10},{10,... | collective-permute-start | bytes 98312 | tf_op jit(solution)/shard_map/ppermute | solution.py:213
  7.3 1.9 %collective-permute-done.1.refs_1_ = bf16[128,128]{1,0:T(8,128)(2,1)S(1)} collective-permute-done((bf16[128,128]{1,0:T(8,128)(2,1)S(1)}, bf16[128,128]{1,0:T(8,128)(2,1)S(1)}, u32[]{:S(2)}, u32[]{:S(2)}) %collective-permute-start.1) | collective-permute-done | bytes 32800 | tf_op jit(solution)/shard_map/ppermute | solution.py:213
  9.1 0.8 %collective-permute-done.2.refs_2_ = bf16[128,128]{1,0:T(8,128)(2,1)S(1)} collective-permute-done((bf16[128,128]{1,0:T(8,128)(2,1)S(1)}, bf16[128,128]{1,0:T(8,128)(2,1)S(1)}, u32[]{:S(2)}, u32[]{:S(2)}) %collective-permute-start.2) | collective-permute-done | bytes 32800 | tf_op jit(solution)/shard_map/ppermute | solution.py:213
  10.0 2.7 %collective-permute-start.4 = (bf16[128,128]{1,0:T(8,128)(2,1)S(1)}, bf16[128,128]{1,0:T(8,128)(2,1)S(1)}, u32[]{:S(2)}, u32[]{:S(2)}) collective-permute-start(bf16[128,128]{1,0:T(8,128)(2,1)S(1)} %add_convert_fusion.1), channel_id=1, source_target_pairs={{0,16},{2,18},{4,20},{6,22},{8,24},{10,26},{12,28},{14,30},{16,0},... | collective-permute-start | bytes 98312 | tf_op jit(solution)/shard_map/ppermute | solution.py:225
  12.7 1.3 %collective-permute-start.5 = (bf16[128,128]{1,0:T(8,128)(2,1)S(1)}, bf16[128,128]{1,0:T(8,128)(2,1)S(1)}, u32[]{:S(2)}, u32[]{:S(2)}) collective-permute-start(bf16[128,128]{1,0:T(8,128)(2,1)S(1)} %add_convert_fusion.1), channel_id=1, source_target_pairs={{0,24},{2,26},{4,28},{6,30},{8,16},{10,18},{12,20},{14,22},{16,0},... | collective-permute-start | bytes 98312 | tf_op jit(solution)/shard_map/ppermute | solution.py:225
  14.2 1.0 %collective-permute-done.4.refs_4_ = bf16[128,128]{1,0:T(8,128)(2,1)S(1)} collective-permute-done((bf16[128,128]{1,0:T(8,128)(2,1)S(1)}, bf16[128,128]{1,0:T(8,128)(2,1)S(1)}, u32[]{:S(2)}, u32[]{:S(2)}) %collective-permute-start.4) | collective-permute-done | bytes 32800 | tf_op jit(solution)/shard_map/ppermute | solution.py:225
  15.2 2.5 %collective-permute-done.5.refs_5_ = bf16[128,128]{1,0:T(8,128)(2,1)S(1)} collective-permute-done((bf16[128,128]{1,0:T(8,128)(2,1)S(1)}, bf16[128,128]{1,0:T(8,128)(2,1)S(1)}, u32[]{:S(2)}, u32[]{:S(2)}) %collective-permute-start.5) | collective-permute-done | bytes 32800 | tf_op jit(solution)/shard_map/ppermute | solution.py:225
  18.2 1.7 %collective-permute-start.8 = (bf16[128,128]{1,0:T(8,128)(2,1)S(1)}, bf16[128,128]{1,0:T(8,128)(2,1)S(1)}, u32[]{:S(2)}, u32[]{:S(2)}) collective-permute-start(bf16[128,128]{1,0:T(8,128)(2,1)S(1)} %get-tuple-element.37), channel_id=1, source_target_pairs={{0,5},{1,4},{2,7},{3,6},{4,1},{5,2},{6,3},{7,0},{8,13},{9,12},{10,... | collective-permute-start | bytes 98312 | tf_op jit(solution)/shard_map/ppermute | solution.py:213
  20.0 0.4 collective-permute-start.10
  20.4 0.7 %shard_map.75 = (bf16[4,256,256]{2,1,0:T(8,128)(2,1)S(1)}, f32[256,512]{1,0:T(8,128)S(1)}) custom-call(bf16[256,512]{1,0:T(8,128)(2,1)S(1)} %copy-done.2, bf16[256,512]{1,0:T(8,128)(2,1)S(1)} %copy-done, bf16[256,512]{1,0:T(8,128)(2,1)S(1)} %copy-done.1), custom_call_target="tpu_custom_call" | custom-call | flops 134217728 | bytes 1835008 | tf_op jit(solution)/shard_map/pallas_call | solution.py:70
  21.1 0.8 %collective-permute-done.7.p0 = bf16[128,128]{1,0:T(8,128)(2,1)S(1)} collective-permute-done((bf16[128,128]{1,0:T(8,128)(2,1)S(1)}, bf16[128,128]{1,0:T(8,128)(2,1)S(1)}, u32[]{:S(2)}, u32[]{:S(2)}) %collective-permute-start.7) | collective-permute-done | bytes 32800 | tf_op jit(solution)/shard_map/ppermute | solution.py:213
  21.9 0.6 %collective-permute-done.8.p1 = bf16[128,128]{1,0:T(8,128)(2,1)S(1)} collective-permute-done((bf16[128,128]{1,0:T(8,128)(2,1)S(1)}, bf16[128,128]{1,0:T(8,128)(2,1)S(1)}, u32[]{:S(2)}, u32[]{:S(2)}) %collective-permute-start.8) | collective-permute-done | bytes 32800 | tf_op jit(solution)/shard_map/ppermute | solution.py:213
  22.5 1.1 %collective-permute-done.9.p2 = bf16[128,128]{1,0:T(8,128)(2,1)S(1)} collective-permute-done((bf16[128,128]{1,0:T(8,128)(2,1)S(1)}, bf16[128,128]{1,0:T(8,128)(2,1)S(1)}, u32[]{:S(2)}, u32[]{:S(2)}) %collective-permute-start.9) | collective-permute-done | bytes 32800 | tf_op jit(solution)/shard_map/ppermute | solution.py:213
  24.2 1.1 %collective-permute-done.11 = f32[2,256]{1,0:T(2,128)S(1)} collective-permute-done((f32[2,256]{1,0:T(2,128)S(1)}, f32[2,256]{1,0:T(2,128)S(1)}, u32[]{:S(2)}, u32[]{:S(2)}) %collective-permute-start.11) | collective-permute-done | bytes 2080 | tf_op jit(solution)/shard_map/ppermute | solution.py:203
  25.2 0.4 %shard_map.79 = (bf16[128,128]{1,0:T(8,128)(2,1)S(1)}, bf16[128,128]{1,0:T(8,128)(2,1)S(1)}, bf16[128,128]{1,0:T(8,128)(2,1)S(1)}, bf16[128,128]{1,0:T(8,128)(2,1)S(1)}, bf16[256,512]{1,0:T(8,128)(2,1)S(1)}) custom-call(f32[256,512]{1,0:T(8,128)S(1)} %get-tuple-element.40.mixed_ref, bf16[256,512]{1,0:T(8,128)(2,1)S(1)} %copy-done.3, ...), custom_call_target="tpu_custom_call" | custom-call | flops 33554432 | bytes 1443840 | tf_op jit(solution)/shard_map/pallas_call | solution.py:70
  25.7 1.1 %collective-permute-start.12 = (bf16[128,128]{1,0:T(8,128)(2,1)S(1)}, bf16[128,128]{1,0:T(8,128)(2,1)S(1)}, u32[]{:S(2)}, u32[]{:S(2)}) collective-permute-start(bf16[128,128]{1,0:T(8,128)(2,1)S(1)} %get-tuple-element.48), channel_id=1, source_target_pairs={{0,7},{1,6},{2,5},{3,4},{4,3},{5,2},{6,1},{7,0},{8,15},{9,14},{10,... | collective-permute-start | bytes 98312 | tf_op jit(solution)/shard_map/ppermute | solution.py:213
  27.0 1.5 %collective-permute-start.14 = (bf16[128,128]{1,0:T(8,128)(2,1)S(1)}, bf16[128,128]{1,0:T(8,128)(2,1)S(1)}, u32[]{:S(2)}, u32[]{:S(2)}) collective-permute-start(bf16[128,128]{1,0:T(8,128)(2,1)S(1)} %get-tuple-element.50), channel_id=1, source_target_pairs={{0,3},{1,4},{2,1},{3,6},{4,7},{5,0},{6,5},{7,2},{8,11},{9,12},{10,... | collective-permute-start | bytes 98312 | tf_op jit(solution)/shard_map/ppermute | solution.py:213
  28.9 1.1 %collective-permute-done.12.refs_0_ = bf16[128,128]{1,0:T(8,128)(2,1)S(1)} collective-permute-done((bf16[128,128]{1,0:T(8,128)(2,1)S(1)}, bf16[128,128]{1,0:T(8,128)(2,1)S(1)}, u32[]{:S(2)}, u32[]{:S(2)}) %collective-permute-start.12) | collective-permute-done | bytes 32800 | tf_op jit(solution)/shard_map/ppermute | solution.py:213
  30.3 0.6 %collective-permute-done.14.refs_2_ = bf16[128,128]{1,0:T(8,128)(2,1)S(1)} collective-permute-done((bf16[128,128]{1,0:T(8,128)(2,1)S(1)}, bf16[128,128]{1,0:T(8,128)(2,1)S(1)}, u32[]{:S(2)}, u32[]{:S(2)}) %collective-permute-start.14) | collective-permute-done | bytes 32800 | tf_op jit(solution)/shard_map/ppermute | solution.py:213
  30.9 1.7 %collective-permute-start.16 = (bf16[128,128]{1,0:T(8,128)(2,1)S(1)}, bf16[128,128]{1,0:T(8,128)(2,1)S(1)}, u32[]{:S(2)}, u32[]{:S(2)}) collective-permute-start(bf16[128,128]{1,0:T(8,128)(2,1)S(1)} %add_convert_fusion), channel_id=1, source_target_pairs={{0,16},{2,18},{4,20},{6,22},{8,24},{10,26},{12,28},{14,30},{16,8},... | collective-permute-start | bytes 98312 | tf_op jit(solution)/shard_map/ppermute | solution.py:225
  32.6 0.9 %collective-permute-start.17 = (bf16[128,128]{1,0:T(8,128)(2,1)S(1)}, bf16[128,128]{1,0:T(8,128)(2,1)S(1)}, u32[]{:S(2)}, u32[]{:S(2)}) collective-permute-start(bf16[128,128]{1,0:T(8,128)(2,1)S(1)} %add_convert_fusion), channel_id=1, source_target_pairs={{0,16},{2,18},{4,20},{6,22},{8,24},{10,26},{12,28},{14,30},{16,0},... | collective-permute-start | bytes 98312 | tf_op jit(solution)/shard_map/ppermute | solution.py:225
  33.5 1.9 %collective-permute-start.18 = (bf16[128,128]{1,0:T(8,128)(2,1)S(1)}, bf16[128,128]{1,0:T(8,128)(2,1)S(1)}, u32[]{:S(2)}, u32[]{:S(2)}) collective-permute-start(bf16[128,128]{1,0:T(8,128)(2,1)S(1)} %add_convert_fusion), channel_id=1, source_target_pairs={{0,8},{2,10},{4,12},{6,14},{8,0},{10,2},{12,4},{14,6},{16,24},{18,... | collective-permute-start | bytes 98312 | tf_op jit(solution)/shard_map/ppermute | solution.py:225
  35.4 2.0 %shard_map.80 = (bf16[256,512]{1,0:T(8,128)(2,1)}, bf16[256,512]{1,0:T(8,128)(2,1)}, f32[256,512]{1,0:T(8,128)S(1)}, f32[256,512]{1,0:T(8,128)S(1)}) custom-call(bf16[256,512]{1,0:T(8,128)(2,1)S(1)} %copy-done.2, bf16[256,512]{1,0:T(8,128)(2,1)S(1)} %copy-done, bf16[256,512]{1,0:T(8,128)(2,1)S(1)} %copy-done.1, ...), custom_call_target="tpu_custom_call" | custom-call | flops 301989888 | bytes 3803136 | tf_op jit(solution)/shard_map/pallas_call | solution.py:70
  38.3 1.7 %collective-permute-start.20 = (bf16[128,128]{1,0:T(8,128)(2,1)S(1)}, bf16[128,128]{1,0:T(8,128)(2,1)S(1)}, u32[]{:S(2)}, u32[]{:S(2)}) collective-permute-start(bf16[128,128]{1,0:T(8,128)(2,1)S(1)} %get-tuple-element.53), channel_id=1, source_target_pairs={{0,5},{1,2},{2,7},{3,4},{4,1},{5,6},{6,3},{7,0},{8,13},{9,10},{10,... | collective-permute-start | bytes 98312 | tf_op jit(solution)/shard_map/ppermute | solution.py:213
  40.0 0.6 %collective-permute-start.21 = (bf16[128,128]{1,0:T(8,128)(2,1)S(1)}, bf16[128,128]{1,0:T(8,128)(2,1)S(1)}, u32[]{:S(2)}, u32[]{:S(2)}) collective-permute-start(bf16[128,128]{1,0:T(8,128)(2,1)S(1)} %get-tuple-element.54), channel_id=1, source_target_pairs={{0,3},{1,6},{2,1},{3,0},{4,7},{5,2},{6,5},{7,4},{8,11},{9,14},{10,... | collective-permute-start | bytes 98312 | tf_op jit(solution)/shard_map/ppermute | solution.py:213
  40.6 1.1 %collective-permute-start.22 = (bf16[128,128]{1,0:T(8,128)(2,1)S(1)}, bf16[128,128]{1,0:T(8,128)(2,1)S(1)}, u32[]{:S(2)}, u32[]{:S(2)}) collective-permute-start(bf16[128,128]{1,0:T(8,128)(2,1)S(1)} %get-tuple-element.55), channel_id=1, source_target_pairs={{0,1},{1,0},{2,3},{3,2},{4,5},{5,4},{6,7},{7,6},{8,9},{9,8},{10,11... | collective-permute-start | bytes 98312 | tf_op jit(solution)/shard_map/ppermute | solution.py:213
  41.7 1.1 %collective-permute-done.20.p1 = bf16[128,128]{1,0:T(8,128)(2,1)S(1)} collective-permute-done((bf16[128,128]{1,0:T(8,128)(2,1)S(1)}, bf16[128,128]{1,0:T(8,128)(2,1)S(1)}, u32[]{:S(2)}, u32[]{:S(2)}) %collective-permute-start.20) | collective-permute-done | bytes 32800 | tf_op jit(solution)/shard_map/ppermute | solution.py:213
  42.8 0.6 %collective-permute-done.21.p2 = bf16[128,128]{1,0:T(8,128)(2,1)S(1)} collective-permute-done((bf16[128,128]{1,0:T(8,128)(2,1)S(1)}, bf16[128,128]{1,0:T(8,128)(2,1)S(1)}, u32[]{:S(2)}, u32[]{:S(2)}) %collective-permute-start.21) | collective-permute-done | bytes 32800 | tf_op jit(solution)/shard_map/ppermute | solution.py:213
  43.4 1.1 %shard_map.82 = (bf16[256,512]{1,0:T(8,128)(2,1)}, bf16[256,512]{1,0:T(8,128)(2,1)}) custom-call(bf16[256,512]{1,0:T(8,128)(2,1)S(1)} %copy-done, bf16[256,512]{1,0:T(8,128)(2,1)S(1)} %copy-done.1, f32[256,512]{1,0:T(8,128)S(1)} %get-tuple-element.46.refs_7_.key_local, f32[256,512]{1,0:T(8,128)S(1)} %get-tuple-element.47.value_local, ...), custom_call_target="tpu_custom_call" | custom-call | flops 67108864 | bytes 2228224 | tf_op jit(solution)/shard_map/pallas_call | solution.py:70
  (33 shorter events, 3.2 us)
Async XLA Ops:
  0.6 19.8 %copy-start.1 = (bf16[256,512]{1,0:T(8,128)(2,1)S(1)}, bf16[256,512]{1,0:T(8,128)(2,1)}, u32[]{:S(2)}) copy-start(bf16[256,512]{1,0:T(8,128)(2,1)} %v_ref.7) | copy-start | bytes 786436
  0.6 19.8 %copy-start.2 = (bf16[256,512]{1,0:T(8,128)(2,1)S(1)}, bf16[256,512]{1,0:T(8,128)(2,1)}, u32[]{:S(2)}) copy-start(bf16[256,512]{1,0:T(8,128)(2,1)} %q_ref.7) | copy-start | bytes 786436
  2.1 18.3 %copy-start = (bf16[256,512]{1,0:T(8,128)(2,1)S(1)}, bf16[256,512]{1,0:T(8,128)(2,1)}, u32[]{:S(2)}) copy-start(bf16[256,512]{1,0:T(8,128)(2,1)} %k_ref.7) | copy-start | bytes 786436
  2.1 5.1 %collective-permute-start = (bf16[128,128]{1,0:T(8,128)(2,1)S(1)}, bf16[128,128]{1,0:T(8,128)(2,1)S(1)}, u32[]{:S(2)}, u32[]{:S(2)}) collective-permute-start(bf16[128,128]{1,0:T(8,128)(2,1)S(1)} %get-tuple-element.32), channel_id=1, source_target_pairs={{0,7},{1,4},{2,5},{3,6},{4,3},{5,2},{6,1},{7,0},{8,15},{9,12},{10,... | collective-permute-start | bytes 98312 | tf_op jit(solution)/shard_map/ppermute | solution.py:213
  5.5 3.6 %collective-permute-start.1 = (bf16[128,128]{1,0:T(8,128)(2,1)S(1)}, bf16[128,128]{1,0:T(8,128)(2,1)S(1)}, u32[]{:S(2)}, u32[]{:S(2)}) collective-permute-start(bf16[128,128]{1,0:T(8,128)(2,1)S(1)} %get-tuple-element.33), channel_id=1, source_target_pairs={{0,3},{1,6},{2,7},{3,4},{4,1},{5,0},{6,5},{7,2},{8,11},{9,14},{10,... | collective-permute-start | bytes 98312 | tf_op jit(solution)/shard_map/ppermute | solution.py:213
  6.4 3.6 %collective-permute-start.2 = (bf16[128,128]{1,0:T(8,128)(2,1)S(1)}, bf16[128,128]{1,0:T(8,128)(2,1)S(1)}, u32[]{:S(2)}, u32[]{:S(2)}) collective-permute-start(bf16[128,128]{1,0:T(8,128)(2,1)S(1)} %get-tuple-element.34), channel_id=1, source_target_pairs={{0,5},{1,2},{2,1},{3,0},{4,7},{5,6},{6,3},{7,4},{8,13},{9,10},{10,... | collective-permute-start | bytes 98312 | tf_op jit(solution)/shard_map/ppermute | solution.py:213
  7.3 2.7 %collective-permute-start.3 = (bf16[128,128]{1,0:T(8,128)(2,1)S(1)}, bf16[128,128]{1,0:T(8,128)(2,1)S(1)}, u32[]{:S(2)}, u32[]{:S(2)}) collective-permute-start(bf16[128,128]{1,0:T(8,128)(2,1)S(1)} %get-tuple-element.35), channel_id=1, source_target_pairs={{0,1},{1,0},{2,3},{3,2},{4,5},{5,4},{6,7},{7,6},{8,9},{9,8},{10,11... | collective-permute-start | bytes 98312 | tf_op jit(solution)/shard_map/ppermute | solution.py:213
  10.0 5.2 %collective-permute-start.4 = (bf16[128,128]{1,0:T(8,128)(2,1)S(1)}, bf16[128,128]{1,0:T(8,128)(2,1)S(1)}, u32[]{:S(2)}, u32[]{:S(2)}) collective-permute-start(bf16[128,128]{1,0:T(8,128)(2,1)S(1)} %add_convert_fusion.1), channel_id=1, source_target_pairs={{0,16},{2,18},{4,20},{6,22},{8,24},{10,26},{12,28},{14,30},{16,0},... | collective-permute-start | bytes 98312 | tf_op jit(solution)/shard_map/ppermute | solution.py:225
  12.7 5.1 %collective-permute-start.5 = (bf16[128,128]{1,0:T(8,128)(2,1)S(1)}, bf16[128,128]{1,0:T(8,128)(2,1)S(1)}, u32[]{:S(2)}, u32[]{:S(2)}) collective-permute-start(bf16[128,128]{1,0:T(8,128)(2,1)S(1)} %add_convert_fusion.1), channel_id=1, source_target_pairs={{0,24},{2,26},{4,28},{6,30},{8,16},{10,18},{12,20},{14,22},{16,0},... | collective-permute-start | bytes 98312 | tf_op jit(solution)/shard_map/ppermute | solution.py:225
  14.0 4.0 %collective-permute-start.6 = (bf16[128,128]{1,0:T(8,128)(2,1)S(1)}, bf16[128,128]{1,0:T(8,128)(2,1)S(1)}, u32[]{:S(2)}, u32[]{:S(2)}) collective-permute-start(bf16[128,128]{1,0:T(8,128)(2,1)S(1)} %add_convert_fusion.1), channel_id=1, source_target_pairs={{0,8},{2,10},{4,12},{6,14},{8,0},{10,2},{12,4},{14,6},{16,24},{18,... | collective-permute-start | bytes 98312 | tf_op jit(solution)/shard_map/ppermute | solution.py:225
  18.2 3.7 %collective-permute-start.7 = (bf16[128,128]{1,0:T(8,128)(2,1)S(1)}, bf16[128,128]{1,0:T(8,128)(2,1)S(1)}, u32[]{:S(2)}, u32[]{:S(2)}) collective-permute-start(bf16[128,128]{1,0:T(8,128)(2,1)S(1)} %get-tuple-element.36), channel_id=1, source_target_pairs={{0,7},{1,6},{2,5},{3,4},{4,3},{5,0},{6,1},{7,2},{8,15},{9,14},{10,... | collective-permute-start | bytes 98312 | tf_op jit(solution)/shard_map/ppermute | solution.py:213
  18.2 4.3 %collective-permute-start.8 = (bf16[128,128]{1,0:T(8,128)(2,1)S(1)}, bf16[128,128]{1,0:T(8,128)(2,1)S(1)}, u32[]{:S(2)}, u32[]{:S(2)}) collective-permute-start(bf16[128,128]{1,0:T(8,128)(2,1)S(1)} %get-tuple-element.37), channel_id=1, source_target_pairs={{0,5},{1,4},{2,7},{3,6},{4,1},{5,2},{6,3},{7,0},{8,13},{9,12},{10,... | collective-permute-start | bytes 98312 | tf_op jit(solution)/shard_map/ppermute | solution.py:213
  20.0 3.7 %collective-permute-start.9 = (bf16[128,128]{1,0:T(8,128)(2,1)S(1)}, bf16[128,128]{1,0:T(8,128)(2,1)S(1)}, u32[]{:S(2)}, u32[]{:S(2)}) collective-permute-start(bf16[128,128]{1,0:T(8,128)(2,1)S(1)} %get-tuple-element.38), channel_id=1, source_target_pairs={{0,3},{1,2},{2,1},{3,0},{4,7},{5,6},{6,5},{7,4},{8,11},{9,10},{10,... | collective-permute-start | bytes 98312 | tf_op jit(solution)/shard_map/ppermute | solution.py:213
  20.0 3.6 %copy-start.3 = (bf16[256,512]{1,0:T(8,128)(2,1)S(1)}, bf16[256,512]{1,0:T(8,128)(2,1)}, u32[]{:S(2)}) copy-start(bf16[256,512]{1,0:T(8,128)(2,1)} %c_ref.3) | copy-start | bytes 786436
  20.0 3.6 %collective-permute-start.10 = (bf16[128,128]{1,0:T(8,128)(2,1)S(1)}, bf16[128,128]{1,0:T(8,128)(2,1)S(1)}, u32[]{:S(2)}, u32[]{:S(2)}) collective-permute-start(bf16[128,128]{1,0:T(8,128)(2,1)S(1)} %get-tuple-element.39), channel_id=1, source_target_pairs={{0,1},{1,0},{2,3},{3,2},{4,5},{5,4},{6,7},{7,6},{8,9},{9,8},{10,11... | collective-permute-start | bytes 98312 | tf_op jit(solution)/shard_map/ppermute | solution.py:213
  24.0 1.2 %collective-permute-start.11 = (f32[2,256]{1,0:T(2,128)S(1)}, f32[2,256]{1,0:T(2,128)S(1)}, u32[]{:S(2)}, u32[]{:S(2)}) collective-permute-start(f32[2,256]{1,0:T(2,128)S(1)} %get-tuple-element.41), channel_id=1, source_target_pairs={{0,1},{1,0},{2,3},{3,2},{4,5},{5,4},{6,7},{7,6},{8,9},{9,8},{10,11... | collective-permute-start | bytes 6152 | tf_op jit(solution)/shard_map/ppermute | solution.py:203
  25.7 4.3 %collective-permute-start.12 = (bf16[128,128]{1,0:T(8,128)(2,1)S(1)}, bf16[128,128]{1,0:T(8,128)(2,1)S(1)}, u32[]{:S(2)}, u32[]{:S(2)}) collective-permute-start(bf16[128,128]{1,0:T(8,128)(2,1)S(1)} %get-tuple-element.48), channel_id=1, source_target_pairs={{0,7},{1,6},{2,5},{3,4},{4,3},{5,2},{6,1},{7,0},{8,15},{9,14},{10,... | collective-permute-start | bytes 98312 | tf_op jit(solution)/shard_map/ppermute | solution.py:213
  26.8 3.5 %collective-permute-start.13 = (bf16[128,128]{1,0:T(8,128)(2,1)S(1)}, bf16[128,128]{1,0:T(8,128)(2,1)S(1)}, u32[]{:S(2)}, u32[]{:S(2)}) collective-permute-start(bf16[128,128]{1,0:T(8,128)(2,1)S(1)} %get-tuple-element.49), channel_id=1, source_target_pairs={{0,5},{1,2},{2,7},{3,0},{4,1},{5,6},{6,3},{7,4},{8,13},{9,10},{10,... | collective-permute-start | bytes 98312 | tf_op jit(solution)/shard_map/ppermute | solution.py:213
  27.0 3.9 %collective-permute-start.14 = (bf16[128,128]{1,0:T(8,128)(2,1)S(1)}, bf16[128,128]{1,0:T(8,128)(2,1)S(1)}, u32[]{:S(2)}, u32[]{:S(2)}) collective-permute-start(bf16[128,128]{1,0:T(8,128)(2,1)S(1)} %get-tuple-element.50), channel_id=1, source_target_pairs={{0,3},{1,4},{2,1},{3,6},{4,7},{5,0},{6,5},{7,2},{8,11},{9,12},{10,... | collective-permute-start | bytes 98312 | tf_op jit(solution)/shard_map/ppermute | solution.py:213
  28.6 2.4 %collective-permute-start.15 = (bf16[128,128]{1,0:T(8,128)(2,1)S(1)}, bf16[128,128]{1,0:T(8,128)(2,1)S(1)}, u32[]{:S(2)}, u32[]{:S(2)}) collective-permute-start(bf16[128,128]{1,0:T(8,128)(2,1)S(1)} %get-tuple-element.51), channel_id=1, source_target_pairs={{0,1},{1,0},{2,3},{3,2},{4,5},{5,4},{6,7},{7,6},{8,9},{9,8},{10,11... | collective-permute-start | bytes 98312 | tf_op jit(solution)/shard_map/ppermute | solution.py:213
  30.9 6.5 %collective-permute-start.16 = (bf16[128,128]{1,0:T(8,128)(2,1)S(1)}, bf16[128,128]{1,0:T(8,128)(2,1)S(1)}, u32[]{:S(2)}, u32[]{:S(2)}) collective-permute-start(bf16[128,128]{1,0:T(8,128)(2,1)S(1)} %add_convert_fusion), channel_id=1, source_target_pairs={{0,16},{2,18},{4,20},{6,22},{8,24},{10,26},{12,28},{14,30},{16,8},... | collective-permute-start | bytes 98312 | tf_op jit(solution)/shard_map/ppermute | solution.py:225
  32.6 5.2 %collective-permute-start.17 = (bf16[128,128]{1,0:T(8,128)(2,1)S(1)}, bf16[128,128]{1,0:T(8,128)(2,1)S(1)}, u32[]{:S(2)}, u32[]{:S(2)}) collective-permute-start(bf16[128,128]{1,0:T(8,128)(2,1)S(1)} %add_convert_fusion), channel_id=1, source_target_pairs={{0,16},{2,18},{4,20},{6,22},{8,24},{10,26},{12,28},{14,30},{16,0},... | collective-permute-start | bytes 98312 | tf_op jit(solution)/shard_map/ppermute | solution.py:225
  33.5 4.6 %collective-permute-start.18 = (bf16[128,128]{1,0:T(8,128)(2,1)S(1)}, bf16[128,128]{1,0:T(8,128)(2,1)S(1)}, u32[]{:S(2)}, u32[]{:S(2)}) collective-permute-start(bf16[128,128]{1,0:T(8,128)(2,1)S(1)} %add_convert_fusion), channel_id=1, source_target_pairs={{0,8},{2,10},{4,12},{6,14},{8,0},{10,2},{12,4},{14,6},{16,24},{18,... | collective-permute-start | bytes 98312 | tf_op jit(solution)/shard_map/ppermute | solution.py:225
  38.2 3.5 %collective-permute-start.19 = (bf16[128,128]{1,0:T(8,128)(2,1)S(1)}, bf16[128,128]{1,0:T(8,128)(2,1)S(1)}, u32[]{:S(2)}, u32[]{:S(2)}) collective-permute-start(bf16[128,128]{1,0:T(8,128)(2,1)S(1)} %get-tuple-element.52), channel_id=1, source_target_pairs={{0,7},{1,4},{2,5},{3,6},{4,3},{5,0},{6,1},{7,2},{8,15},{9,12},{10,... | collective-permute-start | bytes 98312 | tf_op jit(solution)/shard_map/ppermute | solution.py:213
  38.3 4.5 %collective-permute-start.20 = (bf16[128,128]{1,0:T(8,128)(2,1)S(1)}, bf16[128,128]{1,0:T(8,128)(2,1)S(1)}, u32[]{:S(2)}, u32[]{:S(2)}) collective-permute-start(bf16[128,128]{1,0:T(8,128)(2,1)S(1)} %get-tuple-element.53), channel_id=1, source_target_pairs={{0,5},{1,2},{2,7},{3,4},{4,1},{5,6},{6,3},{7,0},{8,13},{9,10},{10,... | collective-permute-start | bytes 98312 | tf_op jit(solution)/shard_map/ppermute | solution.py:213
  40.0 3.3 %collective-permute-start.21 = (bf16[128,128]{1,0:T(8,128)(2,1)S(1)}, bf16[128,128]{1,0:T(8,128)(2,1)S(1)}, u32[]{:S(2)}, u32[]{:S(2)}) collective-permute-start(bf16[128,128]{1,0:T(8,128)(2,1)S(1)} %get-tuple-element.54), channel_id=1, source_target_pairs={{0,3},{1,6},{2,1},{3,0},{4,7},{5,2},{6,5},{7,4},{8,11},{9,14},{10,... | collective-permute-start | bytes 98312 | tf_op jit(solution)/shard_map/ppermute | solution.py:213
  40.6 2.8 %collective-permute-start.22 = (bf16[128,128]{1,0:T(8,128)(2,1)S(1)}, bf16[128,128]{1,0:T(8,128)(2,1)S(1)}, u32[]{:S(2)}, u32[]{:S(2)}) collective-permute-start(bf16[128,128]{1,0:T(8,128)(2,1)S(1)} %get-tuple-element.55), channel_id=1, source_target_pairs={{0,1},{1,0},{2,3},{3,2},{4,5},{5,4},{6,7},{7,6},{8,9},{9,8},{10,11... | collective-permute-start | bytes 98312 | tf_op jit(solution)/shard_map/ppermute | solution.py:213

commit v10 on v9

--- a/solution.py
+++ b/solution.py
@@ -37,10 +37,10 @@
     return lax.axis_index("seq") % QUAD
 
 
-FIRST = (((3, 2, 1, 0), (1, 3, 0, 2), (2, 0, 3, 1)), ((2, 3, 1, 0), (3, 2, 0, 1), (1, 0, 3, 2)))
-BACK = (((3, 2, 1, 0), (2, 3, 0, 1), (1, 0, 3, 2)), ((3, 2, 0, 1), (2, 3, 1, 0), (1, 0, 3, 2)))
-FIRST_GRAD = (((3, 2, 1, 0), (2, 3, 0, 1), (1, 0, 3, 2)), ((3, 2, 1, 0), (1, 0, 3, 2), (2, 3, 0, 1)))
-BACK_GRAD = (((3, 2, 1, 0), (2, 3, 0, 1), (1, 0, 3, 2)), ((2, 3, 0, 1), (1, 2, 3, 0), (3, 0, 1, 2)))
+FIRST = (((3, 2, 1, 0), (2, 3, 0, 1), (1, 0, 3, 2)), ((3, 2, 1, 0), (1, 3, 0, 2), (2, 0, 3, 1)))
+BACK = (((3, 2, 1, 0), (2, 0, 3, 1), (1, 3, 0, 2)), ((2, 3, 0, 1), (3, 2, 1, 0), (1, 0, 3, 2)))
+FIRST_GRAD = (((1, 0, 3, 2), (3, 2, 0, 1), (2, 3, 1, 0)), ((1, 3, 0, 2), (3, 2, 1, 0), (2, 0, 3, 1)))
+BACK_GRAD = (((3, 2, 1, 0), (1, 3, 0, 2), (2, 0, 3, 1)), ((2, 3, 1, 0), (1, 0, 3, 2), (3, 2, 0, 1)))
 SAME = (0, 1, 2, 3)
 
 

time: 44.6 us -> 44.9 us (level)
  starting transfers between devices: 22.9 us -> 25.4 us
  waiting for transfers between devices: 14.6 us -> 12.3 us
    ppermute x16, starting transfers between devices: 14 us -> 16.5 us  [cross(): return lax.ppermute(value, ('seq', 'tp'), pairs)]
    ppermute x16, waiting for transfers between devices: 8.96 us -> 6.66 us  [cross(): return lax.ppermute(value, ('seq', 'tp'), pairs)]
  transfers between devices with their start and end apart: 23 -> 23, of which waited for: 16 -> 14; matrix products, arithmetic and copies ran while one was open for 0% -> 0% of each run, Pallas kernels for 6% -> 6%
where the time goes in v10:
time: 44.9 us; the launch traced here: 44.7 us
  starting transfers between devices  25.4 us (57%)
  waiting for transfers between devices  12.3 us (27%)
  Pallas kernels  6.24 us (14%)
  between operations  0.73 us (2%)
    ppermute x16, starting transfers between devices, cross(): return lax.ppermute(value, ('seq', 'tp'), pairs)  16.5 us
    ppermute x6, starting transfers between devices, exclusive_sum(): got.append(lax.ppermute(total, 'seq', pairs))  8.67 us
    ppermute x16, waiting for transfers between devices, cross(): return lax.ppermute(value, ('seq', 'tp'), pairs)  6.66 us
    pallas_call x8, Pallas kernels, call(): pl.pallas_call(kernel, out_shape=outs, in_specs=in_specs or [pl.BlockSpec...  6.24 us
    ppermute x6, waiting for transfers between devices, exclusive_sum(): got.append(lax.ppermute(total, 'seq', pairs))  4.62 us
    ppermute x1, waiting for transfers between devices, exchange(): return lax.ppermute(value, axis, [(i, i ^ bits) for i in range(size)])  1.05 us
  transfers between devices with their start and end apart: 23, of which 14 were waited for; matrix products, arithmetic and copies ran while one was open for 0% of the time, Pallas kernels for 6%

profile of v10, /device:TPU:0, one launch (start us, length us, event | category | flops | bytes accessed | tf_op | source)
XLA Modules:
  0.0 44.7 jit_solution(4582935113011780741)
XLA Ops:
  0.7 1.4 %shard_map.76 = (bf16[128,128]{1,0:T(8,128)(2,1)S(1)}, bf16[128,128]{1,0:T(8,128)(2,1)S(1)}, bf16[128,128]{1,0:T(8,128)(2,1)S(1)}, bf16[128,128]{1,0:T(8,128)(2,1)S(1)}) custom-call(bf16[256,512]{1,0:T(8,128)(2,1)} %k_ref.7, bf16[256,512]{1,0:T(8,128)(2,1)} %v_ref.7), custom_call_target="tpu_custom_call" | custom-call | flops 33554432 | bytes 655360 | tf_op jit(solution)/shard_map/pallas_call | solution.py:70
  2.1 3.4 %collective-permute-start = (bf16[128,128]{1,0:T(8,128)(2,1)S(1)}, bf16[128,128]{1,0:T(8,128)(2,1)S(1)}, u32[]{:S(2)}, u32[]{:S(2)}) collective-permute-start(bf16[128,128]{1,0:T(8,128)(2,1)S(1)} %get-tuple-element.32), channel_id=1, source_target_pairs={{0,7},{1,6},{2,5},{3,4},{4,3},{5,2},{6,1},{7,0},{8,15},{9,14},{10,... | collective-permute-start | bytes 98312 | tf_op jit(solution)/shard_map/ppermute | solution.py:213
  5.5 0.8 %collective-permute-start.1 = (bf16[128,128]{1,0:T(8,128)(2,1)S(1)}, bf16[128,128]{1,0:T(8,128)(2,1)S(1)}, u32[]{:S(2)}, u32[]{:S(2)}) collective-permute-start(bf16[128,128]{1,0:T(8,128)(2,1)S(1)} %get-tuple-element.33), channel_id=1, source_target_pairs={{0,5},{1,2},{2,7},{3,6},{4,1},{5,0},{6,3},{7,4},{8,13},{9,10},{10,... | collective-permute-start | bytes 98312 | tf_op jit(solution)/shard_map/ppermute | solution.py:213
  6.4 1.5 %collective-permute-start.3 = (bf16[128,128]{1,0:T(8,128)(2,1)S(1)}, bf16[128,128]{1,0:T(8,128)(2,1)S(1)}, u32[]{:S(2)}, u32[]{:S(2)}) collective-permute-start(bf16[128,128]{1,0:T(8,128)(2,1)S(1)} %get-tuple-element.35), channel_id=1, source_target_pairs={{0,1},{1,0},{2,3},{3,2},{4,5},{5,4},{6,7},{7,6},{8,9},{9,8},{10,11... | collective-permute-start | bytes 98312 | tf_op jit(solution)/shard_map/ppermute | solution.py:213
  7.9 0.9 %collective-permute-done.1.refs_1_ = bf16[128,128]{1,0:T(8,128)(2,1)S(1)} collective-permute-done((bf16[128,128]{1,0:T(8,128)(2,1)S(1)}, bf16[128,128]{1,0:T(8,128)(2,1)S(1)}, u32[]{:S(2)}, u32[]{:S(2)}) %collective-permute-start.1) | collective-permute-done | bytes 32800 | tf_op jit(solution)/shard_map/ppermute | solution.py:213
  8.9 1.1 %collective-permute-done.2.refs_2_ = bf16[128,128]{1,0:T(8,128)(2,1)S(1)} collective-permute-done((bf16[128,128]{1,0:T(8,128)(2,1)S(1)}, bf16[128,128]{1,0:T(8,128)(2,1)S(1)}, u32[]{:S(2)}, u32[]{:S(2)}) %collective-permute-start.2) | collective-permute-done | bytes 32800 | tf_op jit(solution)/shard_map/ppermute | solution.py:213
  10.0 2.7 %collective-permute-start.4 = (bf16[128,128]{1,0:T(8,128)(2,1)S(1)}, bf16[128,128]{1,0:T(8,128)(2,1)S(1)}, u32[]{:S(2)}, u32[]{:S(2)}) collective-permute-start(bf16[128,128]{1,0:T(8,128)(2,1)S(1)} %add_convert_fusion.1), channel_id=1, source_target_pairs={{0,16},{2,18},{4,20},{6,22},{8,24},{10,26},{12,28},{14,30},{16,0},... | collective-permute-start | bytes 98312 | tf_op jit(solution)/shard_map/ppermute | solution.py:225
  12.6 1.3 %collective-permute-start.5 = (bf16[128,128]{1,0:T(8,128)(2,1)S(1)}, bf16[128,128]{1,0:T(8,128)(2,1)S(1)}, u32[]{:S(2)}, u32[]{:S(2)}) collective-permute-start(bf16[128,128]{1,0:T(8,128)(2,1)S(1)} %add_convert_fusion.1), channel_id=1, source_target_pairs={{0,24},{2,26},{4,28},{6,30},{8,16},{10,18},{12,20},{14,22},{16,0},... | collective-permute-start | bytes 98312 | tf_op jit(solution)/shard_map/ppermute | solution.py:225
  14.2 1.0 %collective-permute-done.4.refs_4_ = bf16[128,128]{1,0:T(8,128)(2,1)S(1)} collective-permute-done((bf16[128,128]{1,0:T(8,128)(2,1)S(1)}, bf16[128,128]{1,0:T(8,128)(2,1)S(1)}, u32[]{:S(2)}, u32[]{:S(2)}) %collective-permute-start.4) | collective-permute-done | bytes 32800 | tf_op jit(solution)/shard_map/ppermute | solution.py:225
  15.2 2.5 %collective-permute-done.5.refs_5_ = bf16[128,128]{1,0:T(8,128)(2,1)S(1)} collective-permute-done((bf16[128,128]{1,0:T(8,128)(2,1)S(1)}, bf16[128,128]{1,0:T(8,128)(2,1)S(1)}, u32[]{:S(2)}, u32[]{:S(2)}) %collective-permute-start.5) | collective-permute-done | bytes 32800 | tf_op jit(solution)/shard_map/ppermute | solution.py:225
  18.2 1.7 %collective-permute-start.8 = (bf16[128,128]{1,0:T(8,128)(2,1)S(1)}, bf16[128,128]{1,0:T(8,128)(2,1)S(1)}, u32[]{:S(2)}, u32[]{:S(2)}) collective-permute-start(bf16[128,128]{1,0:T(8,128)(2,1)S(1)} %get-tuple-element.37), channel_id=1, source_target_pairs={{0,5},{1,6},{2,1},{3,4},{4,7},{5,2},{6,3},{7,0},{8,13},{9,14},{10,... | collective-permute-start | bytes 98312 | tf_op jit(solution)/shard_map/ppermute | solution.py:213
  19.9 0.7 %collective-permute-start.9 = (bf16[128,128]{1,0:T(8,128)(2,1)S(1)}, bf16[128,128]{1,0:T(8,128)(2,1)S(1)}, u32[]{:S(2)}, u32[]{:S(2)}) collective-permute-start(bf16[128,128]{1,0:T(8,128)(2,1)S(1)} %get-tuple-element.38), channel_id=1, source_target_pairs={{0,3},{1,2},{2,7},{3,0},{4,1},{5,6},{6,5},{7,4},{8,11},{9,10},{10,... | collective-permute-start | bytes 98312 | tf_op jit(solution)/shard_map/ppermute | solution.py:213
  20.7 0.6 %collective-permute-start.10 = (bf16[128,128]{1,0:T(8,128)(2,1)S(1)}, bf16[128,128]{1,0:T(8,128)(2,1)S(1)}, u32[]{:S(2)}, u32[]{:S(2)}) collective-permute-start(bf16[128,128]{1,0:T(8,128)(2,1)S(1)} %get-tuple-element.39), channel_id=1, source_target_pairs={{0,1},{1,0},{2,3},{3,2},{4,5},{5,4},{6,7},{7,6},{8,9},{9,8},{10,11... | collective-permute-start | bytes 98312 | tf_op jit(solution)/shard_map/ppermute | solution.py:213
  21.3 0.7 %shard_map.75 = (bf16[4,256,256]{2,1,0:T(8,128)(2,1)S(1)}, f32[256,512]{1,0:T(8,128)S(1)}) custom-call(bf16[256,512]{1,0:T(8,128)(2,1)S(1)} %copy-done.2, bf16[256,512]{1,0:T(8,128)(2,1)S(1)} %copy-done, bf16[256,512]{1,0:T(8,128)(2,1)S(1)} %copy-done.1), custom_call_target="tpu_custom_call" | custom-call | flops 134217728 | bytes 1835008 | tf_op jit(solution)/shard_map/pallas_call | solution.py:70
  22.0 0.5 %collective-permute-done.8.p1 = bf16[128,128]{1,0:T(8,128)(2,1)S(1)} collective-permute-done((bf16[128,128]{1,0:T(8,128)(2,1)S(1)}, bf16[128,128]{1,0:T(8,128)(2,1)S(1)}, u32[]{:S(2)}, u32[]{:S(2)}) %collective-permute-start.8) | collective-permute-done | bytes 32800 | tf_op jit(solution)/shard_map/ppermute | solution.py:213
  22.5 0.9 %collective-permute-done.9.p2 = bf16[128,128]{1,0:T(8,128)(2,1)S(1)} collective-permute-done((bf16[128,128]{1,0:T(8,128)(2,1)S(1)}, bf16[128,128]{1,0:T(8,128)(2,1)S(1)}, u32[]{:S(2)}, u32[]{:S(2)}) %collective-permute-start.9) | collective-permute-done | bytes 32800 | tf_op jit(solution)/shard_map/ppermute | solution.py:213
  23.9 1.1 %collective-permute-done.11 = f32[2,256]{1,0:T(2,128)S(1)} collective-permute-done((f32[2,256]{1,0:T(2,128)S(1)}, f32[2,256]{1,0:T(2,128)S(1)}, u32[]{:S(2)}, u32[]{:S(2)}) %collective-permute-start.11) | collective-permute-done | bytes 2080 | tf_op jit(solution)/shard_map/ppermute | solution.py:203
  25.5 1.2 %collective-permute-start.12 = (bf16[128,128]{1,0:T(8,128)(2,1)S(1)}, bf16[128,128]{1,0:T(8,128)(2,1)S(1)}, u32[]{:S(2)}, u32[]{:S(2)}) collective-permute-start(bf16[128,128]{1,0:T(8,128)(2,1)S(1)} %get-tuple-element.48), channel_id=1, source_target_pairs={{0,3},{1,2},{2,1},{3,6},{4,7},{5,0},{6,5},{7,4},{8,11},{9,10},{10,... | collective-permute-start | bytes 98312 | tf_op jit(solution)/shard_map/ppermute | solution.py:213
  26.6 0.5 %collective-permute-start.13 = (bf16[128,128]{1,0:T(8,128)(2,1)S(1)}, bf16[128,128]{1,0:T(8,128)(2,1)S(1)}, u32[]{:S(2)}, u32[]{:S(2)}) collective-permute-start(bf16[128,128]{1,0:T(8,128)(2,1)S(1)} %get-tuple-element.49), channel_id=1, source_target_pairs={{0,7},{1,6},{2,5},{3,4},{4,1},{5,2},{6,3},{7,0},{8,15},{9,14},{10,... | collective-permute-start | bytes 98312 | tf_op jit(solution)/shard_map/ppermute | solution.py:213
  27.2 1.3 %collective-permute-start.14 = (bf16[128,128]{1,0:T(8,128)(2,1)S(1)}, bf16[128,128]{1,0:T(8,128)(2,1)S(1)}, u32[]{:S(2)}, u32[]{:S(2)}) collective-permute-start(bf16[128,128]{1,0:T(8,128)(2,1)S(1)} %get-tuple-element.50), channel_id=1, source_target_pairs={{0,5},{1,4},{2,7},{3,0},{4,3},{5,6},{6,1},{7,2},{8,13},{9,12},{10,... | collective-permute-start | bytes 98312 | tf_op jit(solution)/shard_map/ppermute | solution.py:213
  28.8 2.0 %collective-permute-done.13.refs_1_ = bf16[128,128]{1,0:T(8,128)(2,1)S(1)} collective-permute-done((bf16[128,128]{1,0:T(8,128)(2,1)S(1)}, bf16[128,128]{1,0:T(8,128)(2,1)S(1)}, u32[]{:S(2)}, u32[]{:S(2)}) %collective-permute-start.13) | collective-permute-done | bytes 32800 | tf_op jit(solution)/shard_map/ppermute | solution.py:213
  30.9 1.5 %collective-permute-start.16 = (bf16[128,128]{1,0:T(8,128)(2,1)S(1)}, bf16[128,128]{1,0:T(8,128)(2,1)S(1)}, u32[]{:S(2)}, u32[]{:S(2)}) collective-permute-start(bf16[128,128]{1,0:T(8,128)(2,1)S(1)} %add_convert_fusion), channel_id=1, source_target_pairs={{0,16},{2,18},{4,20},{6,22},{8,24},{10,26},{12,28},{14,30},{16,8},... | collective-permute-start | bytes 98312 | tf_op jit(solution)/shard_map/ppermute | solution.py:225
  32.4 1.0 %collective-permute-start.17 = (bf16[128,128]{1,0:T(8,128)(2,1)S(1)}, bf16[128,128]{1,0:T(8,128)(2,1)S(1)}, u32[]{:S(2)}, u32[]{:S(2)}) collective-permute-start(bf16[128,128]{1,0:T(8,128)(2,1)S(1)} %add_convert_fusion), channel_id=1, source_target_pairs={{0,16},{2,18},{4,20},{6,22},{8,24},{10,26},{12,28},{14,30},{16,0},... | collective-permute-start | bytes 98312 | tf_op jit(solution)/shard_map/ppermute | solution.py:225
  33.4 1.9 %collective-permute-start.18 = (bf16[128,128]{1,0:T(8,128)(2,1)S(1)}, bf16[128,128]{1,0:T(8,128)(2,1)S(1)}, u32[]{:S(2)}, u32[]{:S(2)}) collective-permute-start(bf16[128,128]{1,0:T(8,128)(2,1)S(1)} %add_convert_fusion), channel_id=1, source_target_pairs={{0,8},{2,10},{4,12},{6,14},{8,0},{10,2},{12,4},{14,6},{16,24},{18,... | collective-permute-start | bytes 98312 | tf_op jit(solution)/shard_map/ppermute | solution.py:225
  35.4 2.0 %shard_map.80 = (bf16[256,512]{1,0:T(8,128)(2,1)}, bf16[256,512]{1,0:T(8,128)(2,1)}, f32[256,512]{1,0:T(8,128)S(1)}, f32[256,512]{1,0:T(8,128)S(1)}) custom-call(bf16[256,512]{1,0:T(8,128)(2,1)S(1)} %copy-done.2, bf16[256,512]{1,0:T(8,128)(2,1)S(1)} %copy-done, bf16[256,512]{1,0:T(8,128)(2,1)S(1)} %copy-done.1, ...), custom_call_target="tpu_custom_call" | custom-call | flops 301989888 | bytes 3803136 | tf_op jit(solution)/shard_map/pallas_call | solution.py:70
  37.6 0.6 %collective-permute-done.18.refs_6_ = bf16[128,128]{1,0:T(8,128)(2,1)S(1)} collective-permute-done((bf16[128,128]{1,0:T(8,128)(2,1)S(1)}, bf16[128,128]{1,0:T(8,128)(2,1)S(1)}, u32[]{:S(2)}, u32[]{:S(2)}) %collective-permute-start.18) | collective-permute-done | bytes 32800 | tf_op jit(solution)/shard_map/ppermute | solution.py:225
  38.3 1.1 %collective-permute-start.19 = (bf16[128,128]{1,0:T(8,128)(2,1)S(1)}, bf16[128,128]{1,0:T(8,128)(2,1)S(1)}, u32[]{:S(2)}, u32[]{:S(2)}) collective-permute-start(bf16[128,128]{1,0:T(8,128)(2,1)S(1)} %get-tuple-element.52), channel_id=1, source_target_pairs={{0,7},{1,4},{2,5},{3,6},{4,3},{5,2},{6,1},{7,0},{8,15},{9,12},{10,... | collective-permute-start | bytes 98312 | tf_op jit(solution)/shard_map/ppermute | solution.py:213
  39.4 0.6 %collective-permute-start.20 = (bf16[128,128]{1,0:T(8,128)(2,1)S(1)}, bf16[128,128]{1,0:T(8,128)(2,1)S(1)}, u32[]{:S(2)}, u32[]{:S(2)}) collective-permute-start(bf16[128,128]{1,0:T(8,128)(2,1)S(1)} %get-tuple-element.53), channel_id=1, source_target_pairs={{0,3},{1,2},{2,7},{3,0},{4,1},{5,6},{6,5},{7,4},{8,11},{9,10},{10,... | collective-permute-start | bytes 98312 | tf_op jit(solution)/shard_map/ppermute | solution.py:213
  40.0 1.2 %collective-permute-start.21 = (bf16[128,128]{1,0:T(8,128)(2,1)S(1)}, bf16[128,128]{1,0:T(8,128)(2,1)S(1)}, u32[]{:S(2)}, u32[]{:S(2)}) collective-permute-start(bf16[128,128]{1,0:T(8,128)(2,1)S(1)} %get-tuple-element.54), channel_id=1, source_target_pairs={{0,5},{1,6},{2,1},{3,4},{4,7},{5,0},{6,3},{7,2},{8,13},{9,14},{10,... | collective-permute-start | bytes 98312 | tf_op jit(solution)/shard_map/ppermute | solution.py:213
  41.2 1.3 %collective-permute-start.22 = (bf16[128,128]{1,0:T(8,128)(2,1)S(1)}, bf16[128,128]{1,0:T(8,128)(2,1)S(1)}, u32[]{:S(2)}, u32[]{:S(2)}) collective-permute-start(bf16[128,128]{1,0:T(8,128)(2,1)S(1)} %get-tuple-element.55), channel_id=1, source_target_pairs={{0,1},{1,0},{2,3},{3,2},{4,5},{5,4},{6,7},{7,6},{8,9},{9,8},{10,11... | collective-permute-start | bytes 98312 | tf_op jit(solution)/shard_map/ppermute | solution.py:213
  42.7 0.9 %collective-permute-done.21.p2 = bf16[128,128]{1,0:T(8,128)(2,1)S(1)} collective-permute-done((bf16[128,128]{1,0:T(8,128)(2,1)S(1)}, bf16[128,128]{1,0:T(8,128)(2,1)S(1)}, u32[]{:S(2)}, u32[]{:S(2)}) %collective-permute-start.21) | collective-permute-done | bytes 32800 | tf_op jit(solution)/shard_map/ppermute | solution.py:213
  43.6 1.1 %shard_map.82 = (bf16[256,512]{1,0:T(8,128)(2,1)}, bf16[256,512]{1,0:T(8,128)(2,1)}) custom-call(bf16[256,512]{1,0:T(8,128)(2,1)S(1)} %copy-done, bf16[256,512]{1,0:T(8,128)(2,1)S(1)} %copy-done.1, f32[256,512]{1,0:T(8,128)S(1)} %get-tuple-element.46.refs_7_.key_local, f32[256,512]{1,0:T(8,128)S(1)} %get-tuple-element.47.value_local, ...), custom_call_target="tpu_custom_call" | custom-call | flops 67108864 | bytes 2228224 | tf_op jit(solution)/shard_map/pallas_call | solution.py:70
  (33 shorter events, 2.8 us)
Async XLA Ops:
  0.6 20.7 %copy-start.1 = (bf16[256,512]{1,0:T(8,128)(2,1)S(1)}, bf16[256,512]{1,0:T(8,128)(2,1)}, u32[]{:S(2)}) copy-start(bf16[256,512]{1,0:T(8,128)(2,1)} %v_ref.7) | copy-start | bytes 786436
  0.6 20.6 %copy-start.2 = (bf16[256,512]{1,0:T(8,128)(2,1)S(1)}, bf16[256,512]{1,0:T(8,128)(2,1)}, u32[]{:S(2)}) copy-start(bf16[256,512]{1,0:T(8,128)(2,1)} %q_ref.7) | copy-start | bytes 786436
  2.1 19.2 %copy-start = (bf16[256,512]{1,0:T(8,128)(2,1)S(1)}, bf16[256,512]{1,0:T(8,128)(2,1)}, u32[]{:S(2)}) copy-start(bf16[256,512]{1,0:T(8,128)(2,1)} %k_ref.7) | copy-start | bytes 786436
  2.1 5.8 %collective-permute-start = (bf16[128,128]{1,0:T(8,128)(2,1)S(1)}, bf16[128,128]{1,0:T(8,128)(2,1)S(1)}, u32[]{:S(2)}, u32[]{:S(2)}) collective-permute-start(bf16[128,128]{1,0:T(8,128)(2,1)S(1)} %get-tuple-element.32), channel_id=1, source_target_pairs={{0,7},{1,6},{2,5},{3,4},{4,3},{5,2},{6,1},{7,0},{8,15},{9,14},{10,... | collective-permute-start | bytes 98312 | tf_op jit(solution)/shard_map/ppermute | solution.py:213
  5.5 3.3 %collective-permute-start.1 = (bf16[128,128]{1,0:T(8,128)(2,1)S(1)}, bf16[128,128]{1,0:T(8,128)(2,1)S(1)}, u32[]{:S(2)}, u32[]{:S(2)}) collective-permute-start(bf16[128,128]{1,0:T(8,128)(2,1)S(1)} %get-tuple-element.33), channel_id=1, source_target_pairs={{0,5},{1,2},{2,7},{3,6},{4,1},{5,0},{6,3},{7,4},{8,13},{9,10},{10,... | collective-permute-start | bytes 98312 | tf_op jit(solution)/shard_map/ppermute | solution.py:213
  6.3 3.6 %collective-permute-start.2 = (bf16[128,128]{1,0:T(8,128)(2,1)S(1)}, bf16[128,128]{1,0:T(8,128)(2,1)S(1)}, u32[]{:S(2)}, u32[]{:S(2)}) collective-permute-start(bf16[128,128]{1,0:T(8,128)(2,1)S(1)} %get-tuple-element.34), channel_id=1, source_target_pairs={{0,3},{1,4},{2,1},{3,0},{4,7},{5,6},{6,5},{7,2},{8,11},{9,12},{10,... | collective-permute-start | bytes 98312 | tf_op jit(solution)/shard_map/ppermute | solution.py:213
  6.4 3.5 %collective-permute-start.3 = (bf16[128,128]{1,0:T(8,128)(2,1)S(1)}, bf16[128,128]{1,0:T(8,128)(2,1)S(1)}, u32[]{:S(2)}, u32[]{:S(2)}) collective-permute-start(bf16[128,128]{1,0:T(8,128)(2,1)S(1)} %get-tuple-element.35), channel_id=1, source_target_pairs={{0,1},{1,0},{2,3},{3,2},{4,5},{5,4},{6,7},{7,6},{8,9},{9,8},{10,11... | collective-permute-start | bytes 98312 | tf_op jit(solution)/shard_map/ppermute | solution.py:213
  10.0 5.2 %collective-permute-start.4 = (bf16[128,128]{1,0:T(8,128)(2,1)S(1)}, bf16[128,128]{1,0:T(8,128)(2,1)S(1)}, u32[]{:S(2)}, u32[]{:S(2)}) collective-permute-start(bf16[128,128]{1,0:T(8,128)(2,1)S(1)} %add_convert_fusion.1), channel_id=1, source_target_pairs={{0,16},{2,18},{4,20},{6,22},{8,24},{10,26},{12,28},{14,30},{16,0},... | collective-permute-start | bytes 98312 | tf_op jit(solution)/shard_map/ppermute | solution.py:225
  12.6 5.1 %collective-permute-start.5 = (bf16[128,128]{1,0:T(8,128)(2,1)S(1)}, bf16[128,128]{1,0:T(8,128)(2,1)S(1)}, u32[]{:S(2)}, u32[]{:S(2)}) collective-permute-start(bf16[128,128]{1,0:T(8,128)(2,1)S(1)} %add_convert_fusion.1), channel_id=1, source_target_pairs={{0,24},{2,26},{4,28},{6,30},{8,16},{10,18},{12,20},{14,22},{16,0},... | collective-permute-start | bytes 98312 | tf_op jit(solution)/shard_map/ppermute | solution.py:225
  14.0 4.0 %collective-permute-start.6 = (bf16[128,128]{1,0:T(8,128)(2,1)S(1)}, bf16[128,128]{1,0:T(8,128)(2,1)S(1)}, u32[]{:S(2)}, u32[]{:S(2)}) collective-permute-start(bf16[128,128]{1,0:T(8,128)(2,1)S(1)} %add_convert_fusion.1), channel_id=1, source_target_pairs={{0,8},{2,10},{4,12},{6,14},{8,0},{10,2},{12,4},{14,6},{16,24},{18,... | collective-permute-start | bytes 98312 | tf_op jit(solution)/shard_map/ppermute | solution.py:225
  18.1 3.8 %collective-permute-start.7 = (bf16[128,128]{1,0:T(8,128)(2,1)S(1)}, bf16[128,128]{1,0:T(8,128)(2,1)S(1)}, u32[]{:S(2)}, u32[]{:S(2)}) collective-permute-start(bf16[128,128]{1,0:T(8,128)(2,1)S(1)} %get-tuple-element.36), channel_id=1, source_target_pairs={{0,7},{1,4},{2,5},{3,6},{4,3},{5,0},{6,1},{7,2},{8,15},{9,12},{10,... | collective-permute-start | bytes 98312 | tf_op jit(solution)/shard_map/ppermute | solution.py:213
  18.2 4.3 %collective-permute-start.8 = (bf16[128,128]{1,0:T(8,128)(2,1)S(1)}, bf16[128,128]{1,0:T(8,128)(2,1)S(1)}, u32[]{:S(2)}, u32[]{:S(2)}) collective-permute-start(bf16[128,128]{1,0:T(8,128)(2,1)S(1)} %get-tuple-element.37), channel_id=1, source_target_pairs={{0,5},{1,6},{2,1},{3,4},{4,7},{5,2},{6,3},{7,0},{8,13},{9,14},{10,... | collective-permute-start | bytes 98312 | tf_op jit(solution)/shard_map/ppermute | solution.py:213
  19.9 3.5 %collective-permute-start.9 = (bf16[128,128]{1,0:T(8,128)(2,1)S(1)}, bf16[128,128]{1,0:T(8,128)(2,1)S(1)}, u32[]{:S(2)}, u32[]{:S(2)}) collective-permute-start(bf16[128,128]{1,0:T(8,128)(2,1)S(1)} %get-tuple-element.38), channel_id=1, source_target_pairs={{0,3},{1,2},{2,7},{3,0},{4,1},{5,6},{6,5},{7,4},{8,11},{9,10},{10,... | collective-permute-start | bytes 98312 | tf_op jit(solution)/shard_map/ppermute | solution.py:213
  20.7 2.7 %copy-start.3 = (bf16[256,512]{1,0:T(8,128)(2,1)S(1)}, bf16[256,512]{1,0:T(8,128)(2,1)}, u32[]{:S(2)}) copy-start(bf16[256,512]{1,0:T(8,128)(2,1)} %c_ref.3) | copy-start | bytes 786436
  20.7 2.7 %collective-permute-start.10 = (bf16[128,128]{1,0:T(8,128)(2,1)S(1)}, bf16[128,128]{1,0:T(8,128)(2,1)S(1)}, u32[]{:S(2)}, u32[]{:S(2)}) collective-permute-start(bf16[128,128]{1,0:T(8,128)(2,1)S(1)} %get-tuple-element.39), channel_id=1, source_target_pairs={{0,1},{1,0},{2,3},{3,2},{4,5},{5,4},{6,7},{7,6},{8,9},{9,8},{10,11... | collective-permute-start | bytes 98312 | tf_op jit(solution)/shard_map/ppermute | solution.py:213
  23.8 1.2 %collective-permute-start.11 = (f32[2,256]{1,0:T(2,128)S(1)}, f32[2,256]{1,0:T(2,128)S(1)}, u32[]{:S(2)}, u32[]{:S(2)}) collective-permute-start(f32[2,256]{1,0:T(2,128)S(1)} %get-tuple-element.41), channel_id=1, source_target_pairs={{0,1},{1,0},{2,3},{3,2},{4,5},{5,4},{6,7},{7,6},{8,9},{9,8},{10,11... | collective-permute-start | bytes 6152 | tf_op jit(solution)/shard_map/ppermute | solution.py:203
  25.5 3.4 %collective-permute-start.12 = (bf16[128,128]{1,0:T(8,128)(2,1)S(1)}, bf16[128,128]{1,0:T(8,128)(2,1)S(1)}, u32[]{:S(2)}, u32[]{:S(2)}) collective-permute-start(bf16[128,128]{1,0:T(8,128)(2,1)S(1)} %get-tuple-element.48), channel_id=1, source_target_pairs={{0,3},{1,2},{2,1},{3,6},{4,7},{5,0},{6,5},{7,4},{8,11},{9,10},{10,... | collective-permute-start | bytes 98312 | tf_op jit(solution)/shard_map/ppermute | solution.py:213
  26.6 4.2 %collective-permute-start.13 = (bf16[128,128]{1,0:T(8,128)(2,1)S(1)}, bf16[128,128]{1,0:T(8,128)(2,1)S(1)}, u32[]{:S(2)}, u32[]{:S(2)}) collective-permute-start(bf16[128,128]{1,0:T(8,128)(2,1)S(1)} %get-tuple-element.49), channel_id=1, source_target_pairs={{0,7},{1,6},{2,5},{3,4},{4,1},{5,2},{6,3},{7,0},{8,15},{9,14},{10,... | collective-permute-start | bytes 98312 | tf_op jit(solution)/shard_map/ppermute | solution.py:213
  27.2 3.7 %collective-permute-start.14 = (bf16[128,128]{1,0:T(8,128)(2,1)S(1)}, bf16[128,128]{1,0:T(8,128)(2,1)S(1)}, u32[]{:S(2)}, u32[]{:S(2)}) collective-permute-start(bf16[128,128]{1,0:T(8,128)(2,1)S(1)} %get-tuple-element.50), channel_id=1, source_target_pairs={{0,5},{1,4},{2,7},{3,0},{4,3},{5,6},{6,1},{7,2},{8,13},{9,12},{10,... | collective-permute-start | bytes 98312 | tf_op jit(solution)/shard_map/ppermute | solution.py:213
  28.5 2.4 %collective-permute-start.15 = (bf16[128,128]{1,0:T(8,128)(2,1)S(1)}, bf16[128,128]{1,0:T(8,128)(2,1)S(1)}, u32[]{:S(2)}, u32[]{:S(2)}) collective-permute-start(bf16[128,128]{1,0:T(8,128)(2,1)S(1)} %get-tuple-element.51), channel_id=1, source_target_pairs={{0,1},{1,0},{2,3},{3,2},{4,5},{5,4},{6,7},{7,6},{8,9},{9,8},{10,11... | collective-permute-start | bytes 98312 | tf_op jit(solution)/shard_map/ppermute | solution.py:213
  30.9 6.5 %collective-permute-start.16 = (bf16[128,128]{1,0:T(8,128)(2,1)S(1)}, bf16[128,128]{1,0:T(8,128)(2,1)S(1)}, u32[]{:S(2)}, u32[]{:S(2)}) collective-permute-start(bf16[128,128]{1,0:T(8,128)(2,1)S(1)} %add_convert_fusion), channel_id=1, source_target_pairs={{0,16},{2,18},{4,20},{6,22},{8,24},{10,26},{12,28},{14,30},{16,8},... | collective-permute-start | bytes 98312 | tf_op jit(solution)/shard_map/ppermute | solution.py:225
  32.4 5.2 %collective-permute-start.17 = (bf16[128,128]{1,0:T(8,128)(2,1)S(1)}, bf16[128,128]{1,0:T(8,128)(2,1)S(1)}, u32[]{:S(2)}, u32[]{:S(2)}) collective-permute-start(bf16[128,128]{1,0:T(8,128)(2,1)S(1)} %add_convert_fusion), channel_id=1, source_target_pairs={{0,16},{2,18},{4,20},{6,22},{8,24},{10,26},{12,28},{14,30},{16,0},... | collective-permute-start | bytes 98312 | tf_op jit(solution)/shard_map/ppermute | solution.py:225
  33.4 4.7 %collective-permute-start.18 = (bf16[128,128]{1,0:T(8,128)(2,1)S(1)}, bf16[128,128]{1,0:T(8,128)(2,1)S(1)}, u32[]{:S(2)}, u32[]{:S(2)}) collective-permute-start(bf16[128,128]{1,0:T(8,128)(2,1)S(1)} %add_convert_fusion), channel_id=1, source_target_pairs={{0,8},{2,10},{4,12},{6,14},{8,0},{10,2},{12,4},{14,6},{16,24},{18,... | collective-permute-start | bytes 98312 | tf_op jit(solution)/shard_map/ppermute | solution.py:225
  38.3 4.4 %collective-permute-start.19 = (bf16[128,128]{1,0:T(8,128)(2,1)S(1)}, bf16[128,128]{1,0:T(8,128)(2,1)S(1)}, u32[]{:S(2)}, u32[]{:S(2)}) collective-permute-start(bf16[128,128]{1,0:T(8,128)(2,1)S(1)} %get-tuple-element.52), channel_id=1, source_target_pairs={{0,7},{1,4},{2,5},{3,6},{4,3},{5,2},{6,1},{7,0},{8,15},{9,12},{10,... | collective-permute-start | bytes 98312 | tf_op jit(solution)/shard_map/ppermute | solution.py:213
  39.4 3.3 %collective-permute-start.20 = (bf16[128,128]{1,0:T(8,128)(2,1)S(1)}, bf16[128,128]{1,0:T(8,128)(2,1)S(1)}, u32[]{:S(2)}, u32[]{:S(2)}) collective-permute-start(bf16[128,128]{1,0:T(8,128)(2,1)S(1)} %get-tuple-element.53), channel_id=1, source_target_pairs={{0,3},{1,2},{2,7},{3,0},{4,1},{5,6},{6,5},{7,4},{8,11},{9,10},{10,... | collective-permute-start | bytes 98312 | tf_op jit(solution)/shard_map/ppermute | solution.py:213
  40.0 3.7 %collective-permute-start.21 = (bf16[128,128]{1,0:T(8,128)(2,1)S(1)}, bf16[128,128]{1,0:T(8,128)(2,1)S(1)}, u32[]{:S(2)}, u32[]{:S(2)}) collective-permute-start(bf16[128,128]{1,0:T(8,128)(2,1)S(1)} %get-tuple-element.54), channel_id=1, source_target_pairs={{0,5},{1,6},{2,1},{3,4},{4,7},{5,0},{6,3},{7,2},{8,13},{9,14},{10,... | collective-permute-start | bytes 98312 | tf_op jit(solution)/shard_map/ppermute | solution.py:213
  41.2 2.4 %collective-permute-start.22 = (bf16[128,128]{1,0:T(8,128)(2,1)S(1)}, bf16[128,128]{1,0:T(8,128)(2,1)S(1)}, u32[]{:S(2)}, u32[]{:S(2)}) collective-permute-start(bf16[128,128]{1,0:T(8,128)(2,1)S(1)} %get-tuple-element.55), channel_id=1, source_target_pairs={{0,1},{1,0},{2,3},{3,2},{4,5},{5,4},{6,7},{7,6},{8,9},{9,8},{10,11... | collective-permute-start | bytes 98312 | tf_op jit(solution)/shard_map/ppermute | solution.py:213

commit v11 on v9

--- a/solution.py
+++ b/solution.py
@@ -99,9 +99,10 @@
         out[...] = states[op].astype(LOW)
 
 
-def local_kernel(q_ref, k_ref, v_ref, scores_ref, mixed_ref):
+def local_kernel(q_ref, k_ref, v_ref, scores_ref, mixed_ref, turned_ref):
     mask = causal_mask(q_ref.shape[0])
     for h in range(QUAD):
+        turned_ref[h] = fixed(q_ref, h)[...].T
         raw = dot(fixed(q_ref, h)[...], fixed(k_ref, h)[...], ((1,), (1,)))
         scores = jnp.where(mask, raw, 0.0).astype(LOW)
         scores_ref[h] = scores
@@ -130,14 +131,17 @@
     return inverse, projection
 
 
-def grad_kernel(features, mixed_ref, c_ref, q_ref, sums_ref, o0, o1, o2, o3, g_ref):
-    inverse, projection = token_scales(sums_ref, features, q_ref.shape[0])
+def grad_kernel(features, mixed_ref, c_ref, turned_ref, sums_ref, o0, o1, o2, o3, g_ref):
+    count = c_ref.shape[0]
+    inverse = lax.rsqrt(sums_ref[0:1, :] * (1.0 / features) + EPSILON)
+    share = inverse * inverse * (inverse * sums_ref[1:2, :] * (1.0 / features))
+    inverse = jnp.broadcast_to(inverse, (DH, count)).T
+    share = jnp.broadcast_to(share, (DH, count)).T
     for op, out in enumerate((o0, o1, o2, o3)):
         h = sent(FIRST_GRAD, op)
-        normed = head(mixed_ref, h)[...] * inverse
-        grad = (inverse * (head(c_ref, h)[...].astype(WIDE) - normed * projection)).astype(LOW)
+        grad = (inverse * head(c_ref, h)[...].astype(WIDE) - share * head(mixed_ref, h)[...]).astype(LOW)
         head(g_ref, h)[...] = grad
-        out[...] = dot(head(q_ref, h)[...], grad, ((0,), (0,))).astype(LOW)
+        out[...] = dot(turned_ref[h], grad, ((1,), (0,))).astype(LOW)
 
 
 def back_kernel(features, q_ref, k_ref, v_ref, g_ref, scores_ref, mixed_ref, sums_ref, p0, p1, p2, p3,
@@ -256,8 +260,11 @@
         in_specs=[pl.BlockSpec(memory_space=pltpu.HBM)] * 2,
         scratch_shapes=buffers,
     )
-    scores, local = call(
-        local_kernel, [shape((QUAD, count, count), LOW), wide], (q, k, v), 4 * unit
+    scores, local, turned = call(
+        local_kernel,
+        [shape((QUAD, count, count), LOW), wide, shape((QUAD, DH, count), LOW)],
+        (q, k, v),
+        4 * unit,
     )
     prefix = exclusive_sum(held, True)
     mixed, sums = call(
@@ -265,7 +272,7 @@
     )
     sums = sum_over_heads(sums)
     *terms, g = call(
-        functools.partial(grad_kernel, features), [state] * QUAD + [low], (mixed, c, q, sums), unit
+        functools.partial(grad_kernel, features), [state] * QUAD + [low], (mixed, c, turned, sums), unit
     )
     normed_out, query_grad, key_local, value_local = call(
         functools.partial(back_kernel, features),

time: 44.6 us -> 44.5 us (level)
  no operation moved by 1% of the time
where the time goes in v11:
time: 44.5 us; the launch traced here: 44.4 us
  starting transfers between devices  22.9 us (51%)
  waiting for transfers between devices  14.6 us (33%)
  Pallas kernels  6.16 us (14%)
  between operations  0.73 us (2%)
    ppermute x16, starting transfers between devices, cross(): return lax.ppermute(value, ('seq', 'tp'), pairs)  14 us
    ppermute x16, waiting for transfers between devices, cross(): return lax.ppermute(value, ('seq', 'tp'), pairs)  8.99 us
    ppermute x6, starting transfers between devices, exclusive_sum(): got.append(lax.ppermute(total, 'seq', pairs))  8.67 us
    pallas_call x8, Pallas kernels, call(): pl.pallas_call(kernel, out_shape=outs, in_specs=in_specs or [pl.BlockSpec...  6.16 us
    ppermute x6, waiting for transfers between devices, exclusive_sum(): got.append(lax.ppermute(total, 'seq', pairs))  4.53 us
    ppermute x1, waiting for transfers between devices, exchange(): return lax.ppermute(value, axis, [(i, i ^ bits) for i in range(size)])  1.06 us
  transfers between devices with their start and end apart: 23, of which 16 were waited for; matrix products, arithmetic and copies ran while one was open for 0% of the time, Pallas kernels for 6%

profile of v11, /device:TPU:0, one launch (start us, length us, event | category | flops | bytes accessed | tf_op | source)
XLA Modules:
  0.0 44.4 jit_solution(10920627664229368354)
XLA Ops:
  0.7 1.4 %shard_map.76 = (bf16[128,128]{1,0:T(8,128)(2,1)S(1)}, bf16[128,128]{1,0:T(8,128)(2,1)S(1)}, bf16[128,128]{1,0:T(8,128)(2,1)S(1)}, bf16[128,128]{1,0:T(8,128)(2,1)S(1)}) custom-call(bf16[256,512]{1,0:T(8,128)(2,1)} %k_ref.7, bf16[256,512]{1,0:T(8,128)(2,1)} %v_ref.7), custom_call_target="tpu_custom_call" | custom-call | flops 33554432 | bytes 655360 | tf_op jit(solution)/shard_map/pallas_call | solution.py:70
  2.1 3.4 %collective-permute-start = (bf16[128,128]{1,0:T(8,128)(2,1)S(1)}, bf16[128,128]{1,0:T(8,128)(2,1)S(1)}, u32[]{:S(2)}, u32[]{:S(2)}) collective-permute-start(bf16[128,128]{1,0:T(8,128)(2,1)S(1)} %get-tuple-element.33), channel_id=1, source_target_pairs={{0,7},{1,4},{2,5},{3,6},{4,3},{5,2},{6,1},{7,0},{8,15},{9,12},{10,... | collective-permute-start | bytes 98312 | tf_op jit(solution)/shard_map/ppermute | solution.py:217
  5.5 0.8 %collective-permute-start.1 = (bf16[128,128]{1,0:T(8,128)(2,1)S(1)}, bf16[128,128]{1,0:T(8,128)(2,1)S(1)}, u32[]{:S(2)}, u32[]{:S(2)}) collective-permute-start(bf16[128,128]{1,0:T(8,128)(2,1)S(1)} %get-tuple-element.34), channel_id=1, source_target_pairs={{0,3},{1,6},{2,7},{3,4},{4,1},{5,0},{6,5},{7,2},{8,11},{9,14},{10,... | collective-permute-start | bytes 98312 | tf_op jit(solution)/shard_map/ppermute | solution.py:217
  6.4 0.9 %collective-permute-start.2 = (bf16[128,128]{1,0:T(8,128)(2,1)S(1)}, bf16[128,128]{1,0:T(8,128)(2,1)S(1)}, u32[]{:S(2)}, u32[]{:S(2)}) collective-permute-start(bf16[128,128]{1,0:T(8,128)(2,1)S(1)} %get-tuple-element.35), channel_id=1, source_target_pairs={{0,5},{1,2},{2,1},{3,0},{4,7},{5,6},{6,3},{7,4},{8,13},{9,10},{10,... | collective-permute-start | bytes 98312 | tf_op jit(solution)/shard_map/ppermute | solution.py:217
  7.3 1.9 %collective-permute-done.1.refs_1_ = bf16[128,128]{1,0:T(8,128)(2,1)S(1)} collective-permute-done((bf16[128,128]{1,0:T(8,128)(2,1)S(1)}, bf16[128,128]{1,0:T(8,128)(2,1)S(1)}, u32[]{:S(2)}, u32[]{:S(2)}) %collective-permute-start.1) | collective-permute-done | bytes 32800 | tf_op jit(solution)/shard_map/ppermute | solution.py:217
  9.1 0.8 %collective-permute-done.2.refs_2_ = bf16[128,128]{1,0:T(8,128)(2,1)S(1)} collective-permute-done((bf16[128,128]{1,0:T(8,128)(2,1)S(1)}, bf16[128,128]{1,0:T(8,128)(2,1)S(1)}, u32[]{:S(2)}, u32[]{:S(2)}) %collective-permute-start.2) | collective-permute-done | bytes 32800 | tf_op jit(solution)/shard_map/ppermute | solution.py:217
  10.0 2.7 %collective-permute-start.4 = (bf16[128,128]{1,0:T(8,128)(2,1)S(1)}, bf16[128,128]{1,0:T(8,128)(2,1)S(1)}, u32[]{:S(2)}, u32[]{:S(2)}) collective-permute-start(bf16[128,128]{1,0:T(8,128)(2,1)S(1)} %add_convert_fusion.1), channel_id=1, source_target_pairs={{0,16},{2,18},{4,20},{6,22},{8,24},{10,26},{12,28},{14,30},{16,0},... | collective-permute-start | bytes 98312 | tf_op jit(solution)/shard_map/ppermute | solution.py:229
  12.7 1.3 %collective-permute-start.5 = (bf16[128,128]{1,0:T(8,128)(2,1)S(1)}, bf16[128,128]{1,0:T(8,128)(2,1)S(1)}, u32[]{:S(2)}, u32[]{:S(2)}) collective-permute-start(bf16[128,128]{1,0:T(8,128)(2,1)S(1)} %add_convert_fusion.1), channel_id=1, source_target_pairs={{0,24},{2,26},{4,28},{6,30},{8,16},{10,18},{12,20},{14,22},{16,0},... | collective-permute-start | bytes 98312 | tf_op jit(solution)/shard_map/ppermute | solution.py:229
  14.2 1.0 %collective-permute-done.4.refs_4_ = bf16[128,128]{1,0:T(8,128)(2,1)S(1)} collective-permute-done((bf16[128,128]{1,0:T(8,128)(2,1)S(1)}, bf16[128,128]{1,0:T(8,128)(2,1)S(1)}, u32[]{:S(2)}, u32[]{:S(2)}) %collective-permute-start.4) | collective-permute-done | bytes 32800 | tf_op jit(solution)/shard_map/ppermute | solution.py:229
  15.2 2.5 %collective-permute-done.5.refs_5_ = bf16[128,128]{1,0:T(8,128)(2,1)S(1)} collective-permute-done((bf16[128,128]{1,0:T(8,128)(2,1)S(1)}, bf16[128,128]{1,0:T(8,128)(2,1)S(1)}, u32[]{:S(2)}, u32[]{:S(2)}) %collective-permute-start.5) | collective-permute-done | bytes 32800 | tf_op jit(solution)/shard_map/ppermute | solution.py:229
  18.2 1.7 %collective-permute-start.8 = (bf16[128,128]{1,0:T(8,128)(2,1)S(1)}, bf16[128,128]{1,0:T(8,128)(2,1)S(1)}, u32[]{:S(2)}, u32[]{:S(2)}) collective-permute-start(bf16[128,128]{1,0:T(8,128)(2,1)S(1)} %get-tuple-element.38), channel_id=1, source_target_pairs={{0,5},{1,4},{2,7},{3,6},{4,1},{5,2},{6,3},{7,0},{8,13},{9,12},{10,... | collective-permute-start | bytes 98312 | tf_op jit(solution)/shard_map/ppermute | solution.py:217
  20.0 0.4 collective-permute-start.10
  20.4 0.7 %shard_map.75 = (bf16[4,256,256]{2,1,0:T(8,128)(2,1)S(1)}, f32[256,512]{1,0:T(8,128)S(1)}, bf16[4,128,256]{2,1,0:T(8,128)(2,1)S(1)}) custom-call(bf16[256,512]{1,0:T(8,128)(2,1)S(1)} %copy-done.2, bf16[256,512]{1,0:T(8,128)(2,1)S(1)} %copy-done, bf16[256,512]{1,0:T(8,128)(2,1)S(1)} %copy-done.1), custom_call_target="tpu_custom_call" | custom-call | flops 134217728 | bytes 2097152 | tf_op jit(solution)/shard_map/pallas_call | solution.py:70
  21.1 0.8 %collective-permute-done.7.p0 = bf16[128,128]{1,0:T(8,128)(2,1)S(1)} collective-permute-done((bf16[128,128]{1,0:T(8,128)(2,1)S(1)}, bf16[128,128]{1,0:T(8,128)(2,1)S(1)}, u32[]{:S(2)}, u32[]{:S(2)}) %collective-permute-start.7) | collective-permute-done | bytes 32800 | tf_op jit(solution)/shard_map/ppermute | solution.py:217
  21.9 0.6 %collective-permute-done.8.p1 = bf16[128,128]{1,0:T(8,128)(2,1)S(1)} collective-permute-done((bf16[128,128]{1,0:T(8,128)(2,1)S(1)}, bf16[128,128]{1,0:T(8,128)(2,1)S(1)}, u32[]{:S(2)}, u32[]{:S(2)}) %collective-permute-start.8) | collective-permute-done | bytes 32800 | tf_op jit(solution)/shard_map/ppermute | solution.py:217
  22.5 1.1 %collective-permute-done.9.p2 = bf16[128,128]{1,0:T(8,128)(2,1)S(1)} collective-permute-done((bf16[128,128]{1,0:T(8,128)(2,1)S(1)}, bf16[128,128]{1,0:T(8,128)(2,1)S(1)}, u32[]{:S(2)}, u32[]{:S(2)}) %collective-permute-start.9) | collective-permute-done | bytes 32800 | tf_op jit(solution)/shard_map/ppermute | solution.py:217
  24.2 1.1 %collective-permute-done.11 = f32[2,256]{1,0:T(2,128)S(1)} collective-permute-done((f32[2,256]{1,0:T(2,128)S(1)}, f32[2,256]{1,0:T(2,128)S(1)}, u32[]{:S(2)}, u32[]{:S(2)}) %collective-permute-start.11) | collective-permute-done | bytes 2080 | tf_op jit(solution)/shard_map/ppermute | solution.py:207
  25.6 1.1 %collective-permute-start.12 = (bf16[128,128]{1,0:T(8,128)(2,1)S(1)}, bf16[128,128]{1,0:T(8,128)(2,1)S(1)}, u32[]{:S(2)}, u32[]{:S(2)}) collective-permute-start(bf16[128,128]{1,0:T(8,128)(2,1)S(1)} %get-tuple-element.50), channel_id=1, source_target_pairs={{0,7},{1,6},{2,5},{3,4},{4,3},{5,2},{6,1},{7,0},{8,15},{9,14},{10,... | collective-permute-start | bytes 98312 | tf_op jit(solution)/shard_map/ppermute | solution.py:217
  27.0 1.5 %collective-permute-start.14 = (bf16[128,128]{1,0:T(8,128)(2,1)S(1)}, bf16[128,128]{1,0:T(8,128)(2,1)S(1)}, u32[]{:S(2)}, u32[]{:S(2)}) collective-permute-start(bf16[128,128]{1,0:T(8,128)(2,1)S(1)} %get-tuple-element.52), channel_id=1, source_target_pairs={{0,3},{1,4},{2,1},{3,6},{4,7},{5,0},{6,5},{7,2},{8,11},{9,12},{10,... | collective-permute-start | bytes 98312 | tf_op jit(solution)/shard_map/ppermute | solution.py:217
  28.8 1.1 %collective-permute-done.12.refs_0_ = bf16[128,128]{1,0:T(8,128)(2,1)S(1)} collective-permute-done((bf16[128,128]{1,0:T(8,128)(2,1)S(1)}, bf16[128,128]{1,0:T(8,128)(2,1)S(1)}, u32[]{:S(2)}, u32[]{:S(2)}) %collective-permute-start.12) | collective-permute-done | bytes 32800 | tf_op jit(solution)/shard_map/ppermute | solution.py:217
  30.2 0.6 %collective-permute-done.14.refs_2_ = bf16[128,128]{1,0:T(8,128)(2,1)S(1)} collective-permute-done((bf16[128,128]{1,0:T(8,128)(2,1)S(1)}, bf16[128,128]{1,0:T(8,128)(2,1)S(1)}, u32[]{:S(2)}, u32[]{:S(2)}) %collective-permute-start.14) | collective-permute-done | bytes 32800 | tf_op jit(solution)/shard_map/ppermute | solution.py:217
  30.9 1.7 %collective-permute-start.16 = (bf16[128,128]{1,0:T(8,128)(2,1)S(1)}, bf16[128,128]{1,0:T(8,128)(2,1)S(1)}, u32[]{:S(2)}, u32[]{:S(2)}) collective-permute-start(bf16[128,128]{1,0:T(8,128)(2,1)S(1)} %add_convert_fusion), channel_id=1, source_target_pairs={{0,16},{2,18},{4,20},{6,22},{8,24},{10,26},{12,28},{14,30},{16,8},... | collective-permute-start | bytes 98312 | tf_op jit(solution)/shard_map/ppermute | solution.py:229
  32.5 0.9 %collective-permute-start.17 = (bf16[128,128]{1,0:T(8,128)(2,1)S(1)}, bf16[128,128]{1,0:T(8,128)(2,1)S(1)}, u32[]{:S(2)}, u32[]{:S(2)}) collective-permute-start(bf16[128,128]{1,0:T(8,128)(2,1)S(1)} %add_convert_fusion), channel_id=1, source_target_pairs={{0,16},{2,18},{4,20},{6,22},{8,24},{10,26},{12,28},{14,30},{16,0},... | collective-permute-start | bytes 98312 | tf_op jit(solution)/shard_map/ppermute | solution.py:229
  33.4 1.9 %collective-permute-start.18 = (bf16[128,128]{1,0:T(8,128)(2,1)S(1)}, bf16[128,128]{1,0:T(8,128)(2,1)S(1)}, u32[]{:S(2)}, u32[]{:S(2)}) collective-permute-start(bf16[128,128]{1,0:T(8,128)(2,1)S(1)} %add_convert_fusion), channel_id=1, source_target_pairs={{0,8},{2,10},{4,12},{6,14},{8,0},{10,2},{12,4},{14,6},{16,24},{18,... | collective-permute-start | bytes 98312 | tf_op jit(solution)/shard_map/ppermute | solution.py:229
  35.3 2.0 %shard_map.80 = (bf16[256,512]{1,0:T(8,128)(2,1)}, bf16[256,512]{1,0:T(8,128)(2,1)}, f32[256,512]{1,0:T(8,128)S(1)}, f32[256,512]{1,0:T(8,128)S(1)}) custom-call(bf16[256,512]{1,0:T(8,128)(2,1)S(1)} %copy-done.2, bf16[256,512]{1,0:T(8,128)(2,1)S(1)} %copy-done, bf16[256,512]{1,0:T(8,128)(2,1)S(1)} %copy-done.1, ...), custom_call_target="tpu_custom_call" | custom-call | flops 301989888 | bytes 3803136 | tf_op jit(solution)/shard_map/pallas_call | solution.py:70
  37.3 0.4 collective-permute-done.17.refs_5_
  38.2 1.7 %collective-permute-start.20 = (bf16[128,128]{1,0:T(8,128)(2,1)S(1)}, bf16[128,128]{1,0:T(8,128)(2,1)S(1)}, u32[]{:S(2)}, u32[]{:S(2)}) collective-permute-start(bf16[128,128]{1,0:T(8,128)(2,1)S(1)} %get-tuple-element.55), channel_id=1, source_target_pairs={{0,5},{1,2},{2,7},{3,4},{4,1},{5,6},{6,3},{7,0},{8,13},{9,10},{10,... | collective-permute-start | bytes 98312 | tf_op jit(solution)/shard_map/ppermute | solution.py:217
  40.0 0.6 %collective-permute-start.21 = (bf16[128,128]{1,0:T(8,128)(2,1)S(1)}, bf16[128,128]{1,0:T(8,128)(2,1)S(1)}, u32[]{:S(2)}, u32[]{:S(2)}) collective-permute-start(bf16[128,128]{1,0:T(8,128)(2,1)S(1)} %get-tuple-element.56), channel_id=1, source_target_pairs={{0,3},{1,6},{2,1},{3,0},{4,7},{5,2},{6,5},{7,4},{8,11},{9,14},{10,... | collective-permute-start | bytes 98312 | tf_op jit(solution)/shard_map/ppermute | solution.py:217
  40.5 1.1 %collective-permute-start.22 = (bf16[128,128]{1,0:T(8,128)(2,1)S(1)}, bf16[128,128]{1,0:T(8,128)(2,1)S(1)}, u32[]{:S(2)}, u32[]{:S(2)}) collective-permute-start(bf16[128,128]{1,0:T(8,128)(2,1)S(1)} %get-tuple-element.57), channel_id=1, source_target_pairs={{0,1},{1,0},{2,3},{3,2},{4,5},{5,4},{6,7},{7,6},{8,9},{9,8},{10,11... | collective-permute-start | bytes 98312 | tf_op jit(solution)/shard_map/ppermute | solution.py:217
  41.6 1.1 %collective-permute-done.20.p1 = bf16[128,128]{1,0:T(8,128)(2,1)S(1)} collective-permute-done((bf16[128,128]{1,0:T(8,128)(2,1)S(1)}, bf16[128,128]{1,0:T(8,128)(2,1)S(1)}, u32[]{:S(2)}, u32[]{:S(2)}) %collective-permute-start.20) | collective-permute-done | bytes 32800 | tf_op jit(solution)/shard_map/ppermute | solution.py:217
  42.7 0.6 %collective-permute-done.21.p2 = bf16[128,128]{1,0:T(8,128)(2,1)S(1)} collective-permute-done((bf16[128,128]{1,0:T(8,128)(2,1)S(1)}, bf16[128,128]{1,0:T(8,128)(2,1)S(1)}, u32[]{:S(2)}, u32[]{:S(2)}) %collective-permute-start.21) | collective-permute-done | bytes 32800 | tf_op jit(solution)/shard_map/ppermute | solution.py:217
  43.3 1.1 %shard_map.82 = (bf16[256,512]{1,0:T(8,128)(2,1)}, bf16[256,512]{1,0:T(8,128)(2,1)}) custom-call(bf16[256,512]{1,0:T(8,128)(2,1)S(1)} %copy-done, bf16[256,512]{1,0:T(8,128)(2,1)S(1)} %copy-done.1, f32[256,512]{1,0:T(8,128)S(1)} %get-tuple-element.48.refs_7_.key_local, f32[256,512]{1,0:T(8,128)S(1)} %get-tuple-element.49.value_local, ...), custom_call_target="tpu_custom_call" | custom-call | flops 67108864 | bytes 2228224 | tf_op jit(solution)/shard_map/pallas_call | solution.py:70
  (33 shorter events, 3.1 us)
Async XLA Ops:
  0.6 19.8 %copy-start.1 = (bf16[256,512]{1,0:T(8,128)(2,1)S(1)}, bf16[256,512]{1,0:T(8,128)(2,1)}, u32[]{:S(2)}) copy-start(bf16[256,512]{1,0:T(8,128)(2,1)} %v_ref.7) | copy-start | bytes 786436
  0.6 19.8 %copy-start.2 = (bf16[256,512]{1,0:T(8,128)(2,1)S(1)}, bf16[256,512]{1,0:T(8,128)(2,1)}, u32[]{:S(2)}) copy-start(bf16[256,512]{1,0:T(8,128)(2,1)} %q_ref.5) | copy-start | bytes 786436
  2.1 18.3 %copy-start = (bf16[256,512]{1,0:T(8,128)(2,1)S(1)}, bf16[256,512]{1,0:T(8,128)(2,1)}, u32[]{:S(2)}) copy-start(bf16[256,512]{1,0:T(8,128)(2,1)} %k_ref.7) | copy-start | bytes 786436
  2.1 5.1 %collective-permute-start = (bf16[128,128]{1,0:T(8,128)(2,1)S(1)}, bf16[128,128]{1,0:T(8,128)(2,1)S(1)}, u32[]{:S(2)}, u32[]{:S(2)}) collective-permute-start(bf16[128,128]{1,0:T(8,128)(2,1)S(1)} %get-tuple-element.33), channel_id=1, source_target_pairs={{0,7},{1,4},{2,5},{3,6},{4,3},{5,2},{6,1},{7,0},{8,15},{9,12},{10,... | collective-permute-start | bytes 98312 | tf_op jit(solution)/shard_map/ppermute | solution.py:217
  5.5 3.6 %collective-permute-start.1 = (bf16[128,128]{1,0:T(8,128)(2,1)S(1)}, bf16[128,128]{1,0:T(8,128)(2,1)S(1)}, u32[]{:S(2)}, u32[]{:S(2)}) collective-permute-start(bf16[128,128]{1,0:T(8,128)(2,1)S(1)} %get-tuple-element.34), channel_id=1, source_target_pairs={{0,3},{1,6},{2,7},{3,4},{4,1},{5,0},{6,5},{7,2},{8,11},{9,14},{10,... | collective-permute-start | bytes 98312 | tf_op jit(solution)/shard_map/ppermute | solution.py:217
  6.4 3.6 %collective-permute-start.2 = (bf16[128,128]{1,0:T(8,128)(2,1)S(1)}, bf16[128,128]{1,0:T(8,128)(2,1)S(1)}, u32[]{:S(2)}, u32[]{:S(2)}) collective-permute-start(bf16[128,128]{1,0:T(8,128)(2,1)S(1)} %get-tuple-element.35), channel_id=1, source_target_pairs={{0,5},{1,2},{2,1},{3,0},{4,7},{5,6},{6,3},{7,4},{8,13},{9,10},{10,... | collective-permute-start | bytes 98312 | tf_op jit(solution)/shard_map/ppermute | solution.py:217
  7.3 2.7 %collective-permute-start.3 = (bf16[128,128]{1,0:T(8,128)(2,1)S(1)}, bf16[128,128]{1,0:T(8,128)(2,1)S(1)}, u32[]{:S(2)}, u32[]{:S(2)}) collective-permute-start(bf16[128,128]{1,0:T(8,128)(2,1)S(1)} %get-tuple-element.36), channel_id=1, source_target_pairs={{0,1},{1,0},{2,3},{3,2},{4,5},{5,4},{6,7},{7,6},{8,9},{9,8},{10,11... | collective-permute-start | bytes 98312 | tf_op jit(solution)/shard_map/ppermute | solution.py:217
  10.0 5.2 %collective-permute-start.4 = (bf16[128,128]{1,0:T(8,128)(2,1)S(1)}, bf16[128,128]{1,0:T(8,128)(2,1)S(1)}, u32[]{:S(2)}, u32[]{:S(2)}) collective-permute-start(bf16[128,128]{1,0:T(8,128)(2,1)S(1)} %add_convert_fusion.1), channel_id=1, source_target_pairs={{0,16},{2,18},{4,20},{6,22},{8,24},{10,26},{12,28},{14,30},{16,0},... | collective-permute-start | bytes 98312 | tf_op jit(solution)/shard_map/ppermute | solution.py:229
  12.7 5.1 %collective-permute-start.5 = (bf16[128,128]{1,0:T(8,128)(2,1)S(1)}, bf16[128,128]{1,0:T(8,128)(2,1)S(1)}, u32[]{:S(2)}, u32[]{:S(2)}) collective-permute-start(bf16[128,128]{1,0:T(8,128)(2,1)S(1)} %add_convert_fusion.1), channel_id=1, source_target_pairs={{0,24},{2,26},{4,28},{6,30},{8,16},{10,18},{12,20},{14,22},{16,0},... | collective-permute-start | bytes 98312 | tf_op jit(solution)/shard_map/ppermute | solution.py:229
  14.0 4.0 %collective-permute-start.6 = (bf16[128,128]{1,0:T(8,128)(2,1)S(1)}, bf16[128,128]{1,0:T(8,128)(2,1)S(1)}, u32[]{:S(2)}, u32[]{:S(2)}) collective-permute-start(bf16[128,128]{1,0:T(8,128)(2,1)S(1)} %add_convert_fusion.1), channel_id=1, source_target_pairs={{0,8},{2,10},{4,12},{6,14},{8,0},{10,2},{12,4},{14,6},{16,24},{18,... | collective-permute-start | bytes 98312 | tf_op jit(solution)/shard_map/ppermute | solution.py:229
  18.2 3.7 %collective-permute-start.7 = (bf16[128,128]{1,0:T(8,128)(2,1)S(1)}, bf16[128,128]{1,0:T(8,128)(2,1)S(1)}, u32[]{:S(2)}, u32[]{:S(2)}) collective-permute-start(bf16[128,128]{1,0:T(8,128)(2,1)S(1)} %get-tuple-element.37), channel_id=1, source_target_pairs={{0,7},{1,6},{2,5},{3,4},{4,3},{5,0},{6,1},{7,2},{8,15},{9,14},{10,... | collective-permute-start | bytes 98312 | tf_op jit(solution)/shard_map/ppermute | solution.py:217
  18.2 4.3 %collective-permute-start.8 = (bf16[128,128]{1,0:T(8,128)(2,1)S(1)}, bf16[128,128]{1,0:T(8,128)(2,1)S(1)}, u32[]{:S(2)}, u32[]{:S(2)}) collective-permute-start(bf16[128,128]{1,0:T(8,128)(2,1)S(1)} %get-tuple-element.38), channel_id=1, source_target_pairs={{0,5},{1,4},{2,7},{3,6},{4,1},{5,2},{6,3},{7,0},{8,13},{9,12},{10,... | collective-permute-start | bytes 98312 | tf_op jit(solution)/shard_map/ppermute | solution.py:217
  20.0 3.7 %collective-permute-start.9 = (bf16[128,128]{1,0:T(8,128)(2,1)S(1)}, bf16[128,128]{1,0:T(8,128)(2,1)S(1)}, u32[]{:S(2)}, u32[]{:S(2)}) collective-permute-start(bf16[128,128]{1,0:T(8,128)(2,1)S(1)} %get-tuple-element.39), channel_id=1, source_target_pairs={{0,3},{1,2},{2,1},{3,0},{4,7},{5,6},{6,5},{7,4},{8,11},{9,10},{10,... | collective-permute-start | bytes 98312 | tf_op jit(solution)/shard_map/ppermute | solution.py:217
  20.0 3.6 %copy-start.3 = (bf16[256,512]{1,0:T(8,128)(2,1)S(1)}, bf16[256,512]{1,0:T(8,128)(2,1)}, u32[]{:S(2)}) copy-start(bf16[256,512]{1,0:T(8,128)(2,1)} %c_ref.3) | copy-start | bytes 786436
  20.0 3.6 %collective-permute-start.10 = (bf16[128,128]{1,0:T(8,128)(2,1)S(1)}, bf16[128,128]{1,0:T(8,128)(2,1)S(1)}, u32[]{:S(2)}, u32[]{:S(2)}) collective-permute-start(bf16[128,128]{1,0:T(8,128)(2,1)S(1)} %get-tuple-element.40), channel_id=1, source_target_pairs={{0,1},{1,0},{2,3},{3,2},{4,5},{5,4},{6,7},{7,6},{8,9},{9,8},{10,11... | collective-permute-start | bytes 98312 | tf_op jit(solution)/shard_map/ppermute | solution.py:217
  24.0 1.2 %collective-permute-start.11 = (f32[2,256]{1,0:T(2,128)S(1)}, f32[2,256]{1,0:T(2,128)S(1)}, u32[]{:S(2)}, u32[]{:S(2)}) collective-permute-start(f32[2,256]{1,0:T(2,128)S(1)} %get-tuple-element.43), channel_id=1, source_target_pairs={{0,1},{1,0},{2,3},{3,2},{4,5},{5,4},{6,7},{7,6},{8,9},{9,8},{10,11... | collective-permute-start | bytes 6152 | tf_op jit(solution)/shard_map/ppermute | solution.py:207
  25.6 4.3 %collective-permute-start.12 = (bf16[128,128]{1,0:T(8,128)(2,1)S(1)}, bf16[128,128]{1,0:T(8,128)(2,1)S(1)}, u32[]{:S(2)}, u32[]{:S(2)}) collective-permute-start(bf16[128,128]{1,0:T(8,128)(2,1)S(1)} %get-tuple-element.50), channel_id=1, source_target_pairs={{0,7},{1,6},{2,5},{3,4},{4,3},{5,2},{6,1},{7,0},{8,15},{9,14},{10,... | collective-permute-start | bytes 98312 | tf_op jit(solution)/shard_map/ppermute | solution.py:217
  26.7 3.5 %collective-permute-start.13 = (bf16[128,128]{1,0:T(8,128)(2,1)S(1)}, bf16[128,128]{1,0:T(8,128)(2,1)S(1)}, u32[]{:S(2)}, u32[]{:S(2)}) collective-permute-start(bf16[128,128]{1,0:T(8,128)(2,1)S(1)} %get-tuple-element.51), channel_id=1, source_target_pairs={{0,5},{1,2},{2,7},{3,0},{4,1},{5,6},{6,3},{7,4},{8,13},{9,10},{10,... | collective-permute-start | bytes 98312 | tf_op jit(solution)/shard_map/ppermute | solution.py:217
  27.0 3.9 %collective-permute-start.14 = (bf16[128,128]{1,0:T(8,128)(2,1)S(1)}, bf16[128,128]{1,0:T(8,128)(2,1)S(1)}, u32[]{:S(2)}, u32[]{:S(2)}) collective-permute-start(bf16[128,128]{1,0:T(8,128)(2,1)S(1)} %get-tuple-element.52), channel_id=1, source_target_pairs={{0,3},{1,4},{2,1},{3,6},{4,7},{5,0},{6,5},{7,2},{8,11},{9,12},{10,... | collective-permute-start | bytes 98312 | tf_op jit(solution)/shard_map/ppermute | solution.py:217
  28.5 2.4 %collective-permute-start.15 = (bf16[128,128]{1,0:T(8,128)(2,1)S(1)}, bf16[128,128]{1,0:T(8,128)(2,1)S(1)}, u32[]{:S(2)}, u32[]{:S(2)}) collective-permute-start(bf16[128,128]{1,0:T(8,128)(2,1)S(1)} %get-tuple-element.53), channel_id=1, source_target_pairs={{0,1},{1,0},{2,3},{3,2},{4,5},{5,4},{6,7},{7,6},{8,9},{9,8},{10,11... | collective-permute-start | bytes 98312 | tf_op jit(solution)/shard_map/ppermute | solution.py:217
  30.9 6.5 %collective-permute-start.16 = (bf16[128,128]{1,0:T(8,128)(2,1)S(1)}, bf16[128,128]{1,0:T(8,128)(2,1)S(1)}, u32[]{:S(2)}, u32[]{:S(2)}) collective-permute-start(bf16[128,128]{1,0:T(8,128)(2,1)S(1)} %add_convert_fusion), channel_id=1, source_target_pairs={{0,16},{2,18},{4,20},{6,22},{8,24},{10,26},{12,28},{14,30},{16,8},... | collective-permute-start | bytes 98312 | tf_op jit(solution)/shard_map/ppermute | solution.py:229
  32.5 5.2 %collective-permute-start.17 = (bf16[128,128]{1,0:T(8,128)(2,1)S(1)}, bf16[128,128]{1,0:T(8,128)(2,1)S(1)}, u32[]{:S(2)}, u32[]{:S(2)}) collective-permute-start(bf16[128,128]{1,0:T(8,128)(2,1)S(1)} %add_convert_fusion), channel_id=1, source_target_pairs={{0,16},{2,18},{4,20},{6,22},{8,24},{10,26},{12,28},{14,30},{16,0},... | collective-permute-start | bytes 98312 | tf_op jit(solution)/shard_map/ppermute | solution.py:229
  33.4 4.6 %collective-permute-start.18 = (bf16[128,128]{1,0:T(8,128)(2,1)S(1)}, bf16[128,128]{1,0:T(8,128)(2,1)S(1)}, u32[]{:S(2)}, u32[]{:S(2)}) collective-permute-start(bf16[128,128]{1,0:T(8,128)(2,1)S(1)} %add_convert_fusion), channel_id=1, source_target_pairs={{0,8},{2,10},{4,12},{6,14},{8,0},{10,2},{12,4},{14,6},{16,24},{18,... | collective-permute-start | bytes 98312 | tf_op jit(solution)/shard_map/ppermute | solution.py:229
  38.2 3.5 %collective-permute-start.19 = (bf16[128,128]{1,0:T(8,128)(2,1)S(1)}, bf16[128,128]{1,0:T(8,128)(2,1)S(1)}, u32[]{:S(2)}, u32[]{:S(2)}) collective-permute-start(bf16[128,128]{1,0:T(8,128)(2,1)S(1)} %get-tuple-element.54), channel_id=1, source_target_pairs={{0,7},{1,4},{2,5},{3,6},{4,3},{5,0},{6,1},{7,2},{8,15},{9,12},{10,... | collective-permute-start | bytes 98312 | tf_op jit(solution)/shard_map/ppermute | solution.py:217
  38.2 4.5 %collective-permute-start.20 = (bf16[128,128]{1,0:T(8,128)(2,1)S(1)}, bf16[128,128]{1,0:T(8,128)(2,1)S(1)}, u32[]{:S(2)}, u32[]{:S(2)}) collective-permute-start(bf16[128,128]{1,0:T(8,128)(2,1)S(1)} %get-tuple-element.55), channel_id=1, source_target_pairs={{0,5},{1,2},{2,7},{3,4},{4,1},{5,6},{6,3},{7,0},{8,13},{9,10},{10,... | collective-permute-start | bytes 98312 | tf_op jit(solution)/shard_map/ppermute | solution.py:217
  40.0 3.4 %collective-permute-start.21 = (bf16[128,128]{1,0:T(8,128)(2,1)S(1)}, bf16[128,128]{1,0:T(8,128)(2,1)S(1)}, u32[]{:S(2)}, u32[]{:S(2)}) collective-permute-start(bf16[128,128]{1,0:T(8,128)(2,1)S(1)} %get-tuple-element.56), channel_id=1, source_target_pairs={{0,3},{1,6},{2,1},{3,0},{4,7},{5,2},{6,5},{7,4},{8,11},{9,14},{10,... | collective-permute-start | bytes 98312 | tf_op jit(solution)/shard_map/ppermute | solution.py:217
  40.5 2.8 %collective-permute-start.22 = (bf16[128,128]{1,0:T(8,128)(2,1)S(1)}, bf16[128,128]{1,0:T(8,128)(2,1)S(1)}, u32[]{:S(2)}, u32[]{:S(2)}) collective-permute-start(bf16[128,128]{1,0:T(8,128)(2,1)S(1)} %get-tuple-element.57), channel_id=1, source_target_pairs={{0,1},{1,0},{2,3},{3,2},{4,5},{5,4},{6,7},{7,6},{8,9},{9,8},{10,11... | collective-permute-start | bytes 98312 | tf_op jit(solution)/shard_map/ppermute | solution.py:217

commit v12 on v11

--- a/solution.py
+++ b/solution.py
@@ -42,6 +42,7 @@
 FIRST_GRAD = (((3, 2, 1, 0), (2, 3, 0, 1), (1, 0, 3, 2)), ((3, 2, 1, 0), (1, 0, 3, 2), (2, 3, 0, 1)))
 BACK_GRAD = (((3, 2, 1, 0), (2, 3, 0, 1), (1, 0, 3, 2)), ((2, 3, 0, 1), (1, 2, 3, 0), (3, 0, 1, 2)))
 SAME = (0, 1, 2, 3)
+EARLY, LATE = (0, 1), (2, 3)
 
 
 def targets(wave, odd, op):
@@ -109,14 +110,25 @@
         fixed(mixed_ref, h)[...] = dot(scores, fixed(v_ref, h)[...], ((1,), (0,)))
 
 
-def mixed_kernel(local_ref, q_ref, c_ref, p0, p1, p2, p3, mixed_ref, sums_ref):
-    count = q_ref.shape[0]
-    square = jnp.zeros((count, DH), WIDE)
-    product = jnp.zeros((count, DH), WIDE)
-    for op, p_ref in enumerate((p0, p1, p2, p3)):
+def mixed_kernel(ops, *refs):
+    local_ref, q_ref, c_ref = refs[:3]
+    mixed_ref, square_ref, product_ref = refs[-3:]
+    for n, op in enumerate(ops):
+        h = came(BACK, op)
+        mixed = head(local_ref, h)[...] + dot(head(q_ref, h)[...], refs[3 + n][...], ((1,), (0,)))
+        mixed_ref[n] = mixed
+        square = mixed * mixed
+        product = mixed * head(c_ref, h)[...].astype(WIDE)
+        square_ref[...] = square if n == 0 else square_ref[...] + square
+        product_ref[...] = product if n == 0 else product_ref[...] + product
+
+
+def sums_of_tokens_kernel(local_ref, q_ref, c_ref, p2, p3, square_ref, product_ref, mixed_ref, sums_ref):
+    square, product = square_ref[...], product_ref[...]
+    for n, (op, p_ref) in enumerate(zip(LATE, (p2, p3))):
         h = came(BACK, op)
         mixed = head(local_ref, h)[...] + dot(head(q_ref, h)[...], p_ref[...], ((1,), (0,)))
-        head(mixed_ref, h)[...] = mixed
+        mixed_ref[n] = mixed
         square = square + mixed * mixed
         product = product + mixed * head(c_ref, h)[...].astype(WIDE)
     sums_ref[0:1, :] = jnp.sum(square.T, axis=0, keepdims=True)
@@ -131,20 +143,23 @@
     return inverse, projection
 
 
-def grad_kernel(features, mixed_ref, c_ref, turned_ref, sums_ref, o0, o1, o2, o3, g_ref):
+def grad_kernel(features, mixed_ref, late_ref, c_ref, turned_ref, sums_ref, o0, o1, o2, o3, g_ref, terms_ref):
     count = c_ref.shape[0]
     inverse = lax.rsqrt(sums_ref[0:1, :] * (1.0 / features) + EPSILON)
     share = inverse * inverse * (inverse * sums_ref[1:2, :] * (1.0 / features))
     inverse = jnp.broadcast_to(inverse, (DH, count)).T
     share = jnp.broadcast_to(share, (DH, count)).T
+    for op in EARLY + LATE:
+        h = came(BACK, op)
+        mixed = late_ref[LATE.index(op)] if op in LATE else mixed_ref[EARLY.index(op)]
+        grad = (inverse * head(c_ref, h)[...].astype(WIDE) - share * mixed).astype(LOW)
+        head(g_ref, h)[...] = grad
+        terms_ref[h] = dot(turned_ref[h], grad, ((1,), (0,))).astype(LOW)
     for op, out in enumerate((o0, o1, o2, o3)):
-        h = sent(FIRST_GRAD, op)
-        grad = (inverse * head(c_ref, h)[...].astype(WIDE) - share * head(mixed_ref, h)[...]).astype(LOW)
-        head(g_ref, h)[...] = grad
-        out[...] = dot(turned_ref[h], grad, ((1,), (0,))).astype(LOW)
-
-
-def back_kernel(features, q_ref, k_ref, v_ref, g_ref, scores_ref, mixed_ref, sums_ref, p0, p1, p2, p3,
+        out[...] = terms_ref[sent(FIRST_GRAD, op)]
+
+
+def back_kernel(features, q_ref, k_ref, v_ref, g_ref, scores_ref, mixed_ref, late_ref, sums_ref, p0, p1, p2, p3,
                 normed_ref, query_ref, key_ref, value_ref):
     count = q_ref.shape[0]
     mask = causal_mask(count)
@@ -152,7 +167,7 @@
     for op, p_ref in enumerate((p0, p1, p2, p3)):
         h = came(BACK, op)
         grad = head(g_ref, h)[...]
-        head(normed_ref, h)[...] = (head(mixed_ref, h)[...] * inverse).astype(LOW)
+        head(normed_ref, h)[...] = ((late_ref[LATE.index(op)] if op in LATE else mixed_ref[EARLY.index(op)]) * inverse).astype(LOW)
         raw = dot(grad, head(v_ref, h)[...], ((1,), (1,)))
         coefs = jnp.where(mask, raw, 0.0).astype(LOW)
         query = dot(coefs, head(k_ref, h)[...], ((1,), (0,))) + dot(grad, p_ref[...], ((1,), (1,)))
@@ -161,14 +176,28 @@
         head(value_ref, h)[...] = dot(scores_ref[h], grad, ((0,), (0,)))
 
 
-def last_kernel(k_ref, v_ref, key_local, value_local, p0, p1, p2, p3, key_ref, value_ref):
-    for op, p_ref in enumerate((p0, p1, p2, p3)):
+def grads_of(k_ref, v_ref, key_local, value_local, suffix, h):
+    key = head(key_local, h)[...] + dot(head(v_ref, h)[...], suffix, ((1,), (1,)))
+    value = head(value_local, h)[...] + dot(head(k_ref, h)[...], suffix, ((1,), (0,)))
+    return key.astype(LOW), value.astype(LOW)
+
+
+def early_kernel(k_ref, v_ref, key_local, value_local, p0, p1, key_ref, value_ref):
+    for n, (op, p_ref) in enumerate(zip(EARLY, (p0, p1))):
         h = came(BACK_GRAD, op)
-        suffix = p_ref[...]
-        key = head(key_local, h)[...] + dot(head(v_ref, h)[...], suffix, ((1,), (1,)))
-        head(key_ref, h)[...] = key.astype(LOW)
-        value = head(value_local, h)[...] + dot(head(k_ref, h)[...], suffix, ((1,), (0,)))
-        head(value_ref, h)[...] = value.astype(LOW)
+        key_ref[n], value_ref[n] = grads_of(k_ref, v_ref, key_local, value_local, p_ref[...], h)
+
+
+def last_kernel(k_ref, v_ref, key_local, value_local, p2, p3, key_early, value_early, key_ref, value_ref):
+    for n, op in enumerate(EARLY):
+        h = came(BACK_GRAD, op)
+        head(key_ref, h)[...] = key_early[n]
+        head(value_ref, h)[...] = value_early[n]
+    for op, p_ref in zip(LATE, (p2, p3)):
+        h = came(BACK_GRAD, op)
+        key, value = grads_of(k_ref, v_ref, key_local, value_local, p_ref[...], h)
+        head(key_ref, h)[...] = key
+        head(value_ref, h)[...] = value
 
 
 def quad_steps(quads, before):
@@ -267,22 +296,40 @@
         4 * unit,
     )
     prefix = exclusive_sum(held, True)
-    mixed, sums = call(
-        mixed_kernel, [wide, shape((2, count), WIDE)], (local, q, c, *prefix), unit
+    part = shape((count, DH), WIDE)
+    mixed, square, product = call(
+        functools.partial(mixed_kernel, EARLY),
+        [shape((2, count, DH), WIDE), part, part],
+        (local, q, c, *[prefix[op] for op in EARLY]),
+        unit,
+    )
+    late, sums = call(
+        sums_of_tokens_kernel,
+        [shape((2, count, DH), WIDE), shape((2, count), WIDE)],
+        (local, q, c, *[prefix[op] for op in LATE], square, product),
+        unit,
     )
     sums = sum_over_heads(sums)
     *terms, g = call(
-        functools.partial(grad_kernel, features), [state] * QUAD + [low], (mixed, c, turned, sums), unit
+        functools.partial(grad_kernel, features),
+        [state] * QUAD + [low],
+        (mixed, late, c, turned, sums),
+        unit,
+        scratch_shapes=[pltpu.VMEM((QUAD, DH, DH), LOW)],
     )
     normed_out, query_grad, key_local, value_local = call(
         functools.partial(back_kernel, features),
         [low, low, wide, wide],
-        (q, k, v, g, scores, mixed, sums, *prefix),
+        (q, k, v, g, scores, mixed, late, sums, *prefix),
         9 * unit,
     )
     suffix = exclusive_sum(terms, False, key_local)
+    early = shape((2, count, DH), LOW)
+    key_early, value_early = call(
+        early_kernel, [early] * 2, (k, v, key_local, value_local, *[suffix[op] for op in EARLY]), 2 * unit
+    )
     key_grad, value_grad = call(
-        last_kernel, [low, low], (k, v, key_local, value_local, *suffix), 2 * unit
+        last_kernel, [low, low], (k, v, key_local, value_local, *[suffix[op] for op in LATE], key_early, value_early), unit
     )
     return (normed_out, query_grad, key_grad, value_grad)
 

time: 44.5 us -> 44.5 us (level)
    pallas_call x8 -> x10, Pallas kernels: 6.16 us -> 6.46 us  [call(): pl.pallas_call(kernel, out_shape=outs, in_specs=in_specs or [pl.BlockSpec...]
  transfers between devices with their start and end apart: 23 -> 23, of which waited for: 16 -> 16; matrix products, arithmetic and copies ran while one was open for 0% -> 0% of each run, Pallas kernels for 6% -> 7%
where the time goes in v12:
time: 44.5 us; the launch traced here: 44.3 us
  starting transfers between devices  22.8 us (51%)
  waiting for transfers between devices  14.2 us (32%)
  Pallas kernels  6.46 us (15%)
  between operations  0.74 us (2%)
    ppermute x16, starting transfers between devices, cross(): return lax.ppermute(value, ('seq', 'tp'), pairs)  14 us
    ppermute x6, starting transfers between devices, exclusive_sum(): got.append(lax.ppermute(total, 'seq', pairs))  8.67 us
    ppermute x16, waiting for transfers between devices, cross(): return lax.ppermute(value, ('seq', 'tp'), pairs)  8.61 us
    pallas_call x10, Pallas kernels, call(): pl.pallas_call(kernel, out_shape=outs, in_specs=in_specs or [pl.BlockSpec...  6.46 us
    ppermute x6, waiting for transfers between devices, exclusive_sum(): got.append(lax.ppermute(total, 'seq', pairs))  4.52 us
    ppermute x1, waiting for transfers between devices, exchange(): return lax.ppermute(value, axis, [(i, i ^ bits) for i in range(size)])  1.06 us
  transfers between devices with their start and end apart: 23, of which 16 were waited for; matrix products, arithmetic and copies ran while one was open for 0% of the time, Pallas kernels for 7%

profile of v12, /device:TPU:0, one launch (start us, length us, event | category | flops | bytes accessed | tf_op | source)
XLA Modules:
  0.0 44.3 jit_solution(5791246833161602256)
XLA Ops:
  0.7 1.4 %shard_map.76 = (bf16[128,128]{1,0:T(8,128)(2,1)S(1)}, bf16[128,128]{1,0:T(8,128)(2,1)S(1)}, bf16[128,128]{1,0:T(8,128)(2,1)S(1)}, bf16[128,128]{1,0:T(8,128)(2,1)S(1)}) custom-call(bf16[256,512]{1,0:T(8,128)(2,1)} %k_ref.9, bf16[256,512]{1,0:T(8,128)(2,1)} %v_ref.9), custom_call_target="tpu_custom_call" | custom-call | flops 33554432 | bytes 655360 | tf_op jit(solution)/shard_map/pallas_call | solution.py:71
  2.1 3.4 %collective-permute-start = (bf16[128,128]{1,0:T(8,128)(2,1)S(1)}, bf16[128,128]{1,0:T(8,128)(2,1)S(1)}, u32[]{:S(2)}, u32[]{:S(2)}) collective-permute-start(bf16[128,128]{1,0:T(8,128)(2,1)S(1)} %get-tuple-element.38), channel_id=1, source_target_pairs={{0,7},{1,4},{2,5},{3,6},{4,3},{5,2},{6,1},{7,0},{8,15},{9,12},{10,... | collective-permute-start | bytes 98312 | tf_op jit(solution)/shard_map/ppermute | solution.py:246
  5.5 0.8 %collective-permute-start.1 = (bf16[128,128]{1,0:T(8,128)(2,1)S(1)}, bf16[128,128]{1,0:T(8,128)(2,1)S(1)}, u32[]{:S(2)}, u32[]{:S(2)}) collective-permute-start(bf16[128,128]{1,0:T(8,128)(2,1)S(1)} %get-tuple-element.39), channel_id=1, source_target_pairs={{0,3},{1,6},{2,7},{3,4},{4,1},{5,0},{6,5},{7,2},{8,11},{9,14},{10,... | collective-permute-start | bytes 98312 | tf_op jit(solution)/shard_map/ppermute | solution.py:246
  6.4 0.9 %collective-permute-start.2 = (bf16[128,128]{1,0:T(8,128)(2,1)S(1)}, bf16[128,128]{1,0:T(8,128)(2,1)S(1)}, u32[]{:S(2)}, u32[]{:S(2)}) collective-permute-start(bf16[128,128]{1,0:T(8,128)(2,1)S(1)} %get-tuple-element.40), channel_id=1, source_target_pairs={{0,5},{1,2},{2,1},{3,0},{4,7},{5,6},{6,3},{7,4},{8,13},{9,10},{10,... | collective-permute-start | bytes 98312 | tf_op jit(solution)/shard_map/ppermute | solution.py:246
  7.3 1.9 %collective-permute-done.1.refs_1_ = bf16[128,128]{1,0:T(8,128)(2,1)S(1)} collective-permute-done((bf16[128,128]{1,0:T(8,128)(2,1)S(1)}, bf16[128,128]{1,0:T(8,128)(2,1)S(1)}, u32[]{:S(2)}, u32[]{:S(2)}) %collective-permute-start.1) | collective-permute-done | bytes 32800 | tf_op jit(solution)/shard_map/ppermute | solution.py:246
  9.1 0.8 %collective-permute-done.2.refs_2_ = bf16[128,128]{1,0:T(8,128)(2,1)S(1)} collective-permute-done((bf16[128,128]{1,0:T(8,128)(2,1)S(1)}, bf16[128,128]{1,0:T(8,128)(2,1)S(1)}, u32[]{:S(2)}, u32[]{:S(2)}) %collective-permute-start.2) | collective-permute-done | bytes 32800 | tf_op jit(solution)/shard_map/ppermute | solution.py:246
  10.0 2.7 %collective-permute-start.4 = (bf16[128,128]{1,0:T(8,128)(2,1)S(1)}, bf16[128,128]{1,0:T(8,128)(2,1)S(1)}, u32[]{:S(2)}, u32[]{:S(2)}) collective-permute-start(bf16[128,128]{1,0:T(8,128)(2,1)S(1)} %add_convert_fusion.1), channel_id=1, source_target_pairs={{0,16},{2,18},{4,20},{6,22},{8,24},{10,26},{12,28},{14,30},{16,0},... | collective-permute-start | bytes 98312 | tf_op jit(solution)/shard_map/ppermute | solution.py:258
  12.7 1.3 %collective-permute-start.5 = (bf16[128,128]{1,0:T(8,128)(2,1)S(1)}, bf16[128,128]{1,0:T(8,128)(2,1)S(1)}, u32[]{:S(2)}, u32[]{:S(2)}) collective-permute-start(bf16[128,128]{1,0:T(8,128)(2,1)S(1)} %add_convert_fusion.1), channel_id=1, source_target_pairs={{0,24},{2,26},{4,28},{6,30},{8,16},{10,18},{12,20},{14,22},{16,0},... | collective-permute-start | bytes 98312 | tf_op jit(solution)/shard_map/ppermute | solution.py:258
  14.2 1.0 %collective-permute-done.4.refs_4_ = bf16[128,128]{1,0:T(8,128)(2,1)S(1)} collective-permute-done((bf16[128,128]{1,0:T(8,128)(2,1)S(1)}, bf16[128,128]{1,0:T(8,128)(2,1)S(1)}, u32[]{:S(2)}, u32[]{:S(2)}) %collective-permute-start.4) | collective-permute-done | bytes 32800 | tf_op jit(solution)/shard_map/ppermute | solution.py:258
  15.2 2.5 %collective-permute-done.5.refs_5_ = bf16[128,128]{1,0:T(8,128)(2,1)S(1)} collective-permute-done((bf16[128,128]{1,0:T(8,128)(2,1)S(1)}, bf16[128,128]{1,0:T(8,128)(2,1)S(1)}, u32[]{:S(2)}, u32[]{:S(2)}) %collective-permute-start.5) | collective-permute-done | bytes 32800 | tf_op jit(solution)/shard_map/ppermute | solution.py:258
  18.2 1.7 %collective-permute-start.8 = (bf16[128,128]{1,0:T(8,128)(2,1)S(1)}, bf16[128,128]{1,0:T(8,128)(2,1)S(1)}, u32[]{:S(2)}, u32[]{:S(2)}) collective-permute-start(bf16[128,128]{1,0:T(8,128)(2,1)S(1)} %get-tuple-element.43), channel_id=1, source_target_pairs={{0,5},{1,4},{2,7},{3,6},{4,1},{5,2},{6,3},{7,0},{8,13},{9,12},{10,... | collective-permute-start | bytes 98312 | tf_op jit(solution)/shard_map/ppermute | solution.py:246
  20.0 0.4 collective-permute-start.10
  20.4 0.7 %shard_map.75 = (bf16[4,256,256]{2,1,0:T(8,128)(2,1)S(1)}, f32[256,512]{1,0:T(8,128)S(1)}, bf16[4,128,256]{2,1,0:T(8,128)(2,1)S(1)}) custom-call(bf16[256,512]{1,0:T(8,128)(2,1)S(1)} %copy-done.2, bf16[256,512]{1,0:T(8,128)(2,1)S(1)} %copy-done, bf16[256,512]{1,0:T(8,128)(2,1)S(1)} %copy-done.1), custom_call_target="tpu_custom_call" | custom-call | flops 134217728 | bytes 2097152 | tf_op jit(solution)/shard_map/pallas_call | solution.py:71
  21.1 0.8 %collective-permute-done.7.refs_3_.p0 = bf16[128,128]{1,0:T(8,128)(2,1)S(1)} collective-permute-done((bf16[128,128]{1,0:T(8,128)(2,1)S(1)}, bf16[128,128]{1,0:T(8,128)(2,1)S(1)}, u32[]{:S(2)}, u32[]{:S(2)}) %collective-permute-start.7) | collective-permute-done | bytes 32800 | tf_op jit(solution)/shard_map/ppermute | solution.py:246
  21.9 0.6 %collective-permute-done.8.refs_4_.p1 = bf16[128,128]{1,0:T(8,128)(2,1)S(1)} collective-permute-done((bf16[128,128]{1,0:T(8,128)(2,1)S(1)}, bf16[128,128]{1,0:T(8,128)(2,1)S(1)}, u32[]{:S(2)}, u32[]{:S(2)}) %collective-permute-start.8) | collective-permute-done | bytes 32800 | tf_op jit(solution)/shard_map/ppermute | solution.py:246
  22.7 0.9 %collective-permute-done.9.p2 = bf16[128,128]{1,0:T(8,128)(2,1)S(1)} collective-permute-done((bf16[128,128]{1,0:T(8,128)(2,1)S(1)}, bf16[128,128]{1,0:T(8,128)(2,1)S(1)}, u32[]{:S(2)}, u32[]{:S(2)}) %collective-permute-start.9) | collective-permute-done | bytes 32800 | tf_op jit(solution)/shard_map/ppermute | solution.py:246
  24.1 1.1 %collective-permute-done.11 = f32[2,256]{1,0:T(2,128)S(1)} collective-permute-done((f32[2,256]{1,0:T(2,128)S(1)}, f32[2,256]{1,0:T(2,128)S(1)}, u32[]{:S(2)}, u32[]{:S(2)}) %collective-permute-start.11) | collective-permute-done | bytes 2080 | tf_op jit(solution)/shard_map/ppermute | solution.py:236
  25.2 0.4 shard_map.80
  25.6 1.1 %collective-permute-start.12 = (bf16[128,128]{1,0:T(8,128)(2,1)S(1)}, bf16[128,128]{1,0:T(8,128)(2,1)S(1)}, u32[]{:S(2)}, u32[]{:S(2)}) collective-permute-start(bf16[128,128]{1,0:T(8,128)(2,1)S(1)} %get-tuple-element.58), channel_id=1, source_target_pairs={{0,7},{1,6},{2,5},{3,4},{4,3},{5,2},{6,1},{7,0},{8,15},{9,14},{10,... | collective-permute-start | bytes 98312 | tf_op jit(solution)/shard_map/ppermute | solution.py:246
  26.9 1.5 %collective-permute-start.14 = (bf16[128,128]{1,0:T(8,128)(2,1)S(1)}, bf16[128,128]{1,0:T(8,128)(2,1)S(1)}, u32[]{:S(2)}, u32[]{:S(2)}) collective-permute-start(bf16[128,128]{1,0:T(8,128)(2,1)S(1)} %get-tuple-element.60), channel_id=1, source_target_pairs={{0,3},{1,4},{2,1},{3,6},{4,7},{5,0},{6,5},{7,2},{8,11},{9,12},{10,... | collective-permute-start | bytes 98312 | tf_op jit(solution)/shard_map/ppermute | solution.py:246
  28.8 1.1 %collective-permute-done.12.refs_0_ = bf16[128,128]{1,0:T(8,128)(2,1)S(1)} collective-permute-done((bf16[128,128]{1,0:T(8,128)(2,1)S(1)}, bf16[128,128]{1,0:T(8,128)(2,1)S(1)}, u32[]{:S(2)}, u32[]{:S(2)}) %collective-permute-start.12) | collective-permute-done | bytes 32800 | tf_op jit(solution)/shard_map/ppermute | solution.py:246
  30.2 0.6 %collective-permute-done.14.refs_2_ = bf16[128,128]{1,0:T(8,128)(2,1)S(1)} collective-permute-done((bf16[128,128]{1,0:T(8,128)(2,1)S(1)}, bf16[128,128]{1,0:T(8,128)(2,1)S(1)}, u32[]{:S(2)}, u32[]{:S(2)}) %collective-permute-start.14) | collective-permute-done | bytes 32800 | tf_op jit(solution)/shard_map/ppermute | solution.py:246
  30.8 1.8 %collective-permute-start.16 = (bf16[128,128]{1,0:T(8,128)(2,1)S(1)}, bf16[128,128]{1,0:T(8,128)(2,1)S(1)}, u32[]{:S(2)}, u32[]{:S(2)}) collective-permute-start(bf16[128,128]{1,0:T(8,128)(2,1)S(1)} %add_convert_fusion), channel_id=1, source_target_pairs={{0,16},{2,18},{4,20},{6,22},{8,24},{10,26},{12,28},{14,30},{16,8},... | collective-permute-start | bytes 98312 | tf_op jit(solution)/shard_map/ppermute | solution.py:258
  32.6 0.8 %collective-permute-start.17 = (bf16[128,128]{1,0:T(8,128)(2,1)S(1)}, bf16[128,128]{1,0:T(8,128)(2,1)S(1)}, u32[]{:S(2)}, u32[]{:S(2)}) collective-permute-start(bf16[128,128]{1,0:T(8,128)(2,1)S(1)} %add_convert_fusion), channel_id=1, source_target_pairs={{0,16},{2,18},{4,20},{6,22},{8,24},{10,26},{12,28},{14,30},{16,0},... | collective-permute-start | bytes 98312 | tf_op jit(solution)/shard_map/ppermute | solution.py:258
  33.4 1.9 %collective-permute-start.18 = (bf16[128,128]{1,0:T(8,128)(2,1)S(1)}, bf16[128,128]{1,0:T(8,128)(2,1)S(1)}, u32[]{:S(2)}, u32[]{:S(2)}) collective-permute-start(bf16[128,128]{1,0:T(8,128)(2,1)S(1)} %add_convert_fusion), channel_id=1, source_target_pairs={{0,8},{2,10},{4,12},{6,14},{8,0},{10,2},{12,4},{14,6},{16,24},{18,... | collective-permute-start | bytes 98312 | tf_op jit(solution)/shard_map/ppermute | solution.py:258
  35.3 2.0 %shard_map.81 = (bf16[256,512]{1,0:T(8,128)(2,1)}, bf16[256,512]{1,0:T(8,128)(2,1)}, f32[256,512]{1,0:T(8,128)S(1)}, f32[256,512]{1,0:T(8,128)S(1)}) custom-call(bf16[256,512]{1,0:T(8,128)(2,1)S(1)} %copy-done.2, bf16[256,512]{1,0:T(8,128)(2,1)S(1)} %copy-done, bf16[256,512]{1,0:T(8,128)(2,1)S(1)} %copy-done.1, ...), custom_call_target="tpu_custom_call" | custom-call | flops 301989888 | bytes 3803136 | tf_op jit(solution)/shard_map/pallas_call | solution.py:71
  37.3 0.5 %collective-permute-done.17.refs_5_ = bf16[128,128]{1,0:T(8,128)(2,1)S(1)} collective-permute-done((bf16[128,128]{1,0:T(8,128)(2,1)S(1)}, bf16[128,128]{1,0:T(8,128)(2,1)S(1)}, u32[]{:S(2)}, u32[]{:S(2)}) %collective-permute-start.17) | collective-permute-done | bytes 32800 | tf_op jit(solution)/shard_map/ppermute | solution.py:258
  38.2 1.7 %collective-permute-start.22 = (bf16[128,128]{1,0:T(8,128)(2,1)S(1)}, bf16[128,128]{1,0:T(8,128)(2,1)S(1)}, u32[]{:S(2)}, u32[]{:S(2)}) collective-permute-start(bf16[128,128]{1,0:T(8,128)(2,1)S(1)} %get-tuple-element.65), channel_id=1, source_target_pairs={{0,5},{1,2},{2,7},{3,4},{4,1},{5,6},{6,3},{7,0},{8,13},{9,10},{10,... | collective-permute-start | bytes 98312 | tf_op jit(solution)/shard_map/ppermute | solution.py:246
  39.9 0.6 %collective-permute-start.19 = (bf16[128,128]{1,0:T(8,128)(2,1)S(1)}, bf16[128,128]{1,0:T(8,128)(2,1)S(1)}, u32[]{:S(2)}, u32[]{:S(2)}) collective-permute-start(bf16[128,128]{1,0:T(8,128)(2,1)S(1)} %get-tuple-element.62), channel_id=1, source_target_pairs={{0,3},{1,6},{2,1},{3,0},{4,7},{5,2},{6,5},{7,4},{8,11},{9,14},{10,... | collective-permute-start | bytes 98312 | tf_op jit(solution)/shard_map/ppermute | solution.py:246
  40.5 1.0 %collective-permute-start.20 = (bf16[128,128]{1,0:T(8,128)(2,1)S(1)}, bf16[128,128]{1,0:T(8,128)(2,1)S(1)}, u32[]{:S(2)}, u32[]{:S(2)}) collective-permute-start(bf16[128,128]{1,0:T(8,128)(2,1)S(1)} %get-tuple-element.63), channel_id=1, source_target_pairs={{0,1},{1,0},{2,3},{3,2},{4,5},{5,4},{6,7},{7,6},{8,9},{9,8},{10,11... | collective-permute-start | bytes 98312 | tf_op jit(solution)/shard_map/ppermute | solution.py:246
  41.6 1.1 %collective-permute-done.22.p1 = bf16[128,128]{1,0:T(8,128)(2,1)S(1)} collective-permute-done((bf16[128,128]{1,0:T(8,128)(2,1)S(1)}, bf16[128,128]{1,0:T(8,128)(2,1)S(1)}, u32[]{:S(2)}, u32[]{:S(2)}) %collective-permute-start.22) | collective-permute-done | bytes 32800 | tf_op jit(solution)/shard_map/ppermute | solution.py:246
  43.3 1.0 %shard_map.84 = (bf16[256,512]{1,0:T(8,128)(2,1)}, bf16[256,512]{1,0:T(8,128)(2,1)}) custom-call(bf16[256,512]{1,0:T(8,128)(2,1)S(1)} %copy-done, bf16[256,512]{1,0:T(8,128)(2,1)S(1)} %copy-done.1, f32[256,512]{1,0:T(8,128)S(1)} %get-tuple-element.56.refs_7_.key_local, f32[256,512]{1,0:T(8,128)S(1)} %get-tuple-element.57.value_local, ...), custom_call_target="tpu_custom_call" | custom-call | flops 33554432 | bytes 2424832 | tf_op jit(solution)/shard_map/pallas_call | solution.py:71
  (35 shorter events, 3.4 us)
Async XLA Ops:
  0.6 19.8 %copy-start.1 = (bf16[256,512]{1,0:T(8,128)(2,1)S(1)}, bf16[256,512]{1,0:T(8,128)(2,1)}, u32[]{:S(2)}) copy-start(bf16[256,512]{1,0:T(8,128)(2,1)} %v_ref.9) | copy-start | bytes 786436
  0.6 19.8 %copy-start.2 = (bf16[256,512]{1,0:T(8,128)(2,1)S(1)}, bf16[256,512]{1,0:T(8,128)(2,1)}, u32[]{:S(2)}) copy-start(bf16[256,512]{1,0:T(8,128)(2,1)} %q_ref.5) | copy-start | bytes 786436
  2.1 18.3 %copy-start = (bf16[256,512]{1,0:T(8,128)(2,1)S(1)}, bf16[256,512]{1,0:T(8,128)(2,1)}, u32[]{:S(2)}) copy-start(bf16[256,512]{1,0:T(8,128)(2,1)} %k_ref.9) | copy-start | bytes 786436
  2.1 5.1 %collective-permute-start = (bf16[128,128]{1,0:T(8,128)(2,1)S(1)}, bf16[128,128]{1,0:T(8,128)(2,1)S(1)}, u32[]{:S(2)}, u32[]{:S(2)}) collective-permute-start(bf16[128,128]{1,0:T(8,128)(2,1)S(1)} %get-tuple-element.38), channel_id=1, source_target_pairs={{0,7},{1,4},{2,5},{3,6},{4,3},{5,2},{6,1},{7,0},{8,15},{9,12},{10,... | collective-permute-start | bytes 98312 | tf_op jit(solution)/shard_map/ppermute | solution.py:246
  5.5 3.6 %collective-permute-start.1 = (bf16[128,128]{1,0:T(8,128)(2,1)S(1)}, bf16[128,128]{1,0:T(8,128)(2,1)S(1)}, u32[]{:S(2)}, u32[]{:S(2)}) collective-permute-start(bf16[128,128]{1,0:T(8,128)(2,1)S(1)} %get-tuple-element.39), channel_id=1, source_target_pairs={{0,3},{1,6},{2,7},{3,4},{4,1},{5,0},{6,5},{7,2},{8,11},{9,14},{10,... | collective-permute-start | bytes 98312 | tf_op jit(solution)/shard_map/ppermute | solution.py:246
  6.4 3.6 %collective-permute-start.2 = (bf16[128,128]{1,0:T(8,128)(2,1)S(1)}, bf16[128,128]{1,0:T(8,128)(2,1)S(1)}, u32[]{:S(2)}, u32[]{:S(2)}) collective-permute-start(bf16[128,128]{1,0:T(8,128)(2,1)S(1)} %get-tuple-element.40), channel_id=1, source_target_pairs={{0,5},{1,2},{2,1},{3,0},{4,7},{5,6},{6,3},{7,4},{8,13},{9,10},{10,... | collective-permute-start | bytes 98312 | tf_op jit(solution)/shard_map/ppermute | solution.py:246
  7.3 2.7 %collective-permute-start.3 = (bf16[128,128]{1,0:T(8,128)(2,1)S(1)}, bf16[128,128]{1,0:T(8,128)(2,1)S(1)}, u32[]{:S(2)}, u32[]{:S(2)}) collective-permute-start(bf16[128,128]{1,0:T(8,128)(2,1)S(1)} %get-tuple-element.41), channel_id=1, source_target_pairs={{0,1},{1,0},{2,3},{3,2},{4,5},{5,4},{6,7},{7,6},{8,9},{9,8},{10,11... | collective-permute-start | bytes 98312 | tf_op jit(solution)/shard_map/ppermute | solution.py:246
  10.0 5.2 %collective-permute-start.4 = (bf16[128,128]{1,0:T(8,128)(2,1)S(1)}, bf16[128,128]{1,0:T(8,128)(2,1)S(1)}, u32[]{:S(2)}, u32[]{:S(2)}) collective-permute-start(bf16[128,128]{1,0:T(8,128)(2,1)S(1)} %add_convert_fusion.1), channel_id=1, source_target_pairs={{0,16},{2,18},{4,20},{6,22},{8,24},{10,26},{12,28},{14,30},{16,0},... | collective-permute-start | bytes 98312 | tf_op jit(solution)/shard_map/ppermute | solution.py:258
  12.7 5.1 %collective-permute-start.5 = (bf16[128,128]{1,0:T(8,128)(2,1)S(1)}, bf16[128,128]{1,0:T(8,128)(2,1)S(1)}, u32[]{:S(2)}, u32[]{:S(2)}) collective-permute-start(bf16[128,128]{1,0:T(8,128)(2,1)S(1)} %add_convert_fusion.1), channel_id=1, source_target_pairs={{0,24},{2,26},{4,28},{6,30},{8,16},{10,18},{12,20},{14,22},{16,0},... | collective-permute-start | bytes 98312 | tf_op jit(solution)/shard_map/ppermute | solution.py:258
  14.0 4.0 %collective-permute-start.6 = (bf16[128,128]{1,0:T(8,128)(2,1)S(1)}, bf16[128,128]{1,0:T(8,128)(2,1)S(1)}, u32[]{:S(2)}, u32[]{:S(2)}) collective-permute-start(bf16[128,128]{1,0:T(8,128)(2,1)S(1)} %add_convert_fusion.1), channel_id=1, source_target_pairs={{0,8},{2,10},{4,12},{6,14},{8,0},{10,2},{12,4},{14,6},{16,24},{18,... | collective-permute-start | bytes 98312 | tf_op jit(solution)/shard_map/ppermute | solution.py:258
  18.2 3.7 %collective-permute-start.7 = (bf16[128,128]{1,0:T(8,128)(2,1)S(1)}, bf16[128,128]{1,0:T(8,128)(2,1)S(1)}, u32[]{:S(2)}, u32[]{:S(2)}) collective-permute-start(bf16[128,128]{1,0:T(8,128)(2,1)S(1)} %get-tuple-element.42), channel_id=1, source_target_pairs={{0,7},{1,6},{2,5},{3,4},{4,3},{5,0},{6,1},{7,2},{8,15},{9,14},{10,... | collective-permute-start | bytes 98312 | tf_op jit(solution)/shard_map/ppermute | solution.py:246
  18.2 4.3 %collective-permute-start.8 = (bf16[128,128]{1,0:T(8,128)(2,1)S(1)}, bf16[128,128]{1,0:T(8,128)(2,1)S(1)}, u32[]{:S(2)}, u32[]{:S(2)}) collective-permute-start(bf16[128,128]{1,0:T(8,128)(2,1)S(1)} %get-tuple-element.43), channel_id=1, source_target_pairs={{0,5},{1,4},{2,7},{3,6},{4,1},{5,2},{6,3},{7,0},{8,13},{9,12},{10,... | collective-permute-start | bytes 98312 | tf_op jit(solution)/shard_map/ppermute | solution.py:246
  20.0 3.7 %collective-permute-start.9 = (bf16[128,128]{1,0:T(8,128)(2,1)S(1)}, bf16[128,128]{1,0:T(8,128)(2,1)S(1)}, u32[]{:S(2)}, u32[]{:S(2)}) collective-permute-start(bf16[128,128]{1,0:T(8,128)(2,1)S(1)} %get-tuple-element.45), channel_id=1, source_target_pairs={{0,3},{1,2},{2,1},{3,0},{4,7},{5,6},{6,5},{7,4},{8,11},{9,10},{10,... | collective-permute-start | bytes 98312 | tf_op jit(solution)/shard_map/ppermute | solution.py:246
  20.0 2.5 %copy-start.3 = (bf16[256,512]{1,0:T(8,128)(2,1)S(1)}, bf16[256,512]{1,0:T(8,128)(2,1)}, u32[]{:S(2)}) copy-start(bf16[256,512]{1,0:T(8,128)(2,1)} %c_ref.3) | copy-start | bytes 786436
  20.0 3.6 %collective-permute-start.10 = (bf16[128,128]{1,0:T(8,128)(2,1)S(1)}, bf16[128,128]{1,0:T(8,128)(2,1)S(1)}, u32[]{:S(2)}, u32[]{:S(2)}) collective-permute-start(bf16[128,128]{1,0:T(8,128)(2,1)S(1)} %get-tuple-element.46), channel_id=1, source_target_pairs={{0,1},{1,0},{2,3},{3,2},{4,5},{5,4},{6,7},{7,6},{8,9},{9,8},{10,11... | collective-permute-start | bytes 98312 | tf_op jit(solution)/shard_map/ppermute | solution.py:246
  23.9 1.2 %collective-permute-start.11 = (f32[2,256]{1,0:T(2,128)S(1)}, f32[2,256]{1,0:T(2,128)S(1)}, u32[]{:S(2)}, u32[]{:S(2)}) collective-permute-start(f32[2,256]{1,0:T(2,128)S(1)} %get-tuple-element.51), channel_id=1, source_target_pairs={{0,1},{1,0},{2,3},{3,2},{4,5},{5,4},{6,7},{7,6},{8,9},{9,8},{10,11... | collective-permute-start | bytes 6152 | tf_op jit(solution)/shard_map/ppermute | solution.py:236
  25.6 4.3 %collective-permute-start.12 = (bf16[128,128]{1,0:T(8,128)(2,1)S(1)}, bf16[128,128]{1,0:T(8,128)(2,1)S(1)}, u32[]{:S(2)}, u32[]{:S(2)}) collective-permute-start(bf16[128,128]{1,0:T(8,128)(2,1)S(1)} %get-tuple-element.58), channel_id=1, source_target_pairs={{0,7},{1,6},{2,5},{3,4},{4,3},{5,2},{6,1},{7,0},{8,15},{9,14},{10,... | collective-permute-start | bytes 98312 | tf_op jit(solution)/shard_map/ppermute | solution.py:246
  26.7 3.5 %collective-permute-start.13 = (bf16[128,128]{1,0:T(8,128)(2,1)S(1)}, bf16[128,128]{1,0:T(8,128)(2,1)S(1)}, u32[]{:S(2)}, u32[]{:S(2)}) collective-permute-start(bf16[128,128]{1,0:T(8,128)(2,1)S(1)} %get-tuple-element.59), channel_id=1, source_target_pairs={{0,5},{1,2},{2,7},{3,0},{4,1},{5,6},{6,3},{7,4},{8,13},{9,10},{10,... | collective-permute-start | bytes 98312 | tf_op jit(solution)/shard_map/ppermute | solution.py:246
  26.9 3.9 %collective-permute-start.14 = (bf16[128,128]{1,0:T(8,128)(2,1)S(1)}, bf16[128,128]{1,0:T(8,128)(2,1)S(1)}, u32[]{:S(2)}, u32[]{:S(2)}) collective-permute-start(bf16[128,128]{1,0:T(8,128)(2,1)S(1)} %get-tuple-element.60), channel_id=1, source_target_pairs={{0,3},{1,4},{2,1},{3,6},{4,7},{5,0},{6,5},{7,2},{8,11},{9,12},{10,... | collective-permute-start | bytes 98312 | tf_op jit(solution)/shard_map/ppermute | solution.py:246
  28.4 2.4 %collective-permute-start.15 = (bf16[128,128]{1,0:T(8,128)(2,1)S(1)}, bf16[128,128]{1,0:T(8,128)(2,1)S(1)}, u32[]{:S(2)}, u32[]{:S(2)}) collective-permute-start(bf16[128,128]{1,0:T(8,128)(2,1)S(1)} %get-tuple-element.61), channel_id=1, source_target_pairs={{0,1},{1,0},{2,3},{3,2},{4,5},{5,4},{6,7},{7,6},{8,9},{9,8},{10,11... | collective-permute-start | bytes 98312 | tf_op jit(solution)/shard_map/ppermute | solution.py:246
  30.8 6.5 %collective-permute-start.16 = (bf16[128,128]{1,0:T(8,128)(2,1)S(1)}, bf16[128,128]{1,0:T(8,128)(2,1)S(1)}, u32[]{:S(2)}, u32[]{:S(2)}) collective-permute-start(bf16[128,128]{1,0:T(8,128)(2,1)S(1)} %add_convert_fusion), channel_id=1, source_target_pairs={{0,16},{2,18},{4,20},{6,22},{8,24},{10,26},{12,28},{14,30},{16,8},... | collective-permute-start | bytes 98312 | tf_op jit(solution)/shard_map/ppermute | solution.py:258
  32.6 5.2 %collective-permute-start.17 = (bf16[128,128]{1,0:T(8,128)(2,1)S(1)}, bf16[128,128]{1,0:T(8,128)(2,1)S(1)}, u32[]{:S(2)}, u32[]{:S(2)}) collective-permute-start(bf16[128,128]{1,0:T(8,128)(2,1)S(1)} %add_convert_fusion), channel_id=1, source_target_pairs={{0,16},{2,18},{4,20},{6,22},{8,24},{10,26},{12,28},{14,30},{16,0},... | collective-permute-start | bytes 98312 | tf_op jit(solution)/shard_map/ppermute | solution.py:258
  33.4 4.6 %collective-permute-start.18 = (bf16[128,128]{1,0:T(8,128)(2,1)S(1)}, bf16[128,128]{1,0:T(8,128)(2,1)S(1)}, u32[]{:S(2)}, u32[]{:S(2)}) collective-permute-start(bf16[128,128]{1,0:T(8,128)(2,1)S(1)} %add_convert_fusion), channel_id=1, source_target_pairs={{0,8},{2,10},{4,12},{6,14},{8,0},{10,2},{12,4},{14,6},{16,24},{18,... | collective-permute-start | bytes 98312 | tf_op jit(solution)/shard_map/ppermute | solution.py:258
  38.1 3.4 %collective-permute-start.21 = (bf16[128,128]{1,0:T(8,128)(2,1)S(1)}, bf16[128,128]{1,0:T(8,128)(2,1)S(1)}, u32[]{:S(2)}, u32[]{:S(2)}) collective-permute-start(bf16[128,128]{1,0:T(8,128)(2,1)S(1)} %get-tuple-element.64), channel_id=1, source_target_pairs={{0,7},{1,4},{2,5},{3,6},{4,3},{5,0},{6,1},{7,2},{8,15},{9,12},{10,... | collective-permute-start | bytes 98312 | tf_op jit(solution)/shard_map/ppermute | solution.py:246
  38.2 4.5 %collective-permute-start.22 = (bf16[128,128]{1,0:T(8,128)(2,1)S(1)}, bf16[128,128]{1,0:T(8,128)(2,1)S(1)}, u32[]{:S(2)}, u32[]{:S(2)}) collective-permute-start(bf16[128,128]{1,0:T(8,128)(2,1)S(1)} %get-tuple-element.65), channel_id=1, source_target_pairs={{0,5},{1,2},{2,7},{3,4},{4,1},{5,6},{6,3},{7,0},{8,13},{9,10},{10,... | collective-permute-start | bytes 98312 | tf_op jit(solution)/shard_map/ppermute | solution.py:246
  39.9 3.4 %collective-permute-start.19 = (bf16[128,128]{1,0:T(8,128)(2,1)S(1)}, bf16[128,128]{1,0:T(8,128)(2,1)S(1)}, u32[]{:S(2)}, u32[]{:S(2)}) collective-permute-start(bf16[128,128]{1,0:T(8,128)(2,1)S(1)} %get-tuple-element.62), channel_id=1, source_target_pairs={{0,3},{1,6},{2,1},{3,0},{4,7},{5,2},{6,5},{7,4},{8,11},{9,14},{10,... | collective-permute-start | bytes 98312 | tf_op jit(solution)/shard_map/ppermute | solution.py:246
  40.5 2.8 %collective-permute-start.20 = (bf16[128,128]{1,0:T(8,128)(2,1)S(1)}, bf16[128,128]{1,0:T(8,128)(2,1)S(1)}, u32[]{:S(2)}, u32[]{:S(2)}) collective-permute-start(bf16[128,128]{1,0:T(8,128)(2,1)S(1)} %get-tuple-element.63), channel_id=1, source_target_pairs={{0,1},{1,0},{2,3},{3,2},{4,5},{5,4},{6,7},{7,6},{8,9},{9,8},{10,11... | collective-permute-start | bytes 98312 | tf_op jit(solution)/shard_map/ppermute | solution.py:246

commit v13 on v12

--- a/solution.py
+++ b/solution.py
@@ -37,10 +37,10 @@
     return lax.axis_index("seq") % QUAD
 
 
-FIRST = (((3, 2, 1, 0), (1, 3, 0, 2), (2, 0, 3, 1)), ((2, 3, 1, 0), (3, 2, 0, 1), (1, 0, 3, 2)))
+FIRST = (((3, 2, 1, 0), (1, 0, 3, 2), (2, 3, 0, 1)), ((1, 2, 3, 0), (3, 0, 1, 2), (2, 3, 0, 1)))
 BACK = (((3, 2, 1, 0), (2, 3, 0, 1), (1, 0, 3, 2)), ((3, 2, 0, 1), (2, 3, 1, 0), (1, 0, 3, 2)))
-FIRST_GRAD = (((3, 2, 1, 0), (2, 3, 0, 1), (1, 0, 3, 2)), ((3, 2, 1, 0), (1, 0, 3, 2), (2, 3, 0, 1)))
-BACK_GRAD = (((3, 2, 1, 0), (2, 3, 0, 1), (1, 0, 3, 2)), ((2, 3, 0, 1), (1, 2, 3, 0), (3, 0, 1, 2)))
+FIRST_GRAD = (((3, 2, 1, 0), (2, 0, 3, 1), (1, 3, 0, 2)), ((3, 0, 1, 2), (1, 2, 3, 0), (2, 3, 0, 1)))
+BACK_GRAD = (((3, 2, 1, 0), (1, 3, 0, 2), (2, 0, 3, 1)), ((2, 3, 1, 0), (1, 0, 3, 2), (3, 2, 0, 1)))
 SAME = (0, 1, 2, 3)
 EARLY, LATE = (0, 1), (2, 3)
 

time: 44.5 us -> 44.7 us (level)
  no operation moved by 1% of the time
where the time goes in v13:
time: 44.7 us; the launch traced here: 44.6 us
  starting transfers between devices  23.1 us (52%)
  waiting for transfers between devices  14.2 us (32%)
  Pallas kernels  6.47 us (14%)
  between operations  0.73 us (2%)
    ppermute x16, starting transfers between devices, cross(): return lax.ppermute(value, ('seq', 'tp'), pairs)  14.3 us
    ppermute x6, starting transfers between devices, exclusive_sum(): got.append(lax.ppermute(total, 'seq', pairs))  8.67 us
    ppermute x16, waiting for transfers between devices, cross(): return lax.ppermute(value, ('seq', 'tp'), pairs)  8.56 us
    pallas_call x10, Pallas kernels, call(): pl.pallas_call(kernel, out_shape=outs, in_specs=in_specs or [pl.BlockSpec...  6.47 us
    ppermute x6, waiting for transfers between devices, exclusive_sum(): got.append(lax.ppermute(total, 'seq', pairs))  4.63 us
    ppermute x1, waiting for transfers between devices, exchange(): return lax.ppermute(value, axis, [(i, i ^ bits) for i in range(size)])  1.04 us
  transfers between devices with their start and end apart: 23, of which 16 were waited for; matrix products, arithmetic and copies ran while one was open for 0% of the time, Pallas kernels for 7%

profile of v13, /device:TPU:0, one launch (start us, length us, event | category | flops | bytes accessed | tf_op | source)
XLA Modules:
  0.0 44.6 jit_solution(14113620126672273473)
XLA Ops:
  0.7 1.4 %shard_map.76 = (bf16[128,128]{1,0:T(8,128)(2,1)S(1)}, bf16[128,128]{1,0:T(8,128)(2,1)S(1)}, bf16[128,128]{1,0:T(8,128)(2,1)S(1)}, bf16[128,128]{1,0:T(8,128)(2,1)S(1)}) custom-call(bf16[256,512]{1,0:T(8,128)(2,1)} %k_ref.9, bf16[256,512]{1,0:T(8,128)(2,1)} %v_ref.9), custom_call_target="tpu_custom_call" | custom-call | flops 33554432 | bytes 655360 | tf_op jit(solution)/shard_map/pallas_call | solution.py:71
  2.1 3.4 %collective-permute-start = (bf16[128,128]{1,0:T(8,128)(2,1)S(1)}, bf16[128,128]{1,0:T(8,128)(2,1)S(1)}, u32[]{:S(2)}, u32[]{:S(2)}) collective-permute-start(bf16[128,128]{1,0:T(8,128)(2,1)S(1)} %get-tuple-element.38), channel_id=1, source_target_pairs={{0,7},{1,2},{2,5},{3,4},{4,3},{5,6},{6,1},{7,0},{8,15},{9,10},{10,... | collective-permute-start | bytes 98312 | tf_op jit(solution)/shard_map/ppermute | solution.py:246
  5.5 0.8 %collective-permute-start.1 = (bf16[128,128]{1,0:T(8,128)(2,1)S(1)}, bf16[128,128]{1,0:T(8,128)(2,1)S(1)}, u32[]{:S(2)}, u32[]{:S(2)}) collective-permute-start(bf16[128,128]{1,0:T(8,128)(2,1)S(1)} %get-tuple-element.39), channel_id=1, source_target_pairs={{0,3},{1,6},{2,1},{3,0},{4,7},{5,2},{6,5},{7,4},{8,11},{9,14},{10,... | collective-permute-start | bytes 98312 | tf_op jit(solution)/shard_map/ppermute | solution.py:246
  6.3 0.9 %collective-permute-start.2 = (bf16[128,128]{1,0:T(8,128)(2,1)S(1)}, bf16[128,128]{1,0:T(8,128)(2,1)S(1)}, u32[]{:S(2)}, u32[]{:S(2)}) collective-permute-start(bf16[128,128]{1,0:T(8,128)(2,1)S(1)} %get-tuple-element.40), channel_id=1, source_target_pairs={{0,5},{1,4},{2,7},{3,6},{4,1},{5,0},{6,3},{7,2},{8,13},{9,12},{10,... | collective-permute-start | bytes 98312 | tf_op jit(solution)/shard_map/ppermute | solution.py:246
  7.2 1.9 %collective-permute-done.1.refs_1_ = bf16[128,128]{1,0:T(8,128)(2,1)S(1)} collective-permute-done((bf16[128,128]{1,0:T(8,128)(2,1)S(1)}, bf16[128,128]{1,0:T(8,128)(2,1)S(1)}, u32[]{:S(2)}, u32[]{:S(2)}) %collective-permute-start.1) | collective-permute-done | bytes 32800 | tf_op jit(solution)/shard_map/ppermute | solution.py:246
  9.1 0.8 %collective-permute-done.2.refs_2_ = bf16[128,128]{1,0:T(8,128)(2,1)S(1)} collective-permute-done((bf16[128,128]{1,0:T(8,128)(2,1)S(1)}, bf16[128,128]{1,0:T(8,128)(2,1)S(1)}, u32[]{:S(2)}, u32[]{:S(2)}) %collective-permute-start.2) | collective-permute-done | bytes 32800 | tf_op jit(solution)/shard_map/ppermute | solution.py:246
  9.9 2.7 %collective-permute-start.4 = (bf16[128,128]{1,0:T(8,128)(2,1)S(1)}, bf16[128,128]{1,0:T(8,128)(2,1)S(1)}, u32[]{:S(2)}, u32[]{:S(2)}) collective-permute-start(bf16[128,128]{1,0:T(8,128)(2,1)S(1)} %add_convert_fusion.1), channel_id=1, source_target_pairs={{0,16},{2,18},{4,20},{6,22},{8,24},{10,26},{12,28},{14,30},{16,0},... | collective-permute-start | bytes 98312 | tf_op jit(solution)/shard_map/ppermute | solution.py:258
  12.6 1.3 %collective-permute-start.5 = (bf16[128,128]{1,0:T(8,128)(2,1)S(1)}, bf16[128,128]{1,0:T(8,128)(2,1)S(1)}, u32[]{:S(2)}, u32[]{:S(2)}) collective-permute-start(bf16[128,128]{1,0:T(8,128)(2,1)S(1)} %add_convert_fusion.1), channel_id=1, source_target_pairs={{0,24},{2,26},{4,28},{6,30},{8,16},{10,18},{12,20},{14,22},{16,0},... | collective-permute-start | bytes 98312 | tf_op jit(solution)/shard_map/ppermute | solution.py:258
  14.2 1.0 %collective-permute-done.4.refs_4_ = bf16[128,128]{1,0:T(8,128)(2,1)S(1)} collective-permute-done((bf16[128,128]{1,0:T(8,128)(2,1)S(1)}, bf16[128,128]{1,0:T(8,128)(2,1)S(1)}, u32[]{:S(2)}, u32[]{:S(2)}) %collective-permute-start.4) | collective-permute-done | bytes 32800 | tf_op jit(solution)/shard_map/ppermute | solution.py:258
  15.2 2.5 %collective-permute-done.5.refs_5_ = bf16[128,128]{1,0:T(8,128)(2,1)S(1)} collective-permute-done((bf16[128,128]{1,0:T(8,128)(2,1)S(1)}, bf16[128,128]{1,0:T(8,128)(2,1)S(1)}, u32[]{:S(2)}, u32[]{:S(2)}) %collective-permute-start.5) | collective-permute-done | bytes 32800 | tf_op jit(solution)/shard_map/ppermute | solution.py:258
  18.2 1.7 %collective-permute-start.8 = (bf16[128,128]{1,0:T(8,128)(2,1)S(1)}, bf16[128,128]{1,0:T(8,128)(2,1)S(1)}, u32[]{:S(2)}, u32[]{:S(2)}) collective-permute-start(bf16[128,128]{1,0:T(8,128)(2,1)S(1)} %get-tuple-element.43), channel_id=1, source_target_pairs={{0,5},{1,4},{2,7},{3,6},{4,1},{5,2},{6,3},{7,0},{8,13},{9,12},{10,... | collective-permute-start | bytes 98312 | tf_op jit(solution)/shard_map/ppermute | solution.py:246
  20.0 0.6 %collective-permute-start.10 = (bf16[128,128]{1,0:T(8,128)(2,1)S(1)}, bf16[128,128]{1,0:T(8,128)(2,1)S(1)}, u32[]{:S(2)}, u32[]{:S(2)}) collective-permute-start(bf16[128,128]{1,0:T(8,128)(2,1)S(1)} %get-tuple-element.46), channel_id=1, source_target_pairs={{0,1},{1,0},{2,3},{3,2},{4,5},{5,4},{6,7},{7,6},{8,9},{9,8},{10,11... | collective-permute-start | bytes 98312 | tf_op jit(solution)/shard_map/ppermute | solution.py:246
  20.6 0.7 %shard_map.75 = (bf16[4,256,256]{2,1,0:T(8,128)(2,1)S(1)}, f32[256,512]{1,0:T(8,128)S(1)}, bf16[4,128,256]{2,1,0:T(8,128)(2,1)S(1)}) custom-call(bf16[256,512]{1,0:T(8,128)(2,1)S(1)} %copy-done.2, bf16[256,512]{1,0:T(8,128)(2,1)S(1)} %copy-done, bf16[256,512]{1,0:T(8,128)(2,1)S(1)} %copy-done.1), custom_call_target="tpu_custom_call" | custom-call | flops 134217728 | bytes 2097152 | tf_op jit(solution)/shard_map/pallas_call | solution.py:71
  21.3 0.6 %collective-permute-done.7.refs_3_.p0 = bf16[128,128]{1,0:T(8,128)(2,1)S(1)} collective-permute-done((bf16[128,128]{1,0:T(8,128)(2,1)S(1)}, bf16[128,128]{1,0:T(8,128)(2,1)S(1)}, u32[]{:S(2)}, u32[]{:S(2)}) %collective-permute-start.7) | collective-permute-done | bytes 32800 | tf_op jit(solution)/shard_map/ppermute | solution.py:246
  21.9 0.6 %collective-permute-done.8.refs_4_.p1 = bf16[128,128]{1,0:T(8,128)(2,1)S(1)} collective-permute-done((bf16[128,128]{1,0:T(8,128)(2,1)S(1)}, bf16[128,128]{1,0:T(8,128)(2,1)S(1)}, u32[]{:S(2)}, u32[]{:S(2)}) %collective-permute-start.8) | collective-permute-done | bytes 32800 | tf_op jit(solution)/shard_map/ppermute | solution.py:246
  22.7 0.9 %collective-permute-done.9.p2 = bf16[128,128]{1,0:T(8,128)(2,1)S(1)} collective-permute-done((bf16[128,128]{1,0:T(8,128)(2,1)S(1)}, bf16[128,128]{1,0:T(8,128)(2,1)S(1)}, u32[]{:S(2)}, u32[]{:S(2)}) %collective-permute-start.9) | collective-permute-done | bytes 32800 | tf_op jit(solution)/shard_map/ppermute | solution.py:246
  24.0 1.0 %collective-permute-done.11 = f32[2,256]{1,0:T(2,128)S(1)} collective-permute-done((f32[2,256]{1,0:T(2,128)S(1)}, f32[2,256]{1,0:T(2,128)S(1)}, u32[]{:S(2)}, u32[]{:S(2)}) %collective-permute-start.11) | collective-permute-done | bytes 2080 | tf_op jit(solution)/shard_map/ppermute | solution.py:236
  25.5 0.7 %collective-permute-start.12 = (bf16[128,128]{1,0:T(8,128)(2,1)S(1)}, bf16[128,128]{1,0:T(8,128)(2,1)S(1)}, u32[]{:S(2)}, u32[]{:S(2)}) collective-permute-start(bf16[128,128]{1,0:T(8,128)(2,1)S(1)} %get-tuple-element.58), channel_id=1, source_target_pairs={{0,7},{1,6},{2,5},{3,0},{4,3},{5,2},{6,1},{7,4},{8,15},{9,14},{10,... | collective-permute-start | bytes 98312 | tf_op jit(solution)/shard_map/ppermute | solution.py:246
  26.2 1.0 %collective-permute-start.13 = (bf16[128,128]{1,0:T(8,128)(2,1)S(1)}, bf16[128,128]{1,0:T(8,128)(2,1)S(1)}, u32[]{:S(2)}, u32[]{:S(2)}) collective-permute-start(bf16[128,128]{1,0:T(8,128)(2,1)S(1)} %get-tuple-element.59), channel_id=1, source_target_pairs={{0,5},{1,2},{2,1},{3,4},{4,7},{5,6},{6,3},{7,0},{8,13},{9,10},{10,... | collective-permute-start | bytes 98312 | tf_op jit(solution)/shard_map/ppermute | solution.py:246
  27.2 1.2 %collective-permute-start.14 = (bf16[128,128]{1,0:T(8,128)(2,1)S(1)}, bf16[128,128]{1,0:T(8,128)(2,1)S(1)}, u32[]{:S(2)}, u32[]{:S(2)}) collective-permute-start(bf16[128,128]{1,0:T(8,128)(2,1)S(1)} %get-tuple-element.60), channel_id=1, source_target_pairs={{0,3},{1,4},{2,7},{3,6},{4,1},{5,0},{6,5},{7,2},{8,11},{9,12},{10,... | collective-permute-start | bytes 98312 | tf_op jit(solution)/shard_map/ppermute | solution.py:246
  28.9 1.6 %collective-permute-done.13.refs_1_ = bf16[128,128]{1,0:T(8,128)(2,1)S(1)} collective-permute-done((bf16[128,128]{1,0:T(8,128)(2,1)S(1)}, bf16[128,128]{1,0:T(8,128)(2,1)S(1)}, u32[]{:S(2)}, u32[]{:S(2)}) %collective-permute-start.13) | collective-permute-done | bytes 32800 | tf_op jit(solution)/shard_map/ppermute | solution.py:246
  30.8 1.9 %collective-permute-start.16 = (bf16[128,128]{1,0:T(8,128)(2,1)S(1)}, bf16[128,128]{1,0:T(8,128)(2,1)S(1)}, u32[]{:S(2)}, u32[]{:S(2)}) collective-permute-start(bf16[128,128]{1,0:T(8,128)(2,1)S(1)} %add_convert_fusion), channel_id=1, source_target_pairs={{0,16},{2,18},{4,20},{6,22},{8,24},{10,26},{12,28},{14,30},{16,8},... | collective-permute-start | bytes 98312 | tf_op jit(solution)/shard_map/ppermute | solution.py:258
  32.7 0.8 %collective-permute-start.17 = (bf16[128,128]{1,0:T(8,128)(2,1)S(1)}, bf16[128,128]{1,0:T(8,128)(2,1)S(1)}, u32[]{:S(2)}, u32[]{:S(2)}) collective-permute-start(bf16[128,128]{1,0:T(8,128)(2,1)S(1)} %add_convert_fusion), channel_id=1, source_target_pairs={{0,16},{2,18},{4,20},{6,22},{8,24},{10,26},{12,28},{14,30},{16,0},... | collective-permute-start | bytes 98312 | tf_op jit(solution)/shard_map/ppermute | solution.py:258
  33.5 1.7 %collective-permute-start.18 = (bf16[128,128]{1,0:T(8,128)(2,1)S(1)}, bf16[128,128]{1,0:T(8,128)(2,1)S(1)}, u32[]{:S(2)}, u32[]{:S(2)}) collective-permute-start(bf16[128,128]{1,0:T(8,128)(2,1)S(1)} %add_convert_fusion), channel_id=1, source_target_pairs={{0,8},{2,10},{4,12},{6,14},{8,0},{10,2},{12,4},{14,6},{16,24},{18,... | collective-permute-start | bytes 98312 | tf_op jit(solution)/shard_map/ppermute | solution.py:258
  35.3 2.0 %shard_map.81 = (bf16[256,512]{1,0:T(8,128)(2,1)}, bf16[256,512]{1,0:T(8,128)(2,1)}, f32[256,512]{1,0:T(8,128)S(1)}, f32[256,512]{1,0:T(8,128)S(1)}) custom-call(bf16[256,512]{1,0:T(8,128)(2,1)S(1)} %copy-done.2, bf16[256,512]{1,0:T(8,128)(2,1)S(1)} %copy-done, bf16[256,512]{1,0:T(8,128)(2,1)S(1)} %copy-done.1, ...), custom_call_target="tpu_custom_call" | custom-call | flops 301989888 | bytes 3803136 | tf_op jit(solution)/shard_map/pallas_call | solution.py:71
  37.3 0.6 %collective-permute-done.17.refs_5_ = bf16[128,128]{1,0:T(8,128)(2,1)S(1)} collective-permute-done((bf16[128,128]{1,0:T(8,128)(2,1)S(1)}, bf16[128,128]{1,0:T(8,128)(2,1)S(1)}, u32[]{:S(2)}, u32[]{:S(2)}) %collective-permute-start.17) | collective-permute-done | bytes 32800 | tf_op jit(solution)/shard_map/ppermute | solution.py:258
  38.2 0.9 %collective-permute-start.21 = (bf16[128,128]{1,0:T(8,128)(2,1)S(1)}, bf16[128,128]{1,0:T(8,128)(2,1)S(1)}, u32[]{:S(2)}, u32[]{:S(2)}) collective-permute-start(bf16[128,128]{1,0:T(8,128)(2,1)S(1)} %get-tuple-element.64), channel_id=1, source_target_pairs={{0,7},{1,4},{2,5},{3,6},{4,3},{5,2},{6,1},{7,0},{8,15},{9,12},{10,... | collective-permute-start | bytes 98312 | tf_op jit(solution)/shard_map/ppermute | solution.py:246
  39.1 0.6 %collective-permute-start.22 = (bf16[128,128]{1,0:T(8,128)(2,1)S(1)}, bf16[128,128]{1,0:T(8,128)(2,1)S(1)}, u32[]{:S(2)}, u32[]{:S(2)}) collective-permute-start(bf16[128,128]{1,0:T(8,128)(2,1)S(1)} %get-tuple-element.65), channel_id=1, source_target_pairs={{0,3},{1,2},{2,7},{3,0},{4,1},{5,6},{6,5},{7,4},{8,11},{9,10},{10,... | collective-permute-start | bytes 98312 | tf_op jit(solution)/shard_map/ppermute | solution.py:246
  39.7 1.4 %collective-permute-start.19 = (bf16[128,128]{1,0:T(8,128)(2,1)S(1)}, bf16[128,128]{1,0:T(8,128)(2,1)S(1)}, u32[]{:S(2)}, u32[]{:S(2)}) collective-permute-start(bf16[128,128]{1,0:T(8,128)(2,1)S(1)} %get-tuple-element.62), channel_id=1, source_target_pairs={{0,5},{1,6},{2,1},{3,4},{4,7},{5,0},{6,3},{7,2},{8,13},{9,14},{10,... | collective-permute-start | bytes 98312 | tf_op jit(solution)/shard_map/ppermute | solution.py:246
  41.7 1.0 %collective-permute-done.21.p0 = bf16[128,128]{1,0:T(8,128)(2,1)S(1)} collective-permute-done((bf16[128,128]{1,0:T(8,128)(2,1)S(1)}, bf16[128,128]{1,0:T(8,128)(2,1)S(1)}, u32[]{:S(2)}, u32[]{:S(2)}) %collective-permute-start.21) | collective-permute-done | bytes 32800 | tf_op jit(solution)/shard_map/ppermute | solution.py:246
  42.9 0.7 %collective-permute-done.19.p2 = bf16[128,128]{1,0:T(8,128)(2,1)S(1)} collective-permute-done((bf16[128,128]{1,0:T(8,128)(2,1)S(1)}, bf16[128,128]{1,0:T(8,128)(2,1)S(1)}, u32[]{:S(2)}, u32[]{:S(2)}) %collective-permute-start.19) | collective-permute-done | bytes 32800 | tf_op jit(solution)/shard_map/ppermute | solution.py:246
  43.6 1.0 %shard_map.84 = (bf16[256,512]{1,0:T(8,128)(2,1)}, bf16[256,512]{1,0:T(8,128)(2,1)}) custom-call(bf16[256,512]{1,0:T(8,128)(2,1)S(1)} %copy-done, bf16[256,512]{1,0:T(8,128)(2,1)S(1)} %copy-done.1, f32[256,512]{1,0:T(8,128)S(1)} %get-tuple-element.56.refs_7_.key_local, f32[256,512]{1,0:T(8,128)S(1)} %get-tuple-element.57.value_local, ...), custom_call_target="tpu_custom_call" | custom-call | flops 33554432 | bytes 2424832 | tf_op jit(solution)/shard_map/pallas_call | solution.py:71
  (35 shorter events, 3.8 us)
Async XLA Ops:
  0.6 20.0 %copy-start.1 = (bf16[256,512]{1,0:T(8,128)(2,1)S(1)}, bf16[256,512]{1,0:T(8,128)(2,1)}, u32[]{:S(2)}) copy-start(bf16[256,512]{1,0:T(8,128)(2,1)} %v_ref.9) | copy-start | bytes 786436
  0.6 19.9 %copy-start.2 = (bf16[256,512]{1,0:T(8,128)(2,1)S(1)}, bf16[256,512]{1,0:T(8,128)(2,1)}, u32[]{:S(2)}) copy-start(bf16[256,512]{1,0:T(8,128)(2,1)} %q_ref.5) | copy-start | bytes 786436
  2.1 18.5 %copy-start = (bf16[256,512]{1,0:T(8,128)(2,1)S(1)}, bf16[256,512]{1,0:T(8,128)(2,1)}, u32[]{:S(2)}) copy-start(bf16[256,512]{1,0:T(8,128)(2,1)} %k_ref.9) | copy-start | bytes 786436
  2.1 5.1 %collective-permute-start = (bf16[128,128]{1,0:T(8,128)(2,1)S(1)}, bf16[128,128]{1,0:T(8,128)(2,1)S(1)}, u32[]{:S(2)}, u32[]{:S(2)}) collective-permute-start(bf16[128,128]{1,0:T(8,128)(2,1)S(1)} %get-tuple-element.38), channel_id=1, source_target_pairs={{0,7},{1,2},{2,5},{3,4},{4,3},{5,6},{6,1},{7,0},{8,15},{9,10},{10,... | collective-permute-start | bytes 98312 | tf_op jit(solution)/shard_map/ppermute | solution.py:246
  5.5 3.6 %collective-permute-start.1 = (bf16[128,128]{1,0:T(8,128)(2,1)S(1)}, bf16[128,128]{1,0:T(8,128)(2,1)S(1)}, u32[]{:S(2)}, u32[]{:S(2)}) collective-permute-start(bf16[128,128]{1,0:T(8,128)(2,1)S(1)} %get-tuple-element.39), channel_id=1, source_target_pairs={{0,3},{1,6},{2,1},{3,0},{4,7},{5,2},{6,5},{7,4},{8,11},{9,14},{10,... | collective-permute-start | bytes 98312 | tf_op jit(solution)/shard_map/ppermute | solution.py:246
  6.3 3.6 %collective-permute-start.2 = (bf16[128,128]{1,0:T(8,128)(2,1)S(1)}, bf16[128,128]{1,0:T(8,128)(2,1)S(1)}, u32[]{:S(2)}, u32[]{:S(2)}) collective-permute-start(bf16[128,128]{1,0:T(8,128)(2,1)S(1)} %get-tuple-element.40), channel_id=1, source_target_pairs={{0,5},{1,4},{2,7},{3,6},{4,1},{5,0},{6,3},{7,2},{8,13},{9,12},{10,... | collective-permute-start | bytes 98312 | tf_op jit(solution)/shard_map/ppermute | solution.py:246
  7.2 2.7 %collective-permute-start.3 = (bf16[128,128]{1,0:T(8,128)(2,1)S(1)}, bf16[128,128]{1,0:T(8,128)(2,1)S(1)}, u32[]{:S(2)}, u32[]{:S(2)}) collective-permute-start(bf16[128,128]{1,0:T(8,128)(2,1)S(1)} %get-tuple-element.41), channel_id=1, source_target_pairs={{0,1},{1,0},{2,3},{3,2},{4,5},{5,4},{6,7},{7,6},{8,9},{9,8},{10,11... | collective-permute-start | bytes 98312 | tf_op jit(solution)/shard_map/ppermute | solution.py:246
  9.9 5.2 %collective-permute-start.4 = (bf16[128,128]{1,0:T(8,128)(2,1)S(1)}, bf16[128,128]{1,0:T(8,128)(2,1)S(1)}, u32[]{:S(2)}, u32[]{:S(2)}) collective-permute-start(bf16[128,128]{1,0:T(8,128)(2,1)S(1)} %add_convert_fusion.1), channel_id=1, source_target_pairs={{0,16},{2,18},{4,20},{6,22},{8,24},{10,26},{12,28},{14,30},{16,0},... | collective-permute-start | bytes 98312 | tf_op jit(solution)/shard_map/ppermute | solution.py:258
  12.6 5.1 %collective-permute-start.5 = (bf16[128,128]{1,0:T(8,128)(2,1)S(1)}, bf16[128,128]{1,0:T(8,128)(2,1)S(1)}, u32[]{:S(2)}, u32[]{:S(2)}) collective-permute-start(bf16[128,128]{1,0:T(8,128)(2,1)S(1)} %add_convert_fusion.1), channel_id=1, source_target_pairs={{0,24},{2,26},{4,28},{6,30},{8,16},{10,18},{12,20},{14,22},{16,0},... | collective-permute-start | bytes 98312 | tf_op jit(solution)/shard_map/ppermute | solution.py:258
  13.9 4.0 %collective-permute-start.6 = (bf16[128,128]{1,0:T(8,128)(2,1)S(1)}, bf16[128,128]{1,0:T(8,128)(2,1)S(1)}, u32[]{:S(2)}, u32[]{:S(2)}) collective-permute-start(bf16[128,128]{1,0:T(8,128)(2,1)S(1)} %add_convert_fusion.1), channel_id=1, source_target_pairs={{0,8},{2,10},{4,12},{6,14},{8,0},{10,2},{12,4},{14,6},{16,24},{18,... | collective-permute-start | bytes 98312 | tf_op jit(solution)/shard_map/ppermute | solution.py:258
  18.1 3.7 %collective-permute-start.7 = (bf16[128,128]{1,0:T(8,128)(2,1)S(1)}, bf16[128,128]{1,0:T(8,128)(2,1)S(1)}, u32[]{:S(2)}, u32[]{:S(2)}) collective-permute-start(bf16[128,128]{1,0:T(8,128)(2,1)S(1)} %get-tuple-element.42), channel_id=1, source_target_pairs={{0,7},{1,6},{2,5},{3,4},{4,3},{5,0},{6,1},{7,2},{8,15},{9,14},{10,... | collective-permute-start | bytes 98312 | tf_op jit(solution)/shard_map/ppermute | solution.py:246
  18.2 4.3 %collective-permute-start.8 = (bf16[128,128]{1,0:T(8,128)(2,1)S(1)}, bf16[128,128]{1,0:T(8,128)(2,1)S(1)}, u32[]{:S(2)}, u32[]{:S(2)}) collective-permute-start(bf16[128,128]{1,0:T(8,128)(2,1)S(1)} %get-tuple-element.43), channel_id=1, source_target_pairs={{0,5},{1,4},{2,7},{3,6},{4,1},{5,2},{6,3},{7,0},{8,13},{9,12},{10,... | collective-permute-start | bytes 98312 | tf_op jit(solution)/shard_map/ppermute | solution.py:246
  19.9 3.6 %collective-permute-start.9 = (bf16[128,128]{1,0:T(8,128)(2,1)S(1)}, bf16[128,128]{1,0:T(8,128)(2,1)S(1)}, u32[]{:S(2)}, u32[]{:S(2)}) collective-permute-start(bf16[128,128]{1,0:T(8,128)(2,1)S(1)} %get-tuple-element.45), channel_id=1, source_target_pairs={{0,3},{1,2},{2,1},{3,0},{4,7},{5,6},{6,5},{7,4},{8,11},{9,10},{10,... | collective-permute-start | bytes 98312 | tf_op jit(solution)/shard_map/ppermute | solution.py:246
  20.0 2.5 %copy-start.3 = (bf16[256,512]{1,0:T(8,128)(2,1)S(1)}, bf16[256,512]{1,0:T(8,128)(2,1)}, u32[]{:S(2)}) copy-start(bf16[256,512]{1,0:T(8,128)(2,1)} %c_ref.3) | copy-start | bytes 786436
  20.0 3.5 %collective-permute-start.10 = (bf16[128,128]{1,0:T(8,128)(2,1)S(1)}, bf16[128,128]{1,0:T(8,128)(2,1)S(1)}, u32[]{:S(2)}, u32[]{:S(2)}) collective-permute-start(bf16[128,128]{1,0:T(8,128)(2,1)S(1)} %get-tuple-element.46), channel_id=1, source_target_pairs={{0,1},{1,0},{2,3},{3,2},{4,5},{5,4},{6,7},{7,6},{8,9},{9,8},{10,11... | collective-permute-start | bytes 98312 | tf_op jit(solution)/shard_map/ppermute | solution.py:246
  23.9 1.2 %collective-permute-start.11 = (f32[2,256]{1,0:T(2,128)S(1)}, f32[2,256]{1,0:T(2,128)S(1)}, u32[]{:S(2)}, u32[]{:S(2)}) collective-permute-start(f32[2,256]{1,0:T(2,128)S(1)} %get-tuple-element.51), channel_id=1, source_target_pairs={{0,1},{1,0},{2,3},{3,2},{4,5},{5,4},{6,7},{7,6},{8,9},{9,8},{10,11... | collective-permute-start | bytes 6152 | tf_op jit(solution)/shard_map/ppermute | solution.py:236
  25.5 3.4 %collective-permute-start.12 = (bf16[128,128]{1,0:T(8,128)(2,1)S(1)}, bf16[128,128]{1,0:T(8,128)(2,1)S(1)}, u32[]{:S(2)}, u32[]{:S(2)}) collective-permute-start(bf16[128,128]{1,0:T(8,128)(2,1)S(1)} %get-tuple-element.58), channel_id=1, source_target_pairs={{0,7},{1,6},{2,5},{3,0},{4,3},{5,2},{6,1},{7,4},{8,15},{9,14},{10,... | collective-permute-start | bytes 98312 | tf_op jit(solution)/shard_map/ppermute | solution.py:246
  26.2 4.3 %collective-permute-start.13 = (bf16[128,128]{1,0:T(8,128)(2,1)S(1)}, bf16[128,128]{1,0:T(8,128)(2,1)S(1)}, u32[]{:S(2)}, u32[]{:S(2)}) collective-permute-start(bf16[128,128]{1,0:T(8,128)(2,1)S(1)} %get-tuple-element.59), channel_id=1, source_target_pairs={{0,5},{1,2},{2,1},{3,4},{4,7},{5,6},{6,3},{7,0},{8,13},{9,10},{10,... | collective-permute-start | bytes 98312 | tf_op jit(solution)/shard_map/ppermute | solution.py:246
  27.2 3.6 %collective-permute-start.14 = (bf16[128,128]{1,0:T(8,128)(2,1)S(1)}, bf16[128,128]{1,0:T(8,128)(2,1)S(1)}, u32[]{:S(2)}, u32[]{:S(2)}) collective-permute-start(bf16[128,128]{1,0:T(8,128)(2,1)S(1)} %get-tuple-element.60), channel_id=1, source_target_pairs={{0,3},{1,4},{2,7},{3,6},{4,1},{5,0},{6,5},{7,2},{8,11},{9,12},{10,... | collective-permute-start | bytes 98312 | tf_op jit(solution)/shard_map/ppermute | solution.py:246
  28.4 2.4 %collective-permute-start.15 = (bf16[128,128]{1,0:T(8,128)(2,1)S(1)}, bf16[128,128]{1,0:T(8,128)(2,1)S(1)}, u32[]{:S(2)}, u32[]{:S(2)}) collective-permute-start(bf16[128,128]{1,0:T(8,128)(2,1)S(1)} %get-tuple-element.61), channel_id=1, source_target_pairs={{0,1},{1,0},{2,3},{3,2},{4,5},{5,4},{6,7},{7,6},{8,9},{9,8},{10,11... | collective-permute-start | bytes 98312 | tf_op jit(solution)/shard_map/ppermute | solution.py:246
  30.8 6.5 %collective-permute-start.16 = (bf16[128,128]{1,0:T(8,128)(2,1)S(1)}, bf16[128,128]{1,0:T(8,128)(2,1)S(1)}, u32[]{:S(2)}, u32[]{:S(2)}) collective-permute-start(bf16[128,128]{1,0:T(8,128)(2,1)S(1)} %add_convert_fusion), channel_id=1, source_target_pairs={{0,16},{2,18},{4,20},{6,22},{8,24},{10,26},{12,28},{14,30},{16,8},... | collective-permute-start | bytes 98312 | tf_op jit(solution)/shard_map/ppermute | solution.py:258
  32.7 5.2 %collective-permute-start.17 = (bf16[128,128]{1,0:T(8,128)(2,1)S(1)}, bf16[128,128]{1,0:T(8,128)(2,1)S(1)}, u32[]{:S(2)}, u32[]{:S(2)}) collective-permute-start(bf16[128,128]{1,0:T(8,128)(2,1)S(1)} %add_convert_fusion), channel_id=1, source_target_pairs={{0,16},{2,18},{4,20},{6,22},{8,24},{10,26},{12,28},{14,30},{16,0},... | collective-permute-start | bytes 98312 | tf_op jit(solution)/shard_map/ppermute | solution.py:258
  33.5 4.6 %collective-permute-start.18 = (bf16[128,128]{1,0:T(8,128)(2,1)S(1)}, bf16[128,128]{1,0:T(8,128)(2,1)S(1)}, u32[]{:S(2)}, u32[]{:S(2)}) collective-permute-start(bf16[128,128]{1,0:T(8,128)(2,1)S(1)} %add_convert_fusion), channel_id=1, source_target_pairs={{0,8},{2,10},{4,12},{6,14},{8,0},{10,2},{12,4},{14,6},{16,24},{18,... | collective-permute-start | bytes 98312 | tf_op jit(solution)/shard_map/ppermute | solution.py:258
  38.2 4.4 %collective-permute-start.21 = (bf16[128,128]{1,0:T(8,128)(2,1)S(1)}, bf16[128,128]{1,0:T(8,128)(2,1)S(1)}, u32[]{:S(2)}, u32[]{:S(2)}) collective-permute-start(bf16[128,128]{1,0:T(8,128)(2,1)S(1)} %get-tuple-element.64), channel_id=1, source_target_pairs={{0,7},{1,4},{2,5},{3,6},{4,3},{5,2},{6,1},{7,0},{8,15},{9,12},{10,... | collective-permute-start | bytes 98312 | tf_op jit(solution)/shard_map/ppermute | solution.py:246
  39.1 3.6 %collective-permute-start.22 = (bf16[128,128]{1,0:T(8,128)(2,1)S(1)}, bf16[128,128]{1,0:T(8,128)(2,1)S(1)}, u32[]{:S(2)}, u32[]{:S(2)}) collective-permute-start(bf16[128,128]{1,0:T(8,128)(2,1)S(1)} %get-tuple-element.65), channel_id=1, source_target_pairs={{0,3},{1,2},{2,7},{3,0},{4,1},{5,6},{6,5},{7,4},{8,11},{9,10},{10,... | collective-permute-start | bytes 98312 | tf_op jit(solution)/shard_map/ppermute | solution.py:246
  39.7 3.8 %collective-permute-start.19 = (bf16[128,128]{1,0:T(8,128)(2,1)S(1)}, bf16[128,128]{1,0:T(8,128)(2,1)S(1)}, u32[]{:S(2)}, u32[]{:S(2)}) collective-permute-start(bf16[128,128]{1,0:T(8,128)(2,1)S(1)} %get-tuple-element.62), channel_id=1, source_target_pairs={{0,5},{1,6},{2,1},{3,4},{4,7},{5,0},{6,3},{7,2},{8,13},{9,14},{10,... | collective-permute-start | bytes 98312 | tf_op jit(solution)/shard_map/ppermute | solution.py:246
  41.1 2.4 %collective-permute-start.20 = (bf16[128,128]{1,0:T(8,128)(2,1)S(1)}, bf16[128,128]{1,0:T(8,128)(2,1)S(1)}, u32[]{:S(2)}, u32[]{:S(2)}) collective-permute-start(bf16[128,128]{1,0:T(8,128)(2,1)S(1)} %get-tuple-element.63), channel_id=1, source_target_pairs={{0,1},{1,0},{2,3},{3,2},{4,5},{5,4},{6,7},{7,6},{8,9},{9,8},{10,11... | collective-permute-start | bytes 98312 | tf_op jit(solution)/shard_map/ppermute | solution.py:246

commit v14 on v12

--- a/solution.py
+++ b/solution.py
@@ -11,7 +11,7 @@
 EPSILON = 1e-06
 QUAD = 4
 OPS = (0, 1, 2, 3)
-CHUNKS = 4
+CHUNKS = 2
 LOW, WIDE = jnp.bfloat16, jnp.float32
 
 

time: 44.5 us -> 44.5 us (level)
  no operation moved by 1% of the time
where the time goes in v14:
time: 44.5 us; the launch traced here: 44.3 us
  starting transfers between devices  22.8 us (51%)
  waiting for transfers between devices  14.2 us (32%)
  Pallas kernels  6.46 us (15%)
  between operations  0.74 us (2%)
    ppermute x16, starting transfers between devices, cross(): return lax.ppermute(value, ('seq', 'tp'), pairs)  14 us
    ppermute x6, starting transfers between devices, exclusive_sum(): got.append(lax.ppermute(total, 'seq', pairs))  8.67 us
    ppermute x16, waiting for transfers between devices, cross(): return lax.ppermute(value, ('seq', 'tp'), pairs)  8.61 us
    pallas_call x10, Pallas kernels, call(): pl.pallas_call(kernel, out_shape=outs, in_specs=in_specs or [pl.BlockSpec...  6.46 us
    ppermute x6, waiting for transfers between devices, exclusive_sum(): got.append(lax.ppermute(total, 'seq', pairs))  4.52 us
    ppermute x1, waiting for transfers between devices, exchange(): return lax.ppermute(value, axis, [(i, i ^ bits) for i in range(size)])  1.06 us
  transfers between devices with their start and end apart: 23, of which 16 were waited for; matrix products, arithmetic and copies ran while one was open for 0% of the time, Pallas kernels for 7%

profile of v14, /device:TPU:0, one launch (start us, length us, event | category | flops | bytes accessed | tf_op | source)
XLA Modules:
  0.0 44.3 jit_solution(3659140814214041520)
XLA Ops:
  0.7 1.4 %shard_map.76 = (bf16[128,128]{1,0:T(8,128)(2,1)S(1)}, bf16[128,128]{1,0:T(8,128)(2,1)S(1)}, bf16[128,128]{1,0:T(8,128)(2,1)S(1)}, bf16[128,128]{1,0:T(8,128)(2,1)S(1)}) custom-call(bf16[256,512]{1,0:T(8,128)(2,1)} %k_ref.9, bf16[256,512]{1,0:T(8,128)(2,1)} %v_ref.9), custom_call_target="tpu_custom_call" | custom-call | flops 33554432 | bytes 655360 | tf_op jit(solution)/shard_map/pallas_call | solution.py:71
  2.1 3.4 %collective-permute-start = (bf16[128,128]{1,0:T(8,128)(2,1)S(1)}, bf16[128,128]{1,0:T(8,128)(2,1)S(1)}, u32[]{:S(2)}, u32[]{:S(2)}) collective-permute-start(bf16[128,128]{1,0:T(8,128)(2,1)S(1)} %get-tuple-element.38), channel_id=1, source_target_pairs={{0,7},{1,4},{2,5},{3,6},{4,3},{5,2},{6,1},{7,0},{8,15},{9,12},{10,... | collective-permute-start | bytes 98312 | tf_op jit(solution)/shard_map/ppermute | solution.py:246
  5.5 0.8 %collective-permute-start.1 = (bf16[128,128]{1,0:T(8,128)(2,1)S(1)}, bf16[128,128]{1,0:T(8,128)(2,1)S(1)}, u32[]{:S(2)}, u32[]{:S(2)}) collective-permute-start(bf16[128,128]{1,0:T(8,128)(2,1)S(1)} %get-tuple-element.39), channel_id=1, source_target_pairs={{0,3},{1,6},{2,7},{3,4},{4,1},{5,0},{6,5},{7,2},{8,11},{9,14},{10,... | collective-permute-start | bytes 98312 | tf_op jit(solution)/shard_map/ppermute | solution.py:246
  6.4 0.9 %collective-permute-start.2 = (bf16[128,128]{1,0:T(8,128)(2,1)S(1)}, bf16[128,128]{1,0:T(8,128)(2,1)S(1)}, u32[]{:S(2)}, u32[]{:S(2)}) collective-permute-start(bf16[128,128]{1,0:T(8,128)(2,1)S(1)} %get-tuple-element.40), channel_id=1, source_target_pairs={{0,5},{1,2},{2,1},{3,0},{4,7},{5,6},{6,3},{7,4},{8,13},{9,10},{10,... | collective-permute-start | bytes 98312 | tf_op jit(solution)/shard_map/ppermute | solution.py:246
  7.3 1.9 %collective-permute-done.1.refs_1_ = bf16[128,128]{1,0:T(8,128)(2,1)S(1)} collective-permute-done((bf16[128,128]{1,0:T(8,128)(2,1)S(1)}, bf16[128,128]{1,0:T(8,128)(2,1)S(1)}, u32[]{:S(2)}, u32[]{:S(2)}) %collective-permute-start.1) | collective-permute-done | bytes 32800 | tf_op jit(solution)/shard_map/ppermute | solution.py:246
  9.1 0.8 %collective-permute-done.2.refs_2_ = bf16[128,128]{1,0:T(8,128)(2,1)S(1)} collective-permute-done((bf16[128,128]{1,0:T(8,128)(2,1)S(1)}, bf16[128,128]{1,0:T(8,128)(2,1)S(1)}, u32[]{:S(2)}, u32[]{:S(2)}) %collective-permute-start.2) | collective-permute-done | bytes 32800 | tf_op jit(solution)/shard_map/ppermute | solution.py:246
  10.0 2.7 %collective-permute-start.4 = (bf16[128,128]{1,0:T(8,128)(2,1)S(1)}, bf16[128,128]{1,0:T(8,128)(2,1)S(1)}, u32[]{:S(2)}, u32[]{:S(2)}) collective-permute-start(bf16[128,128]{1,0:T(8,128)(2,1)S(1)} %add_convert_fusion.1), channel_id=1, source_target_pairs={{0,16},{2,18},{4,20},{6,22},{8,24},{10,26},{12,28},{14,30},{16,0},... | collective-permute-start | bytes 98312 | tf_op jit(solution)/shard_map/ppermute | solution.py:258
  12.7 1.3 %collective-permute-start.5 = (bf16[128,128]{1,0:T(8,128)(2,1)S(1)}, bf16[128,128]{1,0:T(8,128)(2,1)S(1)}, u32[]{:S(2)}, u32[]{:S(2)}) collective-permute-start(bf16[128,128]{1,0:T(8,128)(2,1)S(1)} %add_convert_fusion.1), channel_id=1, source_target_pairs={{0,24},{2,26},{4,28},{6,30},{8,16},{10,18},{12,20},{14,22},{16,0},... | collective-permute-start | bytes 98312 | tf_op jit(solution)/shard_map/ppermute | solution.py:258
  14.2 1.0 %collective-permute-done.4.refs_4_ = bf16[128,128]{1,0:T(8,128)(2,1)S(1)} collective-permute-done((bf16[128,128]{1,0:T(8,128)(2,1)S(1)}, bf16[128,128]{1,0:T(8,128)(2,1)S(1)}, u32[]{:S(2)}, u32[]{:S(2)}) %collective-permute-start.4) | collective-permute-done | bytes 32800 | tf_op jit(solution)/shard_map/ppermute | solution.py:258
  15.2 2.5 %collective-permute-done.5.refs_5_ = bf16[128,128]{1,0:T(8,128)(2,1)S(1)} collective-permute-done((bf16[128,128]{1,0:T(8,128)(2,1)S(1)}, bf16[128,128]{1,0:T(8,128)(2,1)S(1)}, u32[]{:S(2)}, u32[]{:S(2)}) %collective-permute-start.5) | collective-permute-done | bytes 32800 | tf_op jit(solution)/shard_map/ppermute | solution.py:258
  18.2 1.7 %collective-permute-start.8 = (bf16[128,128]{1,0:T(8,128)(2,1)S(1)}, bf16[128,128]{1,0:T(8,128)(2,1)S(1)}, u32[]{:S(2)}, u32[]{:S(2)}) collective-permute-start(bf16[128,128]{1,0:T(8,128)(2,1)S(1)} %get-tuple-element.43), channel_id=1, source_target_pairs={{0,5},{1,4},{2,7},{3,6},{4,1},{5,2},{6,3},{7,0},{8,13},{9,12},{10,... | collective-permute-start | bytes 98312 | tf_op jit(solution)/shard_map/ppermute | solution.py:246
  20.0 0.4 collective-permute-start.10
  20.4 0.7 %shard_map.75 = (bf16[4,256,256]{2,1,0:T(8,128)(2,1)S(1)}, f32[256,512]{1,0:T(8,128)S(1)}, bf16[4,128,256]{2,1,0:T(8,128)(2,1)S(1)}) custom-call(bf16[256,512]{1,0:T(8,128)(2,1)S(1)} %copy-done.2, bf16[256,512]{1,0:T(8,128)(2,1)S(1)} %copy-done, bf16[256,512]{1,0:T(8,128)(2,1)S(1)} %copy-done.1), custom_call_target="tpu_custom_call" | custom-call | flops 134217728 | bytes 2097152 | tf_op jit(solution)/shard_map/pallas_call | solution.py:71
  21.1 0.8 %collective-permute-done.7.refs_3_.p0 = bf16[128,128]{1,0:T(8,128)(2,1)S(1)} collective-permute-done((bf16[128,128]{1,0:T(8,128)(2,1)S(1)}, bf16[128,128]{1,0:T(8,128)(2,1)S(1)}, u32[]{:S(2)}, u32[]{:S(2)}) %collective-permute-start.7) | collective-permute-done | bytes 32800 | tf_op jit(solution)/shard_map/ppermute | solution.py:246
  21.9 0.6 %collective-permute-done.8.refs_4_.p1 = bf16[128,128]{1,0:T(8,128)(2,1)S(1)} collective-permute-done((bf16[128,128]{1,0:T(8,128)(2,1)S(1)}, bf16[128,128]{1,0:T(8,128)(2,1)S(1)}, u32[]{:S(2)}, u32[]{:S(2)}) %collective-permute-start.8) | collective-permute-done | bytes 32800 | tf_op jit(solution)/shard_map/ppermute | solution.py:246
  22.7 0.9 %collective-permute-done.9.p2 = bf16[128,128]{1,0:T(8,128)(2,1)S(1)} collective-permute-done((bf16[128,128]{1,0:T(8,128)(2,1)S(1)}, bf16[128,128]{1,0:T(8,128)(2,1)S(1)}, u32[]{:S(2)}, u32[]{:S(2)}) %collective-permute-start.9) | collective-permute-done | bytes 32800 | tf_op jit(solution)/shard_map/ppermute | solution.py:246
  24.1 1.1 %collective-permute-done.11 = f32[2,256]{1,0:T(2,128)S(1)} collective-permute-done((f32[2,256]{1,0:T(2,128)S(1)}, f32[2,256]{1,0:T(2,128)S(1)}, u32[]{:S(2)}, u32[]{:S(2)}) %collective-permute-start.11) | collective-permute-done | bytes 2080 | tf_op jit(solution)/shard_map/ppermute | solution.py:236
  25.2 0.4 shard_map.80
  25.6 1.1 %collective-permute-start.12 = (bf16[128,128]{1,0:T(8,128)(2,1)S(1)}, bf16[128,128]{1,0:T(8,128)(2,1)S(1)}, u32[]{:S(2)}, u32[]{:S(2)}) collective-permute-start(bf16[128,128]{1,0:T(8,128)(2,1)S(1)} %get-tuple-element.58), channel_id=1, source_target_pairs={{0,7},{1,6},{2,5},{3,4},{4,3},{5,2},{6,1},{7,0},{8,15},{9,14},{10,... | collective-permute-start | bytes 98312 | tf_op jit(solution)/shard_map/ppermute | solution.py:246
  26.9 1.5 %collective-permute-start.14 = (bf16[128,128]{1,0:T(8,128)(2,1)S(1)}, bf16[128,128]{1,0:T(8,128)(2,1)S(1)}, u32[]{:S(2)}, u32[]{:S(2)}) collective-permute-start(bf16[128,128]{1,0:T(8,128)(2,1)S(1)} %get-tuple-element.60), channel_id=1, source_target_pairs={{0,3},{1,4},{2,1},{3,6},{4,7},{5,0},{6,5},{7,2},{8,11},{9,12},{10,... | collective-permute-start | bytes 98312 | tf_op jit(solution)/shard_map/ppermute | solution.py:246
  28.8 1.1 %collective-permute-done.12.refs_0_ = bf16[128,128]{1,0:T(8,128)(2,1)S(1)} collective-permute-done((bf16[128,128]{1,0:T(8,128)(2,1)S(1)}, bf16[128,128]{1,0:T(8,128)(2,1)S(1)}, u32[]{:S(2)}, u32[]{:S(2)}) %collective-permute-start.12) | collective-permute-done | bytes 32800 | tf_op jit(solution)/shard_map/ppermute | solution.py:246
  30.2 0.6 %collective-permute-done.14.refs_2_ = bf16[128,128]{1,0:T(8,128)(2,1)S(1)} collective-permute-done((bf16[128,128]{1,0:T(8,128)(2,1)S(1)}, bf16[128,128]{1,0:T(8,128)(2,1)S(1)}, u32[]{:S(2)}, u32[]{:S(2)}) %collective-permute-start.14) | collective-permute-done | bytes 32800 | tf_op jit(solution)/shard_map/ppermute | solution.py:246
  30.8 1.8 %collective-permute-start.16 = (bf16[128,128]{1,0:T(8,128)(2,1)S(1)}, bf16[128,128]{1,0:T(8,128)(2,1)S(1)}, u32[]{:S(2)}, u32[]{:S(2)}) collective-permute-start(bf16[128,128]{1,0:T(8,128)(2,1)S(1)} %add_convert_fusion), channel_id=1, source_target_pairs={{0,16},{2,18},{4,20},{6,22},{8,24},{10,26},{12,28},{14,30},{16,8},... | collective-permute-start | bytes 98312 | tf_op jit(solution)/shard_map/ppermute | solution.py:258
  32.6 0.8 %collective-permute-start.17 = (bf16[128,128]{1,0:T(8,128)(2,1)S(1)}, bf16[128,128]{1,0:T(8,128)(2,1)S(1)}, u32[]{:S(2)}, u32[]{:S(2)}) collective-permute-start(bf16[128,128]{1,0:T(8,128)(2,1)S(1)} %add_convert_fusion), channel_id=1, source_target_pairs={{0,16},{2,18},{4,20},{6,22},{8,24},{10,26},{12,28},{14,30},{16,0},... | collective-permute-start | bytes 98312 | tf_op jit(solution)/shard_map/ppermute | solution.py:258
  33.4 1.9 %collective-permute-start.18 = (bf16[128,128]{1,0:T(8,128)(2,1)S(1)}, bf16[128,128]{1,0:T(8,128)(2,1)S(1)}, u32[]{:S(2)}, u32[]{:S(2)}) collective-permute-start(bf16[128,128]{1,0:T(8,128)(2,1)S(1)} %add_convert_fusion), channel_id=1, source_target_pairs={{0,8},{2,10},{4,12},{6,14},{8,0},{10,2},{12,4},{14,6},{16,24},{18,... | collective-permute-start | bytes 98312 | tf_op jit(solution)/shard_map/ppermute | solution.py:258
  35.3 2.0 %shard_map.81 = (bf16[256,512]{1,0:T(8,128)(2,1)}, bf16[256,512]{1,0:T(8,128)(2,1)}, f32[256,512]{1,0:T(8,128)S(1)}, f32[256,512]{1,0:T(8,128)S(1)}) custom-call(bf16[256,512]{1,0:T(8,128)(2,1)S(1)} %copy-done.2, bf16[256,512]{1,0:T(8,128)(2,1)S(1)} %copy-done, bf16[256,512]{1,0:T(8,128)(2,1)S(1)} %copy-done.1, ...), custom_call_target="tpu_custom_call" | custom-call | flops 301989888 | bytes 3803136 | tf_op jit(solution)/shard_map/pallas_call | solution.py:71
  37.3 0.5 %collective-permute-done.17.refs_5_ = bf16[128,128]{1,0:T(8,128)(2,1)S(1)} collective-permute-done((bf16[128,128]{1,0:T(8,128)(2,1)S(1)}, bf16[128,128]{1,0:T(8,128)(2,1)S(1)}, u32[]{:S(2)}, u32[]{:S(2)}) %collective-permute-start.17) | collective-permute-done | bytes 32800 | tf_op jit(solution)/shard_map/ppermute | solution.py:258
  38.2 1.7 %collective-permute-start.22 = (bf16[128,128]{1,0:T(8,128)(2,1)S(1)}, bf16[128,128]{1,0:T(8,128)(2,1)S(1)}, u32[]{:S(2)}, u32[]{:S(2)}) collective-permute-start(bf16[128,128]{1,0:T(8,128)(2,1)S(1)} %get-tuple-element.65), channel_id=1, source_target_pairs={{0,5},{1,2},{2,7},{3,4},{4,1},{5,6},{6,3},{7,0},{8,13},{9,10},{10,... | collective-permute-start | bytes 98312 | tf_op jit(solution)/shard_map/ppermute | solution.py:246
  39.9 0.6 %collective-permute-start.19 = (bf16[128,128]{1,0:T(8,128)(2,1)S(1)}, bf16[128,128]{1,0:T(8,128)(2,1)S(1)}, u32[]{:S(2)}, u32[]{:S(2)}) collective-permute-start(bf16[128,128]{1,0:T(8,128)(2,1)S(1)} %get-tuple-element.62), channel_id=1, source_target_pairs={{0,3},{1,6},{2,1},{3,0},{4,7},{5,2},{6,5},{7,4},{8,11},{9,14},{10,... | collective-permute-start | bytes 98312 | tf_op jit(solution)/shard_map/ppermute | solution.py:246
  40.5 1.0 %collective-permute-start.20 = (bf16[128,128]{1,0:T(8,128)(2,1)S(1)}, bf16[128,128]{1,0:T(8,128)(2,1)S(1)}, u32[]{:S(2)}, u32[]{:S(2)}) collective-permute-start(bf16[128,128]{1,0:T(8,128)(2,1)S(1)} %get-tuple-element.63), channel_id=1, source_target_pairs={{0,1},{1,0},{2,3},{3,2},{4,5},{5,4},{6,7},{7,6},{8,9},{9,8},{10,11... | collective-permute-start | bytes 98312 | tf_op jit(solution)/shard_map/ppermute | solution.py:246
  41.6 1.1 %collective-permute-done.22.p1 = bf16[128,128]{1,0:T(8,128)(2,1)S(1)} collective-permute-done((bf16[128,128]{1,0:T(8,128)(2,1)S(1)}, bf16[128,128]{1,0:T(8,128)(2,1)S(1)}, u32[]{:S(2)}, u32[]{:S(2)}) %collective-permute-start.22) | collective-permute-done | bytes 32800 | tf_op jit(solution)/shard_map/ppermute | solution.py:246
  43.3 1.0 %shard_map.84 = (bf16[256,512]{1,0:T(8,128)(2,1)}, bf16[256,512]{1,0:T(8,128)(2,1)}) custom-call(bf16[256,512]{1,0:T(8,128)(2,1)S(1)} %copy-done, bf16[256,512]{1,0:T(8,128)(2,1)S(1)} %copy-done.1, f32[256,512]{1,0:T(8,128)S(1)} %get-tuple-element.56.refs_7_.key_local, f32[256,512]{1,0:T(8,128)S(1)} %get-tuple-element.57.value_local, ...), custom_call_target="tpu_custom_call" | custom-call | flops 33554432 | bytes 2424832 | tf_op jit(solution)/shard_map/pallas_call | solution.py:71
  (35 shorter events, 3.3 us)
Async XLA Ops:
  0.6 19.8 %copy-start.1 = (bf16[256,512]{1,0:T(8,128)(2,1)S(1)}, bf16[256,512]{1,0:T(8,128)(2,1)}, u32[]{:S(2)}) copy-start(bf16[256,512]{1,0:T(8,128)(2,1)} %v_ref.9) | copy-start | bytes 786436
  0.6 19.8 %copy-start.2 = (bf16[256,512]{1,0:T(8,128)(2,1)S(1)}, bf16[256,512]{1,0:T(8,128)(2,1)}, u32[]{:S(2)}) copy-start(bf16[256,512]{1,0:T(8,128)(2,1)} %q_ref.5) | copy-start | bytes 786436
  2.1 18.3 %copy-start = (bf16[256,512]{1,0:T(8,128)(2,1)S(1)}, bf16[256,512]{1,0:T(8,128)(2,1)}, u32[]{:S(2)}) copy-start(bf16[256,512]{1,0:T(8,128)(2,1)} %k_ref.9) | copy-start | bytes 786436
  2.1 5.1 %collective-permute-start = (bf16[128,128]{1,0:T(8,128)(2,1)S(1)}, bf16[128,128]{1,0:T(8,128)(2,1)S(1)}, u32[]{:S(2)}, u32[]{:S(2)}) collective-permute-start(bf16[128,128]{1,0:T(8,128)(2,1)S(1)} %get-tuple-element.38), channel_id=1, source_target_pairs={{0,7},{1,4},{2,5},{3,6},{4,3},{5,2},{6,1},{7,0},{8,15},{9,12},{10,... | collective-permute-start | bytes 98312 | tf_op jit(solution)/shard_map/ppermute | solution.py:246
  5.5 3.6 %collective-permute-start.1 = (bf16[128,128]{1,0:T(8,128)(2,1)S(1)}, bf16[128,128]{1,0:T(8,128)(2,1)S(1)}, u32[]{:S(2)}, u32[]{:S(2)}) collective-permute-start(bf16[128,128]{1,0:T(8,128)(2,1)S(1)} %get-tuple-element.39), channel_id=1, source_target_pairs={{0,3},{1,6},{2,7},{3,4},{4,1},{5,0},{6,5},{7,2},{8,11},{9,14},{10,... | collective-permute-start | bytes 98312 | tf_op jit(solution)/shard_map/ppermute | solution.py:246
  6.4 3.6 %collective-permute-start.2 = (bf16[128,128]{1,0:T(8,128)(2,1)S(1)}, bf16[128,128]{1,0:T(8,128)(2,1)S(1)}, u32[]{:S(2)}, u32[]{:S(2)}) collective-permute-start(bf16[128,128]{1,0:T(8,128)(2,1)S(1)} %get-tuple-element.40), channel_id=1, source_target_pairs={{0,5},{1,2},{2,1},{3,0},{4,7},{5,6},{6,3},{7,4},{8,13},{9,10},{10,... | collective-permute-start | bytes 98312 | tf_op jit(solution)/shard_map/ppermute | solution.py:246
  7.3 2.7 %collective-permute-start.3 = (bf16[128,128]{1,0:T(8,128)(2,1)S(1)}, bf16[128,128]{1,0:T(8,128)(2,1)S(1)}, u32[]{:S(2)}, u32[]{:S(2)}) collective-permute-start(bf16[128,128]{1,0:T(8,128)(2,1)S(1)} %get-tuple-element.41), channel_id=1, source_target_pairs={{0,1},{1,0},{2,3},{3,2},{4,5},{5,4},{6,7},{7,6},{8,9},{9,8},{10,11... | collective-permute-start | bytes 98312 | tf_op jit(solution)/shard_map/ppermute | solution.py:246
  10.0 5.2 %collective-permute-start.4 = (bf16[128,128]{1,0:T(8,128)(2,1)S(1)}, bf16[128,128]{1,0:T(8,128)(2,1)S(1)}, u32[]{:S(2)}, u32[]{:S(2)}) collective-permute-start(bf16[128,128]{1,0:T(8,128)(2,1)S(1)} %add_convert_fusion.1), channel_id=1, source_target_pairs={{0,16},{2,18},{4,20},{6,22},{8,24},{10,26},{12,28},{14,30},{16,0},... | collective-permute-start | bytes 98312 | tf_op jit(solution)/shard_map/ppermute | solution.py:258
  12.7 5.1 %collective-permute-start.5 = (bf16[128,128]{1,0:T(8,128)(2,1)S(1)}, bf16[128,128]{1,0:T(8,128)(2,1)S(1)}, u32[]{:S(2)}, u32[]{:S(2)}) collective-permute-start(bf16[128,128]{1,0:T(8,128)(2,1)S(1)} %add_convert_fusion.1), channel_id=1, source_target_pairs={{0,24},{2,26},{4,28},{6,30},{8,16},{10,18},{12,20},{14,22},{16,0},... | collective-permute-start | bytes 98312 | tf_op jit(solution)/shard_map/ppermute | solution.py:258
  14.0 4.0 %collective-permute-start.6 = (bf16[128,128]{1,0:T(8,128)(2,1)S(1)}, bf16[128,128]{1,0:T(8,128)(2,1)S(1)}, u32[]{:S(2)}, u32[]{:S(2)}) collective-permute-start(bf16[128,128]{1,0:T(8,128)(2,1)S(1)} %add_convert_fusion.1), channel_id=1, source_target_pairs={{0,8},{2,10},{4,12},{6,14},{8,0},{10,2},{12,4},{14,6},{16,24},{18,... | collective-permute-start | bytes 98312 | tf_op jit(solution)/shard_map/ppermute | solution.py:258
  18.2 3.7 %collective-permute-start.7 = (bf16[128,128]{1,0:T(8,128)(2,1)S(1)}, bf16[128,128]{1,0:T(8,128)(2,1)S(1)}, u32[]{:S(2)}, u32[]{:S(2)}) collective-permute-start(bf16[128,128]{1,0:T(8,128)(2,1)S(1)} %get-tuple-element.42), channel_id=1, source_target_pairs={{0,7},{1,6},{2,5},{3,4},{4,3},{5,0},{6,1},{7,2},{8,15},{9,14},{10,... | collective-permute-start | bytes 98312 | tf_op jit(solution)/shard_map/ppermute | solution.py:246
  18.2 4.3 %collective-permute-start.8 = (bf16[128,128]{1,0:T(8,128)(2,1)S(1)}, bf16[128,128]{1,0:T(8,128)(2,1)S(1)}, u32[]{:S(2)}, u32[]{:S(2)}) collective-permute-start(bf16[128,128]{1,0:T(8,128)(2,1)S(1)} %get-tuple-element.43), channel_id=1, source_target_pairs={{0,5},{1,4},{2,7},{3,6},{4,1},{5,2},{6,3},{7,0},{8,13},{9,12},{10,... | collective-permute-start | bytes 98312 | tf_op jit(solution)/shard_map/ppermute | solution.py:246
  20.0 3.7 %collective-permute-start.9 = (bf16[128,128]{1,0:T(8,128)(2,1)S(1)}, bf16[128,128]{1,0:T(8,128)(2,1)S(1)}, u32[]{:S(2)}, u32[]{:S(2)}) collective-permute-start(bf16[128,128]{1,0:T(8,128)(2,1)S(1)} %get-tuple-element.45), channel_id=1, source_target_pairs={{0,3},{1,2},{2,1},{3,0},{4,7},{5,6},{6,5},{7,4},{8,11},{9,10},{10,... | collective-permute-start | bytes 98312 | tf_op jit(solution)/shard_map/ppermute | solution.py:246
  20.0 2.5 %copy-start.3 = (bf16[256,512]{1,0:T(8,128)(2,1)S(1)}, bf16[256,512]{1,0:T(8,128)(2,1)}, u32[]{:S(2)}) copy-start(bf16[256,512]{1,0:T(8,128)(2,1)} %c_ref.3) | copy-start | bytes 786436
  20.0 3.6 %collective-permute-start.10 = (bf16[128,128]{1,0:T(8,128)(2,1)S(1)}, bf16[128,128]{1,0:T(8,128)(2,1)S(1)}, u32[]{:S(2)}, u32[]{:S(2)}) collective-permute-start(bf16[128,128]{1,0:T(8,128)(2,1)S(1)} %get-tuple-element.46), channel_id=1, source_target_pairs={{0,1},{1,0},{2,3},{3,2},{4,5},{5,4},{6,7},{7,6},{8,9},{9,8},{10,11... | collective-permute-start | bytes 98312 | tf_op jit(solution)/shard_map/ppermute | solution.py:246
  23.9 1.2 %collective-permute-start.11 = (f32[2,256]{1,0:T(2,128)S(1)}, f32[2,256]{1,0:T(2,128)S(1)}, u32[]{:S(2)}, u32[]{:S(2)}) collective-permute-start(f32[2,256]{1,0:T(2,128)S(1)} %get-tuple-element.51), channel_id=1, source_target_pairs={{0,1},{1,0},{2,3},{3,2},{4,5},{5,4},{6,7},{7,6},{8,9},{9,8},{10,11... | collective-permute-start | bytes 6152 | tf_op jit(solution)/shard_map/ppermute | solution.py:236
  25.6 4.3 %collective-permute-start.12 = (bf16[128,128]{1,0:T(8,128)(2,1)S(1)}, bf16[128,128]{1,0:T(8,128)(2,1)S(1)}, u32[]{:S(2)}, u32[]{:S(2)}) collective-permute-start(bf16[128,128]{1,0:T(8,128)(2,1)S(1)} %get-tuple-element.58), channel_id=1, source_target_pairs={{0,7},{1,6},{2,5},{3,4},{4,3},{5,2},{6,1},{7,0},{8,15},{9,14},{10,... | collective-permute-start | bytes 98312 | tf_op jit(solution)/shard_map/ppermute | solution.py:246
  26.7 3.5 %collective-permute-start.13 = (bf16[128,128]{1,0:T(8,128)(2,1)S(1)}, bf16[128,128]{1,0:T(8,128)(2,1)S(1)}, u32[]{:S(2)}, u32[]{:S(2)}) collective-permute-start(bf16[128,128]{1,0:T(8,128)(2,1)S(1)} %get-tuple-element.59), channel_id=1, source_target_pairs={{0,5},{1,2},{2,7},{3,0},{4,1},{5,6},{6,3},{7,4},{8,13},{9,10},{10,... | collective-permute-start | bytes 98312 | tf_op jit(solution)/shard_map/ppermute | solution.py:246
  26.9 3.9 %collective-permute-start.14 = (bf16[128,128]{1,0:T(8,128)(2,1)S(1)}, bf16[128,128]{1,0:T(8,128)(2,1)S(1)}, u32[]{:S(2)}, u32[]{:S(2)}) collective-permute-start(bf16[128,128]{1,0:T(8,128)(2,1)S(1)} %get-tuple-element.60), channel_id=1, source_target_pairs={{0,3},{1,4},{2,1},{3,6},{4,7},{5,0},{6,5},{7,2},{8,11},{9,12},{10,... | collective-permute-start | bytes 98312 | tf_op jit(solution)/shard_map/ppermute | solution.py:246
  28.4 2.4 %collective-permute-start.15 = (bf16[128,128]{1,0:T(8,128)(2,1)S(1)}, bf16[128,128]{1,0:T(8,128)(2,1)S(1)}, u32[]{:S(2)}, u32[]{:S(2)}) collective-permute-start(bf16[128,128]{1,0:T(8,128)(2,1)S(1)} %get-tuple-element.61), channel_id=1, source_target_pairs={{0,1},{1,0},{2,3},{3,2},{4,5},{5,4},{6,7},{7,6},{8,9},{9,8},{10,11... | collective-permute-start | bytes 98312 | tf_op jit(solution)/shard_map/ppermute | solution.py:246
  30.8 6.5 %collective-permute-start.16 = (bf16[128,128]{1,0:T(8,128)(2,1)S(1)}, bf16[128,128]{1,0:T(8,128)(2,1)S(1)}, u32[]{:S(2)}, u32[]{:S(2)}) collective-permute-start(bf16[128,128]{1,0:T(8,128)(2,1)S(1)} %add_convert_fusion), channel_id=1, source_target_pairs={{0,16},{2,18},{4,20},{6,22},{8,24},{10,26},{12,28},{14,30},{16,8},... | collective-permute-start | bytes 98312 | tf_op jit(solution)/shard_map/ppermute | solution.py:258
  32.6 5.2 %collective-permute-start.17 = (bf16[128,128]{1,0:T(8,128)(2,1)S(1)}, bf16[128,128]{1,0:T(8,128)(2,1)S(1)}, u32[]{:S(2)}, u32[]{:S(2)}) collective-permute-start(bf16[128,128]{1,0:T(8,128)(2,1)S(1)} %add_convert_fusion), channel_id=1, source_target_pairs={{0,16},{2,18},{4,20},{6,22},{8,24},{10,26},{12,28},{14,30},{16,0},... | collective-permute-start | bytes 98312 | tf_op jit(solution)/shard_map/ppermute | solution.py:258
  33.4 4.6 %collective-permute-start.18 = (bf16[128,128]{1,0:T(8,128)(2,1)S(1)}, bf16[128,128]{1,0:T(8,128)(2,1)S(1)}, u32[]{:S(2)}, u32[]{:S(2)}) collective-permute-start(bf16[128,128]{1,0:T(8,128)(2,1)S(1)} %add_convert_fusion), channel_id=1, source_target_pairs={{0,8},{2,10},{4,12},{6,14},{8,0},{10,2},{12,4},{14,6},{16,24},{18,... | collective-permute-start | bytes 98312 | tf_op jit(solution)/shard_map/ppermute | solution.py:258
  38.1 3.4 %collective-permute-start.21 = (bf16[128,128]{1,0:T(8,128)(2,1)S(1)}, bf16[128,128]{1,0:T(8,128)(2,1)S(1)}, u32[]{:S(2)}, u32[]{:S(2)}) collective-permute-start(bf16[128,128]{1,0:T(8,128)(2,1)S(1)} %get-tuple-element.64), channel_id=1, source_target_pairs={{0,7},{1,4},{2,5},{3,6},{4,3},{5,0},{6,1},{7,2},{8,15},{9,12},{10,... | collective-permute-start | bytes 98312 | tf_op jit(solution)/shard_map/ppermute | solution.py:246
  38.2 4.5 %collective-permute-start.22 = (bf16[128,128]{1,0:T(8,128)(2,1)S(1)}, bf16[128,128]{1,0:T(8,128)(2,1)S(1)}, u32[]{:S(2)}, u32[]{:S(2)}) collective-permute-start(bf16[128,128]{1,0:T(8,128)(2,1)S(1)} %get-tuple-element.65), channel_id=1, source_target_pairs={{0,5},{1,2},{2,7},{3,4},{4,1},{5,6},{6,3},{7,0},{8,13},{9,10},{10,... | collective-permute-start | bytes 98312 | tf_op jit(solution)/shard_map/ppermute | solution.py:246
  39.9 3.4 %collective-permute-start.19 = (bf16[128,128]{1,0:T(8,128)(2,1)S(1)}, bf16[128,128]{1,0:T(8,128)(2,1)S(1)}, u32[]{:S(2)}, u32[]{:S(2)}) collective-permute-start(bf16[128,128]{1,0:T(8,128)(2,1)S(1)} %get-tuple-element.62), channel_id=1, source_target_pairs={{0,3},{1,6},{2,1},{3,0},{4,7},{5,2},{6,5},{7,4},{8,11},{9,14},{10,... | collective-permute-start | bytes 98312 | tf_op jit(solution)/shard_map/ppermute | solution.py:246
  40.5 2.8 %collective-permute-start.20 = (bf16[128,128]{1,0:T(8,128)(2,1)S(1)}, bf16[128,128]{1,0:T(8,128)(2,1)S(1)}, u32[]{:S(2)}, u32[]{:S(2)}) collective-permute-start(bf16[128,128]{1,0:T(8,128)(2,1)S(1)} %get-tuple-element.63), channel_id=1, source_target_pairs={{0,1},{1,0},{2,3},{3,2},{4,5},{5,4},{6,7},{7,6},{8,9},{9,8},{10,11... | collective-permute-start | bytes 98312 | tf_op jit(solution)/shard_map/ppermute | solution.py:246

commit v15 on v11

--- a/solution.py
+++ b/solution.py
@@ -171,15 +171,22 @@
         head(value_ref, h)[...] = value.astype(LOW)
 
 
+def ring(quads, before):
+    return quads == 4 and before
+
+
 def quad_steps(quads, before):
-    return (2, 3, 1) if quads == 4 and before else range(quads - 1, 0, -1)
+    return (1, 2, 3) if ring(quads, before) else range(quads - 1, 0, -1)
 
 
 def quad_targets(quads, step, before):
-    targets = [z ^ step for z in range(quads)]
-    if quads == 4 and step == 3:
-        targets = [3, 2, 0, 1] if before else [2, 3, 1, 0]
-    return targets
+    if ring(quads, before):
+        return [(z + step) % quads for z in range(quads)]
+    return [2, 3, 1, 0] if quads == 4 and step == 3 else [z ^ step for z in range(quads)]
+
+
+def quad_source(quads, step, before, quad):
+    return (quad + quads - step) % quads if ring(quads, before) else quad ^ step
 
 
 def sums_kernel(before, quads, *refs):
@@ -193,7 +200,7 @@
 
     outer = jnp.zeros((DH, DH), WIDE)
     for step, total in zip(quad_steps(quads, before), got):
-        outer = outer + total[...].astype(WIDE) * counts(quad ^ step, quad)
+        outer = outer + total[...].astype(WIDE) * counts(quad_source(quads, step, before, quad), quad)
     pieces = [piece[...].astype(WIDE) for piece in held]
     for to in OPS:
         inner = outer

time: 44.5 us -> 44.7 us (level)
  starting transfers between devices: 22.9 us -> 24.3 us
  waiting for transfers between devices: 14.6 us -> 13.2 us
    ppermute x6, starting transfers between devices: 8.67 us -> 10 us  [exclusive_sum(): got.append(lax.ppermute(total, 'seq', pairs))]
    ppermute x6, waiting for transfers between devices: 4.53 us -> 3.27 us  [exclusive_sum(): got.append(lax.ppermute(total, 'seq', pairs))]
  transfers between devices with their start and end apart: 23 -> 23, of which waited for: 16 -> 17; matrix products, arithmetic and copies ran while one was open for 0% -> 0% of each run, Pallas kernels for 6% -> 6%
where the time goes in v15:
time: 44.7 us; the launch traced here: 44.5 us
  starting transfers between devices  24.3 us (54%)
  waiting for transfers between devices  13.2 us (30%)
  Pallas kernels  6.17 us (14%)
  between operations  0.72 us (2%)
    ppermute x16, starting transfers between devices, cross(): return lax.ppermute(value, ('seq', 'tp'), pairs)  14.1 us
    ppermute x6, starting transfers between devices, exclusive_sum(): got.append(lax.ppermute(total, 'seq', pairs))  10 us
    ppermute x16, waiting for transfers between devices, cross(): return lax.ppermute(value, ('seq', 'tp'), pairs)  8.92 us
    pallas_call x8, Pallas kernels, call(): pl.pallas_call(kernel, out_shape=outs, in_specs=in_specs or [pl.BlockSpec...  6.17 us
    ppermute x6, waiting for transfers between devices, exclusive_sum(): got.append(lax.ppermute(total, 'seq', pairs))  3.27 us
    ppermute x1, waiting for transfers between devices, exchange(): return lax.ppermute(value, axis, [(i, i ^ bits) for i in range(size)])  1.06 us
  transfers between devices with their start and end apart: 23, of which 17 were waited for; matrix products, arithmetic and copies ran while one was open for 0% of the time, Pallas kernels for 6%

profile of v15, /device:TPU:0, one launch (start us, length us, event | category | flops | bytes accessed | tf_op | source)
XLA Modules:
  0.0 44.5 jit_solution(4435532336622504194)
XLA Ops:
  0.7 1.4 %shard_map.76 = (bf16[128,128]{1,0:T(8,128)(2,1)S(1)}, bf16[128,128]{1,0:T(8,128)(2,1)S(1)}, bf16[128,128]{1,0:T(8,128)(2,1)S(1)}, bf16[128,128]{1,0:T(8,128)(2,1)S(1)}) custom-call(bf16[256,512]{1,0:T(8,128)(2,1)} %k_ref.7, bf16[256,512]{1,0:T(8,128)(2,1)} %v_ref.7), custom_call_target="tpu_custom_call" | custom-call | flops 33554432 | bytes 655360 | tf_op jit(solution)/shard_map/pallas_call | solution.py:70
  2.1 3.4 %collective-permute-start = (bf16[128,128]{1,0:T(8,128)(2,1)S(1)}, bf16[128,128]{1,0:T(8,128)(2,1)S(1)}, u32[]{:S(2)}, u32[]{:S(2)}) collective-permute-start(bf16[128,128]{1,0:T(8,128)(2,1)S(1)} %get-tuple-element.33), channel_id=1, source_target_pairs={{0,7},{1,4},{2,5},{3,6},{4,3},{5,2},{6,1},{7,0},{8,15},{9,12},{10,... | collective-permute-start | bytes 98312 | tf_op jit(solution)/shard_map/ppermute | solution.py:224
  5.5 0.8 %collective-permute-start.1 = (bf16[128,128]{1,0:T(8,128)(2,1)S(1)}, bf16[128,128]{1,0:T(8,128)(2,1)S(1)}, u32[]{:S(2)}, u32[]{:S(2)}) collective-permute-start(bf16[128,128]{1,0:T(8,128)(2,1)S(1)} %get-tuple-element.34), channel_id=1, source_target_pairs={{0,3},{1,6},{2,7},{3,4},{4,1},{5,0},{6,5},{7,2},{8,11},{9,14},{10,... | collective-permute-start | bytes 98312 | tf_op jit(solution)/shard_map/ppermute | solution.py:224
  6.4 0.9 %collective-permute-start.2 = (bf16[128,128]{1,0:T(8,128)(2,1)S(1)}, bf16[128,128]{1,0:T(8,128)(2,1)S(1)}, u32[]{:S(2)}, u32[]{:S(2)}) collective-permute-start(bf16[128,128]{1,0:T(8,128)(2,1)S(1)} %get-tuple-element.35), channel_id=1, source_target_pairs={{0,5},{1,2},{2,1},{3,0},{4,7},{5,6},{6,3},{7,4},{8,13},{9,10},{10,... | collective-permute-start | bytes 98312 | tf_op jit(solution)/shard_map/ppermute | solution.py:224
  7.3 1.9 %collective-permute-done.1.refs_1_ = bf16[128,128]{1,0:T(8,128)(2,1)S(1)} collective-permute-done((bf16[128,128]{1,0:T(8,128)(2,1)S(1)}, bf16[128,128]{1,0:T(8,128)(2,1)S(1)}, u32[]{:S(2)}, u32[]{:S(2)}) %collective-permute-start.1) | collective-permute-done | bytes 32800 | tf_op jit(solution)/shard_map/ppermute | solution.py:224
  9.1 0.8 %collective-permute-done.2.refs_2_ = bf16[128,128]{1,0:T(8,128)(2,1)S(1)} collective-permute-done((bf16[128,128]{1,0:T(8,128)(2,1)S(1)}, bf16[128,128]{1,0:T(8,128)(2,1)S(1)}, u32[]{:S(2)}, u32[]{:S(2)}) %collective-permute-start.2) | collective-permute-done | bytes 32800 | tf_op jit(solution)/shard_map/ppermute | solution.py:224
  10.0 1.6 %collective-permute-start.4 = (bf16[128,128]{1,0:T(8,128)(2,1)S(1)}, bf16[128,128]{1,0:T(8,128)(2,1)S(1)}, u32[]{:S(2)}, u32[]{:S(2)}) collective-permute-start(bf16[128,128]{1,0:T(8,128)(2,1)S(1)} %add_convert_fusion.1), channel_id=1, source_target_pairs={{0,8},{2,10},{4,12},{6,14},{8,16},{10,18},{12,20},{14,22},{16,24},... | collective-permute-start | bytes 98312 | tf_op jit(solution)/shard_map/ppermute | solution.py:236
  11.6 2.6 %collective-permute-start.5 = (bf16[128,128]{1,0:T(8,128)(2,1)S(1)}, bf16[128,128]{1,0:T(8,128)(2,1)S(1)}, u32[]{:S(2)}, u32[]{:S(2)}) collective-permute-start(bf16[128,128]{1,0:T(8,128)(2,1)S(1)} %add_convert_fusion.1), channel_id=1, source_target_pairs={{0,16},{2,18},{4,20},{6,22},{8,24},{10,26},{12,28},{14,30},{16,0},... | collective-permute-start | bytes 98312 | tf_op jit(solution)/shard_map/ppermute | solution.py:236
  14.2 1.3 %collective-permute-start.6 = (bf16[128,128]{1,0:T(8,128)(2,1)S(1)}, bf16[128,128]{1,0:T(8,128)(2,1)S(1)}, u32[]{:S(2)}, u32[]{:S(2)}) collective-permute-start(bf16[128,128]{1,0:T(8,128)(2,1)S(1)} %add_convert_fusion.1), channel_id=1, source_target_pairs={{0,24},{2,26},{4,28},{6,30},{8,0},{10,2},{12,4},{14,6},{16,8},{18,... | collective-permute-start | bytes 98312 | tf_op jit(solution)/shard_map/ppermute | solution.py:236
  15.8 1.3 %collective-permute-done.5.refs_5_ = bf16[128,128]{1,0:T(8,128)(2,1)S(1)} collective-permute-done((bf16[128,128]{1,0:T(8,128)(2,1)S(1)}, bf16[128,128]{1,0:T(8,128)(2,1)S(1)}, u32[]{:S(2)}, u32[]{:S(2)}) %collective-permute-start.5) | collective-permute-done | bytes 32800 | tf_op jit(solution)/shard_map/ppermute | solution.py:236
  17.0 1.1 %collective-permute-done.6.refs_6_ = bf16[128,128]{1,0:T(8,128)(2,1)S(1)} collective-permute-done((bf16[128,128]{1,0:T(8,128)(2,1)S(1)}, bf16[128,128]{1,0:T(8,128)(2,1)S(1)}, u32[]{:S(2)}, u32[]{:S(2)}) %collective-permute-start.6) | collective-permute-done | bytes 32800 | tf_op jit(solution)/shard_map/ppermute | solution.py:236
  18.3 1.7 %collective-permute-start.8 = (bf16[128,128]{1,0:T(8,128)(2,1)S(1)}, bf16[128,128]{1,0:T(8,128)(2,1)S(1)}, u32[]{:S(2)}, u32[]{:S(2)}) collective-permute-start(bf16[128,128]{1,0:T(8,128)(2,1)S(1)} %get-tuple-element.38), channel_id=1, source_target_pairs={{0,5},{1,4},{2,7},{3,6},{4,1},{5,2},{6,3},{7,0},{8,13},{9,12},{10,... | collective-permute-start | bytes 98312 | tf_op jit(solution)/shard_map/ppermute | solution.py:224
  20.1 0.5 %collective-permute-start.10 = (bf16[128,128]{1,0:T(8,128)(2,1)S(1)}, bf16[128,128]{1,0:T(8,128)(2,1)S(1)}, u32[]{:S(2)}, u32[]{:S(2)}) collective-permute-start(bf16[128,128]{1,0:T(8,128)(2,1)S(1)} %get-tuple-element.40), channel_id=1, source_target_pairs={{0,1},{1,0},{2,3},{3,2},{4,5},{5,4},{6,7},{7,6},{8,9},{9,8},{10,11... | collective-permute-start | bytes 98312 | tf_op jit(solution)/shard_map/ppermute | solution.py:224
  20.6 0.7 %shard_map.75 = (bf16[4,256,256]{2,1,0:T(8,128)(2,1)S(1)}, f32[256,512]{1,0:T(8,128)S(1)}, bf16[4,128,256]{2,1,0:T(8,128)(2,1)S(1)}) custom-call(bf16[256,512]{1,0:T(8,128)(2,1)S(1)} %copy-done.2, bf16[256,512]{1,0:T(8,128)(2,1)S(1)} %copy-done, bf16[256,512]{1,0:T(8,128)(2,1)S(1)} %copy-done.1), custom_call_target="tpu_custom_call" | custom-call | flops 134217728 | bytes 2097152 | tf_op jit(solution)/shard_map/pallas_call | solution.py:70
  21.3 0.7 %collective-permute-done.7.p0 = bf16[128,128]{1,0:T(8,128)(2,1)S(1)} collective-permute-done((bf16[128,128]{1,0:T(8,128)(2,1)S(1)}, bf16[128,128]{1,0:T(8,128)(2,1)S(1)}, u32[]{:S(2)}, u32[]{:S(2)}) %collective-permute-start.7) | collective-permute-done | bytes 32800 | tf_op jit(solution)/shard_map/ppermute | solution.py:224
  22.0 0.6 %collective-permute-done.8.p1 = bf16[128,128]{1,0:T(8,128)(2,1)S(1)} collective-permute-done((bf16[128,128]{1,0:T(8,128)(2,1)S(1)}, bf16[128,128]{1,0:T(8,128)(2,1)S(1)}, u32[]{:S(2)}, u32[]{:S(2)}) %collective-permute-start.8) | collective-permute-done | bytes 32800 | tf_op jit(solution)/shard_map/ppermute | solution.py:224
  22.6 1.1 %collective-permute-done.9.p2 = bf16[128,128]{1,0:T(8,128)(2,1)S(1)} collective-permute-done((bf16[128,128]{1,0:T(8,128)(2,1)S(1)}, bf16[128,128]{1,0:T(8,128)(2,1)S(1)}, u32[]{:S(2)}, u32[]{:S(2)}) %collective-permute-start.9) | collective-permute-done | bytes 32800 | tf_op jit(solution)/shard_map/ppermute | solution.py:224
  24.2 1.1 %collective-permute-done.11 = f32[2,256]{1,0:T(2,128)S(1)} collective-permute-done((f32[2,256]{1,0:T(2,128)S(1)}, f32[2,256]{1,0:T(2,128)S(1)}, u32[]{:S(2)}, u32[]{:S(2)}) %collective-permute-start.11) | collective-permute-done | bytes 2080 | tf_op jit(solution)/shard_map/ppermute | solution.py:214
  25.7 1.3 %collective-permute-start.12 = (bf16[128,128]{1,0:T(8,128)(2,1)S(1)}, bf16[128,128]{1,0:T(8,128)(2,1)S(1)}, u32[]{:S(2)}, u32[]{:S(2)}) collective-permute-start(bf16[128,128]{1,0:T(8,128)(2,1)S(1)} %get-tuple-element.50), channel_id=1, source_target_pairs={{0,7},{1,6},{2,5},{3,4},{4,3},{5,2},{6,1},{7,0},{8,15},{9,14},{10,... | collective-permute-start | bytes 98312 | tf_op jit(solution)/shard_map/ppermute | solution.py:224
  27.2 1.5 %collective-permute-start.14 = (bf16[128,128]{1,0:T(8,128)(2,1)S(1)}, bf16[128,128]{1,0:T(8,128)(2,1)S(1)}, u32[]{:S(2)}, u32[]{:S(2)}) collective-permute-start(bf16[128,128]{1,0:T(8,128)(2,1)S(1)} %get-tuple-element.52), channel_id=1, source_target_pairs={{0,3},{1,4},{2,1},{3,6},{4,7},{5,0},{6,5},{7,2},{8,11},{9,12},{10,... | collective-permute-start | bytes 98312 | tf_op jit(solution)/shard_map/ppermute | solution.py:224
  29.1 0.9 %collective-permute-done.12.refs_0_ = bf16[128,128]{1,0:T(8,128)(2,1)S(1)} collective-permute-done((bf16[128,128]{1,0:T(8,128)(2,1)S(1)}, bf16[128,128]{1,0:T(8,128)(2,1)S(1)}, u32[]{:S(2)}, u32[]{:S(2)}) %collective-permute-start.12) | collective-permute-done | bytes 32800 | tf_op jit(solution)/shard_map/ppermute | solution.py:224
  30.3 0.6 %collective-permute-done.14.refs_2_ = bf16[128,128]{1,0:T(8,128)(2,1)S(1)} collective-permute-done((bf16[128,128]{1,0:T(8,128)(2,1)S(1)}, bf16[128,128]{1,0:T(8,128)(2,1)S(1)}, u32[]{:S(2)}, u32[]{:S(2)}) %collective-permute-start.14) | collective-permute-done | bytes 32800 | tf_op jit(solution)/shard_map/ppermute | solution.py:224
  31.0 1.2 %collective-permute-start.16 = (bf16[128,128]{1,0:T(8,128)(2,1)S(1)}, bf16[128,128]{1,0:T(8,128)(2,1)S(1)}, u32[]{:S(2)}, u32[]{:S(2)}) collective-permute-start(bf16[128,128]{1,0:T(8,128)(2,1)S(1)} %add_convert_fusion), channel_id=1, source_target_pairs={{0,16},{2,18},{4,20},{6,22},{8,24},{10,26},{12,28},{14,30},{16,8},... | collective-permute-start | bytes 98312 | tf_op jit(solution)/shard_map/ppermute | solution.py:236
  32.2 0.5 %collective-permute-start.17 = (bf16[128,128]{1,0:T(8,128)(2,1)S(1)}, bf16[128,128]{1,0:T(8,128)(2,1)S(1)}, u32[]{:S(2)}, u32[]{:S(2)}) collective-permute-start(bf16[128,128]{1,0:T(8,128)(2,1)S(1)} %add_convert_fusion), channel_id=1, source_target_pairs={{0,16},{2,18},{4,20},{6,22},{8,24},{10,26},{12,28},{14,30},{16,0},... | collective-permute-start | bytes 98312 | tf_op jit(solution)/shard_map/ppermute | solution.py:236
  32.8 2.7 %collective-permute-start.18 = (bf16[128,128]{1,0:T(8,128)(2,1)S(1)}, bf16[128,128]{1,0:T(8,128)(2,1)S(1)}, u32[]{:S(2)}, u32[]{:S(2)}) collective-permute-start(bf16[128,128]{1,0:T(8,128)(2,1)S(1)} %add_convert_fusion), channel_id=1, source_target_pairs={{0,8},{2,10},{4,12},{6,14},{8,0},{10,2},{12,4},{14,6},{16,24},{18,... | collective-permute-start | bytes 98312 | tf_op jit(solution)/shard_map/ppermute | solution.py:236
  35.4 2.0 %shard_map.80 = (bf16[256,512]{1,0:T(8,128)(2,1)}, bf16[256,512]{1,0:T(8,128)(2,1)}, f32[256,512]{1,0:T(8,128)S(1)}, f32[256,512]{1,0:T(8,128)S(1)}) custom-call(bf16[256,512]{1,0:T(8,128)(2,1)S(1)} %copy-done.2, bf16[256,512]{1,0:T(8,128)(2,1)S(1)} %copy-done, bf16[256,512]{1,0:T(8,128)(2,1)S(1)} %copy-done.1, ...), custom_call_target="tpu_custom_call" | custom-call | flops 301989888 | bytes 3803136 | tf_op jit(solution)/shard_map/pallas_call | solution.py:70
  37.5 0.6 %collective-permute-done.18.refs_6_ = bf16[128,128]{1,0:T(8,128)(2,1)S(1)} collective-permute-done((bf16[128,128]{1,0:T(8,128)(2,1)S(1)}, bf16[128,128]{1,0:T(8,128)(2,1)S(1)}, u32[]{:S(2)}, u32[]{:S(2)}) %collective-permute-start.18) | collective-permute-done | bytes 32800 | tf_op jit(solution)/shard_map/ppermute | solution.py:236
  38.3 1.7 %collective-permute-start.20 = (bf16[128,128]{1,0:T(8,128)(2,1)S(1)}, bf16[128,128]{1,0:T(8,128)(2,1)S(1)}, u32[]{:S(2)}, u32[]{:S(2)}) collective-permute-start(bf16[128,128]{1,0:T(8,128)(2,1)S(1)} %get-tuple-element.55), channel_id=1, source_target_pairs={{0,5},{1,2},{2,7},{3,4},{4,1},{5,6},{6,3},{7,0},{8,13},{9,10},{10,... | collective-permute-start | bytes 98312 | tf_op jit(solution)/shard_map/ppermute | solution.py:224
  40.0 1.2 %collective-permute-start.21 = (bf16[128,128]{1,0:T(8,128)(2,1)S(1)}, bf16[128,128]{1,0:T(8,128)(2,1)S(1)}, u32[]{:S(2)}, u32[]{:S(2)}) collective-permute-start(bf16[128,128]{1,0:T(8,128)(2,1)S(1)} %get-tuple-element.56), channel_id=1, source_target_pairs={{0,3},{1,6},{2,1},{3,0},{4,7},{5,2},{6,5},{7,4},{8,11},{9,14},{10,... | collective-permute-start | bytes 98312 | tf_op jit(solution)/shard_map/ppermute | solution.py:224
  41.6 1.2 %collective-permute-done.20.p1 = bf16[128,128]{1,0:T(8,128)(2,1)S(1)} collective-permute-done((bf16[128,128]{1,0:T(8,128)(2,1)S(1)}, bf16[128,128]{1,0:T(8,128)(2,1)S(1)}, u32[]{:S(2)}, u32[]{:S(2)}) %collective-permute-start.20) | collective-permute-done | bytes 32800 | tf_op jit(solution)/shard_map/ppermute | solution.py:224
  42.8 0.6 %collective-permute-done.21.p2 = bf16[128,128]{1,0:T(8,128)(2,1)S(1)} collective-permute-done((bf16[128,128]{1,0:T(8,128)(2,1)S(1)}, bf16[128,128]{1,0:T(8,128)(2,1)S(1)}, u32[]{:S(2)}, u32[]{:S(2)}) %collective-permute-start.21) | collective-permute-done | bytes 32800 | tf_op jit(solution)/shard_map/ppermute | solution.py:224
  43.4 1.1 %shard_map.82 = (bf16[256,512]{1,0:T(8,128)(2,1)}, bf16[256,512]{1,0:T(8,128)(2,1)}) custom-call(bf16[256,512]{1,0:T(8,128)(2,1)S(1)} %copy-done, bf16[256,512]{1,0:T(8,128)(2,1)S(1)} %copy-done.1, f32[256,512]{1,0:T(8,128)S(1)} %get-tuple-element.48.refs_7_.key_local, f32[256,512]{1,0:T(8,128)S(1)} %get-tuple-element.49.value_local, ...), custom_call_target="tpu_custom_call" | custom-call | flops 67108864 | bytes 2228224 | tf_op jit(solution)/shard_map/pallas_call | solution.py:70
  (33 shorter events, 3.0 us)
Async XLA Ops:
  0.6 20.0 %copy-start.1 = (bf16[256,512]{1,0:T(8,128)(2,1)S(1)}, bf16[256,512]{1,0:T(8,128)(2,1)}, u32[]{:S(2)}) copy-start(bf16[256,512]{1,0:T(8,128)(2,1)} %v_ref.7) | copy-start | bytes 786436
  0.6 20.0 %copy-start.2 = (bf16[256,512]{1,0:T(8,128)(2,1)S(1)}, bf16[256,512]{1,0:T(8,128)(2,1)}, u32[]{:S(2)}) copy-start(bf16[256,512]{1,0:T(8,128)(2,1)} %q_ref.5) | copy-start | bytes 786436
  2.1 18.5 %copy-start = (bf16[256,512]{1,0:T(8,128)(2,1)S(1)}, bf16[256,512]{1,0:T(8,128)(2,1)}, u32[]{:S(2)}) copy-start(bf16[256,512]{1,0:T(8,128)(2,1)} %k_ref.7) | copy-start | bytes 786436
  2.1 5.1 %collective-permute-start = (bf16[128,128]{1,0:T(8,128)(2,1)S(1)}, bf16[128,128]{1,0:T(8,128)(2,1)S(1)}, u32[]{:S(2)}, u32[]{:S(2)}) collective-permute-start(bf16[128,128]{1,0:T(8,128)(2,1)S(1)} %get-tuple-element.33), channel_id=1, source_target_pairs={{0,7},{1,4},{2,5},{3,6},{4,3},{5,2},{6,1},{7,0},{8,15},{9,12},{10,... | collective-permute-start | bytes 98312 | tf_op jit(solution)/shard_map/ppermute | solution.py:224
  5.5 3.6 %collective-permute-start.1 = (bf16[128,128]{1,0:T(8,128)(2,1)S(1)}, bf16[128,128]{1,0:T(8,128)(2,1)S(1)}, u32[]{:S(2)}, u32[]{:S(2)}) collective-permute-start(bf16[128,128]{1,0:T(8,128)(2,1)S(1)} %get-tuple-element.34), channel_id=1, source_target_pairs={{0,3},{1,6},{2,7},{3,4},{4,1},{5,0},{6,5},{7,2},{8,11},{9,14},{10,... | collective-permute-start | bytes 98312 | tf_op jit(solution)/shard_map/ppermute | solution.py:224
  6.4 3.6 %collective-permute-start.2 = (bf16[128,128]{1,0:T(8,128)(2,1)S(1)}, bf16[128,128]{1,0:T(8,128)(2,1)S(1)}, u32[]{:S(2)}, u32[]{:S(2)}) collective-permute-start(bf16[128,128]{1,0:T(8,128)(2,1)S(1)} %get-tuple-element.35), channel_id=1, source_target_pairs={{0,5},{1,2},{2,1},{3,0},{4,7},{5,6},{6,3},{7,4},{8,13},{9,10},{10,... | collective-permute-start | bytes 98312 | tf_op jit(solution)/shard_map/ppermute | solution.py:224
  7.3 2.7 %collective-permute-start.3 = (bf16[128,128]{1,0:T(8,128)(2,1)S(1)}, bf16[128,128]{1,0:T(8,128)(2,1)S(1)}, u32[]{:S(2)}, u32[]{:S(2)}) collective-permute-start(bf16[128,128]{1,0:T(8,128)(2,1)S(1)} %get-tuple-element.36), channel_id=1, source_target_pairs={{0,1},{1,0},{2,3},{3,2},{4,5},{5,4},{6,7},{7,6},{8,9},{9,8},{10,11... | collective-permute-start | bytes 98312 | tf_op jit(solution)/shard_map/ppermute | solution.py:224
  10.0 5.8 %collective-permute-start.4 = (bf16[128,128]{1,0:T(8,128)(2,1)S(1)}, bf16[128,128]{1,0:T(8,128)(2,1)S(1)}, u32[]{:S(2)}, u32[]{:S(2)}) collective-permute-start(bf16[128,128]{1,0:T(8,128)(2,1)S(1)} %add_convert_fusion.1), channel_id=1, source_target_pairs={{0,8},{2,10},{4,12},{6,14},{8,16},{10,18},{12,20},{14,22},{16,24},... | collective-permute-start | bytes 98312 | tf_op jit(solution)/shard_map/ppermute | solution.py:236
  11.6 5.4 %collective-permute-start.5 = (bf16[128,128]{1,0:T(8,128)(2,1)S(1)}, bf16[128,128]{1,0:T(8,128)(2,1)S(1)}, u32[]{:S(2)}, u32[]{:S(2)}) collective-permute-start(bf16[128,128]{1,0:T(8,128)(2,1)S(1)} %add_convert_fusion.1), channel_id=1, source_target_pairs={{0,16},{2,18},{4,20},{6,22},{8,24},{10,26},{12,28},{14,30},{16,0},... | collective-permute-start | bytes 98312 | tf_op jit(solution)/shard_map/ppermute | solution.py:236
  14.2 3.9 %collective-permute-start.6 = (bf16[128,128]{1,0:T(8,128)(2,1)S(1)}, bf16[128,128]{1,0:T(8,128)(2,1)S(1)}, u32[]{:S(2)}, u32[]{:S(2)}) collective-permute-start(bf16[128,128]{1,0:T(8,128)(2,1)S(1)} %add_convert_fusion.1), channel_id=1, source_target_pairs={{0,24},{2,26},{4,28},{6,30},{8,0},{10,2},{12,4},{14,6},{16,8},{18,... | collective-permute-start | bytes 98312 | tf_op jit(solution)/shard_map/ppermute | solution.py:236
  18.2 3.7 %collective-permute-start.7 = (bf16[128,128]{1,0:T(8,128)(2,1)S(1)}, bf16[128,128]{1,0:T(8,128)(2,1)S(1)}, u32[]{:S(2)}, u32[]{:S(2)}) collective-permute-start(bf16[128,128]{1,0:T(8,128)(2,1)S(1)} %get-tuple-element.37), channel_id=1, source_target_pairs={{0,7},{1,6},{2,5},{3,4},{4,3},{5,0},{6,1},{7,2},{8,15},{9,14},{10,... | collective-permute-start | bytes 98312 | tf_op jit(solution)/shard_map/ppermute | solution.py:224
  18.3 4.3 %collective-permute-start.8 = (bf16[128,128]{1,0:T(8,128)(2,1)S(1)}, bf16[128,128]{1,0:T(8,128)(2,1)S(1)}, u32[]{:S(2)}, u32[]{:S(2)}) collective-permute-start(bf16[128,128]{1,0:T(8,128)(2,1)S(1)} %get-tuple-element.38), channel_id=1, source_target_pairs={{0,5},{1,4},{2,7},{3,6},{4,1},{5,2},{6,3},{7,0},{8,13},{9,12},{10,... | collective-permute-start | bytes 98312 | tf_op jit(solution)/shard_map/ppermute | solution.py:224
  20.0 3.7 %collective-permute-start.9 = (bf16[128,128]{1,0:T(8,128)(2,1)S(1)}, bf16[128,128]{1,0:T(8,128)(2,1)S(1)}, u32[]{:S(2)}, u32[]{:S(2)}) collective-permute-start(bf16[128,128]{1,0:T(8,128)(2,1)S(1)} %get-tuple-element.39), channel_id=1, source_target_pairs={{0,3},{1,2},{2,1},{3,0},{4,7},{5,6},{6,5},{7,4},{8,11},{9,10},{10,... | collective-permute-start | bytes 98312 | tf_op jit(solution)/shard_map/ppermute | solution.py:224
  20.1 3.6 %copy-start.3 = (bf16[256,512]{1,0:T(8,128)(2,1)S(1)}, bf16[256,512]{1,0:T(8,128)(2,1)}, u32[]{:S(2)}) copy-start(bf16[256,512]{1,0:T(8,128)(2,1)} %c_ref.3) | copy-start | bytes 786436
  20.1 3.6 %collective-permute-start.10 = (bf16[128,128]{1,0:T(8,128)(2,1)S(1)}, bf16[128,128]{1,0:T(8,128)(2,1)S(1)}, u32[]{:S(2)}, u32[]{:S(2)}) collective-permute-start(bf16[128,128]{1,0:T(8,128)(2,1)S(1)} %get-tuple-element.40), channel_id=1, source_target_pairs={{0,1},{1,0},{2,3},{3,2},{4,5},{5,4},{6,7},{7,6},{8,9},{9,8},{10,11... | collective-permute-start | bytes 98312 | tf_op jit(solution)/shard_map/ppermute | solution.py:224
  24.1 1.2 %collective-permute-start.11 = (f32[2,256]{1,0:T(2,128)S(1)}, f32[2,256]{1,0:T(2,128)S(1)}, u32[]{:S(2)}, u32[]{:S(2)}) collective-permute-start(f32[2,256]{1,0:T(2,128)S(1)} %get-tuple-element.43), channel_id=1, source_target_pairs={{0,1},{1,0},{2,3},{3,2},{4,5},{5,4},{6,7},{7,6},{8,9},{9,8},{10,11... | collective-permute-start | bytes 6152 | tf_op jit(solution)/shard_map/ppermute | solution.py:214
  25.7 4.3 %collective-permute-start.12 = (bf16[128,128]{1,0:T(8,128)(2,1)S(1)}, bf16[128,128]{1,0:T(8,128)(2,1)S(1)}, u32[]{:S(2)}, u32[]{:S(2)}) collective-permute-start(bf16[128,128]{1,0:T(8,128)(2,1)S(1)} %get-tuple-element.50), channel_id=1, source_target_pairs={{0,7},{1,6},{2,5},{3,4},{4,3},{5,2},{6,1},{7,0},{8,15},{9,14},{10,... | collective-permute-start | bytes 98312 | tf_op jit(solution)/shard_map/ppermute | solution.py:224
  27.0 3.3 %collective-permute-start.13 = (bf16[128,128]{1,0:T(8,128)(2,1)S(1)}, bf16[128,128]{1,0:T(8,128)(2,1)S(1)}, u32[]{:S(2)}, u32[]{:S(2)}) collective-permute-start(bf16[128,128]{1,0:T(8,128)(2,1)S(1)} %get-tuple-element.51), channel_id=1, source_target_pairs={{0,5},{1,2},{2,7},{3,0},{4,1},{5,6},{6,3},{7,4},{8,13},{9,10},{10,... | collective-permute-start | bytes 98312 | tf_op jit(solution)/shard_map/ppermute | solution.py:224
  27.2 3.7 %collective-permute-start.14 = (bf16[128,128]{1,0:T(8,128)(2,1)S(1)}, bf16[128,128]{1,0:T(8,128)(2,1)S(1)}, u32[]{:S(2)}, u32[]{:S(2)}) collective-permute-start(bf16[128,128]{1,0:T(8,128)(2,1)S(1)} %get-tuple-element.52), channel_id=1, source_target_pairs={{0,3},{1,4},{2,1},{3,6},{4,7},{5,0},{6,5},{7,2},{8,11},{9,12},{10,... | collective-permute-start | bytes 98312 | tf_op jit(solution)/shard_map/ppermute | solution.py:224
  28.7 2.2 %collective-permute-start.15 = (bf16[128,128]{1,0:T(8,128)(2,1)S(1)}, bf16[128,128]{1,0:T(8,128)(2,1)S(1)}, u32[]{:S(2)}, u32[]{:S(2)}) collective-permute-start(bf16[128,128]{1,0:T(8,128)(2,1)S(1)} %get-tuple-element.53), channel_id=1, source_target_pairs={{0,1},{1,0},{2,3},{3,2},{4,5},{5,4},{6,7},{7,6},{8,9},{9,8},{10,11... | collective-permute-start | bytes 98312 | tf_op jit(solution)/shard_map/ppermute | solution.py:224
  31.0 6.5 %collective-permute-start.16 = (bf16[128,128]{1,0:T(8,128)(2,1)S(1)}, bf16[128,128]{1,0:T(8,128)(2,1)S(1)}, u32[]{:S(2)}, u32[]{:S(2)}) collective-permute-start(bf16[128,128]{1,0:T(8,128)(2,1)S(1)} %add_convert_fusion), channel_id=1, source_target_pairs={{0,16},{2,18},{4,20},{6,22},{8,24},{10,26},{12,28},{14,30},{16,8},... | collective-permute-start | bytes 98312 | tf_op jit(solution)/shard_map/ppermute | solution.py:236
  32.2 5.3 %collective-permute-start.17 = (bf16[128,128]{1,0:T(8,128)(2,1)S(1)}, bf16[128,128]{1,0:T(8,128)(2,1)S(1)}, u32[]{:S(2)}, u32[]{:S(2)}) collective-permute-start(bf16[128,128]{1,0:T(8,128)(2,1)S(1)} %add_convert_fusion), channel_id=1, source_target_pairs={{0,16},{2,18},{4,20},{6,22},{8,24},{10,26},{12,28},{14,30},{16,0},... | collective-permute-start | bytes 98312 | tf_op jit(solution)/shard_map/ppermute | solution.py:236
  32.8 5.4 %collective-permute-start.18 = (bf16[128,128]{1,0:T(8,128)(2,1)S(1)}, bf16[128,128]{1,0:T(8,128)(2,1)S(1)}, u32[]{:S(2)}, u32[]{:S(2)}) collective-permute-start(bf16[128,128]{1,0:T(8,128)(2,1)S(1)} %add_convert_fusion), channel_id=1, source_target_pairs={{0,8},{2,10},{4,12},{6,14},{8,0},{10,2},{12,4},{14,6},{16,24},{18,... | collective-permute-start | bytes 98312 | tf_op jit(solution)/shard_map/ppermute | solution.py:236
  38.2 3.4 %collective-permute-start.19 = (bf16[128,128]{1,0:T(8,128)(2,1)S(1)}, bf16[128,128]{1,0:T(8,128)(2,1)S(1)}, u32[]{:S(2)}, u32[]{:S(2)}) collective-permute-start(bf16[128,128]{1,0:T(8,128)(2,1)S(1)} %get-tuple-element.54), channel_id=1, source_target_pairs={{0,7},{1,4},{2,5},{3,6},{4,3},{5,0},{6,1},{7,2},{8,15},{9,12},{10,... | collective-permute-start | bytes 98312 | tf_op jit(solution)/shard_map/ppermute | solution.py:224
  38.3 4.5 %collective-permute-start.20 = (bf16[128,128]{1,0:T(8,128)(2,1)S(1)}, bf16[128,128]{1,0:T(8,128)(2,1)S(1)}, u32[]{:S(2)}, u32[]{:S(2)}) collective-permute-start(bf16[128,128]{1,0:T(8,128)(2,1)S(1)} %get-tuple-element.55), channel_id=1, source_target_pairs={{0,5},{1,2},{2,7},{3,4},{4,1},{5,6},{6,3},{7,0},{8,13},{9,10},{10,... | collective-permute-start | bytes 98312 | tf_op jit(solution)/shard_map/ppermute | solution.py:224
  40.0 3.4 %collective-permute-start.21 = (bf16[128,128]{1,0:T(8,128)(2,1)S(1)}, bf16[128,128]{1,0:T(8,128)(2,1)S(1)}, u32[]{:S(2)}, u32[]{:S(2)}) collective-permute-start(bf16[128,128]{1,0:T(8,128)(2,1)S(1)} %get-tuple-element.56), channel_id=1, source_target_pairs={{0,3},{1,6},{2,1},{3,0},{4,7},{5,2},{6,5},{7,4},{8,11},{9,14},{10,... | collective-permute-start | bytes 98312 | tf_op jit(solution)/shard_map/ppermute | solution.py:224
  41.2 2.2 %collective-permute-start.22 = (bf16[128,128]{1,0:T(8,128)(2,1)S(1)}, bf16[128,128]{1,0:T(8,128)(2,1)S(1)}, u32[]{:S(2)}, u32[]{:S(2)}) collective-permute-start(bf16[128,128]{1,0:T(8,128)(2,1)S(1)} %get-tuple-element.57), channel_id=1, source_target_pairs={{0,1},{1,0},{2,3},{3,2},{4,5},{5,4},{6,7},{7,6},{8,9},{9,8},{10,11... | collective-permute-start | bytes 98312 | tf_op jit(solution)/shard_map/ppermute | solution.py:224

commit v16 on v14

--- a/solution.py
+++ b/solution.py
@@ -37,7 +37,7 @@
     return lax.axis_index("seq") % QUAD
 
 
-FIRST = (((3, 2, 1, 0), (1, 3, 0, 2), (2, 0, 3, 1)), ((2, 3, 1, 0), (3, 2, 0, 1), (1, 0, 3, 2)))
+FIRST = (((3, 2, 1, 0), (1, 0, 3, 2), (2, 3, 0, 1)), ((1, 2, 3, 0), (3, 0, 1, 2), (2, 3, 0, 1)))
 BACK = (((3, 2, 1, 0), (2, 3, 0, 1), (1, 0, 3, 2)), ((3, 2, 0, 1), (2, 3, 1, 0), (1, 0, 3, 2)))
 FIRST_GRAD = (((3, 2, 1, 0), (2, 3, 0, 1), (1, 0, 3, 2)), ((3, 2, 1, 0), (1, 0, 3, 2), (2, 3, 0, 1)))
 BACK_GRAD = (((3, 2, 1, 0), (2, 3, 0, 1), (1, 0, 3, 2)), ((2, 3, 0, 1), (1, 2, 3, 0), (3, 0, 1, 2)))

time: 44.5 us -> 44.6 us (level)
  no operation moved by 1% of the time
where the time goes in v16:
time: 44.6 us; the launch traced here: 44.4 us
  starting transfers between devices  22.6 us (51%)
  waiting for transfers between devices  14.5 us (33%)
  Pallas kernels  6.47 us (15%)
  between operations  0.74 us (2%)
    ppermute x16, starting transfers between devices, cross(): return lax.ppermute(value, ('seq', 'tp'), pairs)  13.7 us
    ppermute x16, waiting for transfers between devices, cross(): return lax.ppermute(value, ('seq', 'tp'), pairs)  8.87 us
    ppermute x6, starting transfers between devices, exclusive_sum(): got.append(lax.ppermute(total, 'seq', pairs))  8.68 us
    pallas_call x10, Pallas kernels, call(): pl.pallas_call(kernel, out_shape=outs, in_specs=in_specs or [pl.BlockSpec...  6.47 us
    ppermute x6, waiting for transfers between devices, exclusive_sum(): got.append(lax.ppermute(total, 'seq', pairs))  4.63 us
    ppermute x1, waiting for transfers between devices, exchange(): return lax.ppermute(value, axis, [(i, i ^ bits) for i in range(size)])  1.04 us
  transfers between devices with their start and end apart: 23, of which 16 were waited for; matrix products, arithmetic and copies ran while one was open for 0% of the time, Pallas kernels for 7%

profile of v16, /device:TPU:0, one launch (start us, length us, event | category | flops | bytes accessed | tf_op | source)
XLA Modules:
  0.0 44.4 jit_solution(8079981160634821740)
XLA Ops:
  0.7 1.4 %shard_map.76 = (bf16[128,128]{1,0:T(8,128)(2,1)S(1)}, bf16[128,128]{1,0:T(8,128)(2,1)S(1)}, bf16[128,128]{1,0:T(8,128)(2,1)S(1)}, bf16[128,128]{1,0:T(8,128)(2,1)S(1)}) custom-call(bf16[256,512]{1,0:T(8,128)(2,1)} %k_ref.9, bf16[256,512]{1,0:T(8,128)(2,1)} %v_ref.9), custom_call_target="tpu_custom_call" | custom-call | flops 33554432 | bytes 655360 | tf_op jit(solution)/shard_map/pallas_call | solution.py:71
  2.1 3.4 %collective-permute-start = (bf16[128,128]{1,0:T(8,128)(2,1)S(1)}, bf16[128,128]{1,0:T(8,128)(2,1)S(1)}, u32[]{:S(2)}, u32[]{:S(2)}) collective-permute-start(bf16[128,128]{1,0:T(8,128)(2,1)S(1)} %get-tuple-element.38), channel_id=1, source_target_pairs={{0,7},{1,2},{2,5},{3,4},{4,3},{5,6},{6,1},{7,0},{8,15},{9,10},{10,... | collective-permute-start | bytes 98312 | tf_op jit(solution)/shard_map/ppermute | solution.py:246
  5.5 0.8 %collective-permute-start.1 = (bf16[128,128]{1,0:T(8,128)(2,1)S(1)}, bf16[128,128]{1,0:T(8,128)(2,1)S(1)}, u32[]{:S(2)}, u32[]{:S(2)}) collective-permute-start(bf16[128,128]{1,0:T(8,128)(2,1)S(1)} %get-tuple-element.39), channel_id=1, source_target_pairs={{0,3},{1,6},{2,1},{3,0},{4,7},{5,2},{6,5},{7,4},{8,11},{9,14},{10,... | collective-permute-start | bytes 98312 | tf_op jit(solution)/shard_map/ppermute | solution.py:246
  6.3 0.9 %collective-permute-start.2 = (bf16[128,128]{1,0:T(8,128)(2,1)S(1)}, bf16[128,128]{1,0:T(8,128)(2,1)S(1)}, u32[]{:S(2)}, u32[]{:S(2)}) collective-permute-start(bf16[128,128]{1,0:T(8,128)(2,1)S(1)} %get-tuple-element.40), channel_id=1, source_target_pairs={{0,5},{1,4},{2,7},{3,6},{4,1},{5,0},{6,3},{7,2},{8,13},{9,12},{10,... | collective-permute-start | bytes 98312 | tf_op jit(solution)/shard_map/ppermute | solution.py:246
  7.2 1.9 %collective-permute-done.1.refs_1_ = bf16[128,128]{1,0:T(8,128)(2,1)S(1)} collective-permute-done((bf16[128,128]{1,0:T(8,128)(2,1)S(1)}, bf16[128,128]{1,0:T(8,128)(2,1)S(1)}, u32[]{:S(2)}, u32[]{:S(2)}) %collective-permute-start.1) | collective-permute-done | bytes 32800 | tf_op jit(solution)/shard_map/ppermute | solution.py:246
  9.1 0.8 %collective-permute-done.2.refs_2_ = bf16[128,128]{1,0:T(8,128)(2,1)S(1)} collective-permute-done((bf16[128,128]{1,0:T(8,128)(2,1)S(1)}, bf16[128,128]{1,0:T(8,128)(2,1)S(1)}, u32[]{:S(2)}, u32[]{:S(2)}) %collective-permute-start.2) | collective-permute-done | bytes 32800 | tf_op jit(solution)/shard_map/ppermute | solution.py:246
  9.9 2.7 %collective-permute-start.4 = (bf16[128,128]{1,0:T(8,128)(2,1)S(1)}, bf16[128,128]{1,0:T(8,128)(2,1)S(1)}, u32[]{:S(2)}, u32[]{:S(2)}) collective-permute-start(bf16[128,128]{1,0:T(8,128)(2,1)S(1)} %add_convert_fusion.1), channel_id=1, source_target_pairs={{0,16},{2,18},{4,20},{6,22},{8,24},{10,26},{12,28},{14,30},{16,0},... | collective-permute-start | bytes 98312 | tf_op jit(solution)/shard_map/ppermute | solution.py:258
  12.6 1.3 %collective-permute-start.5 = (bf16[128,128]{1,0:T(8,128)(2,1)S(1)}, bf16[128,128]{1,0:T(8,128)(2,1)S(1)}, u32[]{:S(2)}, u32[]{:S(2)}) collective-permute-start(bf16[128,128]{1,0:T(8,128)(2,1)S(1)} %add_convert_fusion.1), channel_id=1, source_target_pairs={{0,24},{2,26},{4,28},{6,30},{8,16},{10,18},{12,20},{14,22},{16,0},... | collective-permute-start | bytes 98312 | tf_op jit(solution)/shard_map/ppermute | solution.py:258
  14.2 1.0 %collective-permute-done.4.refs_4_ = bf16[128,128]{1,0:T(8,128)(2,1)S(1)} collective-permute-done((bf16[128,128]{1,0:T(8,128)(2,1)S(1)}, bf16[128,128]{1,0:T(8,128)(2,1)S(1)}, u32[]{:S(2)}, u32[]{:S(2)}) %collective-permute-start.4) | collective-permute-done | bytes 32800 | tf_op jit(solution)/shard_map/ppermute | solution.py:258
  15.2 2.5 %collective-permute-done.5.refs_5_ = bf16[128,128]{1,0:T(8,128)(2,1)S(1)} collective-permute-done((bf16[128,128]{1,0:T(8,128)(2,1)S(1)}, bf16[128,128]{1,0:T(8,128)(2,1)S(1)}, u32[]{:S(2)}, u32[]{:S(2)}) %collective-permute-start.5) | collective-permute-done | bytes 32800 | tf_op jit(solution)/shard_map/ppermute | solution.py:258
  18.2 1.7 %collective-permute-start.8 = (bf16[128,128]{1,0:T(8,128)(2,1)S(1)}, bf16[128,128]{1,0:T(8,128)(2,1)S(1)}, u32[]{:S(2)}, u32[]{:S(2)}) collective-permute-start(bf16[128,128]{1,0:T(8,128)(2,1)S(1)} %get-tuple-element.43), channel_id=1, source_target_pairs={{0,5},{1,4},{2,7},{3,6},{4,1},{5,2},{6,3},{7,0},{8,13},{9,12},{10,... | collective-permute-start | bytes 98312 | tf_op jit(solution)/shard_map/ppermute | solution.py:246
  20.0 0.6 %collective-permute-start.10 = (bf16[128,128]{1,0:T(8,128)(2,1)S(1)}, bf16[128,128]{1,0:T(8,128)(2,1)S(1)}, u32[]{:S(2)}, u32[]{:S(2)}) collective-permute-start(bf16[128,128]{1,0:T(8,128)(2,1)S(1)} %get-tuple-element.46), channel_id=1, source_target_pairs={{0,1},{1,0},{2,3},{3,2},{4,5},{5,4},{6,7},{7,6},{8,9},{9,8},{10,11... | collective-permute-start | bytes 98312 | tf_op jit(solution)/shard_map/ppermute | solution.py:246
  20.6 0.7 %shard_map.75 = (bf16[4,256,256]{2,1,0:T(8,128)(2,1)S(1)}, f32[256,512]{1,0:T(8,128)S(1)}, bf16[4,128,256]{2,1,0:T(8,128)(2,1)S(1)}) custom-call(bf16[256,512]{1,0:T(8,128)(2,1)S(1)} %copy-done.2, bf16[256,512]{1,0:T(8,128)(2,1)S(1)} %copy-done, bf16[256,512]{1,0:T(8,128)(2,1)S(1)} %copy-done.1), custom_call_target="tpu_custom_call" | custom-call | flops 134217728 | bytes 2097152 | tf_op jit(solution)/shard_map/pallas_call | solution.py:71
  21.3 0.6 %collective-permute-done.7.refs_3_.p0 = bf16[128,128]{1,0:T(8,128)(2,1)S(1)} collective-permute-done((bf16[128,128]{1,0:T(8,128)(2,1)S(1)}, bf16[128,128]{1,0:T(8,128)(2,1)S(1)}, u32[]{:S(2)}, u32[]{:S(2)}) %collective-permute-start.7) | collective-permute-done | bytes 32800 | tf_op jit(solution)/shard_map/ppermute | solution.py:246
  21.9 0.6 %collective-permute-done.8.refs_4_.p1 = bf16[128,128]{1,0:T(8,128)(2,1)S(1)} collective-permute-done((bf16[128,128]{1,0:T(8,128)(2,1)S(1)}, bf16[128,128]{1,0:T(8,128)(2,1)S(1)}, u32[]{:S(2)}, u32[]{:S(2)}) %collective-permute-start.8) | collective-permute-done | bytes 32800 | tf_op jit(solution)/shard_map/ppermute | solution.py:246
  22.7 0.9 %collective-permute-done.9.p2 = bf16[128,128]{1,0:T(8,128)(2,1)S(1)} collective-permute-done((bf16[128,128]{1,0:T(8,128)(2,1)S(1)}, bf16[128,128]{1,0:T(8,128)(2,1)S(1)}, u32[]{:S(2)}, u32[]{:S(2)}) %collective-permute-start.9) | collective-permute-done | bytes 32800 | tf_op jit(solution)/shard_map/ppermute | solution.py:246
  24.0 1.0 %collective-permute-done.11 = f32[2,256]{1,0:T(2,128)S(1)} collective-permute-done((f32[2,256]{1,0:T(2,128)S(1)}, f32[2,256]{1,0:T(2,128)S(1)}, u32[]{:S(2)}, u32[]{:S(2)}) %collective-permute-start.11) | collective-permute-done | bytes 2080 | tf_op jit(solution)/shard_map/ppermute | solution.py:236
  25.5 0.7 %collective-permute-start.12 = (bf16[128,128]{1,0:T(8,128)(2,1)S(1)}, bf16[128,128]{1,0:T(8,128)(2,1)S(1)}, u32[]{:S(2)}, u32[]{:S(2)}) collective-permute-start(bf16[128,128]{1,0:T(8,128)(2,1)S(1)} %get-tuple-element.58), channel_id=1, source_target_pairs={{0,7},{1,6},{2,5},{3,4},{4,3},{5,2},{6,1},{7,0},{8,15},{9,14},{10,... | collective-permute-start | bytes 98312 | tf_op jit(solution)/shard_map/ppermute | solution.py:246
  26.2 1.0 %collective-permute-start.13 = (bf16[128,128]{1,0:T(8,128)(2,1)S(1)}, bf16[128,128]{1,0:T(8,128)(2,1)S(1)}, u32[]{:S(2)}, u32[]{:S(2)}) collective-permute-start(bf16[128,128]{1,0:T(8,128)(2,1)S(1)} %get-tuple-element.59), channel_id=1, source_target_pairs={{0,5},{1,2},{2,7},{3,0},{4,1},{5,6},{6,3},{7,4},{8,13},{9,10},{10,... | collective-permute-start | bytes 98312 | tf_op jit(solution)/shard_map/ppermute | solution.py:246
  27.2 0.8 %collective-permute-start.14 = (bf16[128,128]{1,0:T(8,128)(2,1)S(1)}, bf16[128,128]{1,0:T(8,128)(2,1)S(1)}, u32[]{:S(2)}, u32[]{:S(2)}) collective-permute-start(bf16[128,128]{1,0:T(8,128)(2,1)S(1)} %get-tuple-element.60), channel_id=1, source_target_pairs={{0,3},{1,4},{2,1},{3,6},{4,7},{5,0},{6,5},{7,2},{8,11},{9,12},{10,... | collective-permute-start | bytes 98312 | tf_op jit(solution)/shard_map/ppermute | solution.py:246
  28.3 1.5 %collective-permute-done.12.refs_0_ = bf16[128,128]{1,0:T(8,128)(2,1)S(1)} collective-permute-done((bf16[128,128]{1,0:T(8,128)(2,1)S(1)}, bf16[128,128]{1,0:T(8,128)(2,1)S(1)}, u32[]{:S(2)}, u32[]{:S(2)}) %collective-permute-start.12) | collective-permute-done | bytes 32800 | tf_op jit(solution)/shard_map/ppermute | solution.py:246
  29.8 0.5 %collective-permute-done.13.refs_1_ = bf16[128,128]{1,0:T(8,128)(2,1)S(1)} collective-permute-done((bf16[128,128]{1,0:T(8,128)(2,1)S(1)}, bf16[128,128]{1,0:T(8,128)(2,1)S(1)}, u32[]{:S(2)}, u32[]{:S(2)}) %collective-permute-start.13) | collective-permute-done | bytes 32800 | tf_op jit(solution)/shard_map/ppermute | solution.py:246
  30.9 1.5 %collective-permute-start.16 = (bf16[128,128]{1,0:T(8,128)(2,1)S(1)}, bf16[128,128]{1,0:T(8,128)(2,1)S(1)}, u32[]{:S(2)}, u32[]{:S(2)}) collective-permute-start(bf16[128,128]{1,0:T(8,128)(2,1)S(1)} %add_convert_fusion), channel_id=1, source_target_pairs={{0,16},{2,18},{4,20},{6,22},{8,24},{10,26},{12,28},{14,30},{16,8},... | collective-permute-start | bytes 98312 | tf_op jit(solution)/shard_map/ppermute | solution.py:258
  32.4 1.1 %collective-permute-start.17 = (bf16[128,128]{1,0:T(8,128)(2,1)S(1)}, bf16[128,128]{1,0:T(8,128)(2,1)S(1)}, u32[]{:S(2)}, u32[]{:S(2)}) collective-permute-start(bf16[128,128]{1,0:T(8,128)(2,1)S(1)} %add_convert_fusion), channel_id=1, source_target_pairs={{0,16},{2,18},{4,20},{6,22},{8,24},{10,26},{12,28},{14,30},{16,0},... | collective-permute-start | bytes 98312 | tf_op jit(solution)/shard_map/ppermute | solution.py:258
  33.5 1.8 %collective-permute-start.18 = (bf16[128,128]{1,0:T(8,128)(2,1)S(1)}, bf16[128,128]{1,0:T(8,128)(2,1)S(1)}, u32[]{:S(2)}, u32[]{:S(2)}) collective-permute-start(bf16[128,128]{1,0:T(8,128)(2,1)S(1)} %add_convert_fusion), channel_id=1, source_target_pairs={{0,8},{2,10},{4,12},{6,14},{8,0},{10,2},{12,4},{14,6},{16,24},{18,... | collective-permute-start | bytes 98312 | tf_op jit(solution)/shard_map/ppermute | solution.py:258
  35.3 2.0 %shard_map.81 = (bf16[256,512]{1,0:T(8,128)(2,1)}, bf16[256,512]{1,0:T(8,128)(2,1)}, f32[256,512]{1,0:T(8,128)S(1)}, f32[256,512]{1,0:T(8,128)S(1)}) custom-call(bf16[256,512]{1,0:T(8,128)(2,1)S(1)} %copy-done.2, bf16[256,512]{1,0:T(8,128)(2,1)S(1)} %copy-done, bf16[256,512]{1,0:T(8,128)(2,1)S(1)} %copy-done.1, ...), custom_call_target="tpu_custom_call" | custom-call | flops 301989888 | bytes 3803136 | tf_op jit(solution)/shard_map/pallas_call | solution.py:71
  37.5 0.6 %collective-permute-done.18.refs_6_ = bf16[128,128]{1,0:T(8,128)(2,1)S(1)} collective-permute-done((bf16[128,128]{1,0:T(8,128)(2,1)S(1)}, bf16[128,128]{1,0:T(8,128)(2,1)S(1)}, u32[]{:S(2)}, u32[]{:S(2)}) %collective-permute-start.18) | collective-permute-done | bytes 32800 | tf_op jit(solution)/shard_map/ppermute | solution.py:258
  38.3 1.7 %collective-permute-start.22 = (bf16[128,128]{1,0:T(8,128)(2,1)S(1)}, bf16[128,128]{1,0:T(8,128)(2,1)S(1)}, u32[]{:S(2)}, u32[]{:S(2)}) collective-permute-start(bf16[128,128]{1,0:T(8,128)(2,1)S(1)} %get-tuple-element.65), channel_id=1, source_target_pairs={{0,5},{1,2},{2,7},{3,4},{4,1},{5,6},{6,3},{7,0},{8,13},{9,10},{10,... | collective-permute-start | bytes 98312 | tf_op jit(solution)/shard_map/ppermute | solution.py:246
  40.0 0.6 %collective-permute-start.19 = (bf16[128,128]{1,0:T(8,128)(2,1)S(1)}, bf16[128,128]{1,0:T(8,128)(2,1)S(1)}, u32[]{:S(2)}, u32[]{:S(2)}) collective-permute-start(bf16[128,128]{1,0:T(8,128)(2,1)S(1)} %get-tuple-element.62), channel_id=1, source_target_pairs={{0,3},{1,6},{2,1},{3,0},{4,7},{5,2},{6,5},{7,4},{8,11},{9,14},{10,... | collective-permute-start | bytes 98312 | tf_op jit(solution)/shard_map/ppermute | solution.py:246
  40.6 1.0 %collective-permute-start.20 = (bf16[128,128]{1,0:T(8,128)(2,1)S(1)}, bf16[128,128]{1,0:T(8,128)(2,1)S(1)}, u32[]{:S(2)}, u32[]{:S(2)}) collective-permute-start(bf16[128,128]{1,0:T(8,128)(2,1)S(1)} %get-tuple-element.63), channel_id=1, source_target_pairs={{0,1},{1,0},{2,3},{3,2},{4,5},{5,4},{6,7},{7,6},{8,9},{9,8},{10,11... | collective-permute-start | bytes 98312 | tf_op jit(solution)/shard_map/ppermute | solution.py:246
  41.6 1.2 %collective-permute-done.22.p1 = bf16[128,128]{1,0:T(8,128)(2,1)S(1)} collective-permute-done((bf16[128,128]{1,0:T(8,128)(2,1)S(1)}, bf16[128,128]{1,0:T(8,128)(2,1)S(1)}, u32[]{:S(2)}, u32[]{:S(2)}) %collective-permute-start.22) | collective-permute-done | bytes 32800 | tf_op jit(solution)/shard_map/ppermute | solution.py:246
  43.4 1.0 %shard_map.84 = (bf16[256,512]{1,0:T(8,128)(2,1)}, bf16[256,512]{1,0:T(8,128)(2,1)}) custom-call(bf16[256,512]{1,0:T(8,128)(2,1)S(1)} %copy-done, bf16[256,512]{1,0:T(8,128)(2,1)S(1)} %copy-done.1, f32[256,512]{1,0:T(8,128)S(1)} %get-tuple-element.56.refs_7_.key_local, f32[256,512]{1,0:T(8,128)S(1)} %get-tuple-element.57.value_local, ...), custom_call_target="tpu_custom_call" | custom-call | flops 33554432 | bytes 2424832 | tf_op jit(solution)/shard_map/pallas_call | solution.py:71
  (35 shorter events, 3.7 us)
Async XLA Ops:
  0.6 20.0 %copy-start.1 = (bf16[256,512]{1,0:T(8,128)(2,1)S(1)}, bf16[256,512]{1,0:T(8,128)(2,1)}, u32[]{:S(2)}) copy-start(bf16[256,512]{1,0:T(8,128)(2,1)} %v_ref.9) | copy-start | bytes 786436
  0.6 19.9 %copy-start.2 = (bf16[256,512]{1,0:T(8,128)(2,1)S(1)}, bf16[256,512]{1,0:T(8,128)(2,1)}, u32[]{:S(2)}) copy-start(bf16[256,512]{1,0:T(8,128)(2,1)} %q_ref.5) | copy-start | bytes 786436
  2.1 18.5 %copy-start = (bf16[256,512]{1,0:T(8,128)(2,1)S(1)}, bf16[256,512]{1,0:T(8,128)(2,1)}, u32[]{:S(2)}) copy-start(bf16[256,512]{1,0:T(8,128)(2,1)} %k_ref.9) | copy-start | bytes 786436
  2.1 5.1 %collective-permute-start = (bf16[128,128]{1,0:T(8,128)(2,1)S(1)}, bf16[128,128]{1,0:T(8,128)(2,1)S(1)}, u32[]{:S(2)}, u32[]{:S(2)}) collective-permute-start(bf16[128,128]{1,0:T(8,128)(2,1)S(1)} %get-tuple-element.38), channel_id=1, source_target_pairs={{0,7},{1,2},{2,5},{3,4},{4,3},{5,6},{6,1},{7,0},{8,15},{9,10},{10,... | collective-permute-start | bytes 98312 | tf_op jit(solution)/shard_map/ppermute | solution.py:246
  5.5 3.6 %collective-permute-start.1 = (bf16[128,128]{1,0:T(8,128)(2,1)S(1)}, bf16[128,128]{1,0:T(8,128)(2,1)S(1)}, u32[]{:S(2)}, u32[]{:S(2)}) collective-permute-start(bf16[128,128]{1,0:T(8,128)(2,1)S(1)} %get-tuple-element.39), channel_id=1, source_target_pairs={{0,3},{1,6},{2,1},{3,0},{4,7},{5,2},{6,5},{7,4},{8,11},{9,14},{10,... | collective-permute-start | bytes 98312 | tf_op jit(solution)/shard_map/ppermute | solution.py:246
  6.3 3.6 %collective-permute-start.2 = (bf16[128,128]{1,0:T(8,128)(2,1)S(1)}, bf16[128,128]{1,0:T(8,128)(2,1)S(1)}, u32[]{:S(2)}, u32[]{:S(2)}) collective-permute-start(bf16[128,128]{1,0:T(8,128)(2,1)S(1)} %get-tuple-element.40), channel_id=1, source_target_pairs={{0,5},{1,4},{2,7},{3,6},{4,1},{5,0},{6,3},{7,2},{8,13},{9,12},{10,... | collective-permute-start | bytes 98312 | tf_op jit(solution)/shard_map/ppermute | solution.py:246
  7.2 2.7 %collective-permute-start.3 = (bf16[128,128]{1,0:T(8,128)(2,1)S(1)}, bf16[128,128]{1,0:T(8,128)(2,1)S(1)}, u32[]{:S(2)}, u32[]{:S(2)}) collective-permute-start(bf16[128,128]{1,0:T(8,128)(2,1)S(1)} %get-tuple-element.41), channel_id=1, source_target_pairs={{0,1},{1,0},{2,3},{3,2},{4,5},{5,4},{6,7},{7,6},{8,9},{9,8},{10,11... | collective-permute-start | bytes 98312 | tf_op jit(solution)/shard_map/ppermute | solution.py:246
  9.9 5.2 %collective-permute-start.4 = (bf16[128,128]{1,0:T(8,128)(2,1)S(1)}, bf16[128,128]{1,0:T(8,128)(2,1)S(1)}, u32[]{:S(2)}, u32[]{:S(2)}) collective-permute-start(bf16[128,128]{1,0:T(8,128)(2,1)S(1)} %add_convert_fusion.1), channel_id=1, source_target_pairs={{0,16},{2,18},{4,20},{6,22},{8,24},{10,26},{12,28},{14,30},{16,0},... | collective-permute-start | bytes 98312 | tf_op jit(solution)/shard_map/ppermute | solution.py:258
  12.6 5.1 %collective-permute-start.5 = (bf16[128,128]{1,0:T(8,128)(2,1)S(1)}, bf16[128,128]{1,0:T(8,128)(2,1)S(1)}, u32[]{:S(2)}, u32[]{:S(2)}) collective-permute-start(bf16[128,128]{1,0:T(8,128)(2,1)S(1)} %add_convert_fusion.1), channel_id=1, source_target_pairs={{0,24},{2,26},{4,28},{6,30},{8,16},{10,18},{12,20},{14,22},{16,0},... | collective-permute-start | bytes 98312 | tf_op jit(solution)/shard_map/ppermute | solution.py:258
  13.9 4.1 %collective-permute-start.6 = (bf16[128,128]{1,0:T(8,128)(2,1)S(1)}, bf16[128,128]{1,0:T(8,128)(2,1)S(1)}, u32[]{:S(2)}, u32[]{:S(2)}) collective-permute-start(bf16[128,128]{1,0:T(8,128)(2,1)S(1)} %add_convert_fusion.1), channel_id=1, source_target_pairs={{0,8},{2,10},{4,12},{6,14},{8,0},{10,2},{12,4},{14,6},{16,24},{18,... | collective-permute-start | bytes 98312 | tf_op jit(solution)/shard_map/ppermute | solution.py:258
  18.1 3.7 %collective-permute-start.7 = (bf16[128,128]{1,0:T(8,128)(2,1)S(1)}, bf16[128,128]{1,0:T(8,128)(2,1)S(1)}, u32[]{:S(2)}, u32[]{:S(2)}) collective-permute-start(bf16[128,128]{1,0:T(8,128)(2,1)S(1)} %get-tuple-element.42), channel_id=1, source_target_pairs={{0,7},{1,6},{2,5},{3,4},{4,3},{5,0},{6,1},{7,2},{8,15},{9,14},{10,... | collective-permute-start | bytes 98312 | tf_op jit(solution)/shard_map/ppermute | solution.py:246
  18.2 4.3 %collective-permute-start.8 = (bf16[128,128]{1,0:T(8,128)(2,1)S(1)}, bf16[128,128]{1,0:T(8,128)(2,1)S(1)}, u32[]{:S(2)}, u32[]{:S(2)}) collective-permute-start(bf16[128,128]{1,0:T(8,128)(2,1)S(1)} %get-tuple-element.43), channel_id=1, source_target_pairs={{0,5},{1,4},{2,7},{3,6},{4,1},{5,2},{6,3},{7,0},{8,13},{9,12},{10,... | collective-permute-start | bytes 98312 | tf_op jit(solution)/shard_map/ppermute | solution.py:246
  19.9 3.6 %collective-permute-start.9 = (bf16[128,128]{1,0:T(8,128)(2,1)S(1)}, bf16[128,128]{1,0:T(8,128)(2,1)S(1)}, u32[]{:S(2)}, u32[]{:S(2)}) collective-permute-start(bf16[128,128]{1,0:T(8,128)(2,1)S(1)} %get-tuple-element.45), channel_id=1, source_target_pairs={{0,3},{1,2},{2,1},{3,0},{4,7},{5,6},{6,5},{7,4},{8,11},{9,10},{10,... | collective-permute-start | bytes 98312 | tf_op jit(solution)/shard_map/ppermute | solution.py:246
  20.0 2.5 %copy-start.3 = (bf16[256,512]{1,0:T(8,128)(2,1)S(1)}, bf16[256,512]{1,0:T(8,128)(2,1)}, u32[]{:S(2)}) copy-start(bf16[256,512]{1,0:T(8,128)(2,1)} %c_ref.3) | copy-start | bytes 786436
  20.0 3.5 %collective-permute-start.10 = (bf16[128,128]{1,0:T(8,128)(2,1)S(1)}, bf16[128,128]{1,0:T(8,128)(2,1)S(1)}, u32[]{:S(2)}, u32[]{:S(2)}) collective-permute-start(bf16[128,128]{1,0:T(8,128)(2,1)S(1)} %get-tuple-element.46), channel_id=1, source_target_pairs={{0,1},{1,0},{2,3},{3,2},{4,5},{5,4},{6,7},{7,6},{8,9},{9,8},{10,11... | collective-permute-start | bytes 98312 | tf_op jit(solution)/shard_map/ppermute | solution.py:246
  23.9 1.2 %collective-permute-start.11 = (f32[2,256]{1,0:T(2,128)S(1)}, f32[2,256]{1,0:T(2,128)S(1)}, u32[]{:S(2)}, u32[]{:S(2)}) collective-permute-start(f32[2,256]{1,0:T(2,128)S(1)} %get-tuple-element.51), channel_id=1, source_target_pairs={{0,1},{1,0},{2,3},{3,2},{4,5},{5,4},{6,7},{7,6},{8,9},{9,8},{10,11... | collective-permute-start | bytes 6152 | tf_op jit(solution)/shard_map/ppermute | solution.py:236
  25.5 4.3 %collective-permute-start.12 = (bf16[128,128]{1,0:T(8,128)(2,1)S(1)}, bf16[128,128]{1,0:T(8,128)(2,1)S(1)}, u32[]{:S(2)}, u32[]{:S(2)}) collective-permute-start(bf16[128,128]{1,0:T(8,128)(2,1)S(1)} %get-tuple-element.58), channel_id=1, source_target_pairs={{0,7},{1,6},{2,5},{3,4},{4,3},{5,2},{6,1},{7,0},{8,15},{9,14},{10,... | collective-permute-start | bytes 98312 | tf_op jit(solution)/shard_map/ppermute | solution.py:246
  26.2 4.1 %collective-permute-start.13 = (bf16[128,128]{1,0:T(8,128)(2,1)S(1)}, bf16[128,128]{1,0:T(8,128)(2,1)S(1)}, u32[]{:S(2)}, u32[]{:S(2)}) collective-permute-start(bf16[128,128]{1,0:T(8,128)(2,1)S(1)} %get-tuple-element.59), channel_id=1, source_target_pairs={{0,5},{1,2},{2,7},{3,0},{4,1},{5,6},{6,3},{7,4},{8,13},{9,10},{10,... | collective-permute-start | bytes 98312 | tf_op jit(solution)/shard_map/ppermute | solution.py:246
  27.2 3.6 %collective-permute-start.14 = (bf16[128,128]{1,0:T(8,128)(2,1)S(1)}, bf16[128,128]{1,0:T(8,128)(2,1)S(1)}, u32[]{:S(2)}, u32[]{:S(2)}) collective-permute-start(bf16[128,128]{1,0:T(8,128)(2,1)S(1)} %get-tuple-element.60), channel_id=1, source_target_pairs={{0,3},{1,4},{2,1},{3,6},{4,7},{5,0},{6,5},{7,2},{8,11},{9,12},{10,... | collective-permute-start | bytes 98312 | tf_op jit(solution)/shard_map/ppermute | solution.py:246
  28.0 2.8 %collective-permute-start.15 = (bf16[128,128]{1,0:T(8,128)(2,1)S(1)}, bf16[128,128]{1,0:T(8,128)(2,1)S(1)}, u32[]{:S(2)}, u32[]{:S(2)}) collective-permute-start(bf16[128,128]{1,0:T(8,128)(2,1)S(1)} %get-tuple-element.61), channel_id=1, source_target_pairs={{0,1},{1,0},{2,3},{3,2},{4,5},{5,4},{6,7},{7,6},{8,9},{9,8},{10,11... | collective-permute-start | bytes 98312 | tf_op jit(solution)/shard_map/ppermute | solution.py:246
  30.9 6.5 %collective-permute-start.16 = (bf16[128,128]{1,0:T(8,128)(2,1)S(1)}, bf16[128,128]{1,0:T(8,128)(2,1)S(1)}, u32[]{:S(2)}, u32[]{:S(2)}) collective-permute-start(bf16[128,128]{1,0:T(8,128)(2,1)S(1)} %add_convert_fusion), channel_id=1, source_target_pairs={{0,16},{2,18},{4,20},{6,22},{8,24},{10,26},{12,28},{14,30},{16,8},... | collective-permute-start | bytes 98312 | tf_op jit(solution)/shard_map/ppermute | solution.py:258
  32.4 5.1 %collective-permute-start.17 = (bf16[128,128]{1,0:T(8,128)(2,1)S(1)}, bf16[128,128]{1,0:T(8,128)(2,1)S(1)}, u32[]{:S(2)}, u32[]{:S(2)}) collective-permute-start(bf16[128,128]{1,0:T(8,128)(2,1)S(1)} %add_convert_fusion), channel_id=1, source_target_pairs={{0,16},{2,18},{4,20},{6,22},{8,24},{10,26},{12,28},{14,30},{16,0},... | collective-permute-start | bytes 98312 | tf_op jit(solution)/shard_map/ppermute | solution.py:258
  33.5 4.6 %collective-permute-start.18 = (bf16[128,128]{1,0:T(8,128)(2,1)S(1)}, bf16[128,128]{1,0:T(8,128)(2,1)S(1)}, u32[]{:S(2)}, u32[]{:S(2)}) collective-permute-start(bf16[128,128]{1,0:T(8,128)(2,1)S(1)} %add_convert_fusion), channel_id=1, source_target_pairs={{0,8},{2,10},{4,12},{6,14},{8,0},{10,2},{12,4},{14,6},{16,24},{18,... | collective-permute-start | bytes 98312 | tf_op jit(solution)/shard_map/ppermute | solution.py:258
  38.2 3.4 %collective-permute-start.21 = (bf16[128,128]{1,0:T(8,128)(2,1)S(1)}, bf16[128,128]{1,0:T(8,128)(2,1)S(1)}, u32[]{:S(2)}, u32[]{:S(2)}) collective-permute-start(bf16[128,128]{1,0:T(8,128)(2,1)S(1)} %get-tuple-element.64), channel_id=1, source_target_pairs={{0,7},{1,4},{2,5},{3,6},{4,3},{5,0},{6,1},{7,2},{8,15},{9,12},{10,... | collective-permute-start | bytes 98312 | tf_op jit(solution)/shard_map/ppermute | solution.py:246
  38.3 4.5 %collective-permute-start.22 = (bf16[128,128]{1,0:T(8,128)(2,1)S(1)}, bf16[128,128]{1,0:T(8,128)(2,1)S(1)}, u32[]{:S(2)}, u32[]{:S(2)}) collective-permute-start(bf16[128,128]{1,0:T(8,128)(2,1)S(1)} %get-tuple-element.65), channel_id=1, source_target_pairs={{0,5},{1,2},{2,7},{3,4},{4,1},{5,6},{6,3},{7,0},{8,13},{9,10},{10,... | collective-permute-start | bytes 98312 | tf_op jit(solution)/shard_map/ppermute | solution.py:246
  40.0 3.3 %collective-permute-start.19 = (bf16[128,128]{1,0:T(8,128)(2,1)S(1)}, bf16[128,128]{1,0:T(8,128)(2,1)S(1)}, u32[]{:S(2)}, u32[]{:S(2)}) collective-permute-start(bf16[128,128]{1,0:T(8,128)(2,1)S(1)} %get-tuple-element.62), channel_id=1, source_target_pairs={{0,3},{1,6},{2,1},{3,0},{4,7},{5,2},{6,5},{7,4},{8,11},{9,14},{10,... | collective-permute-start | bytes 98312 | tf_op jit(solution)/shard_map/ppermute | solution.py:246
  40.6 2.8 %collective-permute-start.20 = (bf16[128,128]{1,0:T(8,128)(2,1)S(1)}, bf16[128,128]{1,0:T(8,128)(2,1)S(1)}, u32[]{:S(2)}, u32[]{:S(2)}) collective-permute-start(bf16[128,128]{1,0:T(8,128)(2,1)S(1)} %get-tuple-element.63), channel_id=1, source_target_pairs={{0,1},{1,0},{2,3},{3,2},{4,5},{5,4},{6,7},{7,6},{8,9},{9,8},{10,11... | collective-permute-start | bytes 98312 | tf_op jit(solution)/shard_map/ppermute | solution.py:246
